TPU v7x, 256 devices: a whole 4x4x8 slice. The times are simulated.
256 devices in a mesh: batch: 16 (over z, core), proto: 16 (over y, x).
Axes of the slice: x: 4, y: 4, z: 8, core: 2. Of those that a mesh axis runs over, the one named last changes fastest.
Arguments:
- teacher_feats: bfloat16 [64, 256, 256], P('batch'), may hold values from -64 to 64
- student_feats: bfloat16 [64, 256, 256], P('batch'), may hold values from -64 to 64
- prototypes: bfloat16 [256, 65536], P(None, 'proto'), may hold values from -1 to 1
- mask_index: int32 [64, 128], P('batch'), may hold values from 0 to 255, as said below
Outputs:
- grad_student: float32 [64, 256, 256], P('batch')
- grad_protos: float32 [256, 65536], P('batch', 'proto')
Inputs may be any that keep to these rules, and one draw needn't show every extreme that they name: `mask_index`: within each image the 128 indices are distinct.
All inputs are finite; a program needn't handle non-finite values.
Results may differ from a plain program's by a relative error of at most 0.0083.
Values sent between devices are 32-bit elements; how exact they have to be, the bound alone decides.
No kernel may reach another device: no remote copies, remote signals or barrier semaphores. Data moves between devices by JAX's collectives and lax.ppermute only.
A program may use at most 64 MiB of HBM per device.

v0:
```python
import jax
import jax.numpy as jnp
from jax import lax
from jax.sharding import PartitionSpec as P

ITERS = 3


TEACHER_TEMP = 0.04
STUDENT_TEMP = 0.1
EPSILON = 1e-06


def token_total(values):
    return lax.psum(values, "proto")


def on_device(teacher_feats, student_feats, prototypes, mask_index):
    width = prototypes.shape[0]
    picks = mask_index[:, :, None]
    teacher_rows = (
        jnp.take_along_axis(teacher_feats, picks, axis=1).reshape(-1, width).astype(jnp.float32)
    )
    student_rows = (
        jnp.take_along_axis(student_feats, picks, axis=1).reshape(-1, width).astype(jnp.float32)
    )
    teacher_norm = jnp.sqrt(jnp.sum(teacher_rows * teacher_rows, axis=1, keepdims=True) + EPSILON)
    teacher_unit = (teacher_rows / teacher_norm).astype(jnp.bfloat16)
    student_norm = jnp.sqrt(jnp.sum(student_rows * student_rows, axis=1, keepdims=True) + EPSILON)
    student_full = student_rows / student_norm
    student_unit = student_full.astype(jnp.bfloat16)
    proto_float = prototypes.astype(jnp.float32)
    proto_norm = jnp.sqrt(jnp.sum(proto_float * proto_float, axis=0, keepdims=True) + EPSILON)
    proto_full = proto_float / proto_norm
    proto_unit = proto_full.astype(jnp.bfloat16)
    teacher_exp = jnp.exp(
        jnp.dot(teacher_unit, proto_unit, preferred_element_type=jnp.float32) / TEACHER_TEMP
    )
    cosine = jnp.dot(student_unit, proto_unit, preferred_element_type=jnp.float32)
    student_exp = jnp.exp(cosine / STUDENT_TEMP)
    local_mass = jnp.sum(student_exp, axis=1)
    row_scale = jnp.ones((teacher_exp.shape[0],), jnp.float32)
    col_scale = jnp.ones((teacher_exp.shape[1],), jnp.float32)
    for sweep in range(ITERS):
        column_local = jnp.dot(row_scale, teacher_exp, precision=lax.Precision.HIGHEST)
        col_scale = 1.0 / lax.psum(column_local, "batch")
        row_local = jnp.dot(teacher_exp, col_scale, precision=lax.Precision.HIGHEST)
        row_total = token_total(row_local)
        row_scale = 1.0 / row_total
    mass = lax.psum(local_mass, "proto")
    targets = row_scale[:, None] * teacher_exp * col_scale[None, :]
    probs = student_exp / mass[:, None]
    diff = ((probs - targets) / STUDENT_TEMP).astype(jnp.bfloat16)
    grad_z = lax.psum(jnp.dot(diff, proto_unit.T, preferred_element_type=jnp.float32), "proto")
    row_proj = jnp.sum(student_full * grad_z, axis=1, keepdims=True)
    grad_rows = (grad_z - student_full * row_proj) / student_norm
    image_count = teacher_feats.shape[0]
    image_index = jnp.arange(image_count, dtype=jnp.int32)[:, None]
    grad_student = jnp.zeros(teacher_feats.shape, jnp.float32)
    grad_student = grad_student.at[image_index, mask_index].set(
        grad_rows.reshape(image_count, -1, width)
    )
    share = width // lax.axis_size("batch")
    first_row = lax.axis_index("batch") * share
    local_grad = lax.dot_general(
        student_unit, diff, (((0,), (0,)), ((), ())), preferred_element_type=jnp.float32
    )
    grad_pn = lax.psum(local_grad, "batch")
    col_proj = jnp.sum(proto_unit.astype(jnp.float32) * grad_pn, axis=0, keepdims=True)
    grad_whole = (grad_pn - proto_full * col_proj) / proto_norm
    grad_protos = lax.dynamic_slice_in_dim(grad_whole, first_row, share, 0)
    return (grad_student, grad_protos)


def solution(mesh):
    in_specs = (P("batch", None, None), P("batch", None, None), P(None, "proto"), P("batch", None))
    out_specs = (P("batch", None, None), P("batch", "proto"))
    return jax.shard_map(
        on_device, mesh=mesh, in_specs=in_specs, out_specs=out_specs, check_vma=False
    )
```

profile of v0, /device:TPU:1, one launch (start us, length us, event | category | flops | bytes accessed | tf_op | source)
XLA Modules:
  0.0 563.5 jit_solution(996597212281688358)
XLA Ops:
  7.2 0.8 fusion.13
  8.1 0.7 and_bitcast_fusion
  8.8 3.2 gather_fusion.1
  11.9 7.0 %gather_fusion = bf16[512,256]{1,0:T(8,128)(2,1)S(1)} fusion(bf16[4,256,256]{2,1,0:T(8,128)(2,1)} %param.7, s32[512]{0:T(512)S(1)} %get-tuple-element.9), kind=kCustom, calls=%fused_computation.clone | custom fusion | bytes 528384 | tf_op jit(solution)/shard_map/jit(take_along_axis)/gather | solution.py:25
  19.1 0.4 multiply_reduce_fusion.3
  19.5 0.4 fusion.1
  20.0 0.2 fusion.2
  20.2 1.4 multiply_exponential_fusion
  21.6 4.0 fusion.16
  25.6 48.8 %psum.64 = f32[4096]{0:T(1024)S(1)} all-reduce(f32[4096]{0:T(1024)S(1)} %bitcast.64), channel_id=1, replica_groups=mesh['batch'=16,'proto'=16] {'batch'}, use_global_device_ids=true, to_apply=%region_5.0 | all-reduce | flops 4096 | bytes 32768 | tf_op jit(solution)/shard_map/psum | solution.py:46
  74.4 9.4 %fusion.24 = f32[1,512]{1,0:T(1,128)S(1)} fusion(f32[512,4096]{1,0:T(8,128)} %copy-done.1, f32[4096,1]{0,1:T(1,128)S(1)} %bitcast.60), kind=kOutput, calls=%fused_computation.56 | convolution fusion | flops 25165824 | bytes 8407040 | tf_op jit(solution)/shard_map/dot_general | solution.py:47
  83.9 33.7 %psum.65 = f32[512]{0:T(512)S(1)} all-reduce(f32[512]{0:T(512)S(1)} %bitcast.66), channel_id=1, replica_groups=mesh['batch'=16,'proto'=16] {'proto'}, use_global_device_ids=true, to_apply=%region_6.0 | all-reduce | flops 512 | bytes 4096 | tf_op jit(solution)/shard_map/psum | solution.py:15
  117.6 6.3 %fusion.25 = f32[1,4096]{1,0:T(1,128)S(1)} fusion(f32[512,1]{0,1:T(1,128)S(1)} %bitcast.67, f32[512,4096]{1,0:T(8,128)} %copy-done.1), kind=kOutput, calls=%fused_computation.57 | convolution fusion | flops 25165824 | bytes 8407040 | tf_op jit(solution)/shard_map/dot_general | solution.py:45
  124.0 52.8 %psum.66 = f32[4096]{0:T(1024)S(1)} all-reduce(f32[4096]{0:T(1024)S(1)} %bitcast.61), channel_id=1, replica_groups=mesh['batch'=16,'proto'=16] {'batch'}, use_global_device_ids=true, to_apply=%region_7.0 | all-reduce | flops 4096 | bytes 32768 | tf_op jit(solution)/shard_map/psum | solution.py:46
  176.8 9.4 %fusion.26 = f32[1,512]{1,0:T(1,128)S(1)} fusion(f32[512,4096]{1,0:T(8,128)} %copy-done.1, f32[4096,1]{0,1:T(1,128)S(1)} %bitcast.62), kind=kOutput, calls=%fused_computation.58 | convolution fusion | flops 25165824 | bytes 8407040 | tf_op jit(solution)/shard_map/dot_general | solution.py:47
  186.2 28.5 %psum.67 = f32[512]{0:T(512)S(1)} all-reduce(f32[512]{0:T(512)S(1)} %bitcast.68), channel_id=1, replica_groups=mesh['batch'=16,'proto'=16] {'proto'}, use_global_device_ids=true, to_apply=%region_8.0 | all-reduce | flops 512 | bytes 4096 | tf_op jit(solution)/shard_map/psum | solution.py:15
  214.7 6.3 %fusion.27 = f32[1,4096]{1,0:T(1,128)S(1)} fusion(f32[512,1]{0,1:T(1,128)S(1)} %bitcast.69, f32[512,4096]{1,0:T(8,128)} %copy-done.1), kind=kOutput, calls=%fused_computation.59 | convolution fusion | flops 25165824 | bytes 8407040 | tf_op jit(solution)/shard_map/dot_general | solution.py:45
  221.0 52.9 %psum.68 = f32[4096]{0:T(1024)S(1)} all-reduce(f32[4096]{0:T(1024)S(1)} %bitcast.63), channel_id=1, replica_groups=mesh['batch'=16,'proto'=16] {'batch'}, use_global_device_ids=true, to_apply=%region_9.0 | all-reduce | flops 4096 | bytes 32768 | tf_op jit(solution)/shard_map/psum | solution.py:46
  273.9 9.4 %fusion.28 = f32[1,512]{1,0:T(1,128)S(1)} fusion(f32[512,4096]{1,0:T(8,128)} %copy-done.1, f32[4096,1]{0,1:T(1,128)S(1)} %bitcast.59), kind=kOutput, calls=%fused_computation.60 | convolution fusion | flops 25165824 | bytes 8407040 | tf_op jit(solution)/shard_map/dot_general | solution.py:47
  283.4 5.0 fusion
  288.3 30.3 %all-reduce = (f32[512]{0:T(512)S(1)}, f32[512]{0:T(512)S(1)}) all-reduce(f32[512]{0:T(512)S(1)} %bitcast.65, f32[512]{0:T(512)S(1)} %get-tuple-element.13), channel_id=1, replica_groups=mesh['batch'=16,'proto'=16] {'proto'}, use_global_device_ids=true, to_apply=%region_10.0 | all-reduce | flops 1024 | bytes 8192 | tf_op jit(solution)/shard_map/psum | solution.py:15
  318.7 7.2 %multiply_convert_fusion = bf16[512,4096]{1,0:T(8,128)(2,1)S(1)} fusion(f32[512,4096]{1,0:T(8,128)} %copy-done.1, f32[512,4096]{1,0:T(8,128)} %get-tuple-element.14, f32[4096]{0:T(1024)S(1)} %broadcast_divide_fusion, f32[512]{0:T(512)S(1)} %broadcast_divide_fusion.5, f32[512]{0:T(512)S(1)} %get-tuple-element.6), kind=kLoop, calls=%fused_computation.3 | loop fusion | flops 14680064 | bytes 20992000 | tf_op jit(solution)/shard_map/convert_element_type | solution.py:53
  325.9 2.0 copy-done.2
  327.9 2.2 fusion.20
  330.2 5.4 fusion.4
  335.6 91.4 %all-reduce.4.cloned.1.call-done = f32[512,256]{1,0:T(8,128)} async-done(((f32[512,256]{1,0:T(8,128)}), f32[512,256]{1,0:T(8,128)}) %all-reduce.4.cloned.1.call-update) | async-done | bytes 524304 | tf_op jit(solution)/shard_map/psum | solution.py:54
  427.1 1.2 multiply_reduce_fusion.1
  428.3 1.3 subtract_divide_fusion
  429.6 25.7 %scatter_fusion = f32[4,256,256]{2,1,0:T(8,128)S(1)} fusion(f32[4,256,256]{2,1,0:T(8,128)S(1)} %broadcast_in_dim.14, s32[512]{0:T(512)S(1)} %get-tuple-element.10, f32[512,256]{1,0:T(8,128)S(1)} %subtract_divide_fusion), kind=kCustom, calls=%fused_computation.2 | custom fusion | bytes 1576960 | tf_op jit(solution)/shard_map/scatter | solution.py:60
  455.3 95.9 %all-reduce.6.cloned.1.call-done = f32[256,4096]{1,0:T(8,128)} async-done(((f32[256,4096]{1,0:T(8,128)}), f32[256,4096]{1,0:T(8,128)}) %all-reduce.6.cloned.1.call-update) | async-done | bytes 4194320 | tf_op jit(solution)/shard_map/psum | solution.py:68
  551.2 3.7 multiply_reduce_fusion
  554.9 1.7 fusion.3
  (24 shorter events, 0.4 us)
Async XLA Ops:
  7.2 1.6 copy-start
  7.2 12.3 %copy-start.4 = (bf16[256,4096]{1,0:T(8,128)(2,1)S(1)}, bf16[256,4096]{1,0:T(8,128)(2,1)}, u32[]{:S(2)}) copy-start(bf16[256,4096]{1,0:T(8,128)(2,1)} %param.8) | copy-start | bytes 6291460
  7.2 419.9 %all-reduce.4.cloned.1.call-start = ((), (), s32[]{:S(2)}) async-start(), calls=%async_computation | async-start | bytes 1048576 | tf_op jit(solution)/shard_map/psum | solution.py:54
  21.6 4.0 copy-start.1
  325.9 2.0 copy-start.2
  330.1 221.1 %all-reduce.6.cloned.1.call-start = ((), (), s32[]{:S(2)}) async-start(), calls=%async_computation.1 | async-start | bytes 8388608 | tf_op jit(solution)/shard_map/psum | solution.py:68
  455.3 99.6 %copy-start.3 = (f32[4,256,256]{2,1,0:T(8,128)}, f32[4,256,256]{2,1,0:T(8,128)S(1)}, u32[]{:S(2)}) copy-start(f32[4,256,256]{2,1,0:T(8,128)S(1)} %scatter_fusion) | copy-start | bytes 3145732
Sparse Core Ops, SparseCore 0:
  330.2 96.7 all-reduce.3
  429.6 121.6 all-reduce.5
where the time goes:
time: 564 us; the launch traced here: 563 us
  blocking collectives  247 us (44%)
  waiting for transfers between devices  187 us (33%)
  matrix products  59 us (10%)
  local copies, waits for them, and re-layouts  37.9 us (7%)
  other arithmetic  17.8 us (3%)
  between operations  14.2 us (3%)
    psum x3, blocking collectives, on_device(): col_scale = 1.0 / lax.psum(column_local, 'batch')  154 us
    psum x1, waiting for transfers between devices, on_device(): grad_pn = lax.psum(local_grad, 'batch')  95.9 us
    psum x3, blocking collectives, token_total(): return lax.psum(values, 'proto')  92.6 us
    psum x1, waiting for transfers between devices, on_device(): lax.psum(jnp.dot(diff, proto_unit.T, preferred_element_type=jnp.float32),...  91.4 us
    dot_general x3, matrix products, on_device(): row_local = jnp.dot(teacher_exp, col_scale, precision=lax.Precision.HIGHEST)  28.3 us
    scatter x1, local copies, waits for them, and re-layouts, on_device(): grad_student.at[image_index, mask_index]  25.7 us
    dot_general x3, matrix products, on_device(): jnp.dot(row_scale, teacher_exp, precision=lax.Precision.HIGHEST)  16.7 us
  transfers between devices with their start and end apart: 2, of which 2 were waited for; matrix products, arithmetic and copies ran while one was open for 6% of the time, Pallas kernels for 0%

commit v1 on v0

v1 whole, which is shorter than its diff:
```python
import functools

import jax
import jax.numpy as jnp
from jax import lax
from jax.experimental import pallas as pl
from jax.experimental.pallas import tpu as pltpu
from jax.sharding import PartitionSpec as P

ITERS = 3
TEACHER_TEMP = 0.04
STUDENT_TEMP = 0.1
EPSILON = 1e-06
LANES = 128
Z = 8
RING = 16
WIDE = 256
MIB = 1024 * 1024
F32 = jnp.float32
BF16 = jnp.bfloat16

VMEM = pltpu.VMEM
Z_GROUPS = [[2 * z + c for z in range(Z)] for c in range(2)]
ROW_GROUPS = [[32 * z + i for i in range(32)] for z in range(Z)]


def whole():
    return pl.BlockSpec(memory_space=VMEM)


def params(vmem=24):
    return pltpu.CompilerParams(vmem_limit_bytes=vmem * MIB)


def one_hot_t(mask_row, patches, dtype):
    slots = mask_row.shape[1]
    patch = lax.broadcasted_iota(jnp.int32, (patches, slots), 0)
    return jnp.where(patch == mask_row, 1.0, 0.0).astype(dtype)


def prep_kernel(teacher_ref, student_ref, mask_ref, zt_ref, zs_ref, zsf_ref, norm_ref):
    images, patches, width = teacher_ref.shape
    slots = mask_ref.shape[1]
    for i in range(images):
        hot = one_hot_t(mask_ref[i : i + 1, :], patches, BF16)
        rows = pl.ds(i * slots, slots)

        def taken(ref):
            return lax.dot_general(
                hot, ref[i], (((0,), (0,)), ((), ())), preferred_element_type=F32
            )

        xt = taken(teacher_ref)
        t_norm = jnp.sqrt(jnp.sum(xt * xt, axis=1, keepdims=True) + EPSILON)
        zt_ref[rows, :] = (xt / t_norm).astype(BF16).astype(F32)
        xs = taken(student_ref)
        s_norm = jnp.sqrt(jnp.sum(xs * xs, axis=1, keepdims=True) + EPSILON)
        zsf = xs / s_norm
        zsf_ref[rows, :] = zsf
        zs_ref[rows, :] = zsf.astype(BF16).astype(F32)
        norm_ref[rows, :] = s_norm


def write_lanes(out_ref, value, copies, first=0):
    for i in range(value.shape[1] // LANES):
        piece = value[:, i * LANES : (i + 1) * LANES]
        for m in range(copies):
            out_ref[m, first + i : first + i + 1, :] = piece


def write_rows(out_ref, acc, first=0):
    for i in range(acc.shape[0] // LANES):
        piece = jnp.sum(acc[i * LANES : (i + 1) * LANES, :].T, axis=0, keepdims=True)
        for m in range(out_ref.shape[0]):
            out_ref[m, first + i : first + i + 1, :] = piece


def unit_protos(proto_ref):
    p = proto_ref[...].astype(F32)
    norm = jnp.sqrt(jnp.sum(p * p, axis=0, keepdims=True) + EPSILON)
    return p / norm, norm


def core_rows(where_ref, side, half):
    return pl.ds(pl.multiple_of(lax.rem(where_ref[0] + side, 2) * half, half), half)


def exp_kernel(
    where_ref, proto_ref, zt0_ref, zt1_ref, zs0_ref, zs1_ref,
    e_ref, s_ref, pn_ref, col_ref, mass_ref,
):
    step = pl.program_id(0)
    full, _ = unit_protos(proto_ref)
    unit = full.astype(BF16)
    columns = pl.ds(pl.multiple_of(step * WIDE, WIDE), WIDE)
    pn_ref[:, columns] = unit
    half = zt0_ref.shape[0]
    total = jnp.zeros((1, WIDE), F32)
    for side, (zt, zs) in enumerate(((zt0_ref, zs0_ref), (zt1_ref, zs1_ref))):
        rows = core_rows(where_ref, side, half)
        e = jnp.exp(
            jnp.dot(zt[...].astype(BF16), unit, preferred_element_type=F32)
            * (1.0 / TEACHER_TEMP)
        )
        e_ref[rows, columns] = e
        total += jnp.sum(e, axis=0, keepdims=True)
        s = jnp.exp(
            jnp.dot(zs[...].astype(BF16), unit, preferred_element_type=F32)
            * (1.0 / STUDENT_TEMP)
        )
        s_ref[rows, columns] = s
        part = sum(s[:, j * LANES : (j + 1) * LANES] for j in range(WIDE // LANES))

        @pl.when(step == 0)
        def _():
            mass_ref[rows, :] = part

        @pl.when(step > 0)
        def _():
            mass_ref[rows, :] += part

    for i in range(WIDE // LANES):
        piece = total[:, i * LANES : (i + 1) * LANES]
        for m in range(Z):
            col_ref[m, pl.ds(step * (WIDE // LANES) + i, 1), :] = piece


def row_sums(e_ref, c, acc_ref):
    tiles = c.shape[0]
    block = 64

    def body(b, carry):
        rows = pl.ds(pl.multiple_of(b * block, block), block)
        acc = jnp.zeros((block, LANES), F32)
        for j in range(tiles):
            acc += e_ref[rows, j * LANES : (j + 1) * LANES] * c[j : j + 1, :]
        acc_ref[rows, :] = acc
        return carry

    lax.fori_loop(0, e_ref.shape[0] // block, body, 0)


def row_kernel(e_ref, parts_ref, out_ref, c_ref, acc_ref):
    c = 1.0 / jnp.sum(parts_ref[...], axis=0)
    c_ref[...] = c
    row_sums(e_ref, c, acc_ref)
    write_rows(out_ref, acc_ref[...])


def row_mass_kernel(e_ref, parts_ref, mass_ref, out_ref, c_ref, acc_ref):
    row_kernel(e_ref, parts_ref, out_ref, c_ref, acc_ref)
    write_rows(out_ref, mass_ref[...], first=8)


def spread(ref, value):
    for i in range(value.shape[0]):
        ref[i * LANES : (i + 1) * LANES, :] = jnp.broadcast_to(
            value[i : i + 1, :], (LANES, LANES)
        ).T


def col_kernel(e_ref, parts_ref, out_ref, r_ref):
    spread(r_ref, 1.0 / jnp.sum(parts_ref[:, :8, :], axis=0))
    width = e_ref.shape[1]
    block = 32

    def body(b, acc):
        rows = pl.ds(pl.multiple_of(b * block, block), block)
        r = r_ref[rows, :]
        out = []
        for j in range(width // LANES):
            value = acc[j]
            tile = e_ref[rows, j * LANES : (j + 1) * LANES] * r
            for g in range(block // 8):
                value = value + tile[g * 8 : (g + 1) * 8, :]
            out.append(value)
        return tuple(out)

    zero = tuple(jnp.zeros((8, LANES), F32) for _ in range(width // LANES))
    acc = lax.fori_loop(0, e_ref.shape[0] // block, body, zero)
    for j in range(width // LANES):
        piece = jnp.sum(acc[j], axis=0, keepdims=True)
        for m in range(Z):
            out_ref[m, j : j + 1, :] = piece


def grad_kernel(
    where_ref, proto_ref, e_ref, s_ref, pn_ref, zs0_ref, zs1_ref, c_ref, parts_ref, mass_ref,
    gz_ref, rel0, rel1, rel2, rel3, rel4, rel5, rel6, rel7, r_ref, m_ref, g_ref,
):
    step = pl.program_id(0)
    outs = (rel0, rel1, rel2, rel3, rel4, rel5, rel6, rel7)

    @pl.when(step == 0)
    def _():
        spread(r_ref, 1.0 / jnp.sum(parts_ref[...], axis=0))
        spread(m_ref, 1.0 / jnp.sum(mass_ref[:, 8:, :], axis=0))

    full, norm = unit_protos(proto_ref)
    columns = pl.ds(pl.multiple_of(step * WIDE, WIDE), WIDE)
    unit = pn_ref[:, columns]
    half = zs0_ref.shape[0]
    scale = 1.0 / STUDENT_TEMP
    grad = jnp.zeros((unit.shape[0], WIDE), F32)
    for side, zs in enumerate((zs0_ref, zs1_ref)):
        rows = core_rows(where_ref, side, half)
        pieces = []
        for j in range(WIDE // LANES):
            lanes = pl.ds(pl.multiple_of(step * WIDE + j * LANES, LANES), LANES)
            c = c_ref[pl.ds(step * (WIDE // LANES) + j, 1), :]
            targets = (r_ref[rows, :] * e_ref[rows, lanes]) * c
            probs = s_ref[rows, lanes] * m_ref[rows, :]
            pieces.append(((probs - targets) * scale).astype(BF16))
        diff = jnp.concatenate(pieces, axis=1)
        grad += lax.dot_general(
            zs[...].astype(BF16), diff, (((0,), (0,)), ((), ())), preferred_element_type=F32
        )
        part = lax.dot_general(
            diff, unit, (((1,), (1,)), ((), ())), preferred_element_type=F32
        )

        kept = pl.ds(side * half, half)

        @pl.when(step == 0)
        def _():
            gz_ref[kept, :] = part

        @pl.when(step > 0)
        def _():
            gz_ref[kept, :] += part

    proj = jnp.sum(unit.astype(F32) * grad, axis=0, keepdims=True)
    g_ref[...] = (grad - full * proj) / norm
    z = where_ref[1]
    deep = g_ref.shape[0] // Z
    for j, out in enumerate(outs):
        first = pl.multiple_of(lax.rem(z + j, Z) * deep, deep)
        out[:, columns] = g_ref[pl.ds(first, deep), :]


def last_kernel(gz_ref, zsf_ref, norm_ref, mask_ref, out_ref):
    images, patches, _ = out_ref.shape
    slots = mask_ref.shape[1]
    for i in range(images):
        rows = pl.ds(i * slots, slots)
        gz = gz_ref[rows, :]
        zsf = zsf_ref[rows, :]
        proj = jnp.sum(zsf * gz, axis=1, keepdims=True)
        grad = (gz - zsf * proj) / norm_ref[rows, :]
        hot = one_hot_t(mask_ref[i : i + 1, :], patches, F32)
        out_ref[i] = jnp.dot(
            hot, grad, precision=lax.Precision.HIGHEST, preferred_element_type=F32
        )


def shape(*dims, dtype=F32):
    return jax.ShapeDtypeStruct(dims, dtype)


def hold(*dims, dtype=F32):
    return pltpu.VMEM(dims, dtype)


def call(kernel, outs, *args, scratch=(), vmem=24):
    return pl.pallas_call(
        kernel,
        out_shape=outs,
        in_specs=[whole()] * len(args),
        out_specs=[whole()] * len(outs),
        scratch_shapes=list(scratch),
        compiler_params=params(vmem),
    )(*args)


def other_core(x):
    return lax.ppermute(x, "batch", [(i, i ^ 1) for i in range(RING)])


def along_z(x, d):
    return lax.ppermute(
        x, "batch", [(i, ((i // 2 + d) % Z) * 2 + i % 2) for i in range(RING)]
    )


def all_columns(x):
    return lax.all_to_all(x, "batch", 0, 0, axis_index_groups=Z_GROUPS)


def all_rows(x):
    return lax.all_to_all(x, ("batch", "proto"), 0, 0, axis_index_groups=ROW_GROUPS)


def ring_sum(rel):
    deep = rel[0].shape[0]
    near = deep // 2
    up = along_z(rel[4][:near], 1)
    down = along_z(rel[4][near:], -1)
    up = jnp.concatenate([rel[3][:near] + up, rel[3][near:]])
    down = jnp.concatenate([rel[5][:near], rel[5][near:] + down])
    for j in (2, 1, 0):
        up = along_z(up, 1)
        down = along_z(down, -1)
        if j:
            up = rel[j] + up
            down = rel[8 - j] + down
    return rel[0] + up + down


def on_device(teacher_feats, student_feats, prototypes, mask_index):
    images, patches, width = teacher_feats.shape
    own = images * mask_index.shape[1]
    tokens = 2 * own
    wide = prototypes.shape[1] // 2
    steps = wide // WIDE
    place = lax.axis_index("batch")
    where = jnp.stack([lax.rem(place, 2), lax.div(place, 2)]).astype(jnp.int32)

    zt, zs, zsf, s_norm = call(
        prep_kernel,
        [shape(own, width), shape(own, width), shape(own, width), shape(own, 1)],
        teacher_feats, student_feats, mask_index,
    )
    zt_other = other_core(zt)
    zs_other = other_core(zs)

    proto_spec = pl.BlockSpec((width, WIDE), lambda j, w: (0, w[0] * steps + j))
    e, s, unit, col_out, mass_acc = pl.pallas_call(
        exp_kernel,
        grid_spec=pltpu.PrefetchScalarGridSpec(
            num_scalar_prefetch=1,
            grid=(steps,),
            in_specs=[proto_spec] + [whole()] * 4,
            out_specs=[whole()] * 5,
        ),
        out_shape=[
            hold(tokens, wide), hold(tokens, wide), hold(width, wide, dtype=BF16),
            shape(Z, wide // LANES, LANES), shape(tokens, LANES),
        ],
        compiler_params=params(),
    )(where, prototypes, zt, zt_other, zs, zs_other)

    r_rows = tokens // LANES
    mass = None
    for sweep in range(ITERS):
        col_parts = all_columns(col_out)
        if sweep == 0:
            row_out, c = call(
                row_mass_kernel,
                [shape(32, 2 * r_rows, LANES), shape(wide // LANES, LANES)],
                e, col_parts, mass_acc,
                scratch=[VMEM((tokens, LANES), F32)],
            )
        else:
            row_out, c = call(
                row_kernel,
                [shape(32, r_rows, LANES), shape(wide // LANES, LANES)],
                e, col_parts,
                scratch=[VMEM((tokens, LANES), F32)],
            )
        row_parts = all_rows(row_out)
        if sweep == 0:
            mass = row_parts
        if sweep < ITERS - 1:
            (col_out,) = call(
                col_kernel, [shape(Z, wide // LANES, LANES)], e, row_parts,
                scratch=[VMEM((tokens, LANES), F32)],
            )

    deep = width // Z
    gz, *rel = pl.pallas_call(
        grad_kernel,
        grid_spec=pltpu.PrefetchScalarGridSpec(
            num_scalar_prefetch=1,
            grid=(steps,),
            in_specs=[proto_spec] + [whole()] * 8,
            out_specs=[whole()] * 9,
            scratch_shapes=[
                VMEM((tokens, LANES), F32), VMEM((tokens, LANES), F32), VMEM((width, WIDE), F32),
            ],
        ),
        out_shape=[shape(tokens, width)] + [shape(deep, wide)] * 8,
        compiler_params=params(),
    )(where, prototypes, e, s, unit, zs, zs_other, c, row_parts, mass)

    gz = gz[:own] + other_core(gz[own:])
    gz = jnp.sum(lax.all_to_all(gz.reshape(RING, own // RING, width), "proto", 0, 0), axis=0)
    gz = lax.all_to_all(
        jnp.broadcast_to(gz[None], (RING, own // RING, width)), "proto", 0, 0
    ).reshape(own, width)
    (grad_student,) = call(
        last_kernel, [shape(images, patches, width)], gz, zsf, s_norm, mask_index
    )

    done = ring_sum(rel)
    core = where[0]
    keep = lax.dynamic_slice_in_dim(done, core * (deep // 2), deep // 2, 0)
    give = lax.dynamic_slice_in_dim(done, (1 - core) * (deep // 2), deep // 2, 0)
    got = other_core(give)
    grad_protos = jnp.where(
        core == 0, jnp.concatenate([keep, got], axis=1), jnp.concatenate([got, keep], axis=1)
    )
    return (grad_student, grad_protos)


def solution(mesh):
    in_specs = (P("batch", None, None), P("batch", None, None), P(None, "proto"), P("batch", None))
    out_specs = (P("batch", None, None), P("batch", "proto"))
    return jax.shard_map(
        on_device, mesh=mesh, in_specs=in_specs, out_specs=out_specs, check_vma=False
    )
```

time: 564 us -> 170 us (0.30)
  the two profiles are of different devices: /device:TPU:1 before, /device:TPU:2 now
where the time goes in v1:
time: 170 us; the launch traced here: 169 us
  blocking collectives  75.8 us (45%)
  waiting for transfers between devices  29.3 us (17%)
  Pallas kernels  25.6 us (15%)
  starting transfers between devices  23.9 us (14%)
  other arithmetic  7.03 us (4%)
  local copies, waits for them, and re-layouts  6.78 us (4%)
    all_to_all x3, blocking collectives, all_columns(): return lax.all_to_all(x, 'batch', 0, 0, axis_index_groups=Z_GROUPS)  38.1 us
    all_to_all x3, blocking collectives, all_rows(): lax.all_to_all(x, ('batch', 'proto'), 0, 0, axis_index_groups=ROW_GROUPS)  37.6 us
    ppermute x8, starting transfers between devices, along_z(): lax.ppermute(x, 'batch', [(i, (i // 2 + d) % Z * 2 + i % 2) for i in rang...  13.2 us
    ppermute x8, waiting for transfers between devices, along_z(): lax.ppermute(x, 'batch', [(i, (i // 2 + d) % Z * 2 + i % 2) for i in rang...  11.5 us
    pallas_call x1, Pallas kernels, on_device(): pl.pallas_call(grad_kernel, grid_spec=pltpu.PrefetchScalarGridSpec(num_sc...  10.3 us
    pallas_call x7, Pallas kernels, call(): pl.pallas_call(kernel, out_shape=outs, in_specs=[whole()] * len(args), ou...  8.78 us
    all_to_all x1, waiting for transfers between devices, on_device(): lax.all_to_all(jnp.broadcast_to(gz[None], (RING, own // RING, width)), 'p...  8.14 us
    all_to_all x1, waiting for transfers between devices, on_device(): lax.all_to_all(gz.reshape(RING, own // RING, width), 'proto', 0, 0)  7.55 us
  transfers between devices with their start and end apart: 14, of which 7 were waited for; matrix products, arithmetic and copies ran while one was open for 5% of the time, Pallas kernels for 0%

profile of v1, /device:TPU:2, one launch (start us, length us, event | category | flops | bytes accessed | tf_op | source)
XLA Modules:
  0.0 169.2 jit_solution(2955233246388110057)
XLA Ops:
  0.6 1.0 copy-done.2
  1.7 1.0 copy-done.3
  5.3 1.3 collective-permute-done.1.zs1_ref
  7.4 1.6 copy-done
  8.9 6.6 %shard_map.60 = (f32[1024,2048]{1,0:T(8,128)S(1)}, f32[1024,2048]{1,0:T(8,128)S(1)}, bf16[256,2048]{1,0:T(8,128)(2,1)S(1)}, f32[8,16,128]{2,1,0:T(8,128)S(1)}, f32[1024,128]{1,0:T(8,128)S(1)}) custom-call(s32[2]{0:T(128)S(1)} %pad_add_fusion.where_ref, bf16[256,4096]{1,0:T(8,128)(2,1)S(1)} %copy-done, f32[512,256]{1,0:T(8,128)S(1)} %get-tuple-element.24.zt0_ref, ...), custom_call_target="tpu_custom_call" | custom-call | tf_op jit(solution)/shard_map/pallas_call | solution.py:327
  15.5 16.6 %all_to_all.40.parts_ref = f32[8,16,128]{2,1,0:T(8,128)S(1)} all-to-all(f32[8,16,128]{2,1,0:T(8,128)S(1)} %get-tuple-element.29), channel_id=1, replica_groups={{0,32,64,96,128,160,192,224},{16,48,80,112,144,176,208,240},{1,33,65,97..., dimensions={0} | all-to-all | bytes 131072 | tf_op jit(solution)/shard_map/all_to_all | solution.py:286
  32.2 1.6 shard_map.61
  33.8 15.3 %all_to_all.41.parts_ref.mass_ref = f32[32,16,128]{2,1,0:T(8,128)S(1)} all-to-all(f32[32,16,128]{2,1,0:T(8,128)S(1)} %get-tuple-element.31), channel_id=1, replica_groups={{0,1,2,3,4,5,6,7,8,9,10,11,12,13,14,15,16,17,18,19,20,21,22,23,24,25,26..., dimensions={0} | all-to-all | bytes 524288 | tf_op jit(solution)/shard_map/all_to_all | solution.py:290
  49.0 1.1 shard_map.62
  50.2 10.8 %all_to_all.42.parts_ref = f32[8,16,128]{2,1,0:T(8,128)S(1)} all-to-all(f32[8,16,128]{2,1,0:T(8,128)S(1)} %shard_map.62), channel_id=1, replica_groups={{0,32,64,96,128,160,192,224},{16,48,80,112,144,176,208,240},{1,33,65,97..., dimensions={0} | all-to-all | bytes 131072 | tf_op jit(solution)/shard_map/all_to_all | solution.py:286
  60.9 1.3 shard_map.63
  62.2 11.1 %all_to_all.43.parts_ref = f32[32,8,128]{2,1,0:T(8,128)S(1)} all-to-all(f32[32,8,128]{2,1,0:T(8,128)S(1)} %get-tuple-element.32), channel_id=1, replica_groups={{0,1,2,3,4,5,6,7,8,9,10,11,12,13,14,15,16,17,18,19,20,21,22,23,24,25,26..., dimensions={0} | all-to-all | bytes 262144 | tf_op jit(solution)/shard_map/all_to_all | solution.py:290
  73.3 1.1 shard_map.64
  74.4 10.8 %all_to_all.44.parts_ref = f32[8,16,128]{2,1,0:T(8,128)S(1)} all-to-all(f32[8,16,128]{2,1,0:T(8,128)S(1)} %shard_map.64), channel_id=1, replica_groups={{0,32,64,96,128,160,192,224},{16,48,80,112,144,176,208,240},{1,33,65,97..., dimensions={0} | all-to-all | bytes 131072 | tf_op jit(solution)/shard_map/all_to_all | solution.py:286
  85.2 1.0 shard_map.65
  86.2 11.2 %all_to_all.45.parts_ref = f32[32,8,128]{2,1,0:T(8,128)S(1)} all-to-all(f32[32,8,128]{2,1,0:T(8,128)S(1)} %get-tuple-element.34), channel_id=1, replica_groups={{0,1,2,3,4,5,6,7,8,9,10,11,12,13,14,15,16,17,18,19,20,21,22,23,24,25,26..., dimensions={0} | all-to-all | bytes 262144 | tf_op jit(solution)/shard_map/all_to_all | solution.py:290
  97.4 10.3 %shard_map.66 = (f32[1024,256]{1,0:T(8,128)S(1)}, f32[32,2048]{1,0:T(8,128)S(1)}, f32[32,2048]{1,0:T(8,128)S(1)}, f32[32,2048]{1,0:T(8,128)S(1)}, f32[32,2048]{1...) custom-call(s32[2]{0:T(128)S(1)} %pad_add_fusion.where_ref, ...), custom_call_target="tpu_custom_call" | custom-call | tf_op jit(solution)/shard_map/pallas_call | solution.py:370
  108.3 2.7 %collective-permute-start.7 = (f32[16,2048]{1,0:T(8,128)S(1)}, f32[16,2048]{1,0:T(8,128)S(1)}, u32[]{:S(2)}, u32[]{:S(2)}) collective-permute-start(f32[16,2048]{1,0:T(8,128)S(1)} %get-tuple-element.51), channel_id=1, source_target_pairs={{0,224},{16,240},{32,0},{48,16},{64,32},{80,48},{96,64},{112,80},{... | collective-permute-start | bytes 393224 | tf_op jit(solution)/shard_map/ppermute | solution.py:280
  111.0 3.3 %collective-permute-done.3 = f32[16,2048]{1,0:T(8,128)S(1)} collective-permute-done((f32[16,2048]{1,0:T(8,128)S(1)}, f32[16,2048]{1,0:T(8,128)S(1)}, u32[]{:S(2)}, u32[]{:S(2)}) %collective-permute-start.3) | collective-permute-done | bytes 131104 | tf_op jit(solution)/shard_map/ppermute | solution.py:280
  114.5 3.3 %collective-permute-start.8 = (f32[32,2048]{1,0:T(8,128)S(1)}, f32[32,2048]{1,0:T(8,128)S(1)}, u32[]{:S(2)}, u32[]{:S(2)}) collective-permute-start(f32[32,2048]{1,0:T(8,128)S(1)} %pad_maximum_fusion.1), channel_id=1, source_target_pairs={{0,224},{16,240},{32,0},{48,16},{64,32},{80,48},{96,64},{112,80},{... | collective-permute-start | bytes 786440 | tf_op jit(solution)/shard_map/ppermute | solution.py:280
  118.7 4.3 %collective-permute-done.4 = f32[32,2048]{1,0:T(8,128)S(1)} collective-permute-done((f32[32,2048]{1,0:T(8,128)S(1)}, f32[32,2048]{1,0:T(8,128)S(1)}, u32[]{:S(2)}, u32[]{:S(2)}) %collective-permute-start.4) | collective-permute-done | bytes 262176 | tf_op jit(solution)/shard_map/ppermute | solution.py:280
  124.4 3.2 %collective-permute-start.9 = (f32[32,2048]{1,0:T(8,128)}, f32[32,2048]{1,0:T(8,128)}, u32[]{:S(2)}, u32[]{:S(2)}) collective-permute-start(f32[32,2048]{1,0:T(8,128)} %add.39), channel_id=1, source_target_pairs={{0,224},{16,240},{32,0},{48,16},{64,32},{80,48},{96,64},{112,80},{... | collective-permute-start | bytes 786440 | tf_op jit(solution)/shard_map/ppermute | solution.py:280
  127.7 3.9 %collective-permute-done.5 = f32[32,2048]{1,0:T(8,128)} collective-permute-done((f32[32,2048]{1,0:T(8,128)}, f32[32,2048]{1,0:T(8,128)}, u32[]{:S(2)}, u32[]{:S(2)}) %collective-permute-start.5) | collective-permute-done | bytes 262176 | tf_op jit(solution)/shard_map/ppermute | solution.py:280
  131.6 1.7 %add.36 = f32[32,2048]{1,0:T(8,128)} add(f32[32,2048]{1,0:T(8,128)S(1)} %get-tuple-element.39, f32[32,2048]{1,0:T(8,128)} %collective-permute-done.5) | non-fusion elementwise | flops 65536 | bytes 786432 | tf_op jit(solution)/shard_map/add | solution.py:304
  133.3 1.0 add.40
  134.3 3.3 %collective-permute-start.10 = (f32[32,2048]{1,0:T(8,128)S(1)}, f32[32,2048]{1,0:T(8,128)}, u32[]{:S(2)}, u32[]{:S(2)}) collective-permute-start(f32[32,2048]{1,0:T(8,128)S(1)} %add.40), channel_id=1, source_target_pairs={{0,224},{16,240},{32,0},{48,16},{64,32},{80,48},{96,64},{112,80},{... | collective-permute-start | bytes 786440 | tf_op jit(solution)/shard_map/ppermute | solution.py:280
  138.5 5.3 %all-to-all-start.6 = ((f32[16,32,256]{2,1,0:T(8,128)}), f32[16,32,256]{2,1,0:T(8,128)S(1)}, u32[]{:S(2)}, u32[]{:S(2)}) async-start(f32[16,32,256]{2,1,0:T(8,128)} %bitcast.2), calls=%async_computation.6 | async-start | bytes 1048576 | tf_op jit(solution)/shard_map/all_to_all | solution.py:386
  143.7 1.1 add_add_fusion
  145.0 7.6 %all-to-all-done.6 = f32[16,32,256]{2,1,0:T(8,128)S(1)} async-done(((f32[16,32,256]{2,1,0:T(8,128)}), f32[16,32,256]{2,1,0:T(8,128)S(1)}, u32[]{:S(2)}, u32[]{:S(2)}) %all-to-all-start.6) | async-done | bytes 524320 | tf_op jit(solution)/shard_map/all_to_all | solution.py:386
  153.4 4.8 %all-to-all-start.7 = ((f32[16,32,256]{2,1,0:T(8,128)}), f32[16,32,256]{2,1,0:T(8,128)S(1)}, u32[]{:S(2)}, u32[]{:S(2)}) async-start(f32[16,32,256]{2,1,0:T(8,128)} %broadcast_in_dim.2), calls=%async_computation.7 | async-start | bytes 1048576 | tf_op jit(solution)/shard_map/all_to_all | solution.py:387
  158.9 8.1 %all-to-all-done.7 = f32[16,32,256]{2,1,0:T(8,128)S(1)} async-done(((f32[16,32,256]{2,1,0:T(8,128)}), f32[16,32,256]{2,1,0:T(8,128)S(1)}, u32[]{:S(2)}, u32[]{:S(2)}) %all-to-all-start.7) | async-done | bytes 524320 | tf_op jit(solution)/shard_map/all_to_all | solution.py:387
  167.1 2.2 %shard_map.67 = f32[4,256,256]{2,1,0:T(8,128)} custom-call(f32[512,256]{1,0:T(8,128)S(1)} %bitcast.4, f32[512,256]{1,0:T(8,128)S(1)} %get-tuple-element.36.zsf_ref, f32[512,1]{1,0:T(8,128)S(1)} %copy-done.5, s32[4,128]{1,0:T(4,128)S(1)} %copy-done.7), custom_call_target="tpu_custom_call" | custom-call | tf_op jit(solution)/shard_map/pallas_call | solution.py:265
  (44 shorter events, 9.1 us)
Async XLA Ops:
  0.6 1.0 copy-start.2
  1.7 1.0 copy-start.3
  2.7 0.7 copy-start.6
  4.0 0.7 copy-start.4
  4.7 1.9 %collective-permute-start.1 = (f32[512,256]{1,0:T(8,128)S(1)}, f32[512,256]{1,0:T(8,128)S(1)}, u32[]{:S(2)}, u32[]{:S(2)}) collective-permute-start(f32[512,256]{1,0:T(8,128)S(1)} %get-tuple-element.25.zs0_ref), channel_id=1, source_target_pairs={{0,16},{16,0},{32,48},{48,32},{64,80},{80,64},{96,112},{112,96},{1... | collective-permute-start | bytes 1572872 | tf_op jit(solution)/shard_map/ppermute | solution.py:276
  4.7 2.7 %collective-permute-start = (f32[512,256]{1,0:T(8,128)S(1)}, f32[512,256]{1,0:T(8,128)S(1)}, u32[]{:S(2)}, u32[]{:S(2)}) collective-permute-start(f32[512,256]{1,0:T(8,128)S(1)} %get-tuple-element.24.zt0_ref), channel_id=1, source_target_pairs={{0,16},{16,0},{32,48},{48,32},{64,80},{80,64},{96,112},{112,96},{1... | collective-permute-start | bytes 1572872 | tf_op jit(solution)/shard_map/ppermute | solution.py:276
  7.3 1.6 copy-start
  73.3 24.0 %copy-start.1 = (bf16[256,4096]{1,0:T(8,128)(2,1)S(1)}, bf16[256,4096]{1,0:T(8,128)(2,1)}, u32[]{:S(2)}) copy-start(bf16[256,4096]{1,0:T(8,128)(2,1)} %proto_ref.3) | copy-start | bytes 6291460
  107.6 59.5 %copy-start.5 = (f32[512,1]{1,0:T(8,128)S(1)}, f32[512,1]{1,0:T(8,128)}, u32[]{:S(2)}) copy-start(f32[512,1]{1,0:T(8,128)} %copy-done.4) | copy-start | bytes 6148
  107.6 59.4 %copy-start.7 = (s32[4,128]{1,0:T(4,128)S(1)}, s32[4,128]{1,0:T(4,128)}, u32[]{:S(2)}) copy-start(s32[4,128]{1,0:T(4,128)} %mask_ref.3) | copy-start | bytes 6148
  107.7 6.6 %collective-permute-start.3 = (f32[16,2048]{1,0:T(8,128)S(1)}, f32[16,2048]{1,0:T(8,128)S(1)}, u32[]{:S(2)}, u32[]{:S(2)}) collective-permute-start(f32[16,2048]{1,0:T(8,128)S(1)} %get-tuple-element.50), channel_id=1, source_target_pairs={{0,32},{16,48},{32,64},{48,80},{64,96},{80,112},{96,128},{112,144}... | collective-permute-start | bytes 393224 | tf_op jit(solution)/shard_map/ppermute | solution.py:280
  108.3 6.1 %collective-permute-start.7 = (f32[16,2048]{1,0:T(8,128)S(1)}, f32[16,2048]{1,0:T(8,128)S(1)}, u32[]{:S(2)}, u32[]{:S(2)}) collective-permute-start(f32[16,2048]{1,0:T(8,128)S(1)} %get-tuple-element.51), channel_id=1, source_target_pairs={{0,224},{16,240},{32,0},{48,16},{64,32},{80,48},{96,64},{112,80},{... | collective-permute-start | bytes 393224 | tf_op jit(solution)/shard_map/ppermute | solution.py:280
  114.4 8.6 %collective-permute-start.4 = (f32[32,2048]{1,0:T(8,128)S(1)}, f32[32,2048]{1,0:T(8,128)S(1)}, u32[]{:S(2)}, u32[]{:S(2)}) collective-permute-start(f32[32,2048]{1,0:T(8,128)S(1)} %pad_maximum_fusion), channel_id=1, source_target_pairs={{0,32},{16,48},{32,64},{48,80},{64,96},{80,112},{96,128},{112,144}... | collective-permute-start | bytes 786440 | tf_op jit(solution)/shard_map/ppermute | solution.py:280
  114.5 9.2 %collective-permute-start.8 = (f32[32,2048]{1,0:T(8,128)S(1)}, f32[32,2048]{1,0:T(8,128)S(1)}, u32[]{:S(2)}, u32[]{:S(2)}) collective-permute-start(f32[32,2048]{1,0:T(8,128)S(1)} %pad_maximum_fusion.1), channel_id=1, source_target_pairs={{0,224},{16,240},{32,0},{48,16},{64,32},{80,48},{96,64},{112,80},{... | collective-permute-start | bytes 786440 | tf_op jit(solution)/shard_map/ppermute | solution.py:280
  118.7 19.0 %collective-permute-start.2 = (f32[512,256]{1,0:T(8,128)}, f32[512,256]{1,0:T(8,128)S(1)}, u32[]{:S(2)}, u32[]{:S(2)}) collective-permute-start(f32[512,256]{1,0:T(8,128)} %slice.25), channel_id=1, source_target_pairs={{0,16},{16,0},{32,48},{48,32},{64,80},{80,64},{96,112},{112,96},{1... | collective-permute-start | bytes 1572872 | tf_op jit(solution)/shard_map/ppermute | solution.py:276
  123.7 7.9 %collective-permute-start.5 = (f32[32,2048]{1,0:T(8,128)}, f32[32,2048]{1,0:T(8,128)}, u32[]{:S(2)}, u32[]{:S(2)}) collective-permute-start(f32[32,2048]{1,0:T(8,128)} %add.35), channel_id=1, source_target_pairs={{0,32},{16,48},{32,64},{48,80},{64,96},{80,112},{96,128},{112,144}... | collective-permute-start | bytes 786440 | tf_op jit(solution)/shard_map/ppermute | solution.py:280
  124.4 8.9 %collective-permute-start.9 = (f32[32,2048]{1,0:T(8,128)}, f32[32,2048]{1,0:T(8,128)}, u32[]{:S(2)}, u32[]{:S(2)}) collective-permute-start(f32[32,2048]{1,0:T(8,128)} %add.39), channel_id=1, source_target_pairs={{0,224},{16,240},{32,0},{48,16},{64,32},{80,48},{96,64},{112,80},{... | collective-permute-start | bytes 786440 | tf_op jit(solution)/shard_map/ppermute | solution.py:280
  133.3 10.4 %collective-permute-start.6 = (f32[32,2048]{1,0:T(8,128)}, f32[32,2048]{1,0:T(8,128)}, u32[]{:S(2)}, u32[]{:S(2)}) collective-permute-start(f32[32,2048]{1,0:T(8,128)} %add.36), channel_id=1, source_target_pairs={{0,32},{16,48},{32,64},{48,80},{64,96},{80,112},{96,128},{112,144}... | collective-permute-start | bytes 786440 | tf_op jit(solution)/shard_map/ppermute | solution.py:280
  134.3 9.5 %collective-permute-start.10 = (f32[32,2048]{1,0:T(8,128)S(1)}, f32[32,2048]{1,0:T(8,128)}, u32[]{:S(2)}, u32[]{:S(2)}) collective-permute-start(f32[32,2048]{1,0:T(8,128)S(1)} %add.40), channel_id=1, source_target_pairs={{0,224},{16,240},{32,0},{48,16},{64,32},{80,48},{96,64},{112,80},{... | collective-permute-start | bytes 786440 | tf_op jit(solution)/shard_map/ppermute | solution.py:280
  138.5 14.0 %all-to-all-start.6 = ((f32[16,32,256]{2,1,0:T(8,128)}), f32[16,32,256]{2,1,0:T(8,128)S(1)}, u32[]{:S(2)}, u32[]{:S(2)}) async-start(f32[16,32,256]{2,1,0:T(8,128)} %bitcast.2), calls=%async_computation.6 | async-start | bytes 1048576 | tf_op jit(solution)/shard_map/all_to_all | solution.py:386
  144.9 13.4 %collective-permute-start.11 = (f32[16,2048]{1,0:T(8,128)S(1)}, f32[16,2048]{1,0:T(8,128)S(1)}, u32[]{:S(2)}, u32[]{:S(2)}) collective-permute-start(f32[16,2048]{1,0:T(8,128)S(1)} %get-tuple-element.47), channel_id=1, source_target_pairs={{0,16},{16,0},{32,48},{48,32},{64,80},{80,64},{96,112},{112,96},{1... | collective-permute-start | bytes 393224 | tf_op jit(solution)/shard_map/ppermute | solution.py:276
  153.4 13.7 %all-to-all-start.7 = ((f32[16,32,256]{2,1,0:T(8,128)}), f32[16,32,256]{2,1,0:T(8,128)S(1)}, u32[]{:S(2)}, u32[]{:S(2)}) async-start(f32[16,32,256]{2,1,0:T(8,128)} %broadcast_in_dim.2), calls=%async_computation.7 | async-start | bytes 1048576 | tf_op jit(solution)/shard_map/all_to_all | solution.py:387

commit v2 on v0

v2 whole, which is shorter than its diff:
```python
import jax
import jax.numpy as jnp
from jax import lax
from jax.experimental import pallas as pl
from jax.experimental.pallas import tpu as pltpu
from jax.sharding import PartitionSpec as P

ITERS = 3
TEACHER_TEMP = 0.04
STUDENT_TEMP = 0.1
EPSILON = 1e-06
LANES = 128
Z = 8
RING = 16
ROWS = 32
WIDE = 256
MIB = 1024 * 1024
F32 = jnp.float32
BF16 = jnp.bfloat16

VMEM = pltpu.VMEM
Z_GROUPS = [[2 * z + c for z in range(Z)] for c in range(2)]
ROW_GROUPS = [[ROWS * z + i for i in range(ROWS)] for z in range(Z)]


def whole():
    return pl.BlockSpec(memory_space=VMEM)


def cost(flops, transcendentals=0, moved=0):
    return pl.CostEstimate(
        flops=flops, transcendentals=transcendentals, bytes_accessed=moved
    )


def params(vmem):
    return pltpu.CompilerParams(vmem_limit_bytes=vmem * MIB)


def call(kernel, outs, *args, scratch=(), vmem=16, cost_estimate=None):
    return pl.pallas_call(
        kernel,
        out_shape=outs,
        in_specs=[whole()] * len(args),
        out_specs=[whole()] * len(outs),
        scratch_shapes=list(scratch),
        compiler_params=params(vmem),
        cost_estimate=cost_estimate,
    )(*args)


def one_hot_t(mask_row, patches, dtype):
    slots = mask_row.shape[1]
    patch = lax.broadcasted_iota(jnp.int32, (patches, slots), 0)
    return jnp.where(patch == mask_row, 1.0, 0.0).astype(dtype)


def masked_rows(feats_ref, mask_ref):
    hot = one_hot_t(mask_ref[0], feats_ref.shape[1], BF16)
    rows = lax.dot_general(
        hot, feats_ref[0], (((0,), (0,)), ((), ())), preferred_element_type=F32
    )
    return rows, jnp.sqrt(jnp.sum(rows * rows, axis=1, keepdims=True) + EPSILON)


def teacher_kernel(feats_ref, mask_ref, unit_ref):
    rows, norm = masked_rows(feats_ref, mask_ref)
    unit_ref[...] = (rows / norm).astype(BF16).astype(F32)


def student_kernel(feats_ref, mask_ref, unit_ref, full_ref, norm_ref):
    rows, norm = masked_rows(feats_ref, mask_ref)
    full = rows / norm
    full_ref[...] = full
    unit_ref[...] = full.astype(BF16).astype(F32)
    norm_ref[...] = norm


def core_rows(where_ref, side, half):
    return pl.ds(pl.multiple_of(lax.rem(where_ref[0] + side, 2) * half, half), half)


def write_lanes(out_ref, value, row, copies):
    for m in range(copies):
        out_ref[m, pl.ds(row, 1), :] = value


def write_rows(out_ref, acc_ref):
    pieces = []
    for i in range(acc_ref.shape[0] // LANES):
        tile = acc_ref[i * LANES : (i + 1) * LANES, :].T
        pieces.append(jnp.sum(tile, axis=0, keepdims=True))
    value = jnp.concatenate(pieces, axis=0)
    for m in range(out_ref.shape[0]):
        out_ref[m] = value


def teacher_exp_kernel(
    where_ref, proto_ref, own_ref, other_ref, e_ref, full_ref, norm_ref, col_ref, rows_ref
):
    step = pl.program_id(0)
    half = own_ref.shape[0]

    @pl.when(step == 0)
    def _():
        rows_ref[core_rows(where_ref, 0, half), :] = own_ref[...].astype(BF16)
        rows_ref[core_rows(where_ref, 1, half), :] = other_ref[...].astype(BF16)

    p = proto_ref[...].astype(F32)
    norm = jnp.sqrt(jnp.sum(p * p, axis=0, keepdims=True) + EPSILON)
    full = p / norm
    unit = full.astype(BF16)
    columns = pl.ds(pl.multiple_of(step * WIDE, WIDE), WIDE)
    full_ref[:, columns] = full
    norm_ref[:, columns] = norm
    total = jnp.zeros((8, WIDE), F32)
    block = 128
    for b in range(rows_ref.shape[0] // block):
        rows = pl.ds(b * block, block)
        e = jnp.exp(
            jnp.dot(rows_ref[rows, :], unit, preferred_element_type=F32) * (1.0 / TEACHER_TEMP)
        )
        e_ref[rows, columns] = e
        for g in range(block // 8):
            total += e[g * 8 : (g + 1) * 8, :]
    total = jnp.sum(total, axis=0, keepdims=True)
    for i in range(WIDE // LANES):
        write_lanes(
            col_ref, total[:, i * LANES : (i + 1) * LANES], step * (WIDE // LANES) + i, Z
        )


def student_exp_kernel(
    where_ref, full_ref, own_ref, other_ref, s_ref, mass_ref, turned_ref, rows_ref, acc_ref
):
    step = pl.program_id(0)
    half = own_ref.shape[0]

    @pl.when(step == 0)
    def _():
        for side, ref in enumerate((own_ref, other_ref)):
            rows = core_rows(where_ref, side, half)
            rows_ref[rows, :] = ref[...].astype(BF16)
            turned_ref[:, rows] = ref[...].T.astype(BF16)
        acc_ref[...] = jnp.zeros_like(acc_ref)

    columns = pl.ds(pl.multiple_of(step * WIDE, WIDE), WIDE)
    unit = full_ref[:, columns].astype(BF16)
    block = 128
    for b in range(rows_ref.shape[0] // block):
        rows = pl.ds(b * block, block)
        s = jnp.exp(
            jnp.dot(rows_ref[rows, :], unit, preferred_element_type=F32) * (1.0 / STUDENT_TEMP)
        )
        s_ref[rows, columns] = s
        acc_ref[rows, :] += sum(s[:, j * LANES : (j + 1) * LANES] for j in range(WIDE // LANES))

    @pl.when(step == pl.num_programs(0) - 1)
    def _():
        write_rows(mass_ref, acc_ref)


def row_kernel(e_ref, parts_ref, out_ref, c_ref, acc_ref):
    c = 1.0 / jnp.sum(parts_ref[...], axis=0)
    c_ref[...] = c
    tiles = c.shape[0]
    block = 64

    def body(b, carry):
        rows = pl.ds(pl.multiple_of(b * block, block), block)
        acc = jnp.zeros((block, LANES), F32)
        for j in range(tiles):
            acc += e_ref[rows, j * LANES : (j + 1) * LANES] * c[j : j + 1, :]
        acc_ref[rows, :] = acc
        return carry

    lax.fori_loop(0, e_ref.shape[0] // block, body, 0)
    write_rows(out_ref, acc_ref)


def spread(ref, value):
    for i in range(value.shape[0]):
        ref[i * LANES : (i + 1) * LANES, :] = jnp.broadcast_to(
            value[i : i + 1, :], (LANES, LANES)
        ).T


def col_kernel(e_ref, parts_ref, out_ref, r_ref):
    spread(r_ref, 1.0 / jnp.sum(parts_ref[...], axis=0))
    tiles = e_ref.shape[1] // LANES
    block = 32

    def body(b, acc):
        rows = pl.ds(pl.multiple_of(b * block, block), block)
        r = r_ref[rows, :]
        out = []
        for j in range(tiles):
            value = acc[j]
            tile = e_ref[rows, j * LANES : (j + 1) * LANES] * r
            for g in range(block // 8):
                value = value + tile[g * 8 : (g + 1) * 8, :]
            out.append(value)
        return tuple(out)

    zero = tuple(jnp.zeros((8, LANES), F32) for _ in range(tiles))
    acc = lax.fori_loop(0, e_ref.shape[0] // block, body, zero)
    value = jnp.concatenate([jnp.sum(a, axis=0, keepdims=True) for a in acc], axis=0)
    for m in range(Z):
        out_ref[m] = value


def diff_kernel(part):
    def kernel(
        where_ref, e_ref, s_ref, full_ref, norm_ref, turned_ref, c_ref, parts_ref, mass_ref,
        diff_ref, rel0, rel1, rel2, rel3, rel4, rel5, rel6, rel7, r_ref, m_ref, g_ref,
    ):
        step = pl.program_id(0)
        outs = (rel0, rel1, rel2, rel3, rel4, rel5, rel6, rel7)

        @pl.when(step == 0)
        def _():
            spread(r_ref, 1.0 / jnp.sum(parts_ref[...], axis=0))
            spread(m_ref, 1.0 / jnp.sum(mass_ref[...], axis=0))

        first = part * rel0.shape[1] + step * WIDE
        columns = pl.ds(pl.multiple_of(first, WIDE), WIDE)
        here = pl.ds(pl.multiple_of(step * WIDE, WIDE), WIDE)
        block = 128
        for j in range(WIDE // LANES):
            lanes = pl.ds(pl.multiple_of(first + j * LANES, LANES), LANES)
            inside = pl.ds(pl.multiple_of(step * WIDE + j * LANES, LANES), LANES)
            tile = part * (rel0.shape[1] // LANES) + step * (WIDE // LANES) + j
            c = c_ref[pl.ds(tile, 1), :]
            for b in range(e_ref.shape[0] // block):
                rows = pl.ds(b * block, block)
                targets = (r_ref[rows, :] * e_ref[rows, lanes]) * c
                probs = s_ref[rows, lanes] * m_ref[rows, :]
                diff_ref[rows, inside] = ((probs - targets) * (1.0 / STUDENT_TEMP)).astype(BF16)
        grad = jnp.dot(turned_ref[...], diff_ref[:, here], preferred_element_type=F32)
        full = full_ref[:, columns]
        proj = jnp.sum(full.astype(BF16).astype(F32) * grad, axis=0, keepdims=True)
        g_ref[...] = (grad - full * proj) / norm_ref[:, columns]
        core, z = where_ref[0], where_ref[1]
        deep = g_ref.shape[0] // Z
        near = deep // 2
        for j, out in enumerate(outs):
            top = lax.rem(z + j, Z) * deep
            for side in range(2):
                take = pl.multiple_of(top + lax.rem(core + side, 2) * near, near)
                out[side * near : (side + 1) * near, here] = g_ref[pl.ds(take, near), :]

    return kernel


def token_grad_kernel(diff0_ref, diff1_ref, full_ref, out_ref):
    half = diff0_ref.shape[1]
    block = out_ref.shape[1]
    dims = (((1,), (1,)), ((), ()))
    unit0 = full_ref[:, :half].astype(BF16)
    unit1 = full_ref[:, half:].astype(BF16)
    for m in range(out_ref.shape[0] // 8):
        rows = pl.ds(m * 8 * block, 8 * block)
        grad = lax.dot_general(diff0_ref[rows, :], unit0, dims, preferred_element_type=F32)
        grad += lax.dot_general(diff1_ref[rows, :], unit1, dims, preferred_element_type=F32)
        for i in range(8):
            out_ref[m * 8 + i] = grad[i * block : (i + 1) * block, :]


def share_kernel(parts_ref, out_ref):
    total = jnp.sum(parts_ref[...], axis=0)
    for m in range(out_ref.shape[0]):
        out_ref[m] = total


def last_kernel(gz_ref, zsf_ref, norm_ref, mask_ref, out_ref):
    zsf = zsf_ref[...]
    gz = gz_ref[...]
    proj = jnp.sum(zsf * gz, axis=1, keepdims=True)
    grad = (gz - zsf * proj) / norm_ref[...]
    hot = one_hot_t(mask_ref[0], out_ref.shape[1], BF16)
    total = jnp.zeros(out_ref.shape[1:], F32)
    for _ in range(3):
        piece = grad.astype(BF16)
        total += jnp.dot(hot, piece, preferred_element_type=F32)
        grad = grad - piece.astype(F32)
    out_ref[0] = total


def first_sum_kernel(rel_ref, got_ref, top_ref):
    near = got_ref.shape[0]
    top_ref[:near, :] = rel_ref[:near, :] + got_ref[...]
    top_ref[near:, :] = rel_ref[near:, :]


def first_sum_low_kernel(rel_ref, got_ref, top_ref):
    near = got_ref.shape[0]
    top_ref[:near, :] = rel_ref[:near, :]
    top_ref[near:, :] = rel_ref[near:, :] + got_ref[...]


def sum_kernel(rel_ref, got_ref, out_ref):
    out_ref[...] = rel_ref[...] + got_ref[...]


def last_sum_kernel(rel_ref, up_ref, down_ref, keep_ref, give_ref):
    near = keep_ref.shape[0]
    keep_ref[...] = rel_ref[:near, :] + up_ref[:near, :] + down_ref[:near, :]
    give_ref[...] = rel_ref[near:, :] + up_ref[near:, :] + down_ref[near:, :]


def place_kernel(where_ref, keep0_ref, keep1_ref, got0_ref, got1_ref, out_ref):
    core = where_ref[0]
    half = keep0_ref.shape[1]
    for side, pair in enumerate(((keep0_ref, keep1_ref), (got0_ref, got1_ref))):
        first = lax.rem(core + side, 2) * 2 * half
        for i, ref in enumerate(pair):
            out_ref[:, pl.ds(pl.multiple_of(first + i * half, half), half)] = ref[...]


def shape(*dims, dtype=F32):
    return jax.ShapeDtypeStruct(dims, dtype)


def hold(*dims, dtype=F32):
    return pltpu.VMEM(dims, dtype)


def other_core(x):
    return lax.ppermute(x, "batch", [(i, i ^ 1) for i in range(RING)])


def along_z(x, d):
    return lax.ppermute(
        x, "batch", [(i, ((i // 2 + d) % Z) * 2 + i % 2) for i in range(RING)]
    )


def all_columns(x):
    return lax.all_to_all(x, "batch", 0, 0, axis_index_groups=Z_GROUPS)


def all_rows(x):
    return lax.all_to_all(x, ("batch", "proto"), 0, 0, axis_index_groups=ROW_GROUPS)


def tie(x, y):
    return lax.optimization_barrier((x, y))[0]


def on_device(teacher_feats, student_feats, prototypes, mask_index):
    images, patches, width = teacher_feats.shape
    slots = mask_index.shape[1]
    own = images * slots
    tokens = 2 * own
    wide = prototypes.shape[1] // 2
    steps = wide // WIDE
    lane_tiles = wide // LANES
    place = lax.axis_index("batch")
    where = jnp.stack([lax.rem(place, 2), lax.div(place, 2)]).astype(jnp.int32)
    mask = mask_index.reshape(images, 1, slots)

    feats_spec = pl.BlockSpec((1, patches, width), lambda i: (i, 0, 0))
    mask_spec = pl.BlockSpec((1, 1, slots), lambda i: (i, 0, 0))
    rows_spec = pl.BlockSpec((slots, width), lambda i: (i, 0))
    norm_spec = pl.BlockSpec((slots, 1), lambda i: (i, 0))
    zt = pl.pallas_call(
        teacher_kernel,
        grid=(images,),
        in_specs=[feats_spec, mask_spec],
        out_specs=rows_spec,
        out_shape=shape(own, width),
        compiler_params=params(16),
    )(teacher_feats, mask)
    zt_other = other_core(zt)
    zs, zsf, s_norm = pl.pallas_call(
        student_kernel,
        grid=(images,),
        in_specs=[feats_spec, mask_spec],
        out_specs=[rows_spec, rows_spec, norm_spec],
        out_shape=[shape(own, width), shape(own, width), shape(own, 1)],
        compiler_params=params(16),
    )(student_feats, mask)
    zs_other = other_core(zs)

    e, full, p_norm, col_out = pl.pallas_call(
        teacher_exp_kernel,
        grid_spec=pltpu.PrefetchScalarGridSpec(
            num_scalar_prefetch=1,
            grid=(steps,),
            in_specs=[pl.BlockSpec((width, WIDE), lambda j, w: (0, w[0] * steps + j))]
            + [whole()] * 2,
            out_specs=[whole()] * 4,
            scratch_shapes=[VMEM((tokens, width), BF16)],
        ),
        out_shape=[
            hold(tokens, wide), hold(width, wide), hold(1, wide), shape(Z, lane_tiles, LANES),
        ],
        compiler_params=params(16),
        cost_estimate=cost(2 * tokens * wide * width, tokens * wide),
    )(where, prototypes, zt, zt_other)

    s, mass_out, turned = pl.pallas_call(
        student_exp_kernel,
        grid_spec=pltpu.PrefetchScalarGridSpec(
            num_scalar_prefetch=1,
            grid=(steps,),
            in_specs=[whole()] * 3,
            out_specs=[whole()] * 3,
            scratch_shapes=[VMEM((tokens, width), BF16), VMEM((tokens, LANES), F32)],
        ),
        out_shape=[
            hold(tokens, wide), shape(ROWS, tokens // LANES, LANES),
            hold(width, tokens, dtype=BF16),
        ],
        compiler_params=params(16),
        cost_estimate=cost(2 * tokens * wide * width, tokens * wide),
    )(where, full, zs, zs_other)

    mass = None
    for sweep in range(ITERS):
        col_parts = all_columns(col_out)
        if sweep == 0:
            col_parts, mass_out = lax.optimization_barrier((col_parts, mass_out))
            mass = all_rows(mass_out)
        row_out, c = call(
            row_kernel,
            [shape(ROWS, tokens // LANES, LANES), shape(lane_tiles, LANES)],
            e, col_parts,
            scratch=[VMEM((tokens, LANES), F32)],
        )
        row_parts = all_rows(row_out)
        if sweep < ITERS - 1:
            (col_out,) = call(
                col_kernel, [shape(Z, lane_tiles, LANES)], e, row_parts,
                scratch=[VMEM((tokens, LANES), F32)],
            )

    deep = width // Z
    near = deep // 2
    half = wide // 2
    diffs, rels = [], []
    for part in range(2):
        diff, *rel = pl.pallas_call(
            diff_kernel(part),
            grid_spec=pltpu.PrefetchScalarGridSpec(
                num_scalar_prefetch=1,
                grid=(steps // 2,),
                in_specs=[whole()] * 8,
                out_specs=[whole()] * 9,
                scratch_shapes=[
                    VMEM((tokens, LANES), F32), VMEM((tokens, LANES), F32),
                    VMEM((width, WIDE), F32),
                ],
            ),
            out_shape=[hold(tokens, half, dtype=BF16)] + [hold(deep, half)] * 8,
            compiler_params=params(16),
            cost_estimate=cost(tokens * wide * width),
        )(where, e, s, full, p_norm, turned, c, row_parts, mass)
        diffs.append(diff)
        rels.append(rel)

    (gz_out,) = call(
        token_grad_kernel, [shape(ROWS, tokens // ROWS, width)], *diffs, full,
        cost_estimate=cost(2 * tokens * wide * width),
    )
    gz_parts = all_rows(gz_out)
    (gz_share,) = call(share_kernel, [shape(RING, own // RING, width)], gz_parts)
    gz = lax.all_to_all(gz_share, "proto", 0, 0).reshape(own, width)
    grad_student = pl.pallas_call(
        last_kernel,
        grid=(images,),
        in_specs=[rows_spec, rows_spec, norm_spec, mask_spec],
        out_specs=feats_spec,
        out_shape=shape(images, patches, width),
        compiler_params=params(16),
    )(gz, zsf, s_norm, mask)

    ups = [along_z(rel[4][:near], 1) for rel in rels]
    downs = [along_z(rel[4][near:], -1) for rel in rels]
    part_shape = [hold(deep, half)]
    ups = [along_z(call(first_sum_kernel, part_shape, r[3], u)[0], 1) for r, u in zip(rels, ups)]
    downs = [
        along_z(call(first_sum_low_kernel, part_shape, r[5], d)[0], -1)
        for r, d in zip(rels, downs)
    ]
    for j in (2, 1):
        ups = [along_z(call(sum_kernel, part_shape, r[j], u)[0], 1) for r, u in zip(rels, ups)]
        downs = [
            along_z(call(sum_kernel, part_shape, r[8 - j], d)[0], -1)
            for r, d in zip(rels, downs)
        ]
    keeps, gots = [], []
    for rel, up, down in zip(rels, ups, downs):
        keep, give = call(last_sum_kernel, [hold(near, half)] * 2, rel[0], up, down)
        keeps.append(keep)
        gots.append(other_core(give))
    grad_protos = pl.pallas_call(
        place_kernel,
        grid_spec=pltpu.PrefetchScalarGridSpec(
            num_scalar_prefetch=1,
            grid=(1,),
            in_specs=[whole()] * 4,
            out_specs=whole(),
        ),
        out_shape=shape(near, 2 * wide),
        compiler_params=params(16),
    )(where, *keeps, *gots)
    return (grad_student, grad_protos)


def solution(mesh):
    in_specs = (P("batch", None, None), P("batch", None, None), P(None, "proto"), P("batch", None))
    out_specs = (P("batch", None, None), P("batch", "proto"))
    return jax.shard_map(
        on_device, mesh=mesh, in_specs=in_specs, out_specs=out_specs, check_vma=False
    )
```

time: 564 us -> 205 us (0.36)
  blocking collectives: 247 us -> 62.8 us
  waiting for transfers between devices: 187 us -> 21.7 us
  matrix products: 59 us -> 0 us
  starting transfers between devices: 0.08 us -> 46.5 us
  Pallas kernels: 0 us -> 35.2 us
  other arithmetic: 17.8 us -> 0.07 us
  between operations: 14.2 us -> 1.06 us
    psum x6 -> x0, blocking collectives: 247 us -> none  [the longest x3 154 us: on_device(): col_scale = 1.0 / lax.psum(column_local, 'batch')]
    psum x2 -> x0, waiting for transfers between devices: 187 us -> none  [the longest x1 95.9 us: on_device(): grad_pn = lax.psum(local_grad, 'batch')]
    all_to_all x0 -> x5, blocking collectives: none -> 62.8 us  [the longest x3 39.2 us: all_rows(): lax.all_to_all(x, ('batch', 'proto'), 0, 0, axis_index_groups=ROW_GROUPS)]
    dot_general x10 -> x0, matrix products: 59 us -> none  [the longest x3 28.3 us: on_device(): row_local = jnp.dot(teacher_exp, col_scale, precision=lax.Precision.HIGHEST)]
    pallas_call x0 -> x29, Pallas kernels: none -> 35.2 us  [the longest x21 9.08 us: call(): pl.pallas_call(kernel, out_shape=outs, in_specs=[whole()] * len(args), ou...]
    unnamed x10 -> x94, local copies, waits for them, and re-layouts: 1.99 us -> 35.7 us
    ppermute x0 -> x20, starting transfers between devices: none -> 26.7 us  [the longest x16 15.5 us: along_z(): lax.ppermute(x, 'batch', [(i, (i // 2 + d) % Z * 2 + i % 2) for i in rang...]
    scatter x1 -> x0, local copies, waits for them, and re-layouts: 25.7 us -> none  [on_device(): grad_student.at[image_index, mask_index]]
  transfers between devices with their start and end apart: 2 -> 24, of which waited for: 2 -> 10; matrix products, arithmetic and copies ran while one was open for 6% -> 1% of each run, Pallas kernels for 0% -> 8%
where the time goes in v2:
time: 205 us; the launch traced here: 204 us
  blocking collectives  62.8 us (31%)
  starting transfers between devices  46.5 us (23%)
  local copies, waits for them, and re-layouts  37 us (18%)
  Pallas kernels  35.2 us (17%)
  waiting for transfers between devices  21.7 us (11%)
    all_to_all x3, blocking collectives, all_rows(): lax.all_to_all(x, ('batch', 'proto'), 0, 0, axis_index_groups=ROW_GROUPS)  39.2 us
    unnamed x94, local copies, waits for them, and re-layouts  35.7 us
    all_to_all x2, blocking collectives, all_columns(): return lax.all_to_all(x, 'batch', 0, 0, axis_index_groups=Z_GROUPS)  23.6 us
    ppermute x16, starting transfers between devices, along_z(): lax.ppermute(x, 'batch', [(i, (i // 2 + d) % Z * 2 + i % 2) for i in rang...  15.5 us
    all_to_all x2, waiting for transfers between devices, all_rows(): lax.all_to_all(x, ('batch', 'proto'), 0, 0, axis_index_groups=ROW_GROUPS)  15.4 us
    ppermute x4, starting transfers between devices, other_core(): return lax.ppermute(x, 'batch', [(i, i ^ 1) for i in range(RING)])  11.2 us
    all_to_all x2, starting transfers between devices, all_rows(): lax.all_to_all(x, ('batch', 'proto'), 0, 0, axis_index_groups=ROW_GROUPS)  9.63 us
    pallas_call x21, Pallas kernels, call(): pl.pallas_call(kernel, out_shape=outs, in_specs=[whole()] * len(args), ou...  9.08 us
  transfers between devices with their start and end apart: 24, of which 10 were waited for; matrix products, arithmetic and copies ran while one was open for 1% of the time, Pallas kernels for 8%

profile of v2, /device:TPU:1, one launch (start us, length us, event | category | flops | bytes accessed | tf_op | source)
XLA Modules:
  0.0 204.3 jit_solution(6601382520333816540)
XLA Ops:
  3.6 3.3 %collective-permute-start = (f32[512,256]{1,0:T(8,128)S(1)}, f32[512,256]{1,0:T(8,128)S(1)}, u32[]{:S(2)}, u32[]{:S(2)}) collective-permute-start(f32[512,256]{1,0:T(8,128)S(1)} %shard_map.59.own_ref), channel_id=1, source_target_pairs={{0,16},{16,0},{32,48},{48,32},{64,80},{80,64},{96,112},{112,96},{1... | collective-permute-start | bytes 1572872 | tf_op jit(solution)/shard_map/ppermute | solution.py:329
  8.7 2.2 %shard_map.61 = (f32[512,256]{1,0:T(8,128)}, f32[512,256]{1,0:T(8,128)S(1)}, f32[512,1]{1,0:T(8,128)S(1)}) custom-call(bf16[4,256,256]{2,1,0:T(8,128)(2,1)S(1)} %copy-done.7, s32[4,1,128]{2,1,0:T(1,128)S(1)} %bitcast.6), custom_call_target="tpu_custom_call" | custom-call | tf_op jit(solution)/shard_map/pallas_call | solution.py:375
  15.1 4.8 %shard_map.60 = (f32[1024,2048]{1,0:T(8,128)S(1)}, f32[256,2048]{1,0:T(8,128)S(1)}, f32[1,2048]{1,0:T(1,128)S(1)}, f32[8,16,128]{2,1,0:T(8,128)}) custom-call(s32[2]{0:T(128)S(1)} %pad_add_fusion.where_ref, bf16[256,4096]{1,0:T(8,128)(2,1)S(1)} %copy-done.44, f32[512,256]{1,0:T(8,128)S(1)} %shard_map.59.own_ref, f32[512,256]{1,0:T(8,128)S(1)} %copy-done.46), custom_call_target="tpu_custom_call" | custom-call | flops 1073741824 | tf_op jit(solution)/shard_map/pallas_call | solution.py:385
  19.9 3.4 %copy-done = f32[1024,2048]{1,0:T(8,128)} copy-done((f32[1024,2048]{1,0:T(8,128)}, f32[1024,2048]{1,0:T(8,128)S(1)}, u32[]{:S(2)}) %copy-start) | copy-done | bytes 8388632
  23.3 6.5 %all-to-all-start = ((f32[8,16,128]{2,1,0:T(8,128)}), f32[8,16,128]{2,1,0:T(8,128)S(1)}, u32[]{:S(2)}, u32[]{:S(2)}) async-start(f32[8,16,128]{2,1,0:T(8,128)} %get-tuple-element.46), calls=%async_computation | async-start | bytes 131072 | tf_op jit(solution)/shard_map/all_to_all | solution.py:339
  29.7 5.7 %shard_map.62 = (f32[1024,2048]{1,0:T(8,128)S(1)}, f32[32,8,128]{2,1,0:T(8,128)}, bf16[256,1024]{1,0:T(8,128)(2,1)S(1)}) custom-call(s32[2]{0:T(128)S(1)} %pad_add_fusion.where_ref, f32[256,2048]{1,0:T(8,128)S(1)} %get-tuple-element.41.full_ref, f32[512,256]{1,0:T(8,128)} %get-tuple-element.42.own_ref, f32[512,256]{1,0:T(8,128)} %collective-permute-done.1.other_ref), custom_call_target="tpu_custom_call" | custom-call | flops 1073741824 | tf_op jit(solution)/shard_map/pallas_call | solution.py:402
  35.4 3.3 %copy-done.4 = f32[1024,2048]{1,0:T(8,128)} copy-done((f32[1024,2048]{1,0:T(8,128)}, f32[1024,2048]{1,0:T(8,128)S(1)}, u32[]{:S(2)}) %copy-start.4) | copy-done | bytes 8388632
  38.8 3.4 %copy-done.1 = f32[1024,2048]{1,0:T(8,128)S(1)} copy-done((f32[1024,2048]{1,0:T(8,128)S(1)}, f32[1024,2048]{1,0:T(8,128)}, u32[]{:S(2)}) %copy-start.1) | copy-done | bytes 8388632
  43.5 15.2 %all_to_all.45.parts_ref = f32[32,8,128]{2,1,0:T(8,128)S(1)} all-to-all(f32[32,8,128]{2,1,0:T(8,128)S(1)} %get-tuple-element.49), channel_id=1, replica_groups={{0,1,2,3,4,5,6,7,8,9,10,11,12,13,14,15,16,17,18,19,20,21,22,23,24,25,26..., dimensions={0} | all-to-all | bytes 262144 | tf_op jit(solution)/shard_map/all_to_all | solution.py:343
  59.7 14.0 %all_to_all.46.parts_ref = f32[8,16,128]{2,1,0:T(8,128)S(1)} all-to-all(f32[8,16,128]{2,1,0:T(8,128)S(1)} %shard_map.64), channel_id=1, replica_groups={{0,32,64,96,128,160,192,224},{16,48,80,112,144,176,208,240},{1,33,65,97..., dimensions={0} | all-to-all | bytes 131072 | tf_op jit(solution)/shard_map/all_to_all | solution.py:339
  75.1 12.5 %all_to_all.47.parts_ref = f32[32,8,128]{2,1,0:T(8,128)S(1)} all-to-all(f32[32,8,128]{2,1,0:T(8,128)S(1)} %get-tuple-element.50), channel_id=1, replica_groups={{0,1,2,3,4,5,6,7,8,9,10,11,12,13,14,15,16,17,18,19,20,21,22,23,24,25,26..., dimensions={0} | all-to-all | bytes 262144 | tf_op jit(solution)/shard_map/all_to_all | solution.py:343
  88.7 9.6 %all_to_all.48.parts_ref = f32[8,16,128]{2,1,0:T(8,128)S(1)} all-to-all(f32[8,16,128]{2,1,0:T(8,128)S(1)} %shard_map.66), channel_id=1, replica_groups={{0,32,64,96,128,160,192,224},{16,48,80,112,144,176,208,240},{1,33,65,97..., dimensions={0} | all-to-all | bytes 131072 | tf_op jit(solution)/shard_map/all_to_all | solution.py:339
  98.3 5.3 %all-to-all-start.6 = ((f32[32,8,128]{2,1,0:T(8,128)}), f32[32,8,128]{2,1,0:T(8,128)S(1)}, u32[]{:S(2)}, u32[]{:S(2)}) async-start(f32[32,8,128]{2,1,0:T(8,128)} %get-tuple-element.53), calls=%async_computation.6 | async-start | bytes 262144 | tf_op jit(solution)/shard_map/all_to_all | solution.py:343
  103.6 3.4 %copy-done.2 = f32[1024,2048]{1,0:T(8,128)S(1)} copy-done((f32[1024,2048]{1,0:T(8,128)S(1)}, f32[1024,2048]{1,0:T(8,128)}, u32[]{:S(2)}) %copy-start.2) | copy-done | bytes 8388632
  107.9 3.2 %all-to-all-done.6.mass_ref = f32[32,8,128]{2,1,0:T(8,128)S(1)} async-done(((f32[32,8,128]{2,1,0:T(8,128)}), f32[32,8,128]{2,1,0:T(8,128)S(1)}, u32[]{:S(2)}, u32[]{:S(2)}) %all-to-all-start.6) | async-done | bytes 131104 | tf_op jit(solution)/shard_map/all_to_all | solution.py:343
  111.1 11.5 %all_to_all.49.parts_ref = f32[32,8,128]{2,1,0:T(8,128)S(1)} all-to-all(f32[32,8,128]{2,1,0:T(8,128)S(1)} %get-tuple-element.52), channel_id=1, replica_groups={{0,1,2,3,4,5,6,7,8,9,10,11,12,13,14,15,16,17,18,19,20,21,22,23,24,25,26..., dimensions={0} | all-to-all | bytes 262144 | tf_op jit(solution)/shard_map/all_to_all | solution.py:343
  122.6 3.4 %copy-done.3 = f32[1024,2048]{1,0:T(8,128)S(1)} copy-done((f32[1024,2048]{1,0:T(8,128)S(1)}, f32[1024,2048]{1,0:T(8,128)}, u32[]{:S(2)}) %copy-start.3) | copy-done | bytes 8388632
  126.0 3.4 %copy-done.5 = f32[1024,2048]{1,0:T(8,128)S(1)} copy-done((f32[1024,2048]{1,0:T(8,128)S(1)}, f32[1024,2048]{1,0:T(8,128)}, u32[]{:S(2)}) %copy-start.5) | copy-done | bytes 8388632
  130.0 4.2 %shard_map.69 = (bf16[1024,1024]{1,0:T(8,128)(2,1)S(1)}, f32[32,1024]{1,0:T(8,128)S(1)}, f32[32,1024]{1,0:T(8,128)S(1)}, f32[32,1024]{1,0:T(8,128)S(1)}, f32[32,...) custom-call(s32[2]{0:T(128)S(1)} %copy-done.42, ...), custom_call_target="tpu_custom_call" | custom-call | flops 536870912 | tf_op jit(solution)/shard_map/pallas_call | solution.py:443
  136.8 4.2 %shard_map.68 = (bf16[1024,1024]{1,0:T(8,128)(2,1)S(1)}, f32[32,1024]{1,0:T(8,128)S(1)}, f32[32,1024]{1,0:T(8,128)S(1)}, f32[32,1024]{1,0:T(8,128)S(1)}, f32[32,...) custom-call(s32[2]{0:T(128)S(1)} %copy-done.42, ...), custom_call_target="tpu_custom_call" | custom-call | flops 536870912 | tf_op jit(solution)/shard_map/pallas_call | solution.py:443
  145.6 2.3 %shard_map.70 = f32[32,32,256]{2,1,0:T(8,128)} custom-call(bf16[1024,1024]{1,0:T(8,128)(2,1)S(1)} %get-tuple-element.54.diff0_ref, bf16[1024,1024]{1,0:T(8,128)(2,1)S(1)} %get-tuple-element.55.diff1_ref, f32[256,2048]{1,0:T(8,128)S(1)} %get-tuple-element.41.full_ref), custom_call_target="tpu_custom_call" | custom-call | flops 1073741824 | tf_op jit(solution)/shard_map/pallas_call | solution.py:41
  147.9 4.3 %all-to-all-start.7 = ((f32[32,32,256]{2,1,0:T(8,128)}), f32[32,32,256]{2,1,0:T(8,128)S(1)}, u32[]{:S(2)}, u32[]{:S(2)}) async-start(f32[32,32,256]{2,1,0:T(8,128)} %shard_map.70), calls=%async_computation.7 | async-start | bytes 2097152 | tf_op jit(solution)/shard_map/all_to_all | solution.py:343
  156.6 12.2 %all-to-all-done.7.parts_ref = f32[32,32,256]{2,1,0:T(8,128)S(1)} async-done(((f32[32,32,256]{2,1,0:T(8,128)}), f32[32,32,256]{2,1,0:T(8,128)S(1)}, u32[]{:S(2)}, u32[]{:S(2)}) %all-to-all-start.7) | async-done | bytes 1048608 | tf_op jit(solution)/shard_map/all_to_all | solution.py:343
  169.7 3.7 %all-to-all-start.8 = ((f32[16,32,256]{2,1,0:T(8,128)}), f32[16,32,256]{2,1,0:T(8,128)S(1)}, u32[]{:S(2)}, u32[]{:S(2)}) async-start(f32[16,32,256]{2,1,0:T(8,128)} %shard_map.71), calls=%async_computation.8 | async-start | bytes 1048576 | tf_op jit(solution)/shard_map/all_to_all | solution.py:468
  177.4 2.0 collective-permute-start.16
  180.5 1.7 collective-permute-start.8
  183.4 2.2 %collective-permute-start.17 = (f32[32,1024]{1,0:T(8,128)S(1)}, f32[32,1024]{1,0:T(8,128)S(1)}, u32[]{:S(2)}, u32[]{:S(2)}) collective-permute-start(f32[32,1024]{1,0:T(8,128)S(1)} %shard_map.85), channel_id=1, source_target_pairs={{0,224},{16,240},{32,0},{48,16},{64,32},{80,48},{96,64},{112,80},{... | collective-permute-start | bytes 393224 | tf_op jit(solution)/shard_map/ppermute | solution.py:333
  185.9 3.1 %collective-permute-start.9 = (f32[32,1024]{1,0:T(8,128)S(1)}, f32[32,1024]{1,0:T(8,128)S(1)}, u32[]{:S(2)}, u32[]{:S(2)}) collective-permute-start(f32[32,1024]{1,0:T(8,128)S(1)} %shard_map.78), channel_id=1, source_target_pairs={{0,224},{16,240},{32,0},{48,16},{64,32},{80,48},{96,64},{112,80},{... | collective-permute-start | bytes 393224 | tf_op jit(solution)/shard_map/ppermute | solution.py:333
  189.4 2.3 %collective-permute-done.13.up_ref = f32[32,1024]{1,0:T(8,128)S(1)} collective-permute-done((f32[32,1024]{1,0:T(8,128)S(1)}, f32[32,1024]{1,0:T(8,128)S(1)}, u32[]{:S(2)}, u32[]{:S(2)}) %collective-permute-start.13) | collective-permute-done | bytes 131104 | tf_op jit(solution)/shard_map/ppermute | solution.py:333
  191.7 4.8 %collective-permute-start.19 = (f32[16,1024]{1,0:T(8,128)S(1)}, f32[16,1024]{1,0:T(8,128)S(1)}, u32[]{:S(2)}, u32[]{:S(2)}) collective-permute-start(f32[16,1024]{1,0:T(8,128)S(1)} %get-tuple-element.77), channel_id=1, source_target_pairs={{0,16},{16,0},{32,48},{48,32},{64,80},{80,64},{96,112},{112,96},{1... | collective-permute-start | bytes 196616 | tf_op jit(solution)/shard_map/ppermute | solution.py:329
  196.6 3.0 %collective-permute-start.18 = (f32[16,1024]{1,0:T(8,128)S(1)}, f32[16,1024]{1,0:T(8,128)S(1)}, u32[]{:S(2)}, u32[]{:S(2)}) collective-permute-start(f32[16,1024]{1,0:T(8,128)S(1)} %get-tuple-element.76), channel_id=1, source_target_pairs={{0,16},{16,0},{32,48},{48,32},{64,80},{80,64},{96,112},{112,96},{1... | collective-permute-start | bytes 196616 | tf_op jit(solution)/shard_map/ppermute | solution.py:329
  201.8 2.6 %shard_map.72 = f32[4,256,256]{2,1,0:T(8,128)} custom-call(f32[512,256]{1,0:T(8,128)S(1)} %bitcast.4, f32[512,256]{1,0:T(8,128)S(1)} %get-tuple-element.56.zsf_ref, f32[512,1]{1,0:T(8,128)S(1)} %copy-done.9, s32[4,1,128]{2,1,0:T(1,128)S(1)} %bitcast.7), custom_call_target="tpu_custom_call" | custom-call | tf_op jit(solution)/shard_map/pallas_call | solution.py:469
  (147 shorter events, 36.6 us)
Async XLA Ops:
  3.6 8.1 %collective-permute-start = (f32[512,256]{1,0:T(8,128)S(1)}, f32[512,256]{1,0:T(8,128)S(1)}, u32[]{:S(2)}, u32[]{:S(2)}) collective-permute-start(f32[512,256]{1,0:T(8,128)S(1)} %shard_map.59.own_ref), channel_id=1, source_target_pairs={{0,16},{16,0},{32,48},{48,32},{64,80},{80,64},{96,112},{112,96},{1... | collective-permute-start | bytes 1572872 | tf_op jit(solution)/shard_map/ppermute | solution.py:329
  11.6 18.1 %collective-permute-start.1 = (f32[512,256]{1,0:T(8,128)}, f32[512,256]{1,0:T(8,128)}, u32[]{:S(2)}, u32[]{:S(2)}) collective-permute-start(f32[512,256]{1,0:T(8,128)} %get-tuple-element.42.own_ref), channel_id=1, source_target_pairs={{0,16},{16,0},{32,48},{48,32},{64,80},{80,64},{96,112},{112,96},{1... | collective-permute-start | bytes 1572872 | tf_op jit(solution)/shard_map/ppermute | solution.py:329
  11.7 23.7 %copy-start.41 = (s32[2]{0:T(128)}, s32[2]{0:T(128)S(1)}, u32[]{:S(2)}) copy-start(s32[2]{0:T(128)S(1)} %pad_add_fusion.where_ref) | copy-start | bytes 28
  23.3 15.5 %all-to-all-start = ((f32[8,16,128]{2,1,0:T(8,128)}), f32[8,16,128]{2,1,0:T(8,128)S(1)}, u32[]{:S(2)}, u32[]{:S(2)}) async-start(f32[8,16,128]{2,1,0:T(8,128)} %get-tuple-element.46), calls=%async_computation | async-start | bytes 131072 | tf_op jit(solution)/shard_map/all_to_all | solution.py:339
  98.3 12.8 %all-to-all-start.6 = ((f32[32,8,128]{2,1,0:T(8,128)}), f32[32,8,128]{2,1,0:T(8,128)S(1)}, u32[]{:S(2)}, u32[]{:S(2)}) async-start(f32[32,8,128]{2,1,0:T(8,128)} %get-tuple-element.53), calls=%async_computation.6 | async-start | bytes 262144 | tf_op jit(solution)/shard_map/all_to_all | solution.py:343
  147.9 20.9 %all-to-all-start.7 = ((f32[32,32,256]{2,1,0:T(8,128)}), f32[32,32,256]{2,1,0:T(8,128)S(1)}, u32[]{:S(2)}, u32[]{:S(2)}) async-start(f32[32,32,256]{2,1,0:T(8,128)} %shard_map.70), calls=%async_computation.7 | async-start | bytes 2097152 | tf_op jit(solution)/shard_map/all_to_all | solution.py:343
  152.3 24.2 %copy-start.27 = (f32[32,1024]{1,0:T(8,128)S(1)}, f32[32,1024]{1,0:T(8,128)}, u32[]{:S(2)}) copy-start(f32[32,1024]{1,0:T(8,128)} %copy-done.26) | copy-start | bytes 393220
  153.0 20.5 %collective-permute-start.14 = (f32[16,1024]{1,0:T(8,128)}, f32[16,1024]{1,0:T(8,128)S(1)}, u32[]{:S(2)}, u32[]{:S(2)}) collective-permute-start(f32[16,1024]{1,0:T(8,128)} %get-tuple-element.78), channel_id=1, source_target_pairs={{0,224},{16,240},{32,0},{48,16},{64,32},{80,48},{96,64},{112,80},{... | collective-permute-start | bytes 196616 | tf_op jit(solution)/shard_map/ppermute | solution.py:333
  153.0 20.6 %collective-permute-start.10 = (f32[16,1024]{1,0:T(8,128)}, f32[16,1024]{1,0:T(8,128)S(1)}, u32[]{:S(2)}, u32[]{:S(2)}) collective-permute-start(f32[16,1024]{1,0:T(8,128)} %get-tuple-element.79), channel_id=1, source_target_pairs={{0,32},{16,48},{32,64},{48,80},{64,96},{80,112},{96,128},{112,144}... | collective-permute-start | bytes 196616 | tf_op jit(solution)/shard_map/ppermute | solution.py:333
  154.4 23.0 %copy-start.25 = (f32[32,1024]{1,0:T(8,128)S(1)}, f32[32,1024]{1,0:T(8,128)}, u32[]{:S(2)}) copy-start(f32[32,1024]{1,0:T(8,128)} %copy-done.24) | copy-start | bytes 393220
  155.1 20.0 %collective-permute-start.6 = (f32[16,1024]{1,0:T(8,128)}, f32[16,1024]{1,0:T(8,128)S(1)}, u32[]{:S(2)}, u32[]{:S(2)}) collective-permute-start(f32[16,1024]{1,0:T(8,128)} %get-tuple-element.80), channel_id=1, source_target_pairs={{0,224},{16,240},{32,0},{48,16},{64,32},{80,48},{96,64},{112,80},{... | collective-permute-start | bytes 196616 | tf_op jit(solution)/shard_map/ppermute | solution.py:333
  156.3 23.1 %copy-start.23 = (f32[32,1024]{1,0:T(8,128)S(1)}, f32[32,1024]{1,0:T(8,128)}, u32[]{:S(2)}) copy-start(f32[32,1024]{1,0:T(8,128)} %copy-done.22) | copy-start | bytes 393220
  156.3 24.2 %copy-start.21 = (f32[32,1024]{1,0:T(8,128)S(1)}, f32[32,1024]{1,0:T(8,128)}, u32[]{:S(2)}) copy-start(f32[32,1024]{1,0:T(8,128)} %copy-done.20) | copy-start | bytes 393220
  156.3 20.2 %collective-permute-start.2 = (f32[16,1024]{1,0:T(8,128)}, f32[16,1024]{1,0:T(8,128)S(1)}, u32[]{:S(2)}, u32[]{:S(2)}) collective-permute-start(f32[16,1024]{1,0:T(8,128)} %get-tuple-element.81), channel_id=1, source_target_pairs={{0,32},{16,48},{32,64},{48,80},{64,96},{80,112},{96,128},{112,144}... | collective-permute-start | bytes 196616 | tf_op jit(solution)/shard_map/ppermute | solution.py:333
  169.7 32.1 %all-to-all-start.8 = ((f32[16,32,256]{2,1,0:T(8,128)}), f32[16,32,256]{2,1,0:T(8,128)S(1)}, u32[]{:S(2)}, u32[]{:S(2)}) async-start(f32[16,32,256]{2,1,0:T(8,128)} %shard_map.71), calls=%async_computation.8 | async-start | bytes 1048576 | tf_op jit(solution)/shard_map/all_to_all | solution.py:468
  173.5 3.9 %collective-permute-start.15 = (f32[32,1024]{1,0:T(8,128)S(1)}, f32[32,1024]{1,0:T(8,128)S(1)}, u32[]{:S(2)}, u32[]{:S(2)}) collective-permute-start(f32[32,1024]{1,0:T(8,128)S(1)} %shard_map.83), channel_id=1, source_target_pairs={{0,224},{16,240},{32,0},{48,16},{64,32},{80,48},{96,64},{112,80},{... | collective-permute-start | bytes 393224 | tf_op jit(solution)/shard_map/ppermute | solution.py:333
  173.6 5.8 %collective-permute-start.11 = (f32[32,1024]{1,0:T(8,128)S(1)}, f32[32,1024]{1,0:T(8,128)S(1)}, u32[]{:S(2)}, u32[]{:S(2)}) collective-permute-start(f32[32,1024]{1,0:T(8,128)S(1)} %shard_map.80), channel_id=1, source_target_pairs={{0,32},{16,48},{32,64},{48,80},{64,96},{80,112},{96,128},{112,144}... | collective-permute-start | bytes 393224 | tf_op jit(solution)/shard_map/ppermute | solution.py:333
  175.1 5.4 %collective-permute-start.7 = (f32[32,1024]{1,0:T(8,128)S(1)}, f32[32,1024]{1,0:T(8,128)S(1)}, u32[]{:S(2)}, u32[]{:S(2)}) collective-permute-start(f32[32,1024]{1,0:T(8,128)S(1)} %shard_map.76), channel_id=1, source_target_pairs={{0,224},{16,240},{32,0},{48,16},{64,32},{80,48},{96,64},{112,80},{... | collective-permute-start | bytes 393224 | tf_op jit(solution)/shard_map/ppermute | solution.py:333
  176.5 24.0 %copy-start.43 = (s32[2]{0:T(128)S(1)}, s32[2]{0:T(128)}, u32[]{:S(2)}) copy-start(s32[2]{0:T(128)} %copy-done.41) | copy-start | bytes 28
  176.5 6.0 %collective-permute-start.3 = (f32[32,1024]{1,0:T(8,128)S(1)}, f32[32,1024]{1,0:T(8,128)S(1)}, u32[]{:S(2)}, u32[]{:S(2)}) collective-permute-start(f32[32,1024]{1,0:T(8,128)S(1)} %shard_map.73), channel_id=1, source_target_pairs={{0,32},{16,48},{32,64},{48,80},{64,96},{80,112},{96,128},{112,144}... | collective-permute-start | bytes 393224 | tf_op jit(solution)/shard_map/ppermute | solution.py:333
  177.4 24.4 %copy-start.9 = (f32[512,1]{1,0:T(8,128)S(1)}, f32[512,1]{1,0:T(8,128)}, u32[]{:S(2)}) copy-start(f32[512,1]{1,0:T(8,128)} %copy-done.8) | copy-start | bytes 6148
  177.4 24.4 %copy-start.40 = (s32[4,128]{1,0:T(4,128)S(1)}, s32[4,128]{1,0:T(4,128)}, u32[]{:S(2)}) copy-start(s32[4,128]{1,0:T(4,128)} %param.7) | copy-start | bytes 6148
  177.4 5.9 %collective-permute-start.16 = (f32[32,1024]{1,0:T(8,128)S(1)}, f32[32,1024]{1,0:T(8,128)S(1)}, u32[]{:S(2)}, u32[]{:S(2)}) collective-permute-start(f32[32,1024]{1,0:T(8,128)S(1)} %shard_map.84), channel_id=1, source_target_pairs={{0,224},{16,240},{32,0},{48,16},{64,32},{80,48},{96,64},{112,80},{... | collective-permute-start | bytes 393224 | tf_op jit(solution)/shard_map/ppermute | solution.py:333
  179.4 6.3 %collective-permute-start.12 = (f32[32,1024]{1,0:T(8,128)S(1)}, f32[32,1024]{1,0:T(8,128)S(1)}, u32[]{:S(2)}, u32[]{:S(2)}) collective-permute-start(f32[32,1024]{1,0:T(8,128)S(1)} %shard_map.81), channel_id=1, source_target_pairs={{0,32},{16,48},{32,64},{48,80},{64,96},{80,112},{96,128},{112,144}... | collective-permute-start | bytes 393224 | tf_op jit(solution)/shard_map/ppermute | solution.py:333
  180.5 5.3 %collective-permute-start.8 = (f32[32,1024]{1,0:T(8,128)S(1)}, f32[32,1024]{1,0:T(8,128)S(1)}, u32[]{:S(2)}, u32[]{:S(2)}) collective-permute-start(f32[32,1024]{1,0:T(8,128)S(1)} %shard_map.77), channel_id=1, source_target_pairs={{0,224},{16,240},{32,0},{48,16},{64,32},{80,48},{96,64},{112,80},{... | collective-permute-start | bytes 393224 | tf_op jit(solution)/shard_map/ppermute | solution.py:333
  182.5 6.7 %collective-permute-start.4 = (f32[32,1024]{1,0:T(8,128)S(1)}, f32[32,1024]{1,0:T(8,128)S(1)}, u32[]{:S(2)}, u32[]{:S(2)}) collective-permute-start(f32[32,1024]{1,0:T(8,128)S(1)} %shard_map.74), channel_id=1, source_target_pairs={{0,32},{16,48},{32,64},{48,80},{64,96},{80,112},{96,128},{112,144}... | collective-permute-start | bytes 393224 | tf_op jit(solution)/shard_map/ppermute | solution.py:333
  183.4 6.0 %collective-permute-start.17 = (f32[32,1024]{1,0:T(8,128)S(1)}, f32[32,1024]{1,0:T(8,128)S(1)}, u32[]{:S(2)}, u32[]{:S(2)}) collective-permute-start(f32[32,1024]{1,0:T(8,128)S(1)} %shard_map.85), channel_id=1, source_target_pairs={{0,224},{16,240},{32,0},{48,16},{64,32},{80,48},{96,64},{112,80},{... | collective-permute-start | bytes 393224 | tf_op jit(solution)/shard_map/ppermute | solution.py:333
  185.7 6.0 %collective-permute-start.13 = (f32[32,1024]{1,0:T(8,128)S(1)}, f32[32,1024]{1,0:T(8,128)S(1)}, u32[]{:S(2)}, u32[]{:S(2)}) collective-permute-start(f32[32,1024]{1,0:T(8,128)S(1)} %shard_map.82), channel_id=1, source_target_pairs={{0,32},{16,48},{32,64},{48,80},{64,96},{80,112},{96,128},{112,144}... | collective-permute-start | bytes 393224 | tf_op jit(solution)/shard_map/ppermute | solution.py:333
  185.9 10.7 %collective-permute-start.9 = (f32[32,1024]{1,0:T(8,128)S(1)}, f32[32,1024]{1,0:T(8,128)S(1)}, u32[]{:S(2)}, u32[]{:S(2)}) collective-permute-start(f32[32,1024]{1,0:T(8,128)S(1)} %shard_map.78), channel_id=1, source_target_pairs={{0,224},{16,240},{32,0},{48,16},{64,32},{80,48},{96,64},{112,80},{... | collective-permute-start | bytes 393224 | tf_op jit(solution)/shard_map/ppermute | solution.py:333
  189.3 7.3 %collective-permute-start.5 = (f32[32,1024]{1,0:T(8,128)S(1)}, f32[32,1024]{1,0:T(8,128)S(1)}, u32[]{:S(2)}, u32[]{:S(2)}) collective-permute-start(f32[32,1024]{1,0:T(8,128)S(1)} %shard_map.75), channel_id=1, source_target_pairs={{0,32},{16,48},{32,64},{48,80},{64,96},{80,112},{96,128},{112,144}... | collective-permute-start | bytes 393224 | tf_op jit(solution)/shard_map/ppermute | solution.py:333
  191.7 7.9 %collective-permute-start.19 = (f32[16,1024]{1,0:T(8,128)S(1)}, f32[16,1024]{1,0:T(8,128)S(1)}, u32[]{:S(2)}, u32[]{:S(2)}) collective-permute-start(f32[16,1024]{1,0:T(8,128)S(1)} %get-tuple-element.77), channel_id=1, source_target_pairs={{0,16},{16,0},{32,48},{48,32},{64,80},{80,64},{96,112},{112,96},{1... | collective-permute-start | bytes 196616 | tf_op jit(solution)/shard_map/ppermute | solution.py:329
  196.6 3.9 %collective-permute-start.18 = (f32[16,1024]{1,0:T(8,128)S(1)}, f32[16,1024]{1,0:T(8,128)S(1)}, u32[]{:S(2)}, u32[]{:S(2)}) collective-permute-start(f32[16,1024]{1,0:T(8,128)S(1)} %get-tuple-element.76), channel_id=1, source_target_pairs={{0,16},{16,0},{32,48},{48,32},{64,80},{80,64},{96,112},{112,96},{1... | collective-permute-start | bytes 196616 | tf_op jit(solution)/shard_map/ppermute | solution.py:329
  (39 other events, 195.4 us)

commit v3 on v2

v3 whole, which is shorter than its diff:
```python
import jax
import jax.numpy as jnp
from jax import lax
from jax.experimental import pallas as pl
from jax.experimental.pallas import tpu as pltpu
from jax.sharding import PartitionSpec as P

ITERS = 3
TEACHER_TEMP = 0.04
STUDENT_TEMP = 0.1
EPSILON = 1e-06
LANES = 128
Z = 8
RING = 16
ROWS = 32
WIDE = 1024
MIB = 1024 * 1024
F32 = jnp.float32
BF16 = jnp.bfloat16

VMEM = pltpu.VMEM
Z_GROUPS = [[2 * z + c for z in range(Z)] for c in range(2)]
ROW_GROUPS = [[ROWS * z + i for i in range(ROWS)] for z in range(Z)]


def whole():
    return pl.BlockSpec(memory_space=VMEM)


def cost(flops, transcendentals=0, moved=0):
    return pl.CostEstimate(
        flops=flops, transcendentals=transcendentals, bytes_accessed=moved
    )


def params(vmem):
    return pltpu.CompilerParams(vmem_limit_bytes=vmem * MIB)


def call(kernel, outs, *args, scratch=(), vmem=16, cost_estimate=None):
    return pl.pallas_call(
        kernel,
        out_shape=outs,
        in_specs=[whole()] * len(args),
        out_specs=[whole()] * len(outs),
        scratch_shapes=list(scratch),
        compiler_params=params(vmem),
        cost_estimate=cost_estimate,
    )(*args)


def one_hot_t(mask_row, patches, dtype):
    slots = mask_row.shape[1]
    patch = lax.broadcasted_iota(jnp.int32, (patches, slots), 0)
    return jnp.where(patch == mask_row, 1.0, 0.0).astype(dtype)


def fetch(pairs, sems):
    copies = [pltpu.make_async_copy(src, dst, sems.at[i]) for i, (src, dst) in enumerate(pairs)]
    for copy in copies:
        copy.start()
    return copies


def masked_rows(feats, mask_row):
    hot = one_hot_t(mask_row, feats.shape[0], BF16)
    rows = lax.dot_general(hot, feats, (((0,), (0,)), ((), ())), preferred_element_type=F32)
    return rows, jnp.sqrt(jnp.sum(rows * rows, axis=1, keepdims=True) + EPSILON)


def teacher_kernel(feats_hbm, mask_hbm, unit_ref, feats_ref, mask_ref, sems):
    for copy in fetch(((feats_hbm, feats_ref), (mask_hbm, mask_ref)), sems):
        copy.wait()
    slots = mask_ref.shape[1]
    for i in range(feats_ref.shape[0]):
        rows, norm = masked_rows(feats_ref[i], mask_ref[i : i + 1, :])
        unit_ref[i * slots : (i + 1) * slots, :] = (rows / norm).astype(BF16).astype(F32)


def student_kernel(
    feats_hbm, mask_hbm, unit_ref, full_ref, norm_ref, feats_ref, mask_ref, sems
):
    for copy in fetch(((feats_hbm, feats_ref), (mask_hbm, mask_ref)), sems):
        copy.wait()
    slots = mask_ref.shape[1]
    for i in range(feats_ref.shape[0]):
        take = pl.ds(i * slots, slots)
        rows, norm = masked_rows(feats_ref[i], mask_ref[i : i + 1, :])
        full = rows / norm
        full_ref[take, :] = full
        unit_ref[take, :] = full.astype(BF16).astype(F32)
        norm_ref[take, :] = norm


def proto_kernel(where_ref, proto_ref, full_ref, unit_ref, norm_ref):
    p = proto_ref[...].astype(F32)
    norm = jnp.sqrt(jnp.sum(p * p, axis=0, keepdims=True) + EPSILON)
    full = p / norm
    full_ref[...] = full
    unit_ref[...] = full.astype(BF16)
    norm_ref[...] = norm


def core_rows(where_ref, side, half):
    return pl.ds(pl.multiple_of(lax.rem(where_ref[0] + side, 2) * half, half), half)


def write_lanes(out_ref, value, row, copies):
    for m in range(copies):
        out_ref[m, pl.ds(row, 1), :] = value


def write_rows(out_ref, acc_ref, first=0):
    pieces = []
    for i in range(acc_ref.shape[0] // LANES):
        tile = acc_ref[i * LANES : (i + 1) * LANES, :].T
        pieces.append(jnp.sum(tile, axis=0, keepdims=True))
    value = jnp.concatenate(pieces, axis=0)
    for m in range(out_ref.shape[0]):
        out_ref[m, first : first + 8, :] = value


def teacher_exp_kernel(where_ref, own_ref, other_ref, unit_ref, e_ref, col_ref):
    half = own_ref.shape[0]
    wide = unit_ref.shape[1]
    block = 256
    for w in range(wide // WIDE):
        columns = pl.ds(w * WIDE, WIDE)
        unit = unit_ref[:, columns]
        total = jnp.zeros((8, WIDE), F32)
        for side, ref in enumerate((own_ref, other_ref)):
            place = core_rows(where_ref, side, half)
            for b in range(half // block):
                z = ref[b * block : (b + 1) * block, :].astype(BF16)
                e = jnp.exp(
                    jnp.dot(z, unit, preferred_element_type=F32) * (1.0 / TEACHER_TEMP)
                )
                e_ref[pl.ds(place.start + b * block, block), columns] = e
                for g in range(block // 8):
                    total += e[g * 8 : (g + 1) * 8, :]
        total = jnp.sum(total, axis=0, keepdims=True)
        for i in range(WIDE // LANES):
            write_lanes(
                col_ref, total[:, i * LANES : (i + 1) * LANES], w * (WIDE // LANES) + i, Z
            )


def student_exp_kernel(
    where_ref, own_ref, other_ref, unit_ref, s_ref, mass_ref, turned_ref
):
    half = own_ref.shape[0]
    wide = unit_ref.shape[1]
    block = 256
    for side, ref in enumerate((own_ref, other_ref)):
        turned_ref[:, core_rows(where_ref, side, half)] = ref[...].T.astype(BF16)
    for w in range(wide // WIDE):
        columns = pl.ds(w * WIDE, WIDE)
        unit = unit_ref[:, columns]
        for side, ref in enumerate((own_ref, other_ref)):
            place = core_rows(where_ref, side, half)
            for b in range(half // block):
                rows = pl.ds(place.start + b * block, block)
                z = ref[b * block : (b + 1) * block, :].astype(BF16)
                s = jnp.exp(
                    jnp.dot(z, unit, preferred_element_type=F32) * (1.0 / STUDENT_TEMP)
                )
                s_ref[rows, columns] = s
                part = sum(s[:, j * LANES : (j + 1) * LANES] for j in range(WIDE // LANES))
                if w:
                    mass_ref[rows, :] += part
                else:
                    mass_ref[rows, :] = part


def row_kernel(e_ref, parts_ref, out_ref, c_ref, acc_ref):
    c = 1.0 / jnp.sum(parts_ref[...], axis=0)
    c_ref[...] = c
    tiles = c.shape[0]
    block = 64

    def body(b, carry):
        rows = pl.ds(pl.multiple_of(b * block, block), block)
        acc = jnp.zeros((block, LANES), F32)
        for j in range(tiles):
            acc += e_ref[rows, j * LANES : (j + 1) * LANES] * c[j : j + 1, :]
        acc_ref[rows, :] = acc
        return carry

    lax.fori_loop(0, e_ref.shape[0] // block, body, 0)
    write_rows(out_ref, acc_ref)


def row_mass_kernel(e_ref, parts_ref, mass_ref, out_ref, c_ref, acc_ref):
    row_kernel(e_ref, parts_ref, out_ref, c_ref, acc_ref)
    write_rows(out_ref, mass_ref, first=8)


def spread(ref, value):
    for i in range(value.shape[0]):
        ref[i * LANES : (i + 1) * LANES, :] = jnp.broadcast_to(
            value[i : i + 1, :], (LANES, LANES)
        ).T


def col_kernel(e_ref, parts_ref, out_ref, r_ref):
    spread(r_ref, 1.0 / jnp.sum(parts_ref[:, :8, :], axis=0))
    tiles = e_ref.shape[1] // LANES
    block = 32

    def body(b, acc):
        rows = pl.ds(pl.multiple_of(b * block, block), block)
        r = r_ref[rows, :]
        out = []
        for j in range(tiles):
            value = acc[j]
            tile = e_ref[rows, j * LANES : (j + 1) * LANES] * r
            for g in range(block // 8):
                value = value + tile[g * 8 : (g + 1) * 8, :]
            out.append(value)
        return tuple(out)

    zero = tuple(jnp.zeros((8, LANES), F32) for _ in range(tiles))
    acc = lax.fori_loop(0, e_ref.shape[0] // block, body, zero)
    value = jnp.concatenate([jnp.sum(a, axis=0, keepdims=True) for a in acc], axis=0)
    for m in range(Z):
        out_ref[m] = value


def diff_kernel(part):
    def kernel(
        where_ref, e_ref, s_ref, full_ref, norm_ref, turned_ref, c_ref, parts_ref, mass_ref,
        diff_ref, rel0, rel1, rel2, rel3, rel4u, rel4d, rel5, rel6, rel7,
        r_ref, m_ref, g_ref,
    ):
        spread(r_ref, 1.0 / jnp.sum(parts_ref[...], axis=0))
        spread(m_ref, (1.0 / STUDENT_TEMP) / jnp.sum(mass_ref[:, 8:, :], axis=0))
        half = rel0.shape[1]
        tiles = half // LANES
        block = 16

        def body(b, carry):
            rows = pl.ds(pl.multiple_of(b * block, block), block)
            r = r_ref[rows, :] * (1.0 / STUDENT_TEMP)
            m = m_ref[rows, :]
            for j in range(tiles):
                tile = part * tiles + j
                lanes = slice(tile * LANES, (tile + 1) * LANES)
                targets = (r * e_ref[rows, lanes]) * c_ref[tile : tile + 1, :]
                probs = s_ref[rows, lanes] * m
                diff_ref[rows, j * LANES : (j + 1) * LANES] = (probs - targets).astype(BF16)
            return carry

        lax.fori_loop(0, e_ref.shape[0] // block, body, 0, unroll=2)
        columns = slice(part * half, (part + 1) * half)
        grad = jnp.dot(turned_ref[...], diff_ref[...], preferred_element_type=F32)
        full = full_ref[:, columns]
        proj = jnp.sum(full.astype(BF16).astype(F32) * grad, axis=0, keepdims=True)
        g_ref[...] = (grad - full * proj) / norm_ref[:, columns]
        core, z = where_ref[0], where_ref[1]
        deep = g_ref.shape[0] // Z
        near = deep // 2
        outs = (rel0, rel1, rel2, rel3, (rel4u, rel4d), rel5, rel6, rel7)
        for j, out in enumerate(outs):
            top = lax.rem(z + j, Z) * deep
            for side in range(2):
                take = pl.multiple_of(top + lax.rem(core + side, 2) * near, near)
                value = g_ref[pl.ds(take, near), :]
                if j == 4:
                    out[side][...] = value
                else:
                    out[side * near : (side + 1) * near, :] = value

    return kernel


def token_grad_kernel(where_ref, diff0_ref, diff1_ref, unit_ref, own_ref, other_ref):
    half = diff0_ref.shape[1]
    dims = (((1,), (1,)), ((), ()))
    unit0 = unit_ref[:, :half]
    unit1 = unit_ref[:, half:]
    for side, out in enumerate((own_ref, other_ref)):
        rows = core_rows(where_ref, side, out.shape[0])
        grad = lax.dot_general(diff0_ref[rows, :], unit0, dims, preferred_element_type=F32)
        out[...] = grad + lax.dot_general(
            diff1_ref[rows, :], unit1, dims, preferred_element_type=F32
        )


def share_kernel(parts_ref, out_ref):
    total = sum(parts_ref[i] for i in range(parts_ref.shape[0]))
    for m in range(out_ref.shape[0]):
        out_ref[m] = total


def last_kernel(gz_ref, zsf_ref, norm_ref, mask_ref, out_ref):
    slots = mask_ref.shape[1]
    for i in range(out_ref.shape[0]):
        rows = pl.ds(i * slots, slots)
        zsf = zsf_ref[rows, :]
        gz = gz_ref[rows, :]
        proj = jnp.sum(zsf * gz, axis=1, keepdims=True)
        grad = (gz - zsf * proj) / norm_ref[rows, :]
        hot = one_hot_t(mask_ref[i : i + 1, :], out_ref.shape[1], BF16)
        total = jnp.zeros(out_ref.shape[1:], F32)
        for _ in range(3):
            piece = grad.astype(BF16)
            total += jnp.dot(hot, piece, preferred_element_type=F32)
            grad = grad - piece.astype(F32)
        out_ref[i] = total


def first_sum_kernel(rel_ref, got_ref, top_ref):
    near = got_ref.shape[0]
    top_ref[:near, :] = rel_ref[:near, :] + got_ref[...]
    top_ref[near:, :] = rel_ref[near:, :]


def first_sum_low_kernel(rel_ref, got_ref, top_ref):
    near = got_ref.shape[0]
    top_ref[:near, :] = rel_ref[:near, :]
    top_ref[near:, :] = rel_ref[near:, :] + got_ref[...]


def sum_kernel(rel_ref, got_ref, out_ref):
    out_ref[...] = rel_ref[...] + got_ref[...]


def last_sum_kernel(rel_ref, up_ref, down_ref, keep_ref, give_ref):
    near = keep_ref.shape[0]
    keep_ref[...] = rel_ref[:near, :] + up_ref[:near, :] + down_ref[:near, :]
    give_ref[...] = rel_ref[near:, :] + up_ref[near:, :] + down_ref[near:, :]


def place_kernel(where_ref, keep0_ref, keep1_ref, got0_ref, got1_ref, out_ref):
    core = where_ref[0]
    half = keep0_ref.shape[1]
    for side, pair in enumerate(((keep0_ref, keep1_ref), (got0_ref, got1_ref))):
        first = lax.rem(core + side, 2) * 2 * half
        for i, ref in enumerate(pair):
            out_ref[:, pl.ds(pl.multiple_of(first + i * half, half), half)] = ref[...]


def shape(*dims, dtype=F32):
    return jax.ShapeDtypeStruct(dims, dtype)


def hold(*dims, dtype=F32):
    return pltpu.VMEM(dims, dtype)


def other_core(x):
    return lax.ppermute(x, "batch", [(i, i ^ 1) for i in range(RING)])


def along_z(x, d):
    return lax.ppermute(
        x, "batch", [(i, ((i // 2 + d) % Z) * 2 + i % 2) for i in range(RING)]
    )


def all_columns(x):
    return lax.all_to_all(x, "batch", 0, 0, axis_index_groups=Z_GROUPS)


def all_rows(x):
    return lax.all_to_all(x, ("batch", "proto"), 0, 0, axis_index_groups=ROW_GROUPS)


def tie(x, y):
    return lax.optimization_barrier((x, y))[0]


def on_device(teacher_feats, student_feats, prototypes, mask_index):
    images, patches, width = teacher_feats.shape
    slots = mask_index.shape[1]
    own = images * slots
    tokens = 2 * own
    wide = prototypes.shape[1] // 2
    lane_tiles = wide // LANES
    row_tiles = tokens // LANES
    place = lax.axis_index("batch")
    where = jnp.stack([lax.rem(place, 2), lax.div(place, 2)]).astype(jnp.int32)
    scalars = pl.BlockSpec(memory_space=pltpu.SMEM)

    def in_hbm(x):
        return pltpu.with_memory_space_constraint(x, pltpu.HBM)

    def prep(kernel, outs, feats):
        return pl.pallas_call(
            kernel,
            in_specs=[pl.BlockSpec(memory_space=pl.ANY)] * 2,
            out_specs=[whole()] * len(outs),
            out_shape=outs,
            scratch_shapes=[
                VMEM(feats.shape, BF16), VMEM(mask_index.shape, jnp.int32),
                pltpu.SemaphoreType.DMA((2,)),
            ],
            compiler_params=params(16),
        )(in_hbm(feats), in_hbm(mask_index))

    def placed(kernel, outs, *args, **kw):
        return pl.pallas_call(
            kernel,
            in_specs=[scalars] + [whole()] * len(args),
            out_specs=[whole()] * len(outs),
            out_shape=outs,
            scratch_shapes=kw.get("scratch", []),
            compiler_params=params(16),
            cost_estimate=kw.get("cost_estimate"),
        )(where, *args)

    (zt,) = prep(teacher_kernel, [shape(own, width)], teacher_feats)
    zt_other = other_core(zt)
    zs, zsf, s_norm = prep(
        student_kernel, [shape(own, width), shape(own, width), shape(own, 1)], student_feats
    )
    zs_other = other_core(zs)
    steps = 2
    column_spec = pl.BlockSpec((width, wide // steps), lambda j, w: (0, j))
    full, unit, p_norm = pl.pallas_call(
        proto_kernel,
        grid_spec=pltpu.PrefetchScalarGridSpec(
            num_scalar_prefetch=1,
            grid=(steps,),
            in_specs=[
                pl.BlockSpec((width, wide // steps), lambda j, w: (0, w[0] * steps + j))
            ],
            out_specs=[
                column_spec, column_spec,
                pl.BlockSpec((1, wide // steps), lambda j, w: (0, j)),
            ],
        ),
        out_shape=[shape(width, wide), shape(width, wide, dtype=BF16), shape(1, wide)],
        compiler_params=params(16),
    )(where, in_hbm(prototypes))

    exp_cost = cost(2 * tokens * wide * width, tokens * wide)
    e, col_out = placed(
        teacher_exp_kernel,
        [hold(tokens, wide), shape(Z, lane_tiles, LANES)],
        zt, zt_other, unit, cost_estimate=exp_cost,
    )
    s, mass_acc, turned = placed(
        student_exp_kernel,
        [hold(tokens, wide), shape(tokens, LANES), shape(width, tokens, dtype=BF16)],
        zs, zs_other, unit, cost_estimate=exp_cost,
    )
    col_out = tie(col_out, mass_acc)

    mass = None
    for sweep in range(ITERS):
        col_parts = all_columns(col_out)
        extra = [mass_acc] if sweep == 0 else []
        row_out, c = call(
            row_kernel if sweep else row_mass_kernel,
            [shape(ROWS, row_tiles * (1 + len(extra)), LANES), shape(lane_tiles, LANES)],
            e, col_parts, *extra,
            scratch=[VMEM((tokens, LANES), F32)],
        )
        row_parts = all_rows(row_out)
        if sweep == 0:
            mass = row_parts
        if sweep < ITERS - 1:
            (col_out,) = call(
                col_kernel, [shape(Z, lane_tiles, LANES)], e, row_parts,
                scratch=[VMEM((tokens, LANES), F32)],
            )

    deep = width // Z
    near = deep // 2
    half = wide // 2
    diffs, rels = [], []
    for part in range(2):
        diff, *rel = placed(
            diff_kernel(part),
            [shape(tokens, half, dtype=BF16)] + [shape(deep, half)] * 4
            + [shape(near, half)] * 2 + [shape(deep, half)] * 3,
            e, s, full, p_norm, turned, c, row_parts, mass,
            scratch=[
                VMEM((tokens, LANES), F32), VMEM((tokens, LANES), F32), VMEM((width, half), F32),
            ],
            cost_estimate=cost(tokens * wide * width),
        )
        diffs.append(diff)
        rels.append(rel)

    ups = [along_z(rel[4], 1) for rel in rels]
    downs = [along_z(rel[5], -1) for rel in rels]
    rels = [rel[:4] + [None] + rel[6:] for rel in rels]

    diff0 = tie(diffs[0], ups[0])
    gz, gz_give = placed(
        token_grad_kernel, [shape(own, width)] * 2, diff0, diffs[1], unit,
        cost_estimate=cost(2 * tokens * wide * width),
    )
    gz = gz + other_core(gz_give)
    gz_parts = lax.all_to_all(gz.reshape(RING, own // RING, width), "proto", 0, 0)
    (gz_share,) = call(share_kernel, [shape(RING, own // RING, width)], gz_parts)
    gz = lax.all_to_all(gz_share, "proto", 0, 0).reshape(own, width)
    (grad_student,) = call(
        last_kernel, [shape(images, patches, width)], gz, zsf, s_norm, mask_index
    )

    part_shape = [shape(deep, half)]
    ups = [along_z(call(first_sum_kernel, part_shape, r[3], u)[0], 1) for r, u in zip(rels, ups)]
    downs = [
        along_z(call(first_sum_low_kernel, part_shape, r[5], d)[0], -1)
        for r, d in zip(rels, downs)
    ]
    for j in (2, 1):
        ups = [along_z(call(sum_kernel, part_shape, r[j], u)[0], 1) for r, u in zip(rels, ups)]
        downs = [
            along_z(call(sum_kernel, part_shape, r[8 - j], d)[0], -1)
            for r, d in zip(rels, downs)
        ]
    keeps, gots = [], []
    for rel, up, down in zip(rels, ups, downs):
        keep, give = call(last_sum_kernel, [shape(near, half)] * 2, rel[0], up, down)
        keeps.append(keep)
        gots.append(other_core(give))
    (grad_protos,) = placed(place_kernel, [shape(near, 2 * wide)], *keeps, *gots)
    return (grad_student, grad_protos)


def solution(mesh):
    in_specs = (P("batch", None, None), P("batch", None, None), P(None, "proto"), P("batch", None))
    out_specs = (P("batch", None, None), P("batch", "proto"))
    return jax.shard_map(
        on_device, mesh=mesh, in_specs=in_specs, out_specs=out_specs, check_vma=False
    )
```

time: 205 us -> 159 us (0.78)
  local copies, waits for them, and re-layouts: 37 us -> 0.01 us
  blocking collectives: 62.8 us -> 74.9 us
  waiting for transfers between devices: 21.7 us -> 13.5 us
  Pallas kernels: 35.2 us -> 27.6 us
  starting transfers between devices: 46.5 us -> 40.1 us
    unnamed x94 -> x2, local copies, waits for them, and re-layouts: 35.7 us -> 0.01 us
    all_to_all x3 -> x1, starting transfers between devices: 16.1 us -> 3.57 us  [on_device(): lax.all_to_all(gz.reshape(RING, own // RING, width), 'proto', 0, 0)]
    all_to_all x2 -> x3, blocking collectives: 23.6 us -> 32.7 us  [all_columns(): return lax.all_to_all(x, 'batch', 0, 0, axis_index_groups=Z_GROUPS)]
    all_to_all x3 -> x1, waiting for transfers between devices: 15.4 us -> 7.18 us  [on_device(): lax.all_to_all(gz.reshape(RING, own // RING, width), 'proto', 0, 0)]
    pallas_call x8 -> x9, Pallas kernels: 26.2 us -> 18.7 us  [the longest x6 13.5 us: placed(): pl.pallas_call(kernel, in_specs=[scalars] + [whole()] * len(args), out_sp...]
    ppermute x16, starting transfers between devices: 15.5 us -> 19.9 us  [along_z(): lax.ppermute(x, 'batch', [(i, (i // 2 + d) % Z * 2 + i % 2) for i in rang...]
    all_to_all x3, blocking collectives: 39.2 us -> 42.2 us  [all_rows(): lax.all_to_all(x, ('batch', 'proto'), 0, 0, axis_index_groups=ROW_GROUPS)]
    ppermute x4 -> x5, starting transfers between devices: 11.2 us -> 13 us  [other_core(): return lax.ppermute(x, 'batch', [(i, i ^ 1) for i in range(RING)])]
  transfers between devices with their start and end apart: 24 -> 23, of which waited for: 10 -> 8; matrix products, arithmetic and copies ran while one was open for 1% -> 0% of each run, Pallas kernels for 8% -> 7%
where the time goes in v3:
time: 159 us; the launch traced here: 158 us
  blocking collectives  74.9 us (47%)
  starting transfers between devices  40.1 us (25%)
  Pallas kernels  27.6 us (17%)
  waiting for transfers between devices  13.5 us (8%)
    all_to_all x3, blocking collectives, all_rows(): lax.all_to_all(x, ('batch', 'proto'), 0, 0, axis_index_groups=ROW_GROUPS)  42.2 us
    all_to_all x3, blocking collectives, all_columns(): return lax.all_to_all(x, 'batch', 0, 0, axis_index_groups=Z_GROUPS)  32.7 us
    ppermute x16, starting transfers between devices, along_z(): lax.ppermute(x, 'batch', [(i, (i // 2 + d) % Z * 2 + i % 2) for i in rang...  19.9 us
    pallas_call x6, Pallas kernels, placed(): pl.pallas_call(kernel, in_specs=[scalars] + [whole()] * len(args), out_sp...  13.5 us
    ppermute x5, starting transfers between devices, other_core(): return lax.ppermute(x, 'batch', [(i, i ^ 1) for i in range(RING)])  13 us
    pallas_call x21, Pallas kernels, call(): pl.pallas_call(kernel, out_shape=outs, in_specs=[whole()] * len(args), ou...  8.87 us
    all_to_all x1, waiting for transfers between devices, on_device(): lax.all_to_all(gz.reshape(RING, own // RING, width), 'proto', 0, 0)  7.18 us
    ppermute x16, waiting for transfers between devices, along_z(): lax.ppermute(x, 'batch', [(i, (i // 2 + d) % Z * 2 + i % 2) for i in rang...  3.88 us
  transfers between devices with their start and end apart: 23, of which 8 were waited for; matrix products, arithmetic and copies ran while one was open for 0% of the time, Pallas kernels for 7%

profile of v3, /device:TPU:1, one launch (start us, length us, event | category | flops | bytes accessed | tf_op | source)
XLA Modules:
  0.0 158.0 jit_solution(11399671408156666183)
XLA Ops:
  0.6 1.5 shard_map.62
  2.1 3.3 %collective-permute-start.1 = (f32[512,256]{1,0:T(8,128)S(1)}, f32[512,256]{1,0:T(8,128)S(1)}, u32[]{:S(2)}, u32[]{:S(2)}) collective-permute-start(f32[512,256]{1,0:T(8,128)S(1)} %get-tuple-element.47.own_ref), channel_id=1, source_target_pairs={{0,16},{16,0},{32,48},{48,32},{64,80},{80,64},{96,112},{112,96},{1... | collective-permute-start | bytes 1572872 | tf_op jit(solution)/shard_map/ppermute | solution.py:352
  5.4 1.5 shard_map.59.own_ref
  7.1 2.3 %shard_map.60 = (f32[256,2048]{1,0:T(8,128)S(1)}, bf16[256,2048]{1,0:T(8,128)(2,1)S(1)}, f32[1,2048]{1,0:T(1,128)S(1)}) custom-call(s32[2]{0:T(128)S(1)} %pad_add_fusion.where_ref, bf16[256,4096]{1,0:T(8,128)(2,1)} %proto_ref.1), custom_call_target="tpu_custom_call" | custom-call | tf_op jit(solution)/shard_map/pallas_call | solution.py:420
  9.4 2.0 %shard_map.63 = (f32[1024,2048]{1,0:T(8,128)S(1)}, f32[1024,128]{1,0:T(8,128)S(1)}, bf16[256,1024]{1,0:T(8,128)(2,1)S(1)}) custom-call(s32[2]{0:T(128)S(1)} %pad_add_fusion.where_ref, f32[512,256]{1,0:T(8,128)S(1)} %get-tuple-element.47.own_ref, f32[512,256]{1,0:T(8,128)S(1)} %collective-permute-done.1.other_ref, ...), custom_call_target="tpu_custom_call" | custom-call | flops 1073741824 | tf_op jit(solution)/shard_map/pallas_call | solution.py:402
  11.5 1.9 %shard_map.61 = (f32[1024,2048]{1,0:T(8,128)S(1)}, f32[8,16,128]{2,1,0:T(8,128)S(1)}) custom-call(s32[2]{0:T(128)S(1)} %pad_add_fusion.where_ref, f32[512,256]{1,0:T(8,128)S(1)} %shard_map.59.own_ref, f32[512,256]{1,0:T(8,128)S(1)} %collective-permute-done.other_ref, bf16[256,2048]{1,0:T(8,128)(2,1)S(1)} %get-tuple-element.45.unit_ref), custom_call_target="tpu_custom_call" | custom-call | flops 1073741824 | tf_op jit(solution)/shard_map/pallas_call | solution.py:402
  13.4 13.5 %all_to_all.40.parts_ref = f32[8,16,128]{2,1,0:T(8,128)S(1)} all-to-all(f32[8,16,128]{2,1,0:T(8,128)S(1)} %get-tuple-element.54), channel_id=1, replica_groups={{0,32,64,96,128,160,192,224},{16,48,80,112,144,176,208,240},{1,33,65,97..., dimensions={0} | all-to-all | bytes 131072 | tf_op jit(solution)/shard_map/all_to_all | solution.py:362
  26.9 1.6 shard_map.64
  28.5 17.1 %all_to_all.41.parts_ref.mass_ref = f32[32,16,128]{2,1,0:T(8,128)S(1)} all-to-all(f32[32,16,128]{2,1,0:T(8,128)S(1)} %get-tuple-element.55), channel_id=1, replica_groups={{0,1,2,3,4,5,6,7,8,9,10,11,12,13,14,15,16,17,18,19,20,21,22,23,24,25,26..., dimensions={0} | all-to-all | bytes 524288 | tf_op jit(solution)/shard_map/all_to_all | solution.py:366
  46.6 9.6 %all_to_all.42.parts_ref = f32[8,16,128]{2,1,0:T(8,128)S(1)} all-to-all(f32[8,16,128]{2,1,0:T(8,128)S(1)} %shard_map.65), channel_id=1, replica_groups={{0,32,64,96,128,160,192,224},{16,48,80,112,144,176,208,240},{1,33,65,97..., dimensions={0} | all-to-all | bytes 131072 | tf_op jit(solution)/shard_map/all_to_all | solution.py:362
  56.2 1.3 shard_map.66
  57.5 12.8 %all_to_all.43.parts_ref = f32[32,8,128]{2,1,0:T(8,128)S(1)} all-to-all(f32[32,8,128]{2,1,0:T(8,128)S(1)} %get-tuple-element.56), channel_id=1, replica_groups={{0,1,2,3,4,5,6,7,8,9,10,11,12,13,14,15,16,17,18,19,20,21,22,23,24,25,26..., dimensions={0} | all-to-all | bytes 262144 | tf_op jit(solution)/shard_map/all_to_all | solution.py:366
  71.4 9.6 %all_to_all.44.parts_ref = f32[8,16,128]{2,1,0:T(8,128)S(1)} all-to-all(f32[8,16,128]{2,1,0:T(8,128)S(1)} %shard_map.67), channel_id=1, replica_groups={{0,32,64,96,128,160,192,224},{16,48,80,112,144,176,208,240},{1,33,65,97..., dimensions={0} | all-to-all | bytes 131072 | tf_op jit(solution)/shard_map/all_to_all | solution.py:362
  82.0 12.4 %all_to_all.45.parts_ref = f32[32,8,128]{2,1,0:T(8,128)S(1)} all-to-all(f32[32,8,128]{2,1,0:T(8,128)S(1)} %get-tuple-element.58), channel_id=1, replica_groups={{0,1,2,3,4,5,6,7,8,9,10,11,12,13,14,15,16,17,18,19,20,21,22,23,24,25,26..., dimensions={0} | all-to-all | bytes 262144 | tf_op jit(solution)/shard_map/all_to_all | solution.py:366
  94.3 2.9 %shard_map.69 = (bf16[1024,1024]{1,0:T(8,128)(2,1)S(1)}, f32[32,1024]{1,0:T(8,128)S(1)}, f32[32,1024]{1,0:T(8,128)S(1)}, f32[32,1024]{1,0:T(8,128)S(1)}, f32[32,...) custom-call(s32[2]{0:T(128)S(1)} %pad_add_fusion.where_ref, ...), custom_call_target="tpu_custom_call" | custom-call | flops 536870912 | tf_op jit(solution)/shard_map/pallas_call | solution.py:402
  97.6 3.5 %shard_map.70 = (bf16[1024,1024]{1,0:T(8,128)(2,1)S(1)}, f32[32,1024]{1,0:T(8,128)S(1)}, f32[32,1024]{1,0:T(8,128)S(1)}, f32[32,1024]{1,0:T(8,128)S(1)}, f32[32,...) custom-call(s32[2]{0:T(128)S(1)} %pad_add_fusion.where_ref, ...), custom_call_target="tpu_custom_call" | custom-call | flops 536870912 | tf_op jit(solution)/shard_map/pallas_call | solution.py:402
  101.6 1.8 %shard_map.71 = (f32[512,256]{1,0:T(8,128)S(1)}, f32[512,256]{1,0:T(8,128)S(1)}) custom-call(s32[2]{0:T(128)S(1)} %pad_add_fusion.where_ref, bf16[1024,1024]{1,0:T(8,128)(2,1)S(1)} %get-tuple-element.61.diff0_ref, bf16[1024,1024]{1,0:T(8,128)(2,1)S(1)} %get-tuple-element.62.diff1_ref, bf16[256,2048]{1,0:T(8,128)(2,1)S(1)} %get-tuple-element.45.unit_ref), custom_call_target="tpu_custom_call" | custom-call | flops 1073741824 | tf_op jit(solution)/shard_map/pallas_call | solution.py:402
  103.5 1.9 %collective-permute-start.3 = (f32[512,256]{1,0:T(8,128)S(1)}, f32[512,256]{1,0:T(8,128)S(1)}, u32[]{:S(2)}, u32[]{:S(2)}) collective-permute-start(f32[512,256]{1,0:T(8,128)S(1)} %get-tuple-element.64), channel_id=1, source_target_pairs={{0,16},{16,0},{32,48},{48,32},{64,80},{80,64},{96,112},{112,96},{1... | collective-permute-start | bytes 1572872 | tf_op jit(solution)/shard_map/ppermute | solution.py:352
  105.4 1.5 collective-permute-done.3
  107.8 3.6 %all-to-all-start.6 = ((f32[16,32,256]{2,1,0:T(8,128)}), f32[16,32,256]{2,1,0:T(8,128)S(1)}, u32[]{:S(2)}, u32[]{:S(2)}) async-start(f32[16,32,256]{2,1,0:T(8,128)} %bitcast.5), calls=%async_computation.6 | async-start | bytes 1048576 | tf_op jit(solution)/shard_map/all_to_all | solution.py:497
  112.9 2.2 %collective-permute-start.7 = (f32[16,1024]{1,0:T(8,128)S(1)}, f32[16,1024]{1,0:T(8,128)S(1)}, u32[]{:S(2)}, u32[]{:S(2)}) collective-permute-start(f32[16,1024]{1,0:T(8,128)S(1)} %get-tuple-element.74), channel_id=1, source_target_pairs={{0,224},{16,240},{32,0},{48,16},{64,32},{80,48},{96,64},{112,80},{... | collective-permute-start | bytes 196616 | tf_op jit(solution)/shard_map/ppermute | solution.py:356
  115.2 7.2 %all-to-all-done.6.parts_ref = f32[16,32,256]{2,1,0:T(8,128)S(1)} async-done(((f32[16,32,256]{2,1,0:T(8,128)}), f32[16,32,256]{2,1,0:T(8,128)S(1)}, u32[]{:S(2)}, u32[]{:S(2)}) %all-to-all-start.6) | async-done | bytes 524320 | tf_op jit(solution)/shard_map/all_to_all | solution.py:497
  123.2 3.6 %all-to-all-start.7 = ((f32[16,32,256]{2,1,0:T(8,128)}), f32[16,32,256]{2,1,0:T(8,128)S(1)}, u32[]{:S(2)}, u32[]{:S(2)}) async-start(f32[16,32,256]{2,1,0:T(8,128)} %shard_map.72), calls=%async_computation.7 | async-start | bytes 1048576 | tf_op jit(solution)/shard_map/all_to_all | solution.py:499
  128.5 2.3 %collective-permute-start.8 = (f32[32,1024]{1,0:T(8,128)S(1)}, f32[32,1024]{1,0:T(8,128)S(1)}, u32[]{:S(2)}, u32[]{:S(2)}) collective-permute-start(f32[32,1024]{1,0:T(8,128)S(1)} %shard_map.77), channel_id=1, source_target_pairs={{0,224},{16,240},{32,0},{48,16},{64,32},{80,48},{96,64},{112,80},{... | collective-permute-start | bytes 393224 | tf_op jit(solution)/shard_map/ppermute | solution.py:356
  130.9 2.7 %collective-permute-start.17 = (f32[32,1024]{1,0:T(8,128)S(1)}, f32[32,1024]{1,0:T(8,128)S(1)}, u32[]{:S(2)}, u32[]{:S(2)}) collective-permute-start(f32[32,1024]{1,0:T(8,128)S(1)} %shard_map.85), channel_id=1, source_target_pairs={{0,224},{16,240},{32,0},{48,16},{64,32},{80,48},{96,64},{112,80},{... | collective-permute-start | bytes 393224 | tf_op jit(solution)/shard_map/ppermute | solution.py:356
  133.8 2.9 %collective-permute-start.9 = (f32[32,1024]{1,0:T(8,128)S(1)}, f32[32,1024]{1,0:T(8,128)S(1)}, u32[]{:S(2)}, u32[]{:S(2)}) collective-permute-start(f32[32,1024]{1,0:T(8,128)S(1)} %shard_map.78), channel_id=1, source_target_pairs={{0,224},{16,240},{32,0},{48,16},{64,32},{80,48},{96,64},{112,80},{... | collective-permute-start | bytes 393224 | tf_op jit(solution)/shard_map/ppermute | solution.py:356
  137.1 2.8 %collective-permute-start.18 = (f32[32,1024]{1,0:T(8,128)S(1)}, f32[32,1024]{1,0:T(8,128)S(1)}, u32[]{:S(2)}, u32[]{:S(2)}) collective-permute-start(f32[32,1024]{1,0:T(8,128)S(1)} %shard_map.86), channel_id=1, source_target_pairs={{0,224},{16,240},{32,0},{48,16},{64,32},{80,48},{96,64},{112,80},{... | collective-permute-start | bytes 393224 | tf_op jit(solution)/shard_map/ppermute | solution.py:356
  140.5 3.0 %collective-permute-start.10 = (f32[32,1024]{1,0:T(8,128)S(1)}, f32[32,1024]{1,0:T(8,128)S(1)}, u32[]{:S(2)}, u32[]{:S(2)}) collective-permute-start(f32[32,1024]{1,0:T(8,128)S(1)} %shard_map.79), channel_id=1, source_target_pairs={{0,224},{16,240},{32,0},{48,16},{64,32},{80,48},{96,64},{112,80},{... | collective-permute-start | bytes 393224 | tf_op jit(solution)/shard_map/ppermute | solution.py:356
  143.7 2.7 %collective-permute-done.14.up_ref = f32[32,1024]{1,0:T(8,128)S(1)} collective-permute-done((f32[32,1024]{1,0:T(8,128)S(1)}, f32[32,1024]{1,0:T(8,128)S(1)}, u32[]{:S(2)}, u32[]{:S(2)}) %collective-permute-start.14) | collective-permute-done | bytes 131104 | tf_op jit(solution)/shard_map/ppermute | solution.py:356
  146.3 4.5 %collective-permute-start.20 = (f32[16,1024]{1,0:T(8,128)S(1)}, f32[16,1024]{1,0:T(8,128)S(1)}, u32[]{:S(2)}, u32[]{:S(2)}) collective-permute-start(f32[16,1024]{1,0:T(8,128)S(1)} %get-tuple-element.87), channel_id=1, source_target_pairs={{0,16},{16,0},{32,48},{48,32},{64,80},{80,64},{96,112},{112,96},{1... | collective-permute-start | bytes 196616 | tf_op jit(solution)/shard_map/ppermute | solution.py:352
  150.9 3.1 %collective-permute-start.19 = (f32[16,1024]{1,0:T(8,128)S(1)}, f32[16,1024]{1,0:T(8,128)S(1)}, u32[]{:S(2)}, u32[]{:S(2)}) collective-permute-start(f32[16,1024]{1,0:T(8,128)S(1)} %get-tuple-element.86), channel_id=1, source_target_pairs={{0,16},{16,0},{32,48},{48,32},{64,80},{80,64},{96,112},{112,96},{1... | collective-permute-start | bytes 196616 | tf_op jit(solution)/shard_map/ppermute | solution.py:352
  156.2 1.8 %shard_map.73 = f32[4,256,256]{2,1,0:T(8,128)} custom-call(f32[512,256]{1,0:T(8,128)S(1)} %bitcast.4, f32[512,256]{1,0:T(8,128)S(1)} %get-tuple-element.65.zsf_ref, f32[512,1]{1,0:T(8,128)S(1)} %get-tuple-element.66.norm_ref, s32[4,128]{1,0:T(4,128)S(1)} %copy-done), custom_call_target="tpu_custom_call" | custom-call | tf_op jit(solution)/shard_map/pallas_call | solution.py:41
  (54 shorter events, 12.6 us)
Async XLA Ops:
  2.1 7.3 %collective-permute-start.1 = (f32[512,256]{1,0:T(8,128)S(1)}, f32[512,256]{1,0:T(8,128)S(1)}, u32[]{:S(2)}, u32[]{:S(2)}) collective-permute-start(f32[512,256]{1,0:T(8,128)S(1)} %get-tuple-element.47.own_ref), channel_id=1, source_target_pairs={{0,16},{16,0},{32,48},{48,32},{64,80},{80,64},{96,112},{112,96},{1... | collective-permute-start | bytes 1572872 | tf_op jit(solution)/shard_map/ppermute | solution.py:352
  6.9 4.5 %collective-permute-start = (f32[512,256]{1,0:T(8,128)S(1)}, f32[512,256]{1,0:T(8,128)S(1)}, u32[]{:S(2)}, u32[]{:S(2)}) collective-permute-start(f32[512,256]{1,0:T(8,128)S(1)} %shard_map.59.own_ref), channel_id=1, source_target_pairs={{0,16},{16,0},{32,48},{48,32},{64,80},{80,64},{96,112},{112,96},{1... | collective-permute-start | bytes 1572872 | tf_op jit(solution)/shard_map/ppermute | solution.py:352
  97.2 4.4 %collective-permute-start.2 = (f32[16,1024]{1,0:T(8,128)S(1)}, f32[16,1024]{1,0:T(8,128)S(1)}, u32[]{:S(2)}, u32[]{:S(2)}) collective-permute-start(f32[16,1024]{1,0:T(8,128)S(1)} %get-tuple-element.60), channel_id=1, source_target_pairs={{0,32},{16,48},{32,64},{48,80},{64,96},{80,112},{96,128},{112,144}... | collective-permute-start | bytes 196616 | tf_op jit(solution)/shard_map/ppermute | solution.py:356
  103.5 3.5 %collective-permute-start.3 = (f32[512,256]{1,0:T(8,128)S(1)}, f32[512,256]{1,0:T(8,128)S(1)}, u32[]{:S(2)}, u32[]{:S(2)}) collective-permute-start(f32[512,256]{1,0:T(8,128)S(1)} %get-tuple-element.64), channel_id=1, source_target_pairs={{0,16},{16,0},{32,48},{48,32},{64,80},{80,64},{96,112},{112,96},{1... | collective-permute-start | bytes 1572872 | tf_op jit(solution)/shard_map/ppermute | solution.py:352
  107.8 14.5 %all-to-all-start.6 = ((f32[16,32,256]{2,1,0:T(8,128)}), f32[16,32,256]{2,1,0:T(8,128)S(1)}, u32[]{:S(2)}, u32[]{:S(2)}) async-start(f32[16,32,256]{2,1,0:T(8,128)} %bitcast.5), calls=%async_computation.6 | async-start | bytes 1048576 | tf_op jit(solution)/shard_map/all_to_all | solution.py:497
  111.4 15.4 %collective-permute-start.15 = (f32[16,1024]{1,0:T(8,128)}, f32[16,1024]{1,0:T(8,128)S(1)}, u32[]{:S(2)}, u32[]{:S(2)}) collective-permute-start(f32[16,1024]{1,0:T(8,128)} %get-tuple-element.84), channel_id=1, source_target_pairs={{0,224},{16,240},{32,0},{48,16},{64,32},{80,48},{96,64},{112,80},{... | collective-permute-start | bytes 196616 | tf_op jit(solution)/shard_map/ppermute | solution.py:356
  112.5 15.4 %collective-permute-start.11 = (f32[16,1024]{1,0:T(8,128)S(1)}, f32[16,1024]{1,0:T(8,128)S(1)}, u32[]{:S(2)}, u32[]{:S(2)}) collective-permute-start(f32[16,1024]{1,0:T(8,128)S(1)} %get-tuple-element.80), channel_id=1, source_target_pairs={{0,32},{16,48},{32,64},{48,80},{64,96},{80,112},{96,128},{112,144}... | collective-permute-start | bytes 196616 | tf_op jit(solution)/shard_map/ppermute | solution.py:356
  112.9 15.5 %collective-permute-start.7 = (f32[16,1024]{1,0:T(8,128)S(1)}, f32[16,1024]{1,0:T(8,128)S(1)}, u32[]{:S(2)}, u32[]{:S(2)}) collective-permute-start(f32[16,1024]{1,0:T(8,128)S(1)} %get-tuple-element.74), channel_id=1, source_target_pairs={{0,224},{16,240},{32,0},{48,16},{64,32},{80,48},{96,64},{112,80},{... | collective-permute-start | bytes 196616 | tf_op jit(solution)/shard_map/ppermute | solution.py:356
  123.2 33.0 %all-to-all-start.7 = ((f32[16,32,256]{2,1,0:T(8,128)}), f32[16,32,256]{2,1,0:T(8,128)S(1)}, u32[]{:S(2)}, u32[]{:S(2)}) async-start(f32[16,32,256]{2,1,0:T(8,128)} %shard_map.72), calls=%async_computation.7 | async-start | bytes 1048576 | tf_op jit(solution)/shard_map/all_to_all | solution.py:499
  126.8 4.1 %collective-permute-start.16 = (f32[32,1024]{1,0:T(8,128)S(1)}, f32[32,1024]{1,0:T(8,128)S(1)}, u32[]{:S(2)}, u32[]{:S(2)}) collective-permute-start(f32[32,1024]{1,0:T(8,128)S(1)} %shard_map.84), channel_id=1, source_target_pairs={{0,224},{16,240},{32,0},{48,16},{64,32},{80,48},{96,64},{112,80},{... | collective-permute-start | bytes 393224 | tf_op jit(solution)/shard_map/ppermute | solution.py:356
  127.9 5.7 %collective-permute-start.12 = (f32[32,1024]{1,0:T(8,128)S(1)}, f32[32,1024]{1,0:T(8,128)S(1)}, u32[]{:S(2)}, u32[]{:S(2)}) collective-permute-start(f32[32,1024]{1,0:T(8,128)S(1)} %shard_map.81), channel_id=1, source_target_pairs={{0,32},{16,48},{32,64},{48,80},{64,96},{80,112},{96,128},{112,144}... | collective-permute-start | bytes 393224 | tf_op jit(solution)/shard_map/ppermute | solution.py:356
  128.5 5.3 %collective-permute-start.8 = (f32[32,1024]{1,0:T(8,128)S(1)}, f32[32,1024]{1,0:T(8,128)S(1)}, u32[]{:S(2)}, u32[]{:S(2)}) collective-permute-start(f32[32,1024]{1,0:T(8,128)S(1)} %shard_map.77), channel_id=1, source_target_pairs={{0,224},{16,240},{32,0},{48,16},{64,32},{80,48},{96,64},{112,80},{... | collective-permute-start | bytes 393224 | tf_op jit(solution)/shard_map/ppermute | solution.py:356
  130.8 6.2 %collective-permute-start.4 = (f32[32,1024]{1,0:T(8,128)S(1)}, f32[32,1024]{1,0:T(8,128)S(1)}, u32[]{:S(2)}, u32[]{:S(2)}) collective-permute-start(f32[32,1024]{1,0:T(8,128)S(1)} %shard_map.74), channel_id=1, source_target_pairs={{0,32},{16,48},{32,64},{48,80},{64,96},{80,112},{96,128},{112,144}... | collective-permute-start | bytes 393224 | tf_op jit(solution)/shard_map/ppermute | solution.py:356
  130.9 25.3 %copy-start = (s32[4,128]{1,0:T(4,128)S(1)}, s32[4,128]{1,0:T(4,128)}, u32[]{:S(2)}) copy-start(s32[4,128]{1,0:T(4,128)} %mask_ref.1) | copy-start | bytes 6148
  130.9 6.1 %collective-permute-start.17 = (f32[32,1024]{1,0:T(8,128)S(1)}, f32[32,1024]{1,0:T(8,128)S(1)}, u32[]{:S(2)}, u32[]{:S(2)}) collective-permute-start(f32[32,1024]{1,0:T(8,128)S(1)} %shard_map.85), channel_id=1, source_target_pairs={{0,224},{16,240},{32,0},{48,16},{64,32},{80,48},{96,64},{112,80},{... | collective-permute-start | bytes 393224 | tf_op jit(solution)/shard_map/ppermute | solution.py:356
  133.7 6.6 %collective-permute-start.13 = (f32[32,1024]{1,0:T(8,128)S(1)}, f32[32,1024]{1,0:T(8,128)S(1)}, u32[]{:S(2)}, u32[]{:S(2)}) collective-permute-start(f32[32,1024]{1,0:T(8,128)S(1)} %shard_map.82), channel_id=1, source_target_pairs={{0,32},{16,48},{32,64},{48,80},{64,96},{80,112},{96,128},{112,144}... | collective-permute-start | bytes 393224 | tf_op jit(solution)/shard_map/ppermute | solution.py:356
  133.8 6.6 %collective-permute-start.9 = (f32[32,1024]{1,0:T(8,128)S(1)}, f32[32,1024]{1,0:T(8,128)S(1)}, u32[]{:S(2)}, u32[]{:S(2)}) collective-permute-start(f32[32,1024]{1,0:T(8,128)S(1)} %shard_map.78), channel_id=1, source_target_pairs={{0,224},{16,240},{32,0},{48,16},{64,32},{80,48},{96,64},{112,80},{... | collective-permute-start | bytes 393224 | tf_op jit(solution)/shard_map/ppermute | solution.py:356
  137.0 6.5 %collective-permute-start.5 = (f32[32,1024]{1,0:T(8,128)S(1)}, f32[32,1024]{1,0:T(8,128)S(1)}, u32[]{:S(2)}, u32[]{:S(2)}) collective-permute-start(f32[32,1024]{1,0:T(8,128)S(1)} %shard_map.75), channel_id=1, source_target_pairs={{0,32},{16,48},{32,64},{48,80},{64,96},{80,112},{96,128},{112,144}... | collective-permute-start | bytes 393224 | tf_op jit(solution)/shard_map/ppermute | solution.py:356
  137.1 6.5 %collective-permute-start.18 = (f32[32,1024]{1,0:T(8,128)S(1)}, f32[32,1024]{1,0:T(8,128)S(1)}, u32[]{:S(2)}, u32[]{:S(2)}) collective-permute-start(f32[32,1024]{1,0:T(8,128)S(1)} %shard_map.86), channel_id=1, source_target_pairs={{0,224},{16,240},{32,0},{48,16},{64,32},{80,48},{96,64},{112,80},{... | collective-permute-start | bytes 393224 | tf_op jit(solution)/shard_map/ppermute | solution.py:356
  140.3 6.0 %collective-permute-start.14 = (f32[32,1024]{1,0:T(8,128)S(1)}, f32[32,1024]{1,0:T(8,128)S(1)}, u32[]{:S(2)}, u32[]{:S(2)}) collective-permute-start(f32[32,1024]{1,0:T(8,128)S(1)} %shard_map.83), channel_id=1, source_target_pairs={{0,32},{16,48},{32,64},{48,80},{64,96},{80,112},{96,128},{112,144}... | collective-permute-start | bytes 393224 | tf_op jit(solution)/shard_map/ppermute | solution.py:356
  140.5 10.4 %collective-permute-start.10 = (f32[32,1024]{1,0:T(8,128)S(1)}, f32[32,1024]{1,0:T(8,128)S(1)}, u32[]{:S(2)}, u32[]{:S(2)}) collective-permute-start(f32[32,1024]{1,0:T(8,128)S(1)} %shard_map.79), channel_id=1, source_target_pairs={{0,224},{16,240},{32,0},{48,16},{64,32},{80,48},{96,64},{112,80},{... | collective-permute-start | bytes 393224 | tf_op jit(solution)/shard_map/ppermute | solution.py:356
  143.6 7.3 %collective-permute-start.6 = (f32[32,1024]{1,0:T(8,128)S(1)}, f32[32,1024]{1,0:T(8,128)S(1)}, u32[]{:S(2)}, u32[]{:S(2)}) collective-permute-start(f32[32,1024]{1,0:T(8,128)S(1)} %shard_map.76), channel_id=1, source_target_pairs={{0,32},{16,48},{32,64},{48,80},{64,96},{80,112},{96,128},{112,144}... | collective-permute-start | bytes 393224 | tf_op jit(solution)/shard_map/ppermute | solution.py:356
  146.3 7.7 %collective-permute-start.20 = (f32[16,1024]{1,0:T(8,128)S(1)}, f32[16,1024]{1,0:T(8,128)S(1)}, u32[]{:S(2)}, u32[]{:S(2)}) collective-permute-start(f32[16,1024]{1,0:T(8,128)S(1)} %get-tuple-element.87), channel_id=1, source_target_pairs={{0,16},{16,0},{32,48},{48,32},{64,80},{80,64},{96,112},{112,96},{1... | collective-permute-start | bytes 196616 | tf_op jit(solution)/shard_map/ppermute | solution.py:352
  150.9 4.0 %collective-permute-start.19 = (f32[16,1024]{1,0:T(8,128)S(1)}, f32[16,1024]{1,0:T(8,128)S(1)}, u32[]{:S(2)}, u32[]{:S(2)}) collective-permute-start(f32[16,1024]{1,0:T(8,128)S(1)} %get-tuple-element.86), channel_id=1, source_target_pairs={{0,16},{16,0},{32,48},{48,32},{64,80},{80,64},{96,112},{112,96},{1... | collective-permute-start | bytes 196616 | tf_op jit(solution)/shard_map/ppermute | solution.py:352

commit v4 on v3

--- a/solution.py
+++ b/solution.py
@@ -68,36 +68,36 @@
     return rows, jnp.sqrt(jnp.sum(rows * rows, axis=1, keepdims=True) + EPSILON)
 
 
-def teacher_kernel(feats_hbm, mask_hbm, unit_ref, feats_ref, mask_ref, sems):
-    for copy in fetch(((feats_hbm, feats_ref), (mask_hbm, mask_ref)), sems):
-        copy.wait()
+def prep_kernel(
+    teacher_hbm, student_hbm, mask_hbm, zt_ref, zs_ref, full_ref, norm_ref,
+    teacher_ref, student_ref, mask_ref, sems,
+):
+    mask_copy, teacher_copy, student_copy = fetch(
+        ((mask_hbm, mask_ref), (teacher_hbm, teacher_ref), (student_hbm, student_ref)), sems
+    )
+    mask_copy.wait()
+    teacher_copy.wait()
     slots = mask_ref.shape[1]
-    for i in range(feats_ref.shape[0]):
-        rows, norm = masked_rows(feats_ref[i], mask_ref[i : i + 1, :])
-        unit_ref[i * slots : (i + 1) * slots, :] = (rows / norm).astype(BF16).astype(F32)
-
-
-def student_kernel(
-    feats_hbm, mask_hbm, unit_ref, full_ref, norm_ref, feats_ref, mask_ref, sems
-):
-    for copy in fetch(((feats_hbm, feats_ref), (mask_hbm, mask_ref)), sems):
-        copy.wait()
-    slots = mask_ref.shape[1]
-    for i in range(feats_ref.shape[0]):
+    for i in range(teacher_ref.shape[0]):
+        rows, norm = masked_rows(teacher_ref[i], mask_ref[i : i + 1, :])
+        zt_ref[i * slots : (i + 1) * slots, :] = (rows / norm).astype(BF16).astype(F32)
+    student_copy.wait()
+    for i in range(student_ref.shape[0]):
         take = pl.ds(i * slots, slots)
-        rows, norm = masked_rows(feats_ref[i], mask_ref[i : i + 1, :])
+        rows, norm = masked_rows(student_ref[i], mask_ref[i : i + 1, :])
         full = rows / norm
         full_ref[take, :] = full
-        unit_ref[take, :] = full.astype(BF16).astype(F32)
+        zs_ref[take, :] = full.astype(BF16).astype(F32)
         norm_ref[take, :] = norm
 
 
-def proto_kernel(where_ref, proto_ref, full_ref, unit_ref, norm_ref):
+def proto_kernel(where_ref, proto_ref, full_ref, unit_ref, back_ref, norm_ref):
     p = proto_ref[...].astype(F32)
     norm = jnp.sqrt(jnp.sum(p * p, axis=0, keepdims=True) + EPSILON)
     full = p / norm
     full_ref[...] = full
     unit_ref[...] = full.astype(BF16)
+    back_ref[...] = full.T.astype(BF16)
     norm_ref[...] = norm
 
 
@@ -146,7 +146,8 @@
 
 
 def student_exp_kernel(
-    where_ref, own_ref, other_ref, unit_ref, s_ref, mass_ref, turned_ref
+    where_ref, own_ref, other_ref, unit_ref, back_ref,
+    s_ref, mass_ref, turned_ref, pull_ref, give_ref,
 ):
     half = own_ref.shape[0]
     wide = unit_ref.shape[1]
@@ -159,17 +160,20 @@
         for side, ref in enumerate((own_ref, other_ref)):
             place = core_rows(where_ref, side, half)
             for b in range(half // block):
-                rows = pl.ds(place.start + b * block, block)
+                rows = pl.ds(pl.multiple_of(place.start + b * block, block), block)
                 z = ref[b * block : (b + 1) * block, :].astype(BF16)
                 s = jnp.exp(
                     jnp.dot(z, unit, preferred_element_type=F32) * (1.0 / STUDENT_TEMP)
                 )
-                s_ref[rows, columns] = s
+                s_ref[rows, columns] = s.astype(BF16)
                 part = sum(s[:, j * LANES : (j + 1) * LANES] for j in range(WIDE // LANES))
                 if w:
                     mass_ref[rows, :] += part
                 else:
                     mass_ref[rows, :] = part
+    for side, out in enumerate((pull_ref, give_ref)):
+        rows = core_rows(where_ref, side, half)
+        out[...] = jnp.dot(s_ref[rows, :], back_ref[...], preferred_element_type=F32)
 
 
 def row_kernel(e_ref, parts_ref, out_ref, c_ref, acc_ref):
@@ -193,6 +197,55 @@
 def row_mass_kernel(e_ref, parts_ref, mass_ref, out_ref, c_ref, acc_ref):
     row_kernel(e_ref, parts_ref, out_ref, c_ref, acc_ref)
     write_rows(out_ref, mass_ref, first=8)
+
+
+def row_pull_kernel(
+    where_ref, e_ref, parts_ref, back_ref, own_ref, give_ref, c_ref, acc_ref, weighted_ref
+):
+    c = 1.0 / jnp.sum(parts_ref[...], axis=0)
+    c_ref[...] = c
+    half = own_ref.shape[0]
+    tiles = c.shape[0]
+    block = 64
+
+    def body(b, carry):
+        rows = pl.ds(pl.multiple_of(b * block, block), block)
+        acc = jnp.zeros((block, LANES), F32)
+        for j in range(tiles):
+            x = e_ref[rows, j * LANES : (j + 1) * LANES] * c[j : j + 1, :]
+            acc += x
+            weighted_ref[rows, j * LANES : (j + 1) * LANES] = x.astype(BF16)
+        acc_ref[rows, :] = acc
+        return carry
+
+    lax.fori_loop(0, e_ref.shape[0] // block, body, 0)
+    for side, out in enumerate((own_ref, give_ref)):
+        rows = core_rows(where_ref, side, half)
+        out[:half, :] = jnp.dot(
+            weighted_ref[rows, :], back_ref[...], preferred_element_type=F32
+        )
+    for i in range(acc_ref.shape[0] // LANES):
+        tile = acc_ref[i * LANES : (i + 1) * LANES, :].T
+        give_ref[half + i : half + i + 1, :LANES] = jnp.sum(tile, axis=0, keepdims=True)
+    give_ref[half : half + 8, LANES:] = jnp.zeros((8, LANES), F32)
+
+
+def pack_kernel(own_ref, mine_ref, got_ref, out_ref):
+    half, _ = own_ref.shape
+    share = out_ref.shape[1] - 8
+    sums = mine_ref[half:, :] + got_ref[half:, :]
+    for j in range(out_ref.shape[0]):
+        rows = slice(j * share, (j + 1) * share)
+        out_ref[j, :share, :] = own_ref[rows, :] + got_ref[rows, :]
+        out_ref[j, share:, :] = sums
+
+
+def share_kernel(parts_ref, out_ref, sums_ref):
+    total = sum(parts_ref[i] for i in range(parts_ref.shape[0]))
+    share = out_ref.shape[1]
+    sums_ref[0] = total[share:, :LANES]
+    for m in range(out_ref.shape[0]):
+        out_ref[m] = total[:share, :]
 
 
 def spread(ref, value):
@@ -229,8 +282,8 @@
 def diff_kernel(part):
     def kernel(
         where_ref, e_ref, s_ref, full_ref, norm_ref, turned_ref, c_ref, parts_ref, mass_ref,
-        diff_ref, rel0, rel1, rel2, rel3, rel4u, rel4d, rel5, rel6, rel7,
-        r_ref, m_ref, g_ref,
+        rel0, rel1, rel2, rel3, rel4u, rel4d, rel5, rel6, rel7,
+        r_ref, m_ref, g_ref, diff_ref,
     ):
         spread(r_ref, 1.0 / jnp.sum(parts_ref[...], axis=0))
         spread(m_ref, (1.0 / STUDENT_TEMP) / jnp.sum(mass_ref[:, 8:, :], axis=0))
@@ -246,7 +299,7 @@
                 tile = part * tiles + j
                 lanes = slice(tile * LANES, (tile + 1) * LANES)
                 targets = (r * e_ref[rows, lanes]) * c_ref[tile : tile + 1, :]
-                probs = s_ref[rows, lanes] * m
+                probs = s_ref[rows, lanes].astype(F32) * m
                 diff_ref[rows, j * LANES : (j + 1) * LANES] = (probs - targets).astype(BF16)
             return carry
 
@@ -273,31 +326,22 @@
     return kernel
 
 
-def token_grad_kernel(where_ref, diff0_ref, diff1_ref, unit_ref, own_ref, other_ref):
-    half = diff0_ref.shape[1]
-    dims = (((1,), (1,)), ((), ()))
-    unit0 = unit_ref[:, :half]
-    unit1 = unit_ref[:, half:]
-    for side, out in enumerate((own_ref, other_ref)):
-        rows = core_rows(where_ref, side, out.shape[0])
-        grad = lax.dot_general(diff0_ref[rows, :], unit0, dims, preferred_element_type=F32)
-        out[...] = grad + lax.dot_general(
-            diff1_ref[rows, :], unit1, dims, preferred_element_type=F32
-        )
-
-
-def share_kernel(parts_ref, out_ref):
-    total = sum(parts_ref[i] for i in range(parts_ref.shape[0]))
-    for m in range(out_ref.shape[0]):
-        out_ref[m] = total
-
-
-def last_kernel(gz_ref, zsf_ref, norm_ref, mask_ref, out_ref):
+def last_kernel(
+    where_ref, probs_ref, targets_ref, mass_ref, sums_ref, zsf_ref, norm_ref, mask_ref, out_ref,
+    r_ref, m_ref,
+):
+    spread(r_ref, (1.0 / STUDENT_TEMP) / sums_ref[0])
+    spread(m_ref, (1.0 / STUDENT_TEMP) / jnp.sum(mass_ref[:, 8:, :], axis=0))
     slots = mask_ref.shape[1]
+    half = zsf_ref.shape[0]
+    width = zsf_ref.shape[1]
+    first = core_rows(where_ref, 0, half).start
     for i in range(out_ref.shape[0]):
         rows = pl.ds(i * slots, slots)
+        own = pl.ds(pl.multiple_of(first + i * slots, slots), slots)
         zsf = zsf_ref[rows, :]
-        gz = gz_ref[rows, :]
+        r, m = (jnp.concatenate([x[own, :]] * (width // LANES), axis=1) for x in (r_ref, m_ref))
+        gz = probs_ref[rows, :] * m - targets_ref[rows, :] * r
         proj = jnp.sum(zsf * gz, axis=1, keepdims=True)
         grad = (gz - zsf * proj) / norm_ref[rows, :]
         hot = one_hot_t(mask_ref[i : i + 1, :], out_ref.shape[1], BF16)
@@ -385,19 +429,6 @@
     def in_hbm(x):
         return pltpu.with_memory_space_constraint(x, pltpu.HBM)
 
-    def prep(kernel, outs, feats):
-        return pl.pallas_call(
-            kernel,
-            in_specs=[pl.BlockSpec(memory_space=pl.ANY)] * 2,
-            out_specs=[whole()] * len(outs),
-            out_shape=outs,
-            scratch_shapes=[
-                VMEM(feats.shape, BF16), VMEM(mask_index.shape, jnp.int32),
-                pltpu.SemaphoreType.DMA((2,)),
-            ],
-            compiler_params=params(16),
-        )(in_hbm(feats), in_hbm(mask_index))
-
     def placed(kernel, outs, *args, **kw):
         return pl.pallas_call(
             kernel,
@@ -409,15 +440,24 @@
             cost_estimate=kw.get("cost_estimate"),
         )(where, *args)
 
-    (zt,) = prep(teacher_kernel, [shape(own, width)], teacher_feats)
+    zt, zs, zsf, s_norm = pl.pallas_call(
+        prep_kernel,
+        in_specs=[pl.BlockSpec(memory_space=pl.ANY)] * 3,
+        out_specs=[whole()] * 4,
+        out_shape=[
+            shape(own, width), shape(own, width), shape(own, width), shape(own, 1),
+        ],
+        scratch_shapes=[
+            VMEM(teacher_feats.shape, BF16), VMEM(student_feats.shape, BF16),
+            VMEM(mask_index.shape, jnp.int32), pltpu.SemaphoreType.DMA((3,)),
+        ],
+        compiler_params=params(16),
+    )(in_hbm(teacher_feats), in_hbm(student_feats), in_hbm(mask_index))
     zt_other = other_core(zt)
-    zs, zsf, s_norm = prep(
-        student_kernel, [shape(own, width), shape(own, width), shape(own, 1)], student_feats
-    )
     zs_other = other_core(zs)
     steps = 2
     column_spec = pl.BlockSpec((width, wide // steps), lambda j, w: (0, j))
-    full, unit, p_norm = pl.pallas_call(
+    full, unit, back, p_norm = pl.pallas_call(
         proto_kernel,
         grid_spec=pltpu.PrefetchScalarGridSpec(
             num_scalar_prefetch=1,
@@ -427,10 +467,14 @@
             ],
             out_specs=[
                 column_spec, column_spec,
+                pl.BlockSpec((wide // steps, width), lambda j, w: (j, 0)),
                 pl.BlockSpec((1, wide // steps), lambda j, w: (0, j)),
             ],
         ),
-        out_shape=[shape(width, wide), shape(width, wide, dtype=BF16), shape(1, wide)],
+        out_shape=[
+            shape(width, wide), shape(width, wide, dtype=BF16),
+            shape(wide, width, dtype=BF16), shape(1, wide),
+        ],
         compiler_params=params(16),
     )(where, in_hbm(prototypes))
 
@@ -440,18 +484,26 @@
         [hold(tokens, wide), shape(Z, lane_tiles, LANES)],
         zt, zt_other, unit, cost_estimate=exp_cost,
     )
-    s, mass_acc, turned = placed(
+    s, mass_acc, turned, probs, probs_give = placed(
         student_exp_kernel,
-        [hold(tokens, wide), shape(tokens, LANES), shape(width, tokens, dtype=BF16)],
-        zs, zs_other, unit, cost_estimate=exp_cost,
-    )
+        [
+            hold(tokens, wide, dtype=BF16), shape(tokens, LANES),
+            shape(width, tokens, dtype=BF16),
+            shape(own, width), shape(own, width),
+        ],
+        zs, zs_other, unit, back, cost_estimate=exp_cost,
+    )
+    probs = lax.psum(probs + other_core(probs_give), "proto")
     col_out = tie(col_out, mass_acc)
 
     mass = None
     for sweep in range(ITERS):
         col_parts = all_columns(col_out)
         extra = [mass_acc] if sweep == 0 else []
-        row_out, c = call(
+        if sweep == ITERS - 1:
+            break
+        extra = [mass_acc] if sweep == 0 else []
+        row_out, _ = call(
             row_kernel if sweep else row_mass_kernel,
             [shape(ROWS, row_tiles * (1 + len(extra)), LANES), shape(lane_tiles, LANES)],
             e, col_parts, *extra,
@@ -460,45 +512,53 @@
         row_parts = all_rows(row_out)
         if sweep == 0:
             mass = row_parts
-        if sweep < ITERS - 1:
-            (col_out,) = call(
-                col_kernel, [shape(Z, lane_tiles, LANES)], e, row_parts,
-                scratch=[VMEM((tokens, LANES), F32)],
-            )
+        (col_out,) = call(
+            col_kernel, [shape(Z, lane_tiles, LANES)], e, row_parts,
+            scratch=[VMEM((tokens, LANES), F32)],
+        )
+
+    share = own // RING
+    pull, pull_give, c = placed(
+        row_pull_kernel,
+        [shape(own, width), shape(own + 8, width), shape(lane_tiles, LANES)],
+        e, col_parts, back,
+        scratch=[VMEM((tokens, LANES), F32), VMEM((tokens, wide), BF16)],
+        cost_estimate=cost(4 * tokens * wide * width),
+    )
+    (pull_out,) = call(
+        pack_kernel, [shape(RING, share + 8, width)], pull, pull_give, other_core(pull_give)
+    )
+    pull_parts = lax.all_to_all(pull_out, "proto", 0, 0)
+    pull_share, row_parts = call(
+        share_kernel, [shape(RING, share, width), shape(1, row_tiles, LANES)], pull_parts
+    )
 
     deep = width // Z
     near = deep // 2
     half = wide // 2
-    diffs, rels = [], []
+    rels = []
     for part in range(2):
-        diff, *rel = placed(
+        rel = placed(
             diff_kernel(part),
-            [shape(tokens, half, dtype=BF16)] + [shape(deep, half)] * 4
-            + [shape(near, half)] * 2 + [shape(deep, half)] * 3,
+            [shape(deep, half)] * 4 + [shape(near, half)] * 2 + [shape(deep, half)] * 3,
             e, s, full, p_norm, turned, c, row_parts, mass,
             scratch=[
                 VMEM((tokens, LANES), F32), VMEM((tokens, LANES), F32), VMEM((width, half), F32),
+                VMEM((tokens, half), BF16),
             ],
             cost_estimate=cost(tokens * wide * width),
         )
-        diffs.append(diff)
-        rels.append(rel)
+        rels.append(list(rel))
 
     ups = [along_z(rel[4], 1) for rel in rels]
     downs = [along_z(rel[5], -1) for rel in rels]
     rels = [rel[:4] + [None] + rel[6:] for rel in rels]
 
-    diff0 = tie(diffs[0], ups[0])
-    gz, gz_give = placed(
-        token_grad_kernel, [shape(own, width)] * 2, diff0, diffs[1], unit,
-        cost_estimate=cost(2 * tokens * wide * width),
-    )
-    gz = gz + other_core(gz_give)
-    gz_parts = lax.all_to_all(gz.reshape(RING, own // RING, width), "proto", 0, 0)
-    (gz_share,) = call(share_kernel, [shape(RING, own // RING, width)], gz_parts)
-    gz = lax.all_to_all(gz_share, "proto", 0, 0).reshape(own, width)
-    (grad_student,) = call(
-        last_kernel, [shape(images, patches, width)], gz, zsf, s_norm, mask_index
+    targets = lax.all_to_all(tie(pull_share, [rel[0] for rel in rels]), "proto", 0, 0).reshape(own, width)
+    (grad_student,) = placed(
+        last_kernel, [shape(images, patches, width)],
+        probs, targets, mass, row_parts, zsf, s_norm, mask_index,
+        scratch=[VMEM((tokens, LANES), F32), VMEM((tokens, LANES), F32)],
     )
 
     part_shape = [shape(deep, half)]

time: 159 us -> 244 us (1.53)
  waiting for transfers between devices: 13.5 us -> 69.3 us
  local copies, waits for them, and re-layouts: 0.01 us -> 19.9 us
  between operations: 0.92 us -> 14.5 us
  blocking collectives: 74.9 us -> 62.6 us
  Pallas kernels: 27.6 us -> 33 us
    psum x0 -> x1, waiting for transfers between devices: none -> 53.2 us  [on_device(): probs = lax.psum(probs + other_core(probs_give), 'proto')]
    unnamed x2 -> x72, local copies, waits for them, and re-layouts: 0.01 us -> 19.9 us
    all_to_all x3 -> x2, blocking collectives: 42.2 us -> 29.8 us  [all_rows(): lax.all_to_all(x, ('batch', 'proto'), 0, 0, axis_index_groups=ROW_GROUPS)]
    pallas_call x6 -> x7, Pallas kernels: 13.5 us -> 20.6 us  [placed(): pl.pallas_call(kernel, in_specs=[scalars] + [whole()] * len(args), out_sp...]
    all_to_all x2, waiting for transfers between devices: 7.19 us -> 11.7 us  [the longest x1 11.7 us: on_device(): pull_parts = lax.all_to_all(pull_out, 'proto', 0, 0)]
    ppermute x5 -> x6, starting transfers between devices: 13 us -> 14.5 us  [other_core(): return lax.ppermute(x, 'batch', [(i, i ^ 1) for i in range(RING)])]
    pallas_call x21 -> x20, Pallas kernels: 8.87 us -> 7.86 us  [call(): pl.pallas_call(kernel, out_shape=outs, in_specs=[whole()] * len(args), ou...]
  transfers between devices with their start and end apart: 23 -> 25, of which waited for: 8 -> 5; matrix products, arithmetic and copies ran while one was open for 0% -> 1% of each run, Pallas kernels for 7% -> 7%
where the time goes in v4:
time: 244 us; the launch traced here: 243 us
  waiting for transfers between devices  69.3 us (28%)
  blocking collectives  62.6 us (26%)
  starting transfers between devices  41.9 us (17%)
  Pallas kernels  33 us (14%)
  local copies, waits for them, and re-layouts  19.9 us (8%)
  between operations  14.5 us (6%)
    psum x1, waiting for transfers between devices, on_device(): probs = lax.psum(probs + other_core(probs_give), 'proto')  53.2 us
    all_to_all x3, blocking collectives, all_columns(): return lax.all_to_all(x, 'batch', 0, 0, axis_index_groups=Z_GROUPS)  32.8 us
    all_to_all x2, blocking collectives, all_rows(): lax.all_to_all(x, ('batch', 'proto'), 0, 0, axis_index_groups=ROW_GROUPS)  29.8 us
    pallas_call x7, Pallas kernels, placed(): pl.pallas_call(kernel, in_specs=[scalars] + [whole()] * len(args), out_sp...  20.6 us
    ppermute x16, starting transfers between devices, along_z(): lax.ppermute(x, 'batch', [(i, (i // 2 + d) % Z * 2 + i % 2) for i in rang...  20.3 us
    unnamed x72, local copies, waits for them, and re-layouts  19.9 us
    ppermute x6, starting transfers between devices, other_core(): return lax.ppermute(x, 'batch', [(i, i ^ 1) for i in range(RING)])  14.5 us
    all_to_all x1, waiting for transfers between devices, on_device(): pull_parts = lax.all_to_all(pull_out, 'proto', 0, 0)  11.7 us
  transfers between devices with their start and end apart: 25, of which 5 were waited for; matrix products, arithmetic and copies ran while one was open for 1% of the time, Pallas kernels for 7%

profile of v4, /device:TPU:1, one launch (start us, length us, event | category | flops | bytes accessed | tf_op | source)
XLA Modules:
  0.0 243.1 jit_solution(12516104206748530064)
XLA Ops:
  7.2 1.9 shard_map.59
  10.6 3.2 %collective-permute-start.2 = (f32[512,256]{1,0:T(8,128)S(1)}, f32[512,256]{1,0:T(8,128)}, u32[]{:S(2)}, u32[]{:S(2)}) collective-permute-start(f32[512,256]{1,0:T(8,128)S(1)} %get-tuple-element.53.own_ref), channel_id=1, source_target_pairs={{0,16},{16,0},{32,48},{48,32},{64,80},{80,64},{96,112},{112,96},{1... | collective-permute-start | bytes 1572872 | tf_op jit(solution)/shard_map/ppermute | solution.py:396
  13.9 2.6 %shard_map.60 = (f32[256,2048]{1,0:T(8,128)S(1)}, bf16[256,2048]{1,0:T(8,128)(2,1)S(1)}, bf16[2048,256]{1,0:T(8,128)(2,1)S(1)}, f32[1,2048]{1,0:T(1,128)S(1)}) custom-call(s32[2]{0:T(128)S(1)} %pad_add_fusion.where_ref, bf16[256,4096]{1,0:T(8,128)(2,1)} %proto_ref.1), custom_call_target="tpu_custom_call" | custom-call | tf_op jit(solution)/shard_map/pallas_call | solution.py:460
  16.5 2.4 %shard_map.62 = (f32[1024,2048]{1,0:T(8,128)S(1)}, f32[8,16,128]{2,1,0:T(8,128)S(1)}) custom-call(s32[2]{0:T(128)S(1)} %pad_add_fusion.where_ref, f32[512,256]{1,0:T(8,128)S(1)} %get-tuple-element.53.own_ref, f32[512,256]{1,0:T(8,128)} %collective-permute-done.2.other_ref, bf16[256,2048]{1,0:T(8,128)(2,1)S(1)} %get-tuple-element.49.unit_ref), custom_call_target="tpu_custom_call" | custom-call | flops 1073741824 | tf_op jit(solution)/shard_map/pallas_call | solution.py:433
  20.4 4.3 %shard_map.61 = (bf16[1024,2048]{1,0:T(8,128)(2,1)S(1)}, f32[1024,128]{1,0:T(8,128)S(1)}, bf16[256,1024]{1,0:T(8,128)(2,1)S(1)}, f32[512,256]{1,0:T(8,128)S(1)}, f32[512,256]{1,0:T(8,128)S(1)}) custom-call(s32[2]{0:T(128)S(1)} %pad_add_fusion.where_ref, f32[512,256]{1,0:T(8,128)S(1)} %copy-done.35, f32[512,256]{1,0:T(8,128)} %collective-permute-done.other_ref, ...), custom_call_target="tpu_custom_call" | custom-call | flops 1073741824 | tf_op jit(solution)/shard_map/pallas_call | solution.py:433
  25.5 13.6 %all_to_all.35.parts_ref = f32[8,16,128]{2,1,0:T(8,128)S(1)} all-to-all(f32[8,16,128]{2,1,0:T(8,128)S(1)} %get-tuple-element.57), channel_id=1, replica_groups={{0,32,64,96,128,160,192,224},{16,48,80,112,144,176,208,240},{1,33,65,97..., dimensions={0} | all-to-all | bytes 131072 | tf_op jit(solution)/shard_map/all_to_all | solution.py:406
  39.1 1.6 shard_map.63
  40.7 17.0 %all_to_all.36.parts_ref.mass_ref = f32[32,16,128]{2,1,0:T(8,128)S(1)} all-to-all(f32[32,16,128]{2,1,0:T(8,128)S(1)} %get-tuple-element.58), channel_id=1, replica_groups={{0,1,2,3,4,5,6,7,8,9,10,11,12,13,14,15,16,17,18,19,20,21,22,23,24,25,26..., dimensions={0} | all-to-all | bytes 524288 | tf_op jit(solution)/shard_map/all_to_all | solution.py:410
  58.8 9.6 %all_to_all.37.parts_ref = f32[8,16,128]{2,1,0:T(8,128)S(1)} all-to-all(f32[8,16,128]{2,1,0:T(8,128)S(1)} %shard_map.64), channel_id=1, replica_groups={{0,32,64,96,128,160,192,224},{16,48,80,112,144,176,208,240},{1,33,65,97..., dimensions={0} | all-to-all | bytes 131072 | tf_op jit(solution)/shard_map/all_to_all | solution.py:406
  69.7 12.8 %all_to_all.38.parts_ref = f32[32,8,128]{2,1,0:T(8,128)S(1)} all-to-all(f32[32,8,128]{2,1,0:T(8,128)S(1)} %get-tuple-element.59), channel_id=1, replica_groups={{0,1,2,3,4,5,6,7,8,9,10,11,12,13,14,15,16,17,18,19,20,21,22,23,24,25,26..., dimensions={0} | all-to-all | bytes 262144 | tf_op jit(solution)/shard_map/all_to_all | solution.py:410
  83.6 9.6 %all_to_all.39.parts_ref = f32[8,16,128]{2,1,0:T(8,128)S(1)} all-to-all(f32[8,16,128]{2,1,0:T(8,128)S(1)} %shard_map.66), channel_id=1, replica_groups={{0,32,64,96,128,160,192,224},{16,48,80,112,144,176,208,240},{1,33,65,97..., dimensions={0} | all-to-all | bytes 131072 | tf_op jit(solution)/shard_map/all_to_all | solution.py:406
  93.2 2.8 %shard_map.67 = (f32[512,256]{1,0:T(8,128)S(1)}, f32[520,256]{1,0:T(8,128)S(1)}, f32[16,128]{1,0:T(8,128)S(1)}) custom-call(s32[2]{0:T(128)S(1)} %pad_add_fusion.where_ref, f32[1024,2048]{1,0:T(8,128)S(1)} %get-tuple-element.54.e_ref, f32[8,16,128]{2,1,0:T(8,128)S(1)} %all_to_all.39.parts_ref, bf16[2048,256]{1,0:T(8,128)(2,1)S(1)} %get-tuple-element.50.back_ref), custom_call_target="tpu_custom_call" | custom-call | flops 2147483648 | tf_op jit(solution)/shard_map/pallas_call | solution.py:433
  96.0 1.8 collective-permute-start.3
  100.2 3.6 %all-to-all-start.5 = ((f32[16,40,256]{2,1,0:T(8,128)}), f32[16,40,256]{2,1,0:T(8,128)S(1)}, u32[]{:S(2)}, u32[]{:S(2)}) async-start(f32[16,40,256]{2,1,0:T(8,128)} %copy-done.4), calls=%async_computation.5 | async-start | bytes 1310720 | tf_op jit(solution)/shard_map/all_to_all | solution.py:531
  104.5 11.7 %all-to-all-done.5.parts_ref = f32[16,40,256]{2,1,0:T(8,128)S(1)} async-done(((f32[16,40,256]{2,1,0:T(8,128)}), f32[16,40,256]{2,1,0:T(8,128)S(1)}, u32[]{:S(2)}, u32[]{:S(2)}) %all-to-all-start.5) | async-done | bytes 655392 | tf_op jit(solution)/shard_map/all_to_all | solution.py:531
  117.0 3.4 %copy-done.1 = f32[1024,2048]{1,0:T(8,128)S(1)} copy-done((f32[1024,2048]{1,0:T(8,128)S(1)}, f32[1024,2048]{1,0:T(8,128)}, u32[]{:S(2)}) %copy-start.1) | copy-done | bytes 8388632
  120.4 2.2 copy-done.3
  123.3 3.6 %shard_map.70 = (f32[32,1024]{1,0:T(8,128)S(1)}, f32[32,1024]{1,0:T(8,128)S(1)}, f32[32,1024]{1,0:T(8,128)S(1)}, f32[32,1024]{1,0:T(8,128)S(1)}, f32[16,1024]{1,...) custom-call(s32[2]{0:T(128)S(1)} %pad_add_fusion.where_ref, ...), custom_call_target="tpu_custom_call" | custom-call | flops 536870912 | tf_op jit(solution)/shard_map/pallas_call | solution.py:433
  129.8 2.4 collective-permute-start.8
  132.2 3.6 %shard_map.71 = (f32[32,1024]{1,0:T(8,128)S(1)}, f32[32,1024]{1,0:T(8,128)S(1)}, f32[32,1024]{1,0:T(8,128)S(1)}, f32[32,1024]{1,0:T(8,128)S(1)}, f32[16,1024]{1,...) custom-call(s32[2]{0:T(128)S(1)} %pad_add_fusion.where_ref, ...), custom_call_target="tpu_custom_call" | custom-call | flops 536870912 | tf_op jit(solution)/shard_map/pallas_call | solution.py:433
  140.0 2.0 add.5
  142.0 3.6 %all-to-all-start.6 = ((f32[16,32,256]{2,1,0:T(8,128)}), f32[16,32,256]{2,1,0:T(8,128)S(1)}, u32[]{:S(2)}, u32[]{:S(2)}) async-start(f32[16,32,256]{2,1,0:T(8,128)} %get-tuple-element.71), calls=%async_computation.6 | async-start | bytes 1048576 | tf_op jit(solution)/shard_map/all_to_all | solution.py:557
  151.7 2.6 %collective-permute-start.17 = (f32[32,1024]{1,0:T(8,128)S(1)}, f32[32,1024]{1,0:T(8,128)S(1)}, u32[]{:S(2)}, u32[]{:S(2)}) collective-permute-start(f32[32,1024]{1,0:T(8,128)S(1)} %shard_map.83), channel_id=1, source_target_pairs={{0,224},{16,240},{32,0},{48,16},{64,32},{80,48},{96,64},{112,80},{... | collective-permute-start | bytes 393224 | tf_op jit(solution)/shard_map/ppermute | solution.py:400
  154.5 2.7 %collective-permute-start.10 = (f32[32,1024]{1,0:T(8,128)S(1)}, f32[32,1024]{1,0:T(8,128)S(1)}, u32[]{:S(2)}, u32[]{:S(2)}) collective-permute-start(f32[32,1024]{1,0:T(8,128)S(1)} %shard_map.77), channel_id=1, source_target_pairs={{0,224},{16,240},{32,0},{48,16},{64,32},{80,48},{96,64},{112,80},{... | collective-permute-start | bytes 393224 | tf_op jit(solution)/shard_map/ppermute | solution.py:400
  157.3 2.7 %collective-permute-start.18 = (f32[32,1024]{1,0:T(8,128)S(1)}, f32[32,1024]{1,0:T(8,128)S(1)}, u32[]{:S(2)}, u32[]{:S(2)}) collective-permute-start(f32[32,1024]{1,0:T(8,128)S(1)} %shard_map.84), channel_id=1, source_target_pairs={{0,224},{16,240},{32,0},{48,16},{64,32},{80,48},{96,64},{112,80},{... | collective-permute-start | bytes 393224 | tf_op jit(solution)/shard_map/ppermute | solution.py:400
  160.6 3.3 %collective-permute-start.11 = (f32[32,1024]{1,0:T(8,128)S(1)}, f32[32,1024]{1,0:T(8,128)S(1)}, u32[]{:S(2)}, u32[]{:S(2)}) collective-permute-start(f32[32,1024]{1,0:T(8,128)S(1)} %shard_map.78), channel_id=1, source_target_pairs={{0,224},{16,240},{32,0},{48,16},{64,32},{80,48},{96,64},{112,80},{... | collective-permute-start | bytes 393224 | tf_op jit(solution)/shard_map/ppermute | solution.py:400
  164.0 2.7 %collective-permute-start.19 = (f32[32,1024]{1,0:T(8,128)S(1)}, f32[32,1024]{1,0:T(8,128)S(1)}, u32[]{:S(2)}, u32[]{:S(2)}) collective-permute-start(f32[32,1024]{1,0:T(8,128)S(1)} %shard_map.85), channel_id=1, source_target_pairs={{0,224},{16,240},{32,0},{48,16},{64,32},{80,48},{96,64},{112,80},{... | collective-permute-start | bytes 393224 | tf_op jit(solution)/shard_map/ppermute | solution.py:400
  166.8 2.5 %collective-permute-done.7.up_ref = f32[32,1024]{1,0:T(8,128)S(1)} collective-permute-done((f32[32,1024]{1,0:T(8,128)S(1)}, f32[32,1024]{1,0:T(8,128)S(1)}, u32[]{:S(2)}, u32[]{:S(2)}) %collective-permute-start.7) | collective-permute-done | bytes 131104 | tf_op jit(solution)/shard_map/ppermute | solution.py:400
  169.3 5.4 %collective-permute-start.20 = (f32[16,1024]{1,0:T(8,128)S(1)}, f32[16,1024]{1,0:T(8,128)S(1)}, u32[]{:S(2)}, u32[]{:S(2)}) collective-permute-start(f32[16,1024]{1,0:T(8,128)S(1)} %get-tuple-element.92), channel_id=1, source_target_pairs={{0,16},{16,0},{32,48},{48,32},{64,80},{80,64},{96,112},{112,96},{1... | collective-permute-start | bytes 196616 | tf_op jit(solution)/shard_map/ppermute | solution.py:396
  174.8 3.4 %collective-permute-start.21 = (f32[16,1024]{1,0:T(8,128)S(1)}, f32[16,1024]{1,0:T(8,128)S(1)}, u32[]{:S(2)}, u32[]{:S(2)}) collective-permute-start(f32[16,1024]{1,0:T(8,128)S(1)} %get-tuple-element.93), channel_id=1, source_target_pairs={{0,16},{16,0},{32,48},{48,32},{64,80},{80,64},{96,112},{112,96},{1... | collective-permute-start | bytes 196616 | tf_op jit(solution)/shard_map/ppermute | solution.py:396
  178.2 53.2 %all-reduce.2.cloned.1.call-done.probs_ref = f32[512,256]{1,0:T(8,128)} async-done(((f32[512,256]{1,0:T(8,128)}), f32[512,256]{1,0:T(8,128)}) %all-reduce.2.cloned.1.call-update) | async-done | bytes 524304 | tf_op jit(solution)/shard_map/psum | solution.py:496
  232.4 2.6 %shard_map.72 = f32[4,256,256]{2,1,0:T(8,128)} custom-call(s32[2]{0:T(128)S(1)} %pad_add_fusion.where_ref, f32[512,256]{1,0:T(8,128)S(1)} %copy-done.9, f32[512,256]{1,0:T(8,128)S(1)} %bitcast.3, f32[32,16,128]{2,1,0:T(8,128)S(1)} %all_to_all.36.parts_ref.mass_ref, f32[1,8,128]{2,1,0:T(8,128)S(1)} %get-tuple-element.68.parts_ref.sums_ref, ...), custom_call_target="tpu_custom_call" | custom-call | tf_op jit(solution)/shard_map/pallas_call | solution.py:433
  (127 shorter events, 28.5 us)
Async XLA Ops:
  10.6 5.9 %collective-permute-start.2 = (f32[512,256]{1,0:T(8,128)S(1)}, f32[512,256]{1,0:T(8,128)}, u32[]{:S(2)}, u32[]{:S(2)}) collective-permute-start(f32[512,256]{1,0:T(8,128)S(1)} %get-tuple-element.53.own_ref), channel_id=1, source_target_pairs={{0,16},{16,0},{32,48},{48,32},{64,80},{80,64},{96,112},{112,96},{1... | collective-permute-start | bytes 1572872 | tf_op jit(solution)/shard_map/ppermute | solution.py:396
  13.9 5.1 %collective-permute-start = (f32[512,256]{1,0:T(8,128)S(1)}, f32[512,256]{1,0:T(8,128)}, u32[]{:S(2)}, u32[]{:S(2)}) collective-permute-start(f32[512,256]{1,0:T(8,128)S(1)} %get-tuple-element.48.own_ref), channel_id=1, source_target_pairs={{0,16},{16,0},{32,48},{48,32},{64,80},{80,64},{96,112},{112,96},{1... | collective-permute-start | bytes 1572872 | tf_op jit(solution)/shard_map/ppermute | solution.py:396
  19.0 74.2 %copy-start = (f32[1024,2048]{1,0:T(8,128)}, f32[1024,2048]{1,0:T(8,128)S(1)}, u32[]{:S(2)}) copy-start(f32[1024,2048]{1,0:T(8,128)S(1)} %get-tuple-element.54.e_ref) | copy-start | bytes 25165828
  25.5 44.1 %copy-start.33 = (f32[512,256]{1,0:T(8,128)}, f32[512,256]{1,0:T(8,128)S(1)}, u32[]{:S(2)}) copy-start(f32[512,256]{1,0:T(8,128)S(1)} %get-tuple-element.52) | copy-start | bytes 1572868
  96.0 3.3 %collective-permute-start.3 = (f32[520,256]{1,0:T(8,128)S(1)}, f32[520,256]{1,0:T(8,128)S(1)}, u32[]{:S(2)}, u32[]{:S(2)}) collective-permute-start(f32[520,256]{1,0:T(8,128)S(1)} %get-tuple-element.61.mine_ref), channel_id=1, source_target_pairs={{0,16},{16,0},{32,48},{48,32},{64,80},{80,64},{96,112},{112,96},{1... | collective-permute-start | bytes 1597448 | tf_op jit(solution)/shard_map/ppermute | solution.py:396
  100.2 16.0 %all-to-all-start.5 = ((f32[16,40,256]{2,1,0:T(8,128)}), f32[16,40,256]{2,1,0:T(8,128)S(1)}, u32[]{:S(2)}, u32[]{:S(2)}) async-start(f32[16,40,256]{2,1,0:T(8,128)} %copy-done.4), calls=%async_computation.5 | async-start | bytes 1310720 | tf_op jit(solution)/shard_map/all_to_all | solution.py:531
  103.8 127.6 %all-reduce.2.cloned.1.call-start = ((), (), s32[]{:S(2)}) async-start(), calls=%async_computation.7 | async-start | bytes 1048576 | tf_op jit(solution)/shard_map/psum | solution.py:496
  103.8 36.2 %collective-permute-start.1 = (f32[512,256]{1,0:T(8,128)}, f32[512,256]{1,0:T(8,128)}, u32[]{:S(2)}, u32[]{:S(2)}) collective-permute-start(f32[512,256]{1,0:T(8,128)} %copy-done.33), channel_id=1, source_target_pairs={{0,16},{16,0},{32,48},{48,32},{64,80},{80,64},{96,112},{112,96},{1... | collective-permute-start | bytes 1572872 | tf_op jit(solution)/shard_map/ppermute | solution.py:396
  129.5 19.3 %collective-permute-start.4 = (f32[16,1024]{1,0:T(8,128)}, f32[16,1024]{1,0:T(8,128)}, u32[]{:S(2)}, u32[]{:S(2)}) collective-permute-start(f32[16,1024]{1,0:T(8,128)} %get-tuple-element.77), channel_id=1, source_target_pairs={{0,32},{16,48},{32,64},{48,80},{64,96},{80,112},{96,128},{112,144}... | collective-permute-start | bytes 196616 | tf_op jit(solution)/shard_map/ppermute | solution.py:400
  129.8 15.8 %collective-permute-start.8 = (f32[16,1024]{1,0:T(8,128)}, f32[16,1024]{1,0:T(8,128)}, u32[]{:S(2)}, u32[]{:S(2)}) collective-permute-start(f32[16,1024]{1,0:T(8,128)} %get-tuple-element.81), channel_id=1, source_target_pairs={{0,224},{16,240},{32,0},{48,16},{64,32},{80,48},{96,64},{112,80},{... | collective-permute-start | bytes 196616 | tf_op jit(solution)/shard_map/ppermute | solution.py:400
  138.5 22.0 %copy-start.15 = (f32[32,1024]{1,0:T(8,128)S(1)}, f32[32,1024]{1,0:T(8,128)}, u32[]{:S(2)}) copy-start(f32[32,1024]{1,0:T(8,128)} %copy-done.14) | copy-start | bytes 393220
  138.5 22.1 %copy-start.13 = (f32[32,1024]{1,0:T(8,128)S(1)}, f32[32,1024]{1,0:T(8,128)}, u32[]{:S(2)}) copy-start(f32[32,1024]{1,0:T(8,128)} %copy-done.12) | copy-start | bytes 393220
  138.5 12.4 %collective-permute-start.16 = (f32[16,1024]{1,0:T(8,128)}, f32[16,1024]{1,0:T(8,128)S(1)}, u32[]{:S(2)}, u32[]{:S(2)}) collective-permute-start(f32[16,1024]{1,0:T(8,128)} %get-tuple-element.90), channel_id=1, source_target_pairs={{0,224},{16,240},{32,0},{48,16},{64,32},{80,48},{96,64},{112,80},{... | collective-permute-start | bytes 196616 | tf_op jit(solution)/shard_map/ppermute | solution.py:400
  138.6 15.7 %collective-permute-start.12 = (f32[16,1024]{1,0:T(8,128)}, f32[16,1024]{1,0:T(8,128)S(1)}, u32[]{:S(2)}, u32[]{:S(2)}) collective-permute-start(f32[16,1024]{1,0:T(8,128)} %get-tuple-element.86), channel_id=1, source_target_pairs={{0,32},{16,48},{32,64},{48,80},{64,96},{80,112},{96,128},{112,144}... | collective-permute-start | bytes 196616 | tf_op jit(solution)/shard_map/ppermute | solution.py:400
  140.0 91.3 %copy-start.8 = (f32[512,256]{1,0:T(8,128)S(1)}, f32[512,256]{1,0:T(8,128)}, u32[]{:S(2)}) copy-start(f32[512,256]{1,0:T(8,128)} %copy-done.7) | copy-start | bytes 1572868
  140.0 91.3 %copy-start.11 = (f32[512,1]{1,0:T(8,128)S(1)}, f32[512,1]{1,0:T(8,128)}, u32[]{:S(2)}) copy-start(f32[512,1]{1,0:T(8,128)} %copy-done.10) | copy-start | bytes 6148
  140.0 91.3 %copy-start.32 = (s32[4,128]{1,0:T(4,128)S(1)}, s32[4,128]{1,0:T(4,128)}, u32[]{:S(2)}) copy-start(s32[4,128]{1,0:T(4,128)} %mask_ref.1) | copy-start | bytes 6148
  142.0 89.3 %all-to-all-start.6 = ((f32[16,32,256]{2,1,0:T(8,128)}), f32[16,32,256]{2,1,0:T(8,128)S(1)}, u32[]{:S(2)}, u32[]{:S(2)}) async-start(f32[16,32,256]{2,1,0:T(8,128)} %get-tuple-element.71), calls=%async_computation.6 | async-start | bytes 1048576 | tf_op jit(solution)/shard_map/all_to_all | solution.py:557
  147.4 7.0 %collective-permute-start.9 = (f32[32,1024]{1,0:T(8,128)S(1)}, f32[32,1024]{1,0:T(8,128)S(1)}, u32[]{:S(2)}, u32[]{:S(2)}) collective-permute-start(f32[32,1024]{1,0:T(8,128)S(1)} %shard_map.76), channel_id=1, source_target_pairs={{0,224},{16,240},{32,0},{48,16},{64,32},{80,48},{96,64},{112,80},{... | collective-permute-start | bytes 393224 | tf_op jit(solution)/shard_map/ppermute | solution.py:400
  150.5 6.6 %collective-permute-start.5 = (f32[32,1024]{1,0:T(8,128)S(1)}, f32[32,1024]{1,0:T(8,128)S(1)}, u32[]{:S(2)}, u32[]{:S(2)}) collective-permute-start(f32[32,1024]{1,0:T(8,128)S(1)} %shard_map.73), channel_id=1, source_target_pairs={{0,32},{16,48},{32,64},{48,80},{64,96},{80,112},{96,128},{112,144}... | collective-permute-start | bytes 393224 | tf_op jit(solution)/shard_map/ppermute | solution.py:400
  151.7 5.6 %collective-permute-start.17 = (f32[32,1024]{1,0:T(8,128)S(1)}, f32[32,1024]{1,0:T(8,128)S(1)}, u32[]{:S(2)}, u32[]{:S(2)}) collective-permute-start(f32[32,1024]{1,0:T(8,128)S(1)} %shard_map.83), channel_id=1, source_target_pairs={{0,224},{16,240},{32,0},{48,16},{64,32},{80,48},{96,64},{112,80},{... | collective-permute-start | bytes 393224 | tf_op jit(solution)/shard_map/ppermute | solution.py:400
  154.3 6.1 %collective-permute-start.13 = (f32[32,1024]{1,0:T(8,128)S(1)}, f32[32,1024]{1,0:T(8,128)S(1)}, u32[]{:S(2)}, u32[]{:S(2)}) collective-permute-start(f32[32,1024]{1,0:T(8,128)S(1)} %shard_map.80), channel_id=1, source_target_pairs={{0,32},{16,48},{32,64},{48,80},{64,96},{80,112},{96,128},{112,144}... | collective-permute-start | bytes 393224 | tf_op jit(solution)/shard_map/ppermute | solution.py:400
  154.5 6.1 %collective-permute-start.10 = (f32[32,1024]{1,0:T(8,128)S(1)}, f32[32,1024]{1,0:T(8,128)S(1)}, u32[]{:S(2)}, u32[]{:S(2)}) collective-permute-start(f32[32,1024]{1,0:T(8,128)S(1)} %shard_map.77), channel_id=1, source_target_pairs={{0,224},{16,240},{32,0},{48,16},{64,32},{80,48},{96,64},{112,80},{... | collective-permute-start | bytes 393224 | tf_op jit(solution)/shard_map/ppermute | solution.py:400
  157.2 6.6 %collective-permute-start.6 = (f32[32,1024]{1,0:T(8,128)S(1)}, f32[32,1024]{1,0:T(8,128)S(1)}, u32[]{:S(2)}, u32[]{:S(2)}) collective-permute-start(f32[32,1024]{1,0:T(8,128)S(1)} %shard_map.74), channel_id=1, source_target_pairs={{0,32},{16,48},{32,64},{48,80},{64,96},{80,112},{96,128},{112,144}... | collective-permute-start | bytes 393224 | tf_op jit(solution)/shard_map/ppermute | solution.py:400
  157.3 6.6 %collective-permute-start.18 = (f32[32,1024]{1,0:T(8,128)S(1)}, f32[32,1024]{1,0:T(8,128)S(1)}, u32[]{:S(2)}, u32[]{:S(2)}) collective-permute-start(f32[32,1024]{1,0:T(8,128)S(1)} %shard_map.84), channel_id=1, source_target_pairs={{0,224},{16,240},{32,0},{48,16},{64,32},{80,48},{96,64},{112,80},{... | collective-permute-start | bytes 393224 | tf_op jit(solution)/shard_map/ppermute | solution.py:400
  160.4 6.3 %collective-permute-start.14 = (f32[32,1024]{1,0:T(8,128)S(1)}, f32[32,1024]{1,0:T(8,128)S(1)}, u32[]{:S(2)}, u32[]{:S(2)}) collective-permute-start(f32[32,1024]{1,0:T(8,128)S(1)} %shard_map.81), channel_id=1, source_target_pairs={{0,32},{16,48},{32,64},{48,80},{64,96},{80,112},{96,128},{112,144}... | collective-permute-start | bytes 393224 | tf_op jit(solution)/shard_map/ppermute | solution.py:400
  160.6 6.3 %collective-permute-start.11 = (f32[32,1024]{1,0:T(8,128)S(1)}, f32[32,1024]{1,0:T(8,128)S(1)}, u32[]{:S(2)}, u32[]{:S(2)}) collective-permute-start(f32[32,1024]{1,0:T(8,128)S(1)} %shard_map.78), channel_id=1, source_target_pairs={{0,224},{16,240},{32,0},{48,16},{64,32},{80,48},{96,64},{112,80},{... | collective-permute-start | bytes 393224 | tf_op jit(solution)/shard_map/ppermute | solution.py:400
  163.9 5.4 %collective-permute-start.7 = (f32[32,1024]{1,0:T(8,128)S(1)}, f32[32,1024]{1,0:T(8,128)S(1)}, u32[]{:S(2)}, u32[]{:S(2)}) collective-permute-start(f32[32,1024]{1,0:T(8,128)S(1)} %shard_map.75), channel_id=1, source_target_pairs={{0,32},{16,48},{32,64},{48,80},{64,96},{80,112},{96,128},{112,144}... | collective-permute-start | bytes 393224 | tf_op jit(solution)/shard_map/ppermute | solution.py:400
  164.0 10.8 %collective-permute-start.19 = (f32[32,1024]{1,0:T(8,128)S(1)}, f32[32,1024]{1,0:T(8,128)S(1)}, u32[]{:S(2)}, u32[]{:S(2)}) collective-permute-start(f32[32,1024]{1,0:T(8,128)S(1)} %shard_map.85), channel_id=1, source_target_pairs={{0,224},{16,240},{32,0},{48,16},{64,32},{80,48},{96,64},{112,80},{... | collective-permute-start | bytes 393224 | tf_op jit(solution)/shard_map/ppermute | solution.py:400
  166.7 8.0 %collective-permute-start.15 = (f32[32,1024]{1,0:T(8,128)S(1)}, f32[32,1024]{1,0:T(8,128)S(1)}, u32[]{:S(2)}, u32[]{:S(2)}) collective-permute-start(f32[32,1024]{1,0:T(8,128)S(1)} %shard_map.82), channel_id=1, source_target_pairs={{0,32},{16,48},{32,64},{48,80},{64,96},{80,112},{96,128},{112,144}... | collective-permute-start | bytes 393224 | tf_op jit(solution)/shard_map/ppermute | solution.py:400
  169.3 65.7 %collective-permute-start.20 = (f32[16,1024]{1,0:T(8,128)S(1)}, f32[16,1024]{1,0:T(8,128)S(1)}, u32[]{:S(2)}, u32[]{:S(2)}) collective-permute-start(f32[16,1024]{1,0:T(8,128)S(1)} %get-tuple-element.92), channel_id=1, source_target_pairs={{0,16},{16,0},{32,48},{48,32},{64,80},{80,64},{96,112},{112,96},{1... | collective-permute-start | bytes 196616 | tf_op jit(solution)/shard_map/ppermute | solution.py:396
  174.8 60.2 %collective-permute-start.21 = (f32[16,1024]{1,0:T(8,128)S(1)}, f32[16,1024]{1,0:T(8,128)S(1)}, u32[]{:S(2)}, u32[]{:S(2)}) collective-permute-start(f32[16,1024]{1,0:T(8,128)S(1)} %get-tuple-element.93), channel_id=1, source_target_pairs={{0,16},{16,0},{32,48},{48,32},{64,80},{80,64},{96,112},{112,96},{1... | collective-permute-start | bytes 196616 | tf_op jit(solution)/shard_map/ppermute | solution.py:396
  (29 other events, 133.6 us)
Sparse Core Ops, SparseCore 0:
  142.2 89.1 all-reduce.1

commit v5 on v3

--- a/solution.py
+++ b/solution.py
@@ -68,36 +68,30 @@
     return rows, jnp.sqrt(jnp.sum(rows * rows, axis=1, keepdims=True) + EPSILON)
 
 
-def teacher_kernel(feats_hbm, mask_hbm, unit_ref, feats_ref, mask_ref, sems):
-    for copy in fetch(((feats_hbm, feats_ref), (mask_hbm, mask_ref)), sems):
+def prep_kernel(
+    teacher_hbm, student_hbm, mask_hbm, zt_ref, zs_ref, teacher_ref, student_ref, mask_ref, sems
+):
+    mask_copy, teacher_copy, student_copy = fetch(
+        ((mask_hbm, mask_ref), (teacher_hbm, teacher_ref), (student_hbm, student_ref)), sems
+    )
+    mask_copy.wait()
+    slots = mask_ref.shape[1]
+    for copy, feats, out in (
+        (teacher_copy, teacher_ref, zt_ref), (student_copy, student_ref, zs_ref)
+    ):
         copy.wait()
-    slots = mask_ref.shape[1]
-    for i in range(feats_ref.shape[0]):
-        rows, norm = masked_rows(feats_ref[i], mask_ref[i : i + 1, :])
-        unit_ref[i * slots : (i + 1) * slots, :] = (rows / norm).astype(BF16).astype(F32)
-
-
-def student_kernel(
-    feats_hbm, mask_hbm, unit_ref, full_ref, norm_ref, feats_ref, mask_ref, sems
-):
-    for copy in fetch(((feats_hbm, feats_ref), (mask_hbm, mask_ref)), sems):
-        copy.wait()
-    slots = mask_ref.shape[1]
-    for i in range(feats_ref.shape[0]):
-        take = pl.ds(i * slots, slots)
-        rows, norm = masked_rows(feats_ref[i], mask_ref[i : i + 1, :])
-        full = rows / norm
-        full_ref[take, :] = full
-        unit_ref[take, :] = full.astype(BF16).astype(F32)
-        norm_ref[take, :] = norm
-
-
-def proto_kernel(where_ref, proto_ref, full_ref, unit_ref, norm_ref):
+        for i in range(feats.shape[0]):
+            rows, norm = masked_rows(feats[i], mask_ref[i : i + 1, :])
+            out[i * slots : (i + 1) * slots, :] = (rows / norm).astype(BF16).astype(F32)
+
+
+def proto_kernel(where_ref, proto_ref, full_ref, unit_ref, back_ref, norm_ref):
     p = proto_ref[...].astype(F32)
     norm = jnp.sqrt(jnp.sum(p * p, axis=0, keepdims=True) + EPSILON)
     full = p / norm
     full_ref[...] = full
     unit_ref[...] = full.astype(BF16)
+    back_ref[...] = full.T.astype(BF16)
     norm_ref[...] = norm
 
 
@@ -226,64 +220,59 @@
         out_ref[m] = value
 
 
-def diff_kernel(part):
-    def kernel(
-        where_ref, e_ref, s_ref, full_ref, norm_ref, turned_ref, c_ref, parts_ref, mass_ref,
-        diff_ref, rel0, rel1, rel2, rel3, rel4u, rel4d, rel5, rel6, rel7,
-        r_ref, m_ref, g_ref,
-    ):
-        spread(r_ref, 1.0 / jnp.sum(parts_ref[...], axis=0))
-        spread(m_ref, (1.0 / STUDENT_TEMP) / jnp.sum(mass_ref[:, 8:, :], axis=0))
-        half = rel0.shape[1]
-        tiles = half // LANES
-        block = 16
-
-        def body(b, carry):
-            rows = pl.ds(pl.multiple_of(b * block, block), block)
-            r = r_ref[rows, :] * (1.0 / STUDENT_TEMP)
-            m = m_ref[rows, :]
-            for j in range(tiles):
-                tile = part * tiles + j
-                lanes = slice(tile * LANES, (tile + 1) * LANES)
-                targets = (r * e_ref[rows, lanes]) * c_ref[tile : tile + 1, :]
-                probs = s_ref[rows, lanes] * m
-                diff_ref[rows, j * LANES : (j + 1) * LANES] = (probs - targets).astype(BF16)
-            return carry
-
-        lax.fori_loop(0, e_ref.shape[0] // block, body, 0, unroll=2)
-        columns = slice(part * half, (part + 1) * half)
-        grad = jnp.dot(turned_ref[...], diff_ref[...], preferred_element_type=F32)
+def diff_kernel(
+    e_ref, s_ref, c_ref, parts_ref, mass_ref, diff_ref, r_ref, m_ref
+):
+    scale = 1.0 / STUDENT_TEMP
+    spread(r_ref, scale / jnp.sum(parts_ref[...], axis=0))
+    spread(m_ref, scale / jnp.sum(mass_ref[:, 8:, :], axis=0))
+    tiles = e_ref.shape[1] // LANES
+    block = 16
+
+    def body(b, carry):
+        rows = pl.ds(pl.multiple_of(b * block, block), block)
+        r = r_ref[rows, :]
+        m = m_ref[rows, :]
+        for j in range(tiles):
+            lanes = slice(j * LANES, (j + 1) * LANES)
+            targets = (r * e_ref[rows, lanes]) * c_ref[j : j + 1, :]
+            probs = s_ref[rows, lanes] * m
+            diff_ref[rows, lanes] = (probs - targets).astype(BF16)
+        return carry
+
+    lax.fori_loop(0, e_ref.shape[0] // block, body, 0)
+
+
+def token_kernel(where_ref, diff_ref, back_ref, own_ref, give_ref):
+    for side, out in enumerate((own_ref, give_ref)):
+        rows = core_rows(where_ref, side, out.shape[0])
+        out[...] = jnp.dot(diff_ref[rows, :], back_ref[...], preferred_element_type=F32)
+
+
+def grad_kernel(where_ref, diff_ref, full_ref, norm_ref, turned_ref, *refs):
+    outs, (g_ref, sems) = refs[:-2], refs[-2:]
+    wide = full_ref.shape[1]
+    for w in range(wide // WIDE):
+        columns = slice(w * WIDE, (w + 1) * WIDE)
+        grad = jnp.dot(turned_ref[...], diff_ref[:, columns], preferred_element_type=F32)
         full = full_ref[:, columns]
         proj = jnp.sum(full.astype(BF16).astype(F32) * grad, axis=0, keepdims=True)
-        g_ref[...] = (grad - full * proj) / norm_ref[:, columns]
-        core, z = where_ref[0], where_ref[1]
-        deep = g_ref.shape[0] // Z
-        near = deep // 2
-        outs = (rel0, rel1, rel2, rel3, (rel4u, rel4d), rel5, rel6, rel7)
-        for j, out in enumerate(outs):
-            top = lax.rem(z + j, Z) * deep
-            for side in range(2):
-                take = pl.multiple_of(top + lax.rem(core + side, 2) * near, near)
-                value = g_ref[pl.ds(take, near), :]
-                if j == 4:
-                    out[side][...] = value
-                else:
-                    out[side * near : (side + 1) * near, :] = value
-
-    return kernel
-
-
-def token_grad_kernel(where_ref, diff0_ref, diff1_ref, unit_ref, own_ref, other_ref):
-    half = diff0_ref.shape[1]
-    dims = (((1,), (1,)), ((), ()))
-    unit0 = unit_ref[:, :half]
-    unit1 = unit_ref[:, half:]
-    for side, out in enumerate((own_ref, other_ref)):
-        rows = core_rows(where_ref, side, out.shape[0])
-        grad = lax.dot_general(diff0_ref[rows, :], unit0, dims, preferred_element_type=F32)
-        out[...] = grad + lax.dot_general(
-            diff1_ref[rows, :], unit1, dims, preferred_element_type=F32
-        )
+        g_ref[:, columns] = (grad - full * proj) / norm_ref[:, columns]
+    core, z = where_ref[0], where_ref[1]
+    deep = g_ref.shape[0] // Z
+    near = deep // 2
+    pairs = []
+    for j in range(Z):
+        top = lax.rem(z + j, Z) * deep
+        for side in range(2):
+            take = pl.multiple_of(top + lax.rem(core + side, 2) * near, near)
+            if j == 4:
+                out = outs[4 + side]
+            else:
+                out = outs[j + (j > 4)].at[pl.ds(side * near, near), :]
+            pairs.append((g_ref.at[pl.ds(take, near), :], out))
+    for copy in fetch(pairs, sems):
+        copy.wait()
 
 
 def share_kernel(parts_ref, out_ref):
@@ -292,52 +281,58 @@
         out_ref[m] = total
 
 
-def last_kernel(gz_ref, zsf_ref, norm_ref, mask_ref, out_ref):
+def last_kernel(gz_ref, feats_ref, mask_ref, out_ref):
     slots = mask_ref.shape[1]
     for i in range(out_ref.shape[0]):
-        rows = pl.ds(i * slots, slots)
-        zsf = zsf_ref[rows, :]
-        gz = gz_ref[rows, :]
+        mask = mask_ref[i : i + 1, :]
+        xs, norm = masked_rows(feats_ref[i], mask)
+        zsf = xs / norm
+        gz = gz_ref[i * slots : (i + 1) * slots, :]
         proj = jnp.sum(zsf * gz, axis=1, keepdims=True)
-        grad = (gz - zsf * proj) / norm_ref[rows, :]
-        hot = one_hot_t(mask_ref[i : i + 1, :], out_ref.shape[1], BF16)
-        total = jnp.zeros(out_ref.shape[1:], F32)
-        for _ in range(3):
-            piece = grad.astype(BF16)
-            total += jnp.dot(hot, piece, preferred_element_type=F32)
-            grad = grad - piece.astype(F32)
-        out_ref[i] = total
-
-
-def first_sum_kernel(rel_ref, got_ref, top_ref):
-    near = got_ref.shape[0]
-    top_ref[:near, :] = rel_ref[:near, :] + got_ref[...]
-    top_ref[near:, :] = rel_ref[near:, :]
-
-
-def first_sum_low_kernel(rel_ref, got_ref, top_ref):
-    near = got_ref.shape[0]
-    top_ref[:near, :] = rel_ref[:near, :]
-    top_ref[near:, :] = rel_ref[near:, :] + got_ref[...]
-
-
-def sum_kernel(rel_ref, got_ref, out_ref):
-    out_ref[...] = rel_ref[...] + got_ref[...]
-
-
-def last_sum_kernel(rel_ref, up_ref, down_ref, keep_ref, give_ref):
+        grad = (gz - zsf * proj) / norm
+        hot = one_hot_t(mask, out_ref.shape[1], BF16)
+        high = grad.astype(BF16)
+        low = (grad - high.astype(F32)).astype(BF16)
+        out_ref[i] = jnp.dot(hot, high, preferred_element_type=F32) + jnp.dot(
+            hot, low, preferred_element_type=F32
+        )
+
+
+def sum_kernel(a_ref, b_ref, out_ref):
+    out_ref[...] = a_ref[...] + b_ref[...]
+
+
+def first_step_kernel(low):
+    def kernel(rel_hbm, got_ref, out_ref, sem):
+        for copy in fetch(((rel_hbm, out_ref),), sem):
+            copy.wait()
+        near = got_ref.shape[0]
+        rows = slice(near, 2 * near) if low else slice(0, near)
+        out_ref[rows, :] += got_ref[...]
+
+    return kernel
+
+
+def step_kernel(rel_hbm, got_ref, out_ref, sem):
+    for copy in fetch(((rel_hbm, out_ref),), sem):
+        copy.wait()
+    out_ref[...] += got_ref[...]
+
+
+def last_sum_kernel(rel_hbm, up_ref, down_ref, keep_ref, give_ref, rel, sem):
+    for copy in fetch(((rel_hbm, rel),), sem):
+        copy.wait()
     near = keep_ref.shape[0]
-    keep_ref[...] = rel_ref[:near, :] + up_ref[:near, :] + down_ref[:near, :]
-    give_ref[...] = rel_ref[near:, :] + up_ref[near:, :] + down_ref[near:, :]
-
-
-def place_kernel(where_ref, keep0_ref, keep1_ref, got0_ref, got1_ref, out_ref):
-    core = where_ref[0]
-    half = keep0_ref.shape[1]
-    for side, pair in enumerate(((keep0_ref, keep1_ref), (got0_ref, got1_ref))):
-        first = lax.rem(core + side, 2) * 2 * half
-        for i, ref in enumerate(pair):
-            out_ref[:, pl.ds(pl.multiple_of(first + i * half, half), half)] = ref[...]
+    total = rel[...] + (up_ref[...] + down_ref[...])
+    keep_ref[...] = total[:near, :]
+    give_ref[...] = total[near:, :]
+
+
+def place_kernel(where_ref, keep_ref, got_ref, out_ref):
+    wide = keep_ref.shape[1]
+    for side, ref in enumerate((keep_ref, got_ref)):
+        first = lax.rem(where_ref[0] + side, 2) * wide
+        out_ref[:, pl.ds(pl.multiple_of(first, wide), wide)] = ref[...]
 
 
 def shape(*dims, dtype=F32):
@@ -346,6 +341,14 @@
 
 def hold(*dims, dtype=F32):
     return pltpu.VMEM(dims, dtype)
+
+
+def far(*dims):
+    return pltpu.HBM(dims, F32)
+
+
+def in_hbm(x):
+    return pltpu.with_memory_space_constraint(x, pltpu.HBM)
 
 
 def other_core(x):
@@ -382,22 +385,6 @@
     where = jnp.stack([lax.rem(place, 2), lax.div(place, 2)]).astype(jnp.int32)
     scalars = pl.BlockSpec(memory_space=pltpu.SMEM)
 
-    def in_hbm(x):
-        return pltpu.with_memory_space_constraint(x, pltpu.HBM)
-
-    def prep(kernel, outs, feats):
-        return pl.pallas_call(
-            kernel,
-            in_specs=[pl.BlockSpec(memory_space=pl.ANY)] * 2,
-            out_specs=[whole()] * len(outs),
-            out_shape=outs,
-            scratch_shapes=[
-                VMEM(feats.shape, BF16), VMEM(mask_index.shape, jnp.int32),
-                pltpu.SemaphoreType.DMA((2,)),
-            ],
-            compiler_params=params(16),
-        )(in_hbm(feats), in_hbm(mask_index))
-
     def placed(kernel, outs, *args, **kw):
         return pl.pallas_call(
             kernel,
@@ -409,15 +396,22 @@
             cost_estimate=kw.get("cost_estimate"),
         )(where, *args)
 
-    (zt,) = prep(teacher_kernel, [shape(own, width)], teacher_feats)
+    zt, zs = pl.pallas_call(
+        prep_kernel,
+        in_specs=[pl.BlockSpec(memory_space=pl.ANY)] * 3,
+        out_specs=[whole()] * 2,
+        out_shape=[shape(own, width), shape(own, width)],
+        scratch_shapes=[
+            VMEM(teacher_feats.shape, BF16), VMEM(student_feats.shape, BF16),
+            VMEM(mask_index.shape, jnp.int32), pltpu.SemaphoreType.DMA((3,)),
+        ],
+        compiler_params=params(16),
+    )(in_hbm(teacher_feats), in_hbm(student_feats), in_hbm(mask_index))
     zt_other = other_core(zt)
-    zs, zsf, s_norm = prep(
-        student_kernel, [shape(own, width), shape(own, width), shape(own, 1)], student_feats
-    )
     zs_other = other_core(zs)
     steps = 2
     column_spec = pl.BlockSpec((width, wide // steps), lambda j, w: (0, j))
-    full, unit, p_norm = pl.pallas_call(
+    full, unit, back, p_norm = pl.pallas_call(
         proto_kernel,
         grid_spec=pltpu.PrefetchScalarGridSpec(
             num_scalar_prefetch=1,
@@ -427,10 +421,14 @@
             ],
             out_specs=[
                 column_spec, column_spec,
+                pl.BlockSpec((wide // steps, width), lambda j, w: (j, 0)),
                 pl.BlockSpec((1, wide // steps), lambda j, w: (0, j)),
             ],
         ),
-        out_shape=[shape(width, wide), shape(width, wide, dtype=BF16), shape(1, wide)],
+        out_shape=[
+            shape(width, wide), shape(width, wide, dtype=BF16),
+            shape(wide, width, dtype=BF16), shape(1, wide),
+        ],
         compiler_params=params(16),
     )(where, in_hbm(prototypes))
 
@@ -466,59 +464,65 @@
                 scratch=[VMEM((tokens, LANES), F32)],
             )
 
+    (diff,) = call(
+        diff_kernel, [shape(tokens, wide, dtype=BF16)], e, s, c, row_parts, mass,
+        scratch=[VMEM((tokens, LANES), F32), VMEM((tokens, LANES), F32)],
+    )
     deep = width // Z
     near = deep // 2
-    half = wide // 2
-    diffs, rels = [], []
-    for part in range(2):
-        diff, *rel = placed(
-            diff_kernel(part),
-            [shape(tokens, half, dtype=BF16)] + [shape(deep, half)] * 4
-            + [shape(near, half)] * 2 + [shape(deep, half)] * 3,
-            e, s, full, p_norm, turned, c, row_parts, mass,
-            scratch=[
-                VMEM((tokens, LANES), F32), VMEM((tokens, LANES), F32), VMEM((width, half), F32),
-            ],
-            cost_estimate=cost(tokens * wide * width),
-        )
-        diffs.append(diff)
-        rels.append(rel)
-
-    ups = [along_z(rel[4], 1) for rel in rels]
-    downs = [along_z(rel[5], -1) for rel in rels]
-    rels = [rel[:4] + [None] + rel[6:] for rel in rels]
-
-    diff0 = tie(diffs[0], ups[0])
+    anywhere = pl.BlockSpec(memory_space=pltpu.HBM)
+    rel = pl.pallas_call(
+        grad_kernel,
+        in_specs=[scalars] + [whole()] * 4,
+        out_specs=[anywhere] * 9,
+        out_shape=[far(deep, wide)] * 4 + [far(near, wide)] * 2 + [far(deep, wide)] * 3,
+        scratch_shapes=[VMEM((width, wide), F32), pltpu.SemaphoreType.DMA((2 * Z,))],
+        compiler_params=params(16),
+        cost_estimate=cost(2 * tokens * wide * width),
+    )(where, diff, full, p_norm, turned)
+
+    def step(kernel, term, got):
+        return pl.pallas_call(
+            kernel,
+            in_specs=[anywhere, whole()],
+            out_specs=whole(),
+            out_shape=shape(deep, wide),
+            scratch_shapes=[pltpu.SemaphoreType.DMA((1,))],
+            compiler_params=params(16),
+        )(term, got)
+
+    up, down = along_z(rel[4], 1), along_z(rel[5], -1)
     gz, gz_give = placed(
-        token_grad_kernel, [shape(own, width)] * 2, diff0, diffs[1], unit,
+        token_kernel, [shape(own, width)] * 2, tie(diff, rel), back,
         cost_estimate=cost(2 * tokens * wide * width),
     )
-    gz = gz + other_core(gz_give)
-    gz_parts = lax.all_to_all(gz.reshape(RING, own // RING, width), "proto", 0, 0)
+    gz_got = other_core(gz_give)
+    up = step(first_step_kernel(False), rel[3], up)
+    down = step(first_step_kernel(True), rel[6], down)
+    (gz,) = call(sum_kernel, [shape(own, width)], gz, gz_got)
+    gz_parts = lax.all_to_all(
+        tie(gz, (up, down)).reshape(RING, own // RING, width), "proto", 0, 0
+    )
+    up = step(step_kernel, rel[2], along_z(up, 1))
+    down = step(step_kernel, rel[7], along_z(down, -1))
     (gz_share,) = call(share_kernel, [shape(RING, own // RING, width)], gz_parts)
-    gz = lax.all_to_all(gz_share, "proto", 0, 0).reshape(own, width)
+    gz = lax.all_to_all(tie(gz_share, (up, down)), "proto", 0, 0).reshape(own, width)
+    up = step(step_kernel, rel[1], along_z(up, 1))
+    down = step(step_kernel, rel[8], along_z(down, -1))
+    up, down = along_z(up, 1), along_z(down, -1)
+    keep, give = pl.pallas_call(
+        last_sum_kernel,
+        in_specs=[anywhere, whole(), whole()],
+        out_specs=[whole()] * 2,
+        out_shape=[shape(near, wide)] * 2,
+        scratch_shapes=[VMEM((deep, wide), F32), pltpu.SemaphoreType.DMA((1,))],
+        compiler_params=params(16),
+    )(rel[0], up, down)
+    got = other_core(give)
     (grad_student,) = call(
-        last_kernel, [shape(images, patches, width)], gz, zsf, s_norm, mask_index
-    )
-
-    part_shape = [shape(deep, half)]
-    ups = [along_z(call(first_sum_kernel, part_shape, r[3], u)[0], 1) for r, u in zip(rels, ups)]
-    downs = [
-        along_z(call(first_sum_low_kernel, part_shape, r[5], d)[0], -1)
-        for r, d in zip(rels, downs)
-    ]
-    for j in (2, 1):
-        ups = [along_z(call(sum_kernel, part_shape, r[j], u)[0], 1) for r, u in zip(rels, ups)]
-        downs = [
-            along_z(call(sum_kernel, part_shape, r[8 - j], d)[0], -1)
-            for r, d in zip(rels, downs)
-        ]
-    keeps, gots = [], []
-    for rel, up, down in zip(rels, ups, downs):
-        keep, give = call(last_sum_kernel, [shape(near, half)] * 2, rel[0], up, down)
-        keeps.append(keep)
-        gots.append(other_core(give))
-    (grad_protos,) = placed(place_kernel, [shape(near, 2 * wide)], *keeps, *gots)
+        last_kernel, [shape(images, patches, width)], gz, student_feats, mask_index
+    )
+    (grad_protos,) = placed(place_kernel, [shape(near, 2 * wide)], keep, got)
     return (grad_student, grad_protos)
 
 

time: 159 us -> 150 us (0.943)
  starting transfers between devices: 40.1 us -> 29.6 us
  waiting for transfers between devices: 13.5 us -> 16 us
    ppermute x16 -> x8, waiting for transfers between devices: 3.88 us -> 15 us  [along_z(): lax.ppermute(x, 'batch', [(i, (i // 2 + d) % Z * 2 + i % 2) for i in rang...]
    ppermute x16 -> x8, starting transfers between devices: 19.9 us -> 11.2 us  [along_z(): lax.ppermute(x, 'batch', [(i, (i // 2 + d) % Z * 2 + i % 2) for i in rang...]
    all_to_all x2, waiting for transfers between devices: 7.19 us -> 0.01 us  [the longest x1 0.01 us: on_device(): lax.all_to_all(tie(gz_share, (up, down)), 'proto', 0, 0).reshape(own, width)]
    pallas_call x6 -> x4, Pallas kernels: 13.5 us -> 7 us  [placed(): pl.pallas_call(kernel, in_specs=[scalars] + [whole()] * len(args), out_sp...]
    ppermute x5 -> x4, starting transfers between devices: 13 us -> 8.5 us  [other_core(): return lax.ppermute(x, 'batch', [(i, i ^ 1) for i in range(RING)])]
    pallas_call x21 -> x9, Pallas kernels: 8.87 us -> 12.2 us  [call(): pl.pallas_call(kernel, out_shape=outs, in_specs=[whole()] * len(args), ou...]
    pallas_call x2 -> x9, Pallas kernels: 2.96 us -> 6.05 us  [the longest x1 3.73 us: on_device(): pl.pallas_call(grad_kernel, in_specs=[scalars] + [whole()] * 4, out_specs...]
    all_to_all x2, starting transfers between devices: 7.15 us -> 9.94 us  [the longest x1 6.24 us: on_device(): lax.all_to_all(tie(gz_share, (up, down)), 'proto', 0, 0).reshape(own, width)]
  transfers between devices with their start and end apart: 23 -> 14, of which waited for: 8 -> 5; matrix products, arithmetic and copies ran while one was open for 0% -> 0% of each run, Pallas kernels for 7% -> 5%
where the time goes in v5:
time: 150 us; the launch traced here: 149 us
  blocking collectives  74.8 us (50%)
  starting transfers between devices  29.6 us (20%)
  Pallas kernels  27.8 us (19%)
  waiting for transfers between devices  16 us (11%)
    all_to_all x3, blocking collectives, all_rows(): lax.all_to_all(x, ('batch', 'proto'), 0, 0, axis_index_groups=ROW_GROUPS)  42.1 us
    all_to_all x3, blocking collectives, all_columns(): return lax.all_to_all(x, 'batch', 0, 0, axis_index_groups=Z_GROUPS)  32.7 us
    ppermute x8, waiting for transfers between devices, along_z(): lax.ppermute(x, 'batch', [(i, (i // 2 + d) % Z * 2 + i % 2) for i in rang...  15 us
    pallas_call x9, Pallas kernels, call(): pl.pallas_call(kernel, out_shape=outs, in_specs=[whole()] * len(args), ou...  12.2 us
    ppermute x8, starting transfers between devices, along_z(): lax.ppermute(x, 'batch', [(i, (i // 2 + d) % Z * 2 + i % 2) for i in rang...  11.2 us
    ppermute x4, starting transfers between devices, other_core(): return lax.ppermute(x, 'batch', [(i, i ^ 1) for i in range(RING)])  8.5 us
    pallas_call x4, Pallas kernels, placed(): pl.pallas_call(kernel, in_specs=[scalars] + [whole()] * len(args), out_sp...  7 us
    all_to_all x1, starting transfers between devices, on_device(): lax.all_to_all(tie(gz_share, (up, down)), 'proto', 0, 0).reshape(own, width)  6.24 us
  transfers between devices with their start and end apart: 14, of which 5 were waited for; matrix products, arithmetic and copies ran while one was open for 0% of the time, Pallas kernels for 5%

profile of v5, /device:TPU:1, one launch (start us, length us, event | category | flops | bytes accessed | tf_op | source)
XLA Modules:
  0.0 149.3 jit_solution(13827123943559915880)
XLA Ops:
  0.6 1.9 %shard_map.59 = (f32[512,256]{1,0:T(8,128)S(1)}, f32[512,256]{1,0:T(8,128)S(1)}) custom-call(bf16[4,256,256]{2,1,0:T(8,128)(2,1)} %teacher_hbm.1, bf16[4,256,256]{2,1,0:T(8,128)(2,1)} %feats_ref.1, s32[4,128]{1,0:T(4,128)} %mask_ref.1), custom_call_target="tpu_custom_call" | custom-call | tf_op jit(solution)/shard_map/pallas_call | solution.py:399
  2.6 3.3 %collective-permute-start = (f32[512,256]{1,0:T(8,128)S(1)}, f32[512,256]{1,0:T(8,128)S(1)}, u32[]{:S(2)}, u32[]{:S(2)}) collective-permute-start(f32[512,256]{1,0:T(8,128)S(1)} %get-tuple-element.34.own_ref), channel_id=1, source_target_pairs={{0,16},{16,0},{32,48},{48,32},{64,80},{80,64},{96,112},{112,96},{1... | collective-permute-start | bytes 1572872 | tf_op jit(solution)/shard_map/ppermute | solution.py:355
  6.1 2.6 %shard_map.60 = (f32[256,2048]{1,0:T(8,128)S(1)}, bf16[256,2048]{1,0:T(8,128)(2,1)S(1)}, bf16[2048,256]{1,0:T(8,128)(2,1)S(1)}, f32[1,2048]{1,0:T(1,128)S(1)}) custom-call(s32[2]{0:T(128)S(1)} %pad_add_fusion.where_ref, bf16[256,4096]{1,0:T(8,128)(2,1)} %proto_ref.1), custom_call_target="tpu_custom_call" | custom-call | tf_op jit(solution)/shard_map/pallas_call | solution.py:414
  8.7 1.9 %shard_map.61 = (f32[1024,2048]{1,0:T(8,128)S(1)}, f32[8,16,128]{2,1,0:T(8,128)S(1)}) custom-call(s32[2]{0:T(128)S(1)} %pad_add_fusion.where_ref, f32[512,256]{1,0:T(8,128)S(1)} %get-tuple-element.34.own_ref, f32[512,256]{1,0:T(8,128)S(1)} %collective-permute-done.other_ref, bf16[256,2048]{1,0:T(8,128)(2,1)S(1)} %get-tuple-element.35.unit_ref), custom_call_target="tpu_custom_call" | custom-call | flops 1073741824 | tf_op jit(solution)/shard_map/pallas_call | solution.py:389
  10.6 2.0 %shard_map.62 = (f32[1024,2048]{1,0:T(8,128)S(1)}, f32[1024,128]{1,0:T(8,128)S(1)}, bf16[256,1024]{1,0:T(8,128)(2,1)S(1)}) custom-call(s32[2]{0:T(128)S(1)} %pad_add_fusion.where_ref, f32[512,256]{1,0:T(8,128)S(1)} %get-tuple-element.37.own_ref, f32[512,256]{1,0:T(8,128)S(1)} %collective-permute-done.1.other_ref, ...), custom_call_target="tpu_custom_call" | custom-call | flops 1073741824 | tf_op jit(solution)/shard_map/pallas_call | solution.py:389
  12.6 13.5 %all_to_all.40.parts_ref = f32[8,16,128]{2,1,0:T(8,128)S(1)} all-to-all(f32[8,16,128]{2,1,0:T(8,128)S(1)} %get-tuple-element.41), channel_id=1, replica_groups={{0,32,64,96,128,160,192,224},{16,48,80,112,144,176,208,240},{1,33,65,97..., dimensions={0} | all-to-all | bytes 131072 | tf_op jit(solution)/shard_map/all_to_all | solution.py:365
  26.1 1.6 %shard_map.63 = (f32[32,16,128]{2,1,0:T(8,128)S(1)}, f32[16,128]{1,0:T(8,128)}) custom-call(f32[1024,2048]{1,0:T(8,128)S(1)} %get-tuple-element.36.e_ref, f32[8,16,128]{2,1,0:T(8,128)S(1)} %all_to_all.40.parts_ref, f32[1024,128]{1,0:T(8,128)S(1)} %get-tuple-element.40.mass_ref), custom_call_target="tpu_custom_call" | custom-call | tf_op jit(solution)/shard_map/pallas_call | solution.py:41
  27.7 17.0 %all_to_all.41.parts_ref.mass_ref = f32[32,16,128]{2,1,0:T(8,128)S(1)} all-to-all(f32[32,16,128]{2,1,0:T(8,128)S(1)} %get-tuple-element.42), channel_id=1, replica_groups={{0,1,2,3,4,5,6,7,8,9,10,11,12,13,14,15,16,17,18,19,20,21,22,23,24,25,26..., dimensions={0} | all-to-all | bytes 524288 | tf_op jit(solution)/shard_map/all_to_all | solution.py:369
  44.7 1.1 shard_map.64
  45.8 9.6 %all_to_all.42.parts_ref = f32[8,16,128]{2,1,0:T(8,128)S(1)} all-to-all(f32[8,16,128]{2,1,0:T(8,128)S(1)} %shard_map.64), channel_id=1, replica_groups={{0,32,64,96,128,160,192,224},{16,48,80,112,144,176,208,240},{1,33,65,97..., dimensions={0} | all-to-all | bytes 131072 | tf_op jit(solution)/shard_map/all_to_all | solution.py:365
  55.4 1.3 shard_map.65
  56.7 12.8 %all_to_all.43.parts_ref = f32[32,8,128]{2,1,0:T(8,128)S(1)} all-to-all(f32[32,8,128]{2,1,0:T(8,128)S(1)} %get-tuple-element.43), channel_id=1, replica_groups={{0,1,2,3,4,5,6,7,8,9,10,11,12,13,14,15,16,17,18,19,20,21,22,23,24,25,26..., dimensions={0} | all-to-all | bytes 262144 | tf_op jit(solution)/shard_map/all_to_all | solution.py:369
  69.5 1.1 shard_map.66
  70.5 9.6 %all_to_all.44.parts_ref = f32[8,16,128]{2,1,0:T(8,128)S(1)} all-to-all(f32[8,16,128]{2,1,0:T(8,128)S(1)} %shard_map.66), channel_id=1, replica_groups={{0,32,64,96,128,160,192,224},{16,48,80,112,144,176,208,240},{1,33,65,97..., dimensions={0} | all-to-all | bytes 131072 | tf_op jit(solution)/shard_map/all_to_all | solution.py:365
  81.1 12.4 %all_to_all.45.parts_ref = f32[32,8,128]{2,1,0:T(8,128)S(1)} all-to-all(f32[32,8,128]{2,1,0:T(8,128)S(1)} %get-tuple-element.45), channel_id=1, replica_groups={{0,1,2,3,4,5,6,7,8,9,10,11,12,13,14,15,16,17,18,19,20,21,22,23,24,25,26..., dimensions={0} | all-to-all | bytes 262144 | tf_op jit(solution)/shard_map/all_to_all | solution.py:369
  93.5 2.3 %shard_map.68.diff_ref = bf16[1024,2048]{1,0:T(8,128)(2,1)S(1)} custom-call(f32[1024,2048]{1,0:T(8,128)S(1)} %get-tuple-element.36.e_ref, f32[1024,2048]{1,0:T(8,128)S(1)} %get-tuple-element.38.s_ref, f32[16,128]{1,0:T(8,128)S(1)} %get-tuple-element.44.c_ref, f32[32,8,128]{2,1,0:T(8,128)S(1)} %all_to_all.45.parts_ref, ...), custom_call_target="tpu_custom_call" | custom-call | tf_op jit(solution)/shard_map/pallas_call | solution.py:41
  95.8 3.7 %shard_map.69 = (f32[32,2048]{1,0:T(8,128)}, f32[32,2048]{1,0:T(8,128)}, f32[32,2048]{1,0:T(8,128)}, f32[32,2048]{1,0:T(8,128)}, f32[16,2048]{1,0:T(8,128)}, /*i...) custom-call(s32[2]{0:T(128)S(1)} %pad_add_fusion.where_ref, ...), custom_call_target="tpu_custom_call" | custom-call | flops 1073741824 | tf_op jit(solution)/shard_map/pallas_call | solution.py:474
  99.6 1.8 %shard_map.70 = (f32[512,256]{1,0:T(8,128)S(1)}, f32[512,256]{1,0:T(8,128)S(1)}) custom-call(s32[2]{0:T(128)S(1)} %pad_add_fusion.where_ref, bf16[1024,2048]{1,0:T(8,128)(2,1)S(1)} %shard_map.68.diff_ref, bf16[2048,256]{1,0:T(8,128)(2,1)S(1)} %get-tuple-element.59.back_ref), custom_call_target="tpu_custom_call" | custom-call | flops 1073741824 | tf_op jit(solution)/shard_map/pallas_call | solution.py:389
  102.3 2.4 %collective-permute-start.4 = (f32[16,2048]{1,0:T(8,128)S(1)}, f32[16,2048]{1,0:T(8,128)S(1)}, u32[]{:S(2)}, u32[]{:S(2)}) collective-permute-start(f32[16,2048]{1,0:T(8,128)S(1)} %copy-done.9), channel_id=1, source_target_pairs={{0,224},{16,240},{32,0},{48,16},{64,32},{80,48},{96,64},{112,80},{... | collective-permute-start | bytes 393224 | tf_op jit(solution)/shard_map/ppermute | solution.py:359
  104.7 3.6 %collective-permute-done.3.got_ref = f32[16,2048]{1,0:T(8,128)S(1)} collective-permute-done((f32[16,2048]{1,0:T(8,128)S(1)}, f32[16,2048]{1,0:T(8,128)S(1)}, u32[]{:S(2)}, u32[]{:S(2)}) %collective-permute-start.3) | collective-permute-done | bytes 131104 | tf_op jit(solution)/shard_map/ppermute | solution.py:359
  109.3 3.7 %all-to-all-start.6 = ((f32[16,32,256]{2,1,0:T(8,128)}), f32[16,32,256]{2,1,0:T(8,128)S(1)}, u32[]{:S(2)}, u32[]{:S(2)}) async-start(f32[16,32,256]{2,1,0:T(8,128)} %bitcast.2), calls=%async_computation.6 | async-start | bytes 1048576 | tf_op jit(solution)/shard_map/all_to_all | solution.py:503
  113.0 2.4 %collective-permute-start.6 = (f32[32,2048]{1,0:T(8,128)S(1)}, f32[32,2048]{1,0:T(8,128)S(1)}, u32[]{:S(2)}, u32[]{:S(2)}) collective-permute-start(f32[32,2048]{1,0:T(8,128)S(1)} %shard_map.73), channel_id=1, source_target_pairs={{0,224},{16,240},{32,0},{48,16},{64,32},{80,48},{96,64},{112,80},{... | collective-permute-start | bytes 786440 | tf_op jit(solution)/shard_map/ppermute | solution.py:359
  115.3 4.7 %collective-permute-done.6.got_ref = f32[32,2048]{1,0:T(8,128)S(1)} collective-permute-done((f32[32,2048]{1,0:T(8,128)S(1)}, f32[32,2048]{1,0:T(8,128)S(1)}, u32[]{:S(2)}, u32[]{:S(2)}) %collective-permute-start.6) | collective-permute-done | bytes 262176 | tf_op jit(solution)/shard_map/ppermute | solution.py:359
  120.1 3.2 %collective-permute-start.9 = (f32[32,2048]{1,0:T(8,128)S(1)}, f32[32,2048]{1,0:T(8,128)S(1)}, u32[]{:S(2)}, u32[]{:S(2)}) collective-permute-start(f32[32,2048]{1,0:T(8,128)S(1)} %shard_map.76), channel_id=1, source_target_pairs={{0,224},{16,240},{32,0},{48,16},{64,32},{80,48},{96,64},{112,80},{... | collective-permute-start | bytes 786440 | tf_op jit(solution)/shard_map/ppermute | solution.py:359
  124.3 6.2 %all-to-all-start.7 = ((f32[16,32,256]{2,1,0:T(8,128)}), f32[16,32,256]{2,1,0:T(8,128)S(1)}, u32[]{:S(2)}, u32[]{:S(2)}) async-start(f32[16,32,256]{2,1,0:T(8,128)} %shard_map.74), calls=%async_computation.7 | async-start | bytes 1048576 | tf_op jit(solution)/shard_map/all_to_all | solution.py:509
  130.7 2.7 %collective-permute-start.10 = (f32[32,2048]{1,0:T(8,128)S(1)}, f32[32,2048]{1,0:T(8,128)S(1)}, u32[]{:S(2)}, u32[]{:S(2)}) collective-permute-start(f32[32,2048]{1,0:T(8,128)S(1)} %shard_map.79), channel_id=1, source_target_pairs={{0,224},{16,240},{32,0},{48,16},{64,32},{80,48},{96,64},{112,80},{... | collective-permute-start | bytes 786440 | tf_op jit(solution)/shard_map/ppermute | solution.py:359
  133.6 3.2 %collective-permute-done.10.down_ref = f32[32,2048]{1,0:T(8,128)S(1)} collective-permute-done((f32[32,2048]{1,0:T(8,128)S(1)}, f32[32,2048]{1,0:T(8,128)S(1)}, u32[]{:S(2)}, u32[]{:S(2)}) %collective-permute-start.10) | collective-permute-done | bytes 262176 | tf_op jit(solution)/shard_map/ppermute | solution.py:359
  136.7 3.6 %collective-permute-done.8.up_ref = f32[32,2048]{1,0:T(8,128)S(1)} collective-permute-done((f32[32,2048]{1,0:T(8,128)S(1)}, f32[32,2048]{1,0:T(8,128)S(1)}, u32[]{:S(2)}, u32[]{:S(2)}) %collective-permute-start.8) | collective-permute-done | bytes 262176 | tf_op jit(solution)/shard_map/ppermute | solution.py:359
  140.4 4.5 %collective-permute-start.11 = (f32[16,2048]{1,0:T(8,128)S(1)}, f32[16,2048]{1,0:T(8,128)S(1)}, u32[]{:S(2)}, u32[]{:S(2)}) collective-permute-start(f32[16,2048]{1,0:T(8,128)S(1)} %get-tuple-element.65), channel_id=1, source_target_pairs={{0,16},{16,0},{32,48},{48,32},{64,80},{80,64},{96,112},{112,96},{1... | collective-permute-start | bytes 393224 | tf_op jit(solution)/shard_map/ppermute | solution.py:355
  144.8 1.0 collective-permute-done.11.got_ref
  145.8 1.3 shard_map.81
  147.1 2.2 %shard_map.77 = f32[4,256,256]{2,1,0:T(8,128)} custom-call(f32[512,256]{1,0:T(8,128)S(1)} %bitcast.4, bf16[4,256,256]{2,1,0:T(8,128)(2,1)S(1)} %copy-done, s32[4,128]{1,0:T(4,128)S(1)} %copy-done.8), custom_call_target="tpu_custom_call" | custom-call | tf_op jit(solution)/shard_map/pallas_call | solution.py:41
  (48 shorter events, 4.4 us)
Async XLA Ops:
  2.6 6.1 %collective-permute-start = (f32[512,256]{1,0:T(8,128)S(1)}, f32[512,256]{1,0:T(8,128)S(1)}, u32[]{:S(2)}, u32[]{:S(2)}) collective-permute-start(f32[512,256]{1,0:T(8,128)S(1)} %get-tuple-element.34.own_ref), channel_id=1, source_target_pairs={{0,16},{16,0},{32,48},{48,32},{64,80},{80,64},{96,112},{112,96},{1... | collective-permute-start | bytes 1572872 | tf_op jit(solution)/shard_map/ppermute | solution.py:355
  5.9 4.7 %collective-permute-start.1 = (f32[512,256]{1,0:T(8,128)S(1)}, f32[512,256]{1,0:T(8,128)S(1)}, u32[]{:S(2)}, u32[]{:S(2)}) collective-permute-start(f32[512,256]{1,0:T(8,128)S(1)} %get-tuple-element.37.own_ref), channel_id=1, source_target_pairs={{0,16},{16,0},{32,48},{48,32},{64,80},{80,64},{96,112},{112,96},{1... | collective-permute-start | bytes 1572872 | tf_op jit(solution)/shard_map/ppermute | solution.py:355
  99.5 2.5 %copy-start.10 = (f32[16,2048]{1,0:T(8,128)S(1)}, f32[16,2048]{1,0:T(8,128)}, u32[]{:S(2)}) copy-start(f32[16,2048]{1,0:T(8,128)} %get-tuple-element.53) | copy-start | bytes 393220
  99.5 2.8 %copy-start.9 = (f32[16,2048]{1,0:T(8,128)S(1)}, f32[16,2048]{1,0:T(8,128)}, u32[]{:S(2)}) copy-start(f32[16,2048]{1,0:T(8,128)} %get-tuple-element.54) | copy-start | bytes 393220
  99.5 8.7 %copy-start.7 = (f32[32,2048]{1,0:T(8,128)S(1)}, f32[32,2048]{1,0:T(8,128)}, u32[]{:S(2)}) copy-start(f32[32,2048]{1,0:T(8,128)} %get-tuple-element.52.rel_hbm) | copy-start | bytes 786436
  99.5 8.8 %copy-start.6 = (f32[32,2048]{1,0:T(8,128)S(1)}, f32[32,2048]{1,0:T(8,128)}, u32[]{:S(2)}) copy-start(f32[32,2048]{1,0:T(8,128)} %get-tuple-element.55.rel_hbm) | copy-start | bytes 786436
  99.5 20.5 %copy-start.5 = (f32[32,2048]{1,0:T(8,128)S(1)}, f32[32,2048]{1,0:T(8,128)}, u32[]{:S(2)}) copy-start(f32[32,2048]{1,0:T(8,128)} %get-tuple-element.56.rel_hbm) | copy-start | bytes 786436
  99.5 23.7 %copy-start.4 = (f32[32,2048]{1,0:T(8,128)S(1)}, f32[32,2048]{1,0:T(8,128)}, u32[]{:S(2)}) copy-start(f32[32,2048]{1,0:T(8,128)} %get-tuple-element.51.rel_hbm) | copy-start | bytes 786436
  101.3 29.2 %copy-start.3 = (f32[32,2048]{1,0:T(8,128)S(1)}, f32[32,2048]{1,0:T(8,128)}, u32[]{:S(2)}) copy-start(f32[32,2048]{1,0:T(8,128)} %get-tuple-element.57.rel_hbm) | copy-start | bytes 786436
  101.4 32.0 %copy-start.2 = (f32[32,2048]{1,0:T(8,128)S(1)}, f32[32,2048]{1,0:T(8,128)}, u32[]{:S(2)}) copy-start(f32[32,2048]{1,0:T(8,128)} %get-tuple-element.50.rel_hbm) | copy-start | bytes 786436
  101.4 7.0 %collective-permute-start.2 = (f32[512,256]{1,0:T(8,128)S(1)}, f32[512,256]{1,0:T(8,128)S(1)}, u32[]{:S(2)}, u32[]{:S(2)}) collective-permute-start(f32[512,256]{1,0:T(8,128)S(1)} %get-tuple-element.61), channel_id=1, source_target_pairs={{0,16},{16,0},{32,48},{48,32},{64,80},{80,64},{96,112},{112,96},{1... | collective-permute-start | bytes 1572872 | tf_op jit(solution)/shard_map/ppermute | solution.py:355
  102.0 6.3 %collective-permute-start.3 = (f32[16,2048]{1,0:T(8,128)S(1)}, f32[16,2048]{1,0:T(8,128)S(1)}, u32[]{:S(2)}, u32[]{:S(2)}) collective-permute-start(f32[16,2048]{1,0:T(8,128)S(1)} %copy-done.10), channel_id=1, source_target_pairs={{0,32},{16,48},{32,64},{48,80},{64,96},{80,112},{96,128},{112,144}... | collective-permute-start | bytes 393224 | tf_op jit(solution)/shard_map/ppermute | solution.py:359
  102.3 6.0 %collective-permute-start.4 = (f32[16,2048]{1,0:T(8,128)S(1)}, f32[16,2048]{1,0:T(8,128)S(1)}, u32[]{:S(2)}, u32[]{:S(2)}) collective-permute-start(f32[16,2048]{1,0:T(8,128)S(1)} %copy-done.9), channel_id=1, source_target_pairs={{0,224},{16,240},{32,0},{48,16},{64,32},{80,48},{96,64},{112,80},{... | collective-permute-start | bytes 393224 | tf_op jit(solution)/shard_map/ppermute | solution.py:359
  108.3 32.0 %copy-start.1 = (f32[32,2048]{1,0:T(8,128)S(1)}, f32[32,2048]{1,0:T(8,128)}, u32[]{:S(2)}) copy-start(f32[32,2048]{1,0:T(8,128)} %get-tuple-element.49.rel_hbm) | copy-start | bytes 786436
  109.3 37.8 %copy-start = (bf16[4,256,256]{2,1,0:T(8,128)(2,1)S(1)}, bf16[4,256,256]{2,1,0:T(8,128)(2,1)}, u32[]{:S(2)}) copy-start(bf16[4,256,256]{2,1,0:T(8,128)(2,1)} %feats_ref.1) | copy-start | bytes 1572868
  109.3 37.8 %copy-start.8 = (s32[4,128]{1,0:T(4,128)S(1)}, s32[4,128]{1,0:T(4,128)}, u32[]{:S(2)}) copy-start(s32[4,128]{1,0:T(4,128)} %mask_ref.1) | copy-start | bytes 6148
  109.3 14.2 %all-to-all-start.6 = ((f32[16,32,256]{2,1,0:T(8,128)}), f32[16,32,256]{2,1,0:T(8,128)S(1)}, u32[]{:S(2)}, u32[]{:S(2)}) async-start(f32[16,32,256]{2,1,0:T(8,128)} %bitcast.2), calls=%async_computation.6 | async-start | bytes 1048576 | tf_op jit(solution)/shard_map/all_to_all | solution.py:503
  113.0 7.0 %collective-permute-start.6 = (f32[32,2048]{1,0:T(8,128)S(1)}, f32[32,2048]{1,0:T(8,128)S(1)}, u32[]{:S(2)}, u32[]{:S(2)}) collective-permute-start(f32[32,2048]{1,0:T(8,128)S(1)} %shard_map.73), channel_id=1, source_target_pairs={{0,224},{16,240},{32,0},{48,16},{64,32},{80,48},{96,64},{112,80},{... | collective-permute-start | bytes 786440 | tf_op jit(solution)/shard_map/ppermute | solution.py:359
  115.3 8.0 %collective-permute-start.5 = (f32[32,2048]{1,0:T(8,128)S(1)}, f32[32,2048]{1,0:T(8,128)S(1)}, u32[]{:S(2)}, u32[]{:S(2)}) collective-permute-start(f32[32,2048]{1,0:T(8,128)S(1)} %shard_map.72), channel_id=1, source_target_pairs={{0,32},{16,48},{32,64},{48,80},{64,96},{80,112},{96,128},{112,144}... | collective-permute-start | bytes 786440 | tf_op jit(solution)/shard_map/ppermute | solution.py:359
  120.1 10.5 %collective-permute-start.9 = (f32[32,2048]{1,0:T(8,128)S(1)}, f32[32,2048]{1,0:T(8,128)S(1)}, u32[]{:S(2)}, u32[]{:S(2)}) collective-permute-start(f32[32,2048]{1,0:T(8,128)S(1)} %shard_map.76), channel_id=1, source_target_pairs={{0,224},{16,240},{32,0},{48,16},{64,32},{80,48},{96,64},{112,80},{... | collective-permute-start | bytes 786440 | tf_op jit(solution)/shard_map/ppermute | solution.py:359
  123.4 10.0 %collective-permute-start.7 = (f32[32,2048]{1,0:T(8,128)S(1)}, f32[32,2048]{1,0:T(8,128)S(1)}, u32[]{:S(2)}, u32[]{:S(2)}) collective-permute-start(f32[32,2048]{1,0:T(8,128)S(1)} %shard_map.75), channel_id=1, source_target_pairs={{0,32},{16,48},{32,64},{48,80},{64,96},{80,112},{96,128},{112,144}... | collective-permute-start | bytes 786440 | tf_op jit(solution)/shard_map/ppermute | solution.py:359
  124.3 22.7 %all-to-all-start.7 = ((f32[16,32,256]{2,1,0:T(8,128)}), f32[16,32,256]{2,1,0:T(8,128)S(1)}, u32[]{:S(2)}, u32[]{:S(2)}) async-start(f32[16,32,256]{2,1,0:T(8,128)} %shard_map.74), calls=%async_computation.7 | async-start | bytes 1048576 | tf_op jit(solution)/shard_map/all_to_all | solution.py:509
  130.7 6.0 %collective-permute-start.10 = (f32[32,2048]{1,0:T(8,128)S(1)}, f32[32,2048]{1,0:T(8,128)S(1)}, u32[]{:S(2)}, u32[]{:S(2)}) collective-permute-start(f32[32,2048]{1,0:T(8,128)S(1)} %shard_map.79), channel_id=1, source_target_pairs={{0,224},{16,240},{32,0},{48,16},{64,32},{80,48},{96,64},{112,80},{... | collective-permute-start | bytes 786440 | tf_op jit(solution)/shard_map/ppermute | solution.py:359
  133.5 6.8 %collective-permute-start.8 = (f32[32,2048]{1,0:T(8,128)S(1)}, f32[32,2048]{1,0:T(8,128)S(1)}, u32[]{:S(2)}, u32[]{:S(2)}) collective-permute-start(f32[32,2048]{1,0:T(8,128)S(1)} %shard_map.78), channel_id=1, source_target_pairs={{0,32},{16,48},{32,64},{48,80},{64,96},{80,112},{96,128},{112,144}... | collective-permute-start | bytes 786440 | tf_op jit(solution)/shard_map/ppermute | solution.py:359
  140.4 5.4 %collective-permute-start.11 = (f32[16,2048]{1,0:T(8,128)S(1)}, f32[16,2048]{1,0:T(8,128)S(1)}, u32[]{:S(2)}, u32[]{:S(2)}) collective-permute-start(f32[16,2048]{1,0:T(8,128)S(1)} %get-tuple-element.65), channel_id=1, source_target_pairs={{0,16},{16,0},{32,48},{48,32},{64,80},{80,64},{96,112},{112,96},{1... | collective-permute-start | bytes 393224 | tf_op jit(solution)/shard_map/ppermute | solution.py:355

commit v6 on v5

--- a/solution.py
+++ b/solution.py
@@ -468,6 +468,11 @@
         diff_kernel, [shape(tokens, wide, dtype=BF16)], e, s, c, row_parts, mass,
         scratch=[VMEM((tokens, LANES), F32), VMEM((tokens, LANES), F32)],
     )
+    gz, gz_give = placed(
+        token_kernel, [shape(own, width)] * 2, diff, back,
+        cost_estimate=cost(2 * tokens * wide * width),
+    )
+    gz_got = other_core(gz_give)
     deep = width // Z
     near = deep // 2
     anywhere = pl.BlockSpec(memory_space=pltpu.HBM)
@@ -479,9 +484,9 @@
         scratch_shapes=[VMEM((width, wide), F32), pltpu.SemaphoreType.DMA((2 * Z,))],
         compiler_params=params(16),
         cost_estimate=cost(2 * tokens * wide * width),
-    )(where, diff, full, p_norm, turned)
-
-    def step(kernel, term, got):
+    )(where, tie(diff, (gz, gz_give)), full, p_norm, turned)
+
+    def step(kernel, term, got, work=10**9):
         return pl.pallas_call(
             kernel,
             in_specs=[anywhere, whole()],
@@ -489,27 +494,31 @@
             out_shape=shape(deep, wide),
             scratch_shapes=[pltpu.SemaphoreType.DMA((1,))],
             compiler_params=params(16),
+            cost_estimate=cost(work) if work else None,
         )(term, got)
 
     up, down = along_z(rel[4], 1), along_z(rel[5], -1)
-    gz, gz_give = placed(
-        token_kernel, [shape(own, width)] * 2, tie(diff, rel), back,
-        cost_estimate=cost(2 * tokens * wide * width),
-    )
-    gz_got = other_core(gz_give)
     up = step(first_step_kernel(False), rel[3], up)
     down = step(first_step_kernel(True), rel[6], down)
     (gz,) = call(sum_kernel, [shape(own, width)], gz, gz_got)
     gz_parts = lax.all_to_all(
-        tie(gz, (up, down)).reshape(RING, own // RING, width), "proto", 0, 0
-    )
-    up = step(step_kernel, rel[2], along_z(up, 1))
-    down = step(step_kernel, rel[7], along_z(down, -1))
+        tie(gz, rel).reshape(RING, own // RING, width), "proto", 0, 0
+    )
     (gz_share,) = call(share_kernel, [shape(RING, own // RING, width)], gz_parts)
-    gz = lax.all_to_all(tie(gz_share, (up, down)), "proto", 0, 0).reshape(own, width)
-    up = step(step_kernel, rel[1], along_z(up, 1))
-    down = step(step_kernel, rel[8], along_z(down, -1))
     up, down = along_z(up, 1), along_z(down, -1)
+    up, down = tie((up, down), gz_share)
+    up = step(step_kernel, rel[2], up)
+    down = step(step_kernel, rel[7], down)
+    gz = lax.all_to_all(gz_share, "proto", 0, 0).reshape(own, width)
+    (grad_student,) = call(
+        last_kernel, [shape(images, patches, width)], gz, student_feats, mask_index
+    )
+    up, down = along_z(up, 1), along_z(down, -1)
+    up, down = tie((up, down), gz)
+    up = step(step_kernel, rel[1], up)
+    down = step(step_kernel, rel[8], down)
+    up, down = along_z(up, 1), along_z(down, -1)
+    up, down, grad_student = lax.optimization_barrier((up, down, grad_student))
     keep, give = pl.pallas_call(
         last_sum_kernel,
         in_specs=[anywhere, whole(), whole()],
@@ -519,9 +528,6 @@
         compiler_params=params(16),
     )(rel[0], up, down)
     got = other_core(give)
-    (grad_student,) = call(
-        last_kernel, [shape(images, patches, width)], gz, student_feats, mask_index
-    )
     (grad_protos,) = placed(place_kernel, [shape(near, 2 * wide)], keep, got)
     return (grad_student, grad_protos)
 

time: 150 us -> 147 us (0.980)
  starting transfers between devices: 29.6 us -> 21.9 us
  waiting for transfers between devices: 16 us -> 19.6 us
    all_to_all x2, waiting for transfers between devices: 0.01 us -> 6.82 us  [the longest x1 4.47 us: on_device(): lax.all_to_all(tie(gz, rel).reshape(RING, own // RING, width), 'proto', 0...]
    ppermute x8, starting transfers between devices: 11.2 us -> 6.21 us  [along_z(): lax.ppermute(x, 'batch', [(i, (i // 2 + d) % Z * 2 + i % 2) for i in rang...]
    ppermute x8, waiting for transfers between devices: 15 us -> 11.7 us  [along_z(): lax.ppermute(x, 'batch', [(i, (i // 2 + d) % Z * 2 + i % 2) for i in rang...]
    all_to_all x2, starting transfers between devices: 9.94 us -> 7.46 us  [the longest x1 3.75 us: on_device(): lax.all_to_all(tie(gz, rel).reshape(RING, own // RING, width), 'proto', 0...]
  transfers between devices with their start and end apart: 14 -> 14, of which waited for: 5 -> 8; matrix products, arithmetic and copies ran while one was open for 0% -> 0% of each run, Pallas kernels for 5% -> 8%
where the time goes in v6:
time: 147 us; the launch traced here: 146 us
  blocking collectives  74.8 us (51%)
  Pallas kernels  27.8 us (19%)
  starting transfers between devices  21.9 us (15%)
  waiting for transfers between devices  19.6 us (13%)
    all_to_all x3, blocking collectives, all_rows(): lax.all_to_all(x, ('batch', 'proto'), 0, 0, axis_index_groups=ROW_GROUPS)  42.1 us
    all_to_all x3, blocking collectives, all_columns(): return lax.all_to_all(x, 'batch', 0, 0, axis_index_groups=Z_GROUPS)  32.7 us
    pallas_call x9, Pallas kernels, call(): pl.pallas_call(kernel, out_shape=outs, in_specs=[whole()] * len(args), ou...  12.1 us
    ppermute x8, waiting for transfers between devices, along_z(): lax.ppermute(x, 'batch', [(i, (i // 2 + d) % Z * 2 + i % 2) for i in rang...  11.7 us
    ppermute x4, starting transfers between devices, other_core(): return lax.ppermute(x, 'batch', [(i, i ^ 1) for i in range(RING)])  8.28 us
    pallas_call x4, Pallas kernels, placed(): pl.pallas_call(kernel, in_specs=[scalars] + [whole()] * len(args), out_sp...  7.02 us
    ppermute x8, starting transfers between devices, along_z(): lax.ppermute(x, 'batch', [(i, (i // 2 + d) % Z * 2 + i % 2) for i in rang...  6.21 us
    all_to_all x1, waiting for transfers between devices, on_device(): lax.all_to_all(tie(gz, rel).reshape(RING, own // RING, width), 'proto', 0...  4.47 us
  transfers between devices with their start and end apart: 14, of which 8 were waited for; matrix products, arithmetic and copies ran while one was open for 0% of the time, Pallas kernels for 8%

profile of v6, /device:TPU:1, one launch (start us, length us, event | category | flops | bytes accessed | tf_op | source)
XLA Modules:
  0.0 146.1 jit_solution(8611482575872016937)
XLA Ops:
  0.6 1.9 %shard_map.59 = (f32[512,256]{1,0:T(8,128)S(1)}, f32[512,256]{1,0:T(8,128)S(1)}) custom-call(bf16[4,256,256]{2,1,0:T(8,128)(2,1)} %teacher_hbm.1, bf16[4,256,256]{2,1,0:T(8,128)(2,1)} %feats_ref.1, s32[4,128]{1,0:T(4,128)} %mask_ref.1), custom_call_target="tpu_custom_call" | custom-call | tf_op jit(solution)/shard_map/pallas_call | solution.py:399
  2.6 3.3 %collective-permute-start = (f32[512,256]{1,0:T(8,128)S(1)}, f32[512,256]{1,0:T(8,128)S(1)}, u32[]{:S(2)}, u32[]{:S(2)}) collective-permute-start(f32[512,256]{1,0:T(8,128)S(1)} %get-tuple-element.40.own_ref), channel_id=1, source_target_pairs={{0,16},{16,0},{32,48},{48,32},{64,80},{80,64},{96,112},{112,96},{1... | collective-permute-start | bytes 1572872 | tf_op jit(solution)/shard_map/ppermute | solution.py:355
  6.1 2.6 %shard_map.60 = (f32[256,2048]{1,0:T(8,128)S(1)}, bf16[256,2048]{1,0:T(8,128)(2,1)S(1)}, bf16[2048,256]{1,0:T(8,128)(2,1)S(1)}, f32[1,2048]{1,0:T(1,128)S(1)}) custom-call(s32[2]{0:T(128)S(1)} %pad_add_fusion.where_ref, bf16[256,4096]{1,0:T(8,128)(2,1)} %proto_ref.1), custom_call_target="tpu_custom_call" | custom-call | tf_op jit(solution)/shard_map/pallas_call | solution.py:414
  8.7 1.9 %shard_map.61 = (f32[1024,2048]{1,0:T(8,128)S(1)}, f32[8,16,128]{2,1,0:T(8,128)S(1)}) custom-call(s32[2]{0:T(128)S(1)} %pad_add_fusion.where_ref, f32[512,256]{1,0:T(8,128)S(1)} %get-tuple-element.40.own_ref, f32[512,256]{1,0:T(8,128)S(1)} %collective-permute-done.other_ref, bf16[256,2048]{1,0:T(8,128)(2,1)S(1)} %get-tuple-element.41.unit_ref), custom_call_target="tpu_custom_call" | custom-call | flops 1073741824 | tf_op jit(solution)/shard_map/pallas_call | solution.py:389
  10.6 2.0 %shard_map.62 = (f32[1024,2048]{1,0:T(8,128)S(1)}, f32[1024,128]{1,0:T(8,128)S(1)}, bf16[256,1024]{1,0:T(8,128)(2,1)S(1)}) custom-call(s32[2]{0:T(128)S(1)} %pad_add_fusion.where_ref, f32[512,256]{1,0:T(8,128)S(1)} %get-tuple-element.43.own_ref, f32[512,256]{1,0:T(8,128)S(1)} %collective-permute-done.1.other_ref, ...), custom_call_target="tpu_custom_call" | custom-call | flops 1073741824 | tf_op jit(solution)/shard_map/pallas_call | solution.py:389
  12.7 13.5 %all_to_all.40.parts_ref = f32[8,16,128]{2,1,0:T(8,128)S(1)} all-to-all(f32[8,16,128]{2,1,0:T(8,128)S(1)} %get-tuple-element.47), channel_id=1, replica_groups={{0,32,64,96,128,160,192,224},{16,48,80,112,144,176,208,240},{1,33,65,97..., dimensions={0} | all-to-all | bytes 131072 | tf_op jit(solution)/shard_map/all_to_all | solution.py:365
  26.2 1.6 %shard_map.63 = (f32[32,16,128]{2,1,0:T(8,128)S(1)}, f32[16,128]{1,0:T(8,128)}) custom-call(f32[1024,2048]{1,0:T(8,128)S(1)} %get-tuple-element.42.e_ref, f32[8,16,128]{2,1,0:T(8,128)S(1)} %all_to_all.40.parts_ref, f32[1024,128]{1,0:T(8,128)S(1)} %get-tuple-element.46.mass_ref), custom_call_target="tpu_custom_call" | custom-call | tf_op jit(solution)/shard_map/pallas_call | solution.py:41
  27.7 17.0 %all_to_all.41.parts_ref.mass_ref = f32[32,16,128]{2,1,0:T(8,128)S(1)} all-to-all(f32[32,16,128]{2,1,0:T(8,128)S(1)} %get-tuple-element.48), channel_id=1, replica_groups={{0,1,2,3,4,5,6,7,8,9,10,11,12,13,14,15,16,17,18,19,20,21,22,23,24,25,26..., dimensions={0} | all-to-all | bytes 524288 | tf_op jit(solution)/shard_map/all_to_all | solution.py:369
  44.7 1.1 shard_map.64
  45.8 9.6 %all_to_all.42.parts_ref = f32[8,16,128]{2,1,0:T(8,128)S(1)} all-to-all(f32[8,16,128]{2,1,0:T(8,128)S(1)} %shard_map.64), channel_id=1, replica_groups={{0,32,64,96,128,160,192,224},{16,48,80,112,144,176,208,240},{1,33,65,97..., dimensions={0} | all-to-all | bytes 131072 | tf_op jit(solution)/shard_map/all_to_all | solution.py:365
  55.4 1.3 shard_map.65
  56.7 12.8 %all_to_all.43.parts_ref = f32[32,8,128]{2,1,0:T(8,128)S(1)} all-to-all(f32[32,8,128]{2,1,0:T(8,128)S(1)} %get-tuple-element.49), channel_id=1, replica_groups={{0,1,2,3,4,5,6,7,8,9,10,11,12,13,14,15,16,17,18,19,20,21,22,23,24,25,26..., dimensions={0} | all-to-all | bytes 262144 | tf_op jit(solution)/shard_map/all_to_all | solution.py:369
  70.6 9.6 %all_to_all.44.parts_ref = f32[8,16,128]{2,1,0:T(8,128)S(1)} all-to-all(f32[8,16,128]{2,1,0:T(8,128)S(1)} %shard_map.66), channel_id=1, replica_groups={{0,32,64,96,128,160,192,224},{16,48,80,112,144,176,208,240},{1,33,65,97..., dimensions={0} | all-to-all | bytes 131072 | tf_op jit(solution)/shard_map/all_to_all | solution.py:365
  81.1 12.4 %all_to_all.45.parts_ref = f32[32,8,128]{2,1,0:T(8,128)S(1)} all-to-all(f32[32,8,128]{2,1,0:T(8,128)S(1)} %get-tuple-element.51), channel_id=1, replica_groups={{0,1,2,3,4,5,6,7,8,9,10,11,12,13,14,15,16,17,18,19,20,21,22,23,24,25,26..., dimensions={0} | all-to-all | bytes 262144 | tf_op jit(solution)/shard_map/all_to_all | solution.py:369
  93.5 2.2 %shard_map.68.diff_ref = bf16[1024,2048]{1,0:T(8,128)(2,1)S(1)} custom-call(f32[1024,2048]{1,0:T(8,128)S(1)} %get-tuple-element.42.e_ref, f32[1024,2048]{1,0:T(8,128)S(1)} %get-tuple-element.44.s_ref, f32[16,128]{1,0:T(8,128)S(1)} %get-tuple-element.50.c_ref, f32[32,8,128]{2,1,0:T(8,128)S(1)} %all_to_all.45.parts_ref, ...), custom_call_target="tpu_custom_call" | custom-call | tf_op jit(solution)/shard_map/pallas_call | solution.py:41
  95.7 1.8 %shard_map.69 = (f32[512,256]{1,0:T(8,128)S(1)}, f32[512,256]{1,0:T(8,128)S(1)}) custom-call(s32[2]{0:T(128)S(1)} %pad_add_fusion.where_ref, bf16[1024,2048]{1,0:T(8,128)(2,1)S(1)} %shard_map.68.diff_ref, bf16[2048,256]{1,0:T(8,128)(2,1)S(1)} %get-tuple-element.52.back_ref), custom_call_target="tpu_custom_call" | custom-call | flops 1073741824 | tf_op jit(solution)/shard_map/pallas_call | solution.py:389
  98.1 3.7 %shard_map.70 = (f32[32,2048]{1,0:T(8,128)}, f32[32,2048]{1,0:T(8,128)}, f32[32,2048]{1,0:T(8,128)}, f32[32,2048]{1,0:T(8,128)}, f32[16,2048]{1,0:T(8,128)}, /*i...) custom-call(s32[2]{0:T(128)S(1)} %pad_add_fusion.where_ref, ...), custom_call_target="tpu_custom_call" | custom-call | flops 1073741824 | tf_op jit(solution)/shard_map/pallas_call | solution.py:479
  102.8 3.8 %all-to-all-start.6 = ((f32[16,32,256]{2,1,0:T(8,128)}), f32[16,32,256]{2,1,0:T(8,128)S(1)}, u32[]{:S(2)}, u32[]{:S(2)}) async-start(f32[16,32,256]{2,1,0:T(8,128)} %bitcast.2), calls=%async_computation.6 | async-start | bytes 1048576 | tf_op jit(solution)/shard_map/all_to_all | solution.py:504
  106.6 1.5 %collective-permute-start.2 = (f32[16,2048]{1,0:T(8,128)}, f32[16,2048]{1,0:T(8,128)S(1)}, u32[]{:S(2)}, u32[]{:S(2)}) collective-permute-start(f32[16,2048]{1,0:T(8,128)} %get-tuple-element.62), channel_id=1, source_target_pairs={{0,32},{16,48},{32,64},{48,80},{64,96},{80,112},{96,128},{112,144}... | collective-permute-start | bytes 393224 | tf_op jit(solution)/shard_map/ppermute | solution.py:359
  109.1 1.3 collective-permute-start.5
  110.4 2.5 %collective-permute-done.2.got_ref = f32[16,2048]{1,0:T(8,128)S(1)} collective-permute-done((f32[16,2048]{1,0:T(8,128)}, f32[16,2048]{1,0:T(8,128)S(1)}, u32[]{:S(2)}, u32[]{:S(2)}) %collective-permute-start.2) | collective-permute-done | bytes 131104 | tf_op jit(solution)/shard_map/ppermute | solution.py:359
  113.2 4.5 %all-to-all-done.6.parts_ref = f32[16,32,256]{2,1,0:T(8,128)S(1)} async-done(((f32[16,32,256]{2,1,0:T(8,128)}), f32[16,32,256]{2,1,0:T(8,128)S(1)}, u32[]{:S(2)}, u32[]{:S(2)}) %all-to-all-start.6) | async-done | bytes 524320 | tf_op jit(solution)/shard_map/all_to_all | solution.py:504
  118.6 3.7 %all-to-all-start.7 = ((f32[16,32,256]{2,1,0:T(8,128)}), f32[16,32,256]{2,1,0:T(8,128)S(1)}, u32[]{:S(2)}, u32[]{:S(2)}) async-start(f32[16,32,256]{2,1,0:T(8,128)} %shard_map.74), calls=%async_computation.7 | async-start | bytes 1048576 | tf_op jit(solution)/shard_map/all_to_all | solution.py:512
  124.0 5.0 %collective-permute-done.8.got_ref = f32[32,2048]{1,0:T(8,128)S(1)} collective-permute-done((f32[32,2048]{1,0:T(8,128)S(1)}, f32[32,2048]{1,0:T(8,128)S(1)}, u32[]{:S(2)}, u32[]{:S(2)}) %collective-permute-start.8) | collective-permute-done | bytes 262176 | tf_op jit(solution)/shard_map/ppermute | solution.py:359
  129.0 1.1 collective-permute-done.7.got_ref
  130.2 2.3 %all-to-all-done.7 = f32[16,32,256]{2,1,0:T(8,128)S(1)} async-done(((f32[16,32,256]{2,1,0:T(8,128)}), f32[16,32,256]{2,1,0:T(8,128)S(1)}, u32[]{:S(2)}, u32[]{:S(2)}) %all-to-all-start.7) | async-done | bytes 524320 | tf_op jit(solution)/shard_map/all_to_all | solution.py:512
  133.1 1.1 collective-permute-start.9
  134.2 2.2 %shard_map.79 = f32[4,256,256]{2,1,0:T(8,128)} custom-call(f32[512,256]{1,0:T(8,128)S(1)} %bitcast.4, bf16[4,256,256]{2,1,0:T(8,128)(2,1)S(1)} %copy-done, s32[4,128]{1,0:T(4,128)S(1)} %copy-done.2), custom_call_target="tpu_custom_call" | custom-call | tf_op jit(solution)/shard_map/pallas_call | solution.py:41
  136.5 1.9 %collective-permute-done.10.down_ref = f32[32,2048]{1,0:T(8,128)S(1)} collective-permute-done((f32[32,2048]{1,0:T(8,128)S(1)}, f32[32,2048]{1,0:T(8,128)S(1)}, u32[]{:S(2)}, u32[]{:S(2)}) %collective-permute-start.10) | collective-permute-done | bytes 262176 | tf_op jit(solution)/shard_map/ppermute | solution.py:359
  138.3 1.2 collective-permute-done.9.up_ref
  139.6 4.2 %collective-permute-start.11 = (f32[16,2048]{1,0:T(8,128)S(1)}, f32[16,2048]{1,0:T(8,128)S(1)}, u32[]{:S(2)}, u32[]{:S(2)}) collective-permute-start(f32[16,2048]{1,0:T(8,128)S(1)} %get-tuple-element.77), channel_id=1, source_target_pairs={{0,16},{16,0},{32,48},{48,32},{64,80},{80,64},{96,112},{112,96},{1... | collective-permute-start | bytes 393224 | tf_op jit(solution)/shard_map/ppermute | solution.py:355
  144.8 1.3 shard_map.81
  (44 shorter events, 9.2 us)
Async XLA Ops:
  2.6 6.1 %collective-permute-start = (f32[512,256]{1,0:T(8,128)S(1)}, f32[512,256]{1,0:T(8,128)S(1)}, u32[]{:S(2)}, u32[]{:S(2)}) collective-permute-start(f32[512,256]{1,0:T(8,128)S(1)} %get-tuple-element.40.own_ref), channel_id=1, source_target_pairs={{0,16},{16,0},{32,48},{48,32},{64,80},{80,64},{96,112},{112,96},{1... | collective-permute-start | bytes 1572872 | tf_op jit(solution)/shard_map/ppermute | solution.py:355
  5.9 4.7 %collective-permute-start.1 = (f32[512,256]{1,0:T(8,128)S(1)}, f32[512,256]{1,0:T(8,128)S(1)}, u32[]{:S(2)}, u32[]{:S(2)}) collective-permute-start(f32[512,256]{1,0:T(8,128)S(1)} %get-tuple-element.43.own_ref), channel_id=1, source_target_pairs={{0,16},{16,0},{32,48},{48,32},{64,80},{80,64},{96,112},{112,96},{1... | collective-permute-start | bytes 1572872 | tf_op jit(solution)/shard_map/ppermute | solution.py:355
  97.5 4.4 %collective-permute-start.6 = (f32[512,256]{1,0:T(8,128)S(1)}, f32[512,256]{1,0:T(8,128)S(1)}, u32[]{:S(2)}, u32[]{:S(2)}) collective-permute-start(f32[512,256]{1,0:T(8,128)S(1)} %get-tuple-element.54), channel_id=1, source_target_pairs={{0,16},{16,0},{32,48},{48,32},{64,80},{80,64},{96,112},{112,96},{1... | collective-permute-start | bytes 1572872 | tf_op jit(solution)/shard_map/ppermute | solution.py:355
  101.8 11.1 %copy-start.7 = (f32[32,2048]{1,0:T(8,128)S(1)}, f32[32,2048]{1,0:T(8,128)}, u32[]{:S(2)}) copy-start(f32[32,2048]{1,0:T(8,128)} %get-tuple-element.61.rel_hbm) | copy-start | bytes 786436
  101.8 6.3 %collective-permute-start.4 = (f32[16,2048]{1,0:T(8,128)}, f32[16,2048]{1,0:T(8,128)S(1)}, u32[]{:S(2)}, u32[]{:S(2)}) collective-permute-start(f32[16,2048]{1,0:T(8,128)} %get-tuple-element.64), channel_id=1, source_target_pairs={{0,224},{16,240},{32,0},{48,16},{64,32},{80,48},{96,64},{112,80},{... | collective-permute-start | bytes 393224 | tf_op jit(solution)/shard_map/ppermute | solution.py:359
  102.8 14.9 %all-to-all-start.6 = ((f32[16,32,256]{2,1,0:T(8,128)}), f32[16,32,256]{2,1,0:T(8,128)S(1)}, u32[]{:S(2)}, u32[]{:S(2)}) async-start(f32[16,32,256]{2,1,0:T(8,128)} %bitcast.2), calls=%async_computation.6 | async-start | bytes 1048576 | tf_op jit(solution)/shard_map/all_to_all | solution.py:504
  106.6 15.7 %copy-start.6 = (f32[32,2048]{1,0:T(8,128)S(1)}, f32[32,2048]{1,0:T(8,128)}, u32[]{:S(2)}) copy-start(f32[32,2048]{1,0:T(8,128)} %get-tuple-element.60.rel_hbm) | copy-start | bytes 786436
  106.6 6.4 %collective-permute-start.2 = (f32[16,2048]{1,0:T(8,128)}, f32[16,2048]{1,0:T(8,128)S(1)}, u32[]{:S(2)}, u32[]{:S(2)}) collective-permute-start(f32[16,2048]{1,0:T(8,128)} %get-tuple-element.62), channel_id=1, source_target_pairs={{0,32},{16,48},{32,64},{48,80},{64,96},{80,112},{96,128},{112,144}... | collective-permute-start | bytes 393224 | tf_op jit(solution)/shard_map/ppermute | solution.py:359
  108.1 1.0 copy-start.8
  109.1 13.3 %copy-start.5 = (f32[32,2048]{1,0:T(8,128)S(1)}, f32[32,2048]{1,0:T(8,128)}, u32[]{:S(2)}) copy-start(f32[32,2048]{1,0:T(8,128)} %get-tuple-element.66.rel_hbm) | copy-start | bytes 786436
  109.1 13.2 %collective-permute-start.5 = (f32[32,2048]{1,0:T(8,128)S(1)}, f32[32,2048]{1,0:T(8,128)S(1)}, u32[]{:S(2)}, u32[]{:S(2)}) collective-permute-start(f32[32,2048]{1,0:T(8,128)S(1)} %shard_map.72), channel_id=1, source_target_pairs={{0,224},{16,240},{32,0},{48,16},{64,32},{80,48},{96,64},{112,80},{... | collective-permute-start | bytes 786440 | tf_op jit(solution)/shard_map/ppermute | solution.py:359
  113.0 9.3 %collective-permute-start.3 = (f32[32,2048]{1,0:T(8,128)S(1)}, f32[32,2048]{1,0:T(8,128)S(1)}, u32[]{:S(2)}, u32[]{:S(2)}) collective-permute-start(f32[32,2048]{1,0:T(8,128)S(1)} %shard_map.71), channel_id=1, source_target_pairs={{0,32},{16,48},{32,64},{48,80},{64,96},{80,112},{96,128},{112,144}... | collective-permute-start | bytes 786440 | tf_op jit(solution)/shard_map/ppermute | solution.py:359
  118.6 14.0 %copy-start.4 = (f32[32,2048]{1,0:T(8,128)S(1)}, f32[32,2048]{1,0:T(8,128)}, u32[]{:S(2)}) copy-start(f32[32,2048]{1,0:T(8,128)} %get-tuple-element.59.rel_hbm) | copy-start | bytes 786436
  118.6 14.0 %all-to-all-start.7 = ((f32[16,32,256]{2,1,0:T(8,128)}), f32[16,32,256]{2,1,0:T(8,128)S(1)}, u32[]{:S(2)}, u32[]{:S(2)}) async-start(f32[16,32,256]{2,1,0:T(8,128)} %shard_map.74), calls=%async_computation.7 | async-start | bytes 1048576 | tf_op jit(solution)/shard_map/all_to_all | solution.py:512
  122.4 10.2 %copy-start.3 = (f32[32,2048]{1,0:T(8,128)S(1)}, f32[32,2048]{1,0:T(8,128)}, u32[]{:S(2)}) copy-start(f32[32,2048]{1,0:T(8,128)} %get-tuple-element.67.rel_hbm) | copy-start | bytes 786436
  122.5 11.8 %copy-start = (bf16[4,256,256]{2,1,0:T(8,128)(2,1)S(1)}, bf16[4,256,256]{2,1,0:T(8,128)(2,1)}, u32[]{:S(2)}) copy-start(bf16[4,256,256]{2,1,0:T(8,128)(2,1)} %feats_ref.1) | copy-start | bytes 1572868
  122.5 11.7 %copy-start.2 = (s32[4,128]{1,0:T(4,128)S(1)}, s32[4,128]{1,0:T(4,128)}, u32[]{:S(2)}) copy-start(s32[4,128]{1,0:T(4,128)} %mask_ref.1) | copy-start | bytes 6148
  122.5 6.6 %collective-permute-start.8 = (f32[32,2048]{1,0:T(8,128)S(1)}, f32[32,2048]{1,0:T(8,128)S(1)}, u32[]{:S(2)}, u32[]{:S(2)}) collective-permute-start(f32[32,2048]{1,0:T(8,128)S(1)} %shard_map.76), channel_id=1, source_target_pairs={{0,224},{16,240},{32,0},{48,16},{64,32},{80,48},{96,64},{112,80},{... | collective-permute-start | bytes 786440 | tf_op jit(solution)/shard_map/ppermute | solution.py:359
  123.3 6.8 %collective-permute-start.7 = (f32[32,2048]{1,0:T(8,128)S(1)}, f32[32,2048]{1,0:T(8,128)S(1)}, u32[]{:S(2)}, u32[]{:S(2)}) collective-permute-start(f32[32,2048]{1,0:T(8,128)S(1)} %shard_map.75), channel_id=1, source_target_pairs={{0,32},{16,48},{32,64},{48,80},{64,96},{80,112},{96,128},{112,144}... | collective-permute-start | bytes 786440 | tf_op jit(solution)/shard_map/ppermute | solution.py:359
  132.5 7.0 %copy-start.1 = (f32[32,2048]{1,0:T(8,128)S(1)}, f32[32,2048]{1,0:T(8,128)}, u32[]{:S(2)}) copy-start(f32[32,2048]{1,0:T(8,128)} %get-tuple-element.65.rel_hbm) | copy-start | bytes 786436
  132.7 5.7 %collective-permute-start.10 = (f32[32,2048]{1,0:T(8,128)S(1)}, f32[32,2048]{1,0:T(8,128)S(1)}, u32[]{:S(2)}, u32[]{:S(2)}) collective-permute-start(f32[32,2048]{1,0:T(8,128)S(1)} %shard_map.78), channel_id=1, source_target_pairs={{0,224},{16,240},{32,0},{48,16},{64,32},{80,48},{96,64},{112,80},{... | collective-permute-start | bytes 786440 | tf_op jit(solution)/shard_map/ppermute | solution.py:359
  133.1 6.4 %collective-permute-start.9 = (f32[32,2048]{1,0:T(8,128)S(1)}, f32[32,2048]{1,0:T(8,128)S(1)}, u32[]{:S(2)}, u32[]{:S(2)}) collective-permute-start(f32[32,2048]{1,0:T(8,128)S(1)} %shard_map.77), channel_id=1, source_target_pairs={{0,32},{16,48},{32,64},{48,80},{64,96},{80,112},{96,128},{112,144}... | collective-permute-start | bytes 786440 | tf_op jit(solution)/shard_map/ppermute | solution.py:359
  139.6 5.2 %collective-permute-start.11 = (f32[16,2048]{1,0:T(8,128)S(1)}, f32[16,2048]{1,0:T(8,128)S(1)}, u32[]{:S(2)}, u32[]{:S(2)}) collective-permute-start(f32[16,2048]{1,0:T(8,128)S(1)} %get-tuple-element.77), channel_id=1, source_target_pairs={{0,16},{16,0},{32,48},{48,32},{64,80},{80,64},{96,112},{112,96},{1... | collective-permute-start | bytes 393224 | tf_op jit(solution)/shard_map/ppermute | solution.py:355

commit v7 on v6

--- a/solution.py
+++ b/solution.py
@@ -85,14 +85,14 @@
             out[i * slots : (i + 1) * slots, :] = (rows / norm).astype(BF16).astype(F32)
 
 
-def proto_kernel(where_ref, proto_ref, full_ref, unit_ref, back_ref, norm_ref):
+def proto_kernel(where_ref, proto_ref, full_ref, unit_ref, back_ref, scale_ref):
     p = proto_ref[...].astype(F32)
-    norm = jnp.sqrt(jnp.sum(p * p, axis=0, keepdims=True) + EPSILON)
-    full = p / norm
+    scale = 1.0 / jnp.sqrt(jnp.sum(p * p, axis=0, keepdims=True) + EPSILON)
+    full = p * scale
     full_ref[...] = full
     unit_ref[...] = full.astype(BF16)
     back_ref[...] = full.T.astype(BF16)
-    norm_ref[...] = norm
+    scale_ref[...] = scale
 
 
 def core_rows(where_ref, side, half):
@@ -249,29 +249,31 @@
         out[...] = jnp.dot(diff_ref[rows, :], back_ref[...], preferred_element_type=F32)
 
 
-def grad_kernel(where_ref, diff_ref, full_ref, norm_ref, turned_ref, *refs):
+def grad_kernel(where_ref, diff_ref, full_ref, scale_ref, turned_ref, *refs):
     outs, (g_ref, sems) = refs[:-2], refs[-2:]
     wide = full_ref.shape[1]
+    core, z = where_ref[0], where_ref[1]
+    deep = g_ref.shape[0] // Z
+    near = deep // 2
+    copies = []
     for w in range(wide // WIDE):
         columns = slice(w * WIDE, (w + 1) * WIDE)
         grad = jnp.dot(turned_ref[...], diff_ref[:, columns], preferred_element_type=F32)
         full = full_ref[:, columns]
         proj = jnp.sum(full.astype(BF16).astype(F32) * grad, axis=0, keepdims=True)
-        g_ref[:, columns] = (grad - full * proj) / norm_ref[:, columns]
-    core, z = where_ref[0], where_ref[1]
-    deep = g_ref.shape[0] // Z
-    near = deep // 2
-    pairs = []
-    for j in range(Z):
-        top = lax.rem(z + j, Z) * deep
-        for side in range(2):
-            take = pl.multiple_of(top + lax.rem(core + side, 2) * near, near)
-            if j == 4:
-                out = outs[4 + side]
-            else:
-                out = outs[j + (j > 4)].at[pl.ds(side * near, near), :]
-            pairs.append((g_ref.at[pl.ds(take, near), :], out))
-    for copy in fetch(pairs, sems):
+        g_ref[:, columns] = (grad - full * proj) * scale_ref[:, columns]
+        pairs = []
+        for j in range(Z):
+            top = lax.rem(z + j, Z) * deep
+            for side in range(2):
+                take = pl.multiple_of(top + lax.rem(core + side, 2) * near, near)
+                if j == 4:
+                    out = outs[4 + side].at[:, columns]
+                else:
+                    out = outs[j + (j > 4)].at[pl.ds(side * near, near), columns]
+                pairs.append((g_ref.at[pl.ds(take, near), columns], out))
+        copies += fetch(pairs, sems.at[w])
+    for copy in copies:
         copy.wait()
 
 
@@ -411,7 +413,7 @@
     zs_other = other_core(zs)
     steps = 2
     column_spec = pl.BlockSpec((width, wide // steps), lambda j, w: (0, j))
-    full, unit, back, p_norm = pl.pallas_call(
+    full, unit, back, p_scale = pl.pallas_call(
         proto_kernel,
         grid_spec=pltpu.PrefetchScalarGridSpec(
             num_scalar_prefetch=1,
@@ -481,12 +483,12 @@
         in_specs=[scalars] + [whole()] * 4,
         out_specs=[anywhere] * 9,
         out_shape=[far(deep, wide)] * 4 + [far(near, wide)] * 2 + [far(deep, wide)] * 3,
-        scratch_shapes=[VMEM((width, wide), F32), pltpu.SemaphoreType.DMA((2 * Z,))],
+        scratch_shapes=[VMEM((width, wide), F32), pltpu.SemaphoreType.DMA((wide // WIDE, 2 * Z))],
         compiler_params=params(16),
         cost_estimate=cost(2 * tokens * wide * width),
-    )(where, tie(diff, (gz, gz_give)), full, p_norm, turned)
-
-    def step(kernel, term, got, work=10**9):
+    )(where, tie(diff, (gz, gz_give)), full, p_scale, turned)
+
+    def step(kernel, term, got, work=0):
         return pl.pallas_call(
             kernel,
             in_specs=[anywhere, whole()],
@@ -498,15 +500,14 @@
         )(term, got)
 
     up, down = along_z(rel[4], 1), along_z(rel[5], -1)
-    up = step(first_step_kernel(False), rel[3], up)
-    down = step(first_step_kernel(True), rel[6], down)
+    up = step(first_step_kernel(False), rel[3], up, 2 * 10**9)
+    down = step(first_step_kernel(True), rel[6], down, 2 * 10**9)
     (gz,) = call(sum_kernel, [shape(own, width)], gz, gz_got)
     gz_parts = lax.all_to_all(
         tie(gz, rel).reshape(RING, own // RING, width), "proto", 0, 0
     )
     (gz_share,) = call(share_kernel, [shape(RING, own // RING, width)], gz_parts)
     up, down = along_z(up, 1), along_z(down, -1)
-    up, down = tie((up, down), gz_share)
     up = step(step_kernel, rel[2], up)
     down = step(step_kernel, rel[7], down)
     gz = lax.all_to_all(gz_share, "proto", 0, 0).reshape(own, width)
@@ -514,11 +515,11 @@
         last_kernel, [shape(images, patches, width)], gz, student_feats, mask_index
     )
     up, down = along_z(up, 1), along_z(down, -1)
-    up, down = tie((up, down), gz)
+    up, down = tie((up, down), gz_share)
     up = step(step_kernel, rel[1], up)
     down = step(step_kernel, rel[8], down)
     up, down = along_z(up, 1), along_z(down, -1)
-    up, down, grad_student = lax.optimization_barrier((up, down, grad_student))
+    up = tie(up, gz)
     keep, give = pl.pallas_call(
         last_sum_kernel,
         in_specs=[anywhere, whole(), whole()],

time: 147 us -> 143 us (0.973)
  waiting for transfers between devices: 19.6 us -> 12.4 us
  starting transfers between devices: 21.9 us -> 26.1 us
    all_to_all x1, waiting for transfers between devices: 4.47 us -> 0.01 us  [on_device(): lax.all_to_all(tie(gz, rel).reshape(RING, own // RING, width), 'proto', 0...]
    ppermute x8, starting transfers between devices: 6.21 us -> 9.17 us  [along_z(): lax.ppermute(x, 'batch', [(i, (i // 2 + d) % Z * 2 + i % 2) for i in rang...]
    all_to_all x1, starting transfers between devices: 3.71 us -> 6.27 us  [on_device(): gz = lax.all_to_all(gz_share, 'proto', 0, 0).reshape(own, width)]
    ppermute x8, waiting for transfers between devices: 11.7 us -> 9.97 us  [along_z(): lax.ppermute(x, 'batch', [(i, (i // 2 + d) % Z * 2 + i % 2) for i in rang...]
  transfers between devices with their start and end apart: 14 -> 14, of which waited for: 8 -> 4; matrix products, arithmetic and copies ran while one was open for 0% -> 0% of each run, Pallas kernels for 8% -> 9%
where the time goes in v7:
time: 143 us
  blocking collectives  74.8 us (52%)
  Pallas kernels  27.5 us (19%)
  starting transfers between devices  26.1 us (18%)
  waiting for transfers between devices  12.4 us (9%)
    all_to_all x3, blocking collectives, all_rows(): lax.all_to_all(x, ('batch', 'proto'), 0, 0, axis_index_groups=ROW_GROUPS)  42.1 us
    all_to_all x3, blocking collectives, all_columns(): return lax.all_to_all(x, 'batch', 0, 0, axis_index_groups=Z_GROUPS)  32.7 us
    pallas_call x9, Pallas kernels, call(): pl.pallas_call(kernel, out_shape=outs, in_specs=[whole()] * len(args), ou...  12.1 us
    ppermute x8, waiting for transfers between devices, along_z(): lax.ppermute(x, 'batch', [(i, (i // 2 + d) % Z * 2 + i % 2) for i in rang...  9.97 us
    ppermute x8, starting transfers between devices, along_z(): lax.ppermute(x, 'batch', [(i, (i // 2 + d) % Z * 2 + i % 2) for i in rang...  9.17 us
    pallas_call x4, Pallas kernels, placed(): pl.pallas_call(kernel, in_specs=[scalars] + [whole()] * len(args), out_sp...  6.99 us
    ppermute x4, starting transfers between devices, other_core(): return lax.ppermute(x, 'batch', [(i, i ^ 1) for i in range(RING)])  6.95 us
    all_to_all x1, starting transfers between devices, on_device(): gz = lax.all_to_all(gz_share, 'proto', 0, 0).reshape(own, width)  6.27 us
  transfers between devices with their start and end apart: 14, of which 4 were waited for; matrix products, arithmetic and copies ran while one was open for 0% of the time, Pallas kernels for 9%

profile of v7, /device:TPU:1, one launch (start us, length us, event | category | flops | bytes accessed | tf_op | source)
XLA Modules:
  0.0 142.8 jit_solution(8682147930916864427)
XLA Ops:
  0.6 1.9 %shard_map.59 = (f32[512,256]{1,0:T(8,128)S(1)}, f32[512,256]{1,0:T(8,128)S(1)}) custom-call(bf16[4,256,256]{2,1,0:T(8,128)(2,1)} %teacher_hbm.1, bf16[4,256,256]{2,1,0:T(8,128)(2,1)} %feats_ref.1, s32[4,128]{1,0:T(4,128)} %mask_ref.1), custom_call_target="tpu_custom_call" | custom-call | tf_op jit(solution)/shard_map/pallas_call | solution.py:401
  2.6 3.3 %collective-permute-start = (f32[512,256]{1,0:T(8,128)S(1)}, f32[512,256]{1,0:T(8,128)S(1)}, u32[]{:S(2)}, u32[]{:S(2)}) collective-permute-start(f32[512,256]{1,0:T(8,128)S(1)} %get-tuple-element.36.own_ref), channel_id=1, source_target_pairs={{0,16},{16,0},{32,48},{48,32},{64,80},{80,64},{96,112},{112,96},{1... | collective-permute-start | bytes 1572872 | tf_op jit(solution)/shard_map/ppermute | solution.py:357
  6.1 2.6 %shard_map.60 = (f32[256,2048]{1,0:T(8,128)S(1)}, bf16[256,2048]{1,0:T(8,128)(2,1)S(1)}, bf16[2048,256]{1,0:T(8,128)(2,1)S(1)}, f32[1,2048]{1,0:T(1,128)S(1)}) custom-call(s32[2]{0:T(128)S(1)} %pad_add_fusion.where_ref, bf16[256,4096]{1,0:T(8,128)(2,1)} %proto_ref.1), custom_call_target="tpu_custom_call" | custom-call | tf_op jit(solution)/shard_map/pallas_call | solution.py:416
  8.7 1.9 %shard_map.61 = (f32[1024,2048]{1,0:T(8,128)S(1)}, f32[8,16,128]{2,1,0:T(8,128)S(1)}) custom-call(s32[2]{0:T(128)S(1)} %pad_add_fusion.where_ref, f32[512,256]{1,0:T(8,128)S(1)} %get-tuple-element.36.own_ref, f32[512,256]{1,0:T(8,128)S(1)} %collective-permute-done.other_ref, bf16[256,2048]{1,0:T(8,128)(2,1)S(1)} %get-tuple-element.37.unit_ref), custom_call_target="tpu_custom_call" | custom-call | flops 1073741824 | tf_op jit(solution)/shard_map/pallas_call | solution.py:391
  10.6 2.0 %shard_map.62 = (f32[1024,2048]{1,0:T(8,128)S(1)}, f32[1024,128]{1,0:T(8,128)S(1)}, bf16[256,1024]{1,0:T(8,128)(2,1)S(1)}) custom-call(s32[2]{0:T(128)S(1)} %pad_add_fusion.where_ref, f32[512,256]{1,0:T(8,128)S(1)} %get-tuple-element.39.own_ref, f32[512,256]{1,0:T(8,128)S(1)} %collective-permute-done.1.other_ref, ...), custom_call_target="tpu_custom_call" | custom-call | flops 1073741824 | tf_op jit(solution)/shard_map/pallas_call | solution.py:391
  12.6 13.5 %all_to_all.40.parts_ref = f32[8,16,128]{2,1,0:T(8,128)S(1)} all-to-all(f32[8,16,128]{2,1,0:T(8,128)S(1)} %get-tuple-element.43), channel_id=1, replica_groups={{0,32,64,96,128,160,192,224},{16,48,80,112,144,176,208,240},{1,33,65,97..., dimensions={0} | all-to-all | bytes 131072 | tf_op jit(solution)/shard_map/all_to_all | solution.py:367
  26.1 1.6 %shard_map.63 = (f32[32,16,128]{2,1,0:T(8,128)S(1)}, f32[16,128]{1,0:T(8,128)}) custom-call(f32[1024,2048]{1,0:T(8,128)S(1)} %get-tuple-element.38.e_ref, f32[8,16,128]{2,1,0:T(8,128)S(1)} %all_to_all.40.parts_ref, f32[1024,128]{1,0:T(8,128)S(1)} %get-tuple-element.42.mass_ref), custom_call_target="tpu_custom_call" | custom-call | tf_op jit(solution)/shard_map/pallas_call | solution.py:41
  27.7 17.0 %all_to_all.41.parts_ref.mass_ref = f32[32,16,128]{2,1,0:T(8,128)S(1)} all-to-all(f32[32,16,128]{2,1,0:T(8,128)S(1)} %get-tuple-element.44), channel_id=1, replica_groups={{0,1,2,3,4,5,6,7,8,9,10,11,12,13,14,15,16,17,18,19,20,21,22,23,24,25,26..., dimensions={0} | all-to-all | bytes 524288 | tf_op jit(solution)/shard_map/all_to_all | solution.py:371
  44.7 1.1 shard_map.64
  45.8 9.6 %all_to_all.42.parts_ref = f32[8,16,128]{2,1,0:T(8,128)S(1)} all-to-all(f32[8,16,128]{2,1,0:T(8,128)S(1)} %shard_map.64), channel_id=1, replica_groups={{0,32,64,96,128,160,192,224},{16,48,80,112,144,176,208,240},{1,33,65,97..., dimensions={0} | all-to-all | bytes 131072 | tf_op jit(solution)/shard_map/all_to_all | solution.py:367
  55.4 1.3 shard_map.65
  56.7 12.8 %all_to_all.43.parts_ref = f32[32,8,128]{2,1,0:T(8,128)S(1)} all-to-all(f32[32,8,128]{2,1,0:T(8,128)S(1)} %get-tuple-element.45), channel_id=1, replica_groups={{0,1,2,3,4,5,6,7,8,9,10,11,12,13,14,15,16,17,18,19,20,21,22,23,24,25,26..., dimensions={0} | all-to-all | bytes 262144 | tf_op jit(solution)/shard_map/all_to_all | solution.py:371
  69.5 1.1 shard_map.66
  70.5 9.6 %all_to_all.44.parts_ref = f32[8,16,128]{2,1,0:T(8,128)S(1)} all-to-all(f32[8,16,128]{2,1,0:T(8,128)S(1)} %shard_map.66), channel_id=1, replica_groups={{0,32,64,96,128,160,192,224},{16,48,80,112,144,176,208,240},{1,33,65,97..., dimensions={0} | all-to-all | bytes 131072 | tf_op jit(solution)/shard_map/all_to_all | solution.py:367
  80.1 0.9 shard_map.67
  81.1 12.4 %all_to_all.45.parts_ref = f32[32,8,128]{2,1,0:T(8,128)S(1)} all-to-all(f32[32,8,128]{2,1,0:T(8,128)S(1)} %get-tuple-element.47), channel_id=1, replica_groups={{0,1,2,3,4,5,6,7,8,9,10,11,12,13,14,15,16,17,18,19,20,21,22,23,24,25,26..., dimensions={0} | all-to-all | bytes 262144 | tf_op jit(solution)/shard_map/all_to_all | solution.py:371
  93.5 2.2 %shard_map.68.diff_ref = bf16[1024,2048]{1,0:T(8,128)(2,1)S(1)} custom-call(f32[1024,2048]{1,0:T(8,128)S(1)} %get-tuple-element.38.e_ref, f32[1024,2048]{1,0:T(8,128)S(1)} %get-tuple-element.40.s_ref, f32[16,128]{1,0:T(8,128)S(1)} %get-tuple-element.46.c_ref, f32[32,8,128]{2,1,0:T(8,128)S(1)} %all_to_all.45.parts_ref, ...), custom_call_target="tpu_custom_call" | custom-call | tf_op jit(solution)/shard_map/pallas_call | solution.py:41
  95.7 1.8 %shard_map.69 = (f32[512,256]{1,0:T(8,128)S(1)}, f32[512,256]{1,0:T(8,128)S(1)}) custom-call(s32[2]{0:T(128)S(1)} %pad_add_fusion.where_ref, bf16[1024,2048]{1,0:T(8,128)(2,1)S(1)} %shard_map.68.diff_ref, bf16[2048,256]{1,0:T(8,128)(2,1)S(1)} %get-tuple-element.48.back_ref), custom_call_target="tpu_custom_call" | custom-call | flops 1073741824 | tf_op jit(solution)/shard_map/pallas_call | solution.py:391
  98.1 3.5 %shard_map.71 = (f32[32,2048]{1,0:T(8,128)}, f32[32,2048]{1,0:T(8,128)}, f32[32,2048]{1,0:T(8,128)}, f32[32,2048]{1,0:T(8,128)}, f32[16,2048]{1,0:T(8,128)}, /*i...) custom-call(s32[2]{0:T(128)S(1)} %pad_add_fusion.where_ref, ...), custom_call_target="tpu_custom_call" | custom-call | flops 1073741824 | tf_op jit(solution)/shard_map/pallas_call | solution.py:481
  101.7 1.5 %collective-permute-start.3 = (f32[16,2048]{1,0:T(8,128)}, f32[16,2048]{1,0:T(8,128)S(1)}, u32[]{:S(2)}, u32[]{:S(2)}) collective-permute-start(f32[16,2048]{1,0:T(8,128)} %get-tuple-element.59), channel_id=1, source_target_pairs={{0,32},{16,48},{32,64},{48,80},{64,96},{80,112},{96,128},{112,144}... | collective-permute-start | bytes 393224 | tf_op jit(solution)/shard_map/ppermute | solution.py:361
  104.0 3.7 %all-to-all-start.6 = ((f32[16,32,256]{2,1,0:T(8,128)}), f32[16,32,256]{2,1,0:T(8,128)S(1)}, u32[]{:S(2)}, u32[]{:S(2)}) async-start(f32[16,32,256]{2,1,0:T(8,128)} %bitcast.2), calls=%async_computation.6 | async-start | bytes 1048576 | tf_op jit(solution)/shard_map/all_to_all | solution.py:506
  107.8 0.9 copy-done.8
  108.8 1.6 %collective-permute-start.7 = (f32[32,2048]{1,0:T(8,128)S(1)}, f32[32,2048]{1,0:T(8,128)S(1)}, u32[]{:S(2)}, u32[]{:S(2)}) collective-permute-start(f32[32,2048]{1,0:T(8,128)S(1)} %shard_map.76), channel_id=1, source_target_pairs={{0,224},{16,240},{32,0},{48,16},{64,32},{80,48},{96,64},{112,80},{... | collective-permute-start | bytes 786440 | tf_op jit(solution)/shard_map/ppermute | solution.py:361
  110.5 5.6 %collective-permute-done.7.got_ref = f32[32,2048]{1,0:T(8,128)S(1)} collective-permute-done((f32[32,2048]{1,0:T(8,128)S(1)}, f32[32,2048]{1,0:T(8,128)S(1)}, u32[]{:S(2)}, u32[]{:S(2)}) %collective-permute-start.7) | collective-permute-done | bytes 262176 | tf_op jit(solution)/shard_map/ppermute | solution.py:361
  116.2 3.1 %collective-permute-start.8 = (f32[32,2048]{1,0:T(8,128)S(1)}, f32[32,2048]{1,0:T(8,128)S(1)}, u32[]{:S(2)}, u32[]{:S(2)}) collective-permute-start(f32[32,2048]{1,0:T(8,128)S(1)} %shard_map.77), channel_id=1, source_target_pairs={{0,224},{16,240},{32,0},{48,16},{64,32},{80,48},{96,64},{112,80},{... | collective-permute-start | bytes 786440 | tf_op jit(solution)/shard_map/ppermute | solution.py:361
  120.3 6.3 %all-to-all-start.7 = ((f32[16,32,256]{2,1,0:T(8,128)}), f32[16,32,256]{2,1,0:T(8,128)S(1)}, u32[]{:S(2)}, u32[]{:S(2)}) async-start(f32[16,32,256]{2,1,0:T(8,128)} %shard_map.72), calls=%async_computation.7 | async-start | bytes 1048576 | tf_op jit(solution)/shard_map/all_to_all | solution.py:513
  127.3 2.7 %collective-permute-start.10 = (f32[32,2048]{1,0:T(8,128)S(1)}, f32[32,2048]{1,0:T(8,128)S(1)}, u32[]{:S(2)}, u32[]{:S(2)}) collective-permute-start(f32[32,2048]{1,0:T(8,128)S(1)} %shard_map.79), channel_id=1, source_target_pairs={{0,224},{16,240},{32,0},{48,16},{64,32},{80,48},{96,64},{112,80},{... | collective-permute-start | bytes 786440 | tf_op jit(solution)/shard_map/ppermute | solution.py:361
  130.0 3.9 %collective-permute-done.9.up_ref = f32[32,2048]{1,0:T(8,128)S(1)} collective-permute-done((f32[32,2048]{1,0:T(8,128)S(1)}, f32[32,2048]{1,0:T(8,128)S(1)}, u32[]{:S(2)}, u32[]{:S(2)}) %collective-permute-start.9) | collective-permute-done | bytes 262176 | tf_op jit(solution)/shard_map/ppermute | solution.py:361
  133.9 2.4 %all-to-all-done.7 = f32[16,32,256]{2,1,0:T(8,128)S(1)} async-done(((f32[16,32,256]{2,1,0:T(8,128)}), f32[16,32,256]{2,1,0:T(8,128)S(1)}, u32[]{:S(2)}, u32[]{:S(2)}) %all-to-all-start.7) | async-done | bytes 524320 | tf_op jit(solution)/shard_map/all_to_all | solution.py:513
  136.4 2.9 %collective-permute-start.11 = (f32[16,2048]{1,0:T(8,128)S(1)}, f32[16,2048]{1,0:T(8,128)S(1)}, u32[]{:S(2)}, u32[]{:S(2)}) collective-permute-start(f32[16,2048]{1,0:T(8,128)S(1)} %get-tuple-element.69), channel_id=1, source_target_pairs={{0,16},{16,0},{32,48},{48,32},{64,80},{80,64},{96,112},{112,96},{1... | collective-permute-start | bytes 393224 | tf_op jit(solution)/shard_map/ppermute | solution.py:357
  139.3 2.2 %shard_map.73 = f32[4,256,256]{2,1,0:T(8,128)} custom-call(f32[512,256]{1,0:T(8,128)S(1)} %bitcast.4, bf16[4,256,256]{2,1,0:T(8,128)(2,1)S(1)} %copy-done, s32[4,128]{1,0:T(4,128)S(1)} %copy-done.6), custom_call_target="tpu_custom_call" | custom-call | tf_op jit(solution)/shard_map/pallas_call | solution.py:41
  141.6 1.3 shard_map.81
  (44 shorter events, 3.8 us)
Async XLA Ops:
  2.6 6.1 %collective-permute-start = (f32[512,256]{1,0:T(8,128)S(1)}, f32[512,256]{1,0:T(8,128)S(1)}, u32[]{:S(2)}, u32[]{:S(2)}) collective-permute-start(f32[512,256]{1,0:T(8,128)S(1)} %get-tuple-element.36.own_ref), channel_id=1, source_target_pairs={{0,16},{16,0},{32,48},{48,32},{64,80},{80,64},{96,112},{112,96},{1... | collective-permute-start | bytes 1572872 | tf_op jit(solution)/shard_map/ppermute | solution.py:357
  5.9 4.7 %collective-permute-start.1 = (f32[512,256]{1,0:T(8,128)S(1)}, f32[512,256]{1,0:T(8,128)S(1)}, u32[]{:S(2)}, u32[]{:S(2)}) collective-permute-start(f32[512,256]{1,0:T(8,128)S(1)} %get-tuple-element.39.own_ref), channel_id=1, source_target_pairs={{0,16},{16,0},{32,48},{48,32},{64,80},{80,64},{96,112},{112,96},{1... | collective-permute-start | bytes 1572872 | tf_op jit(solution)/shard_map/ppermute | solution.py:357
  97.4 5.7 %collective-permute-start.2 = (f32[512,256]{1,0:T(8,128)S(1)}, f32[512,256]{1,0:T(8,128)S(1)}, u32[]{:S(2)}, u32[]{:S(2)}) collective-permute-start(f32[512,256]{1,0:T(8,128)S(1)} %get-tuple-element.50), channel_id=1, source_target_pairs={{0,16},{16,0},{32,48},{48,32},{64,80},{80,64},{96,112},{112,96},{1... | collective-permute-start | bytes 1572872 | tf_op jit(solution)/shard_map/ppermute | solution.py:357
  101.6 6.1 %collective-permute-start.6 = (f32[16,2048]{1,0:T(8,128)}, f32[16,2048]{1,0:T(8,128)S(1)}, u32[]{:S(2)}, u32[]{:S(2)}) collective-permute-start(f32[16,2048]{1,0:T(8,128)} %get-tuple-element.60), channel_id=1, source_target_pairs={{0,224},{16,240},{32,0},{48,16},{64,32},{80,48},{96,64},{112,80},{... | collective-permute-start | bytes 393224 | tf_op jit(solution)/shard_map/ppermute | solution.py:361
  101.7 8.7 %collective-permute-start.3 = (f32[16,2048]{1,0:T(8,128)}, f32[16,2048]{1,0:T(8,128)S(1)}, u32[]{:S(2)}, u32[]{:S(2)}) collective-permute-start(f32[16,2048]{1,0:T(8,128)} %get-tuple-element.59), channel_id=1, source_target_pairs={{0,32},{16,48},{32,64},{48,80},{64,96},{80,112},{96,128},{112,144}... | collective-permute-start | bytes 393224 | tf_op jit(solution)/shard_map/ppermute | solution.py:361
  104.0 6.3 %copy-start.7 = (f32[32,2048]{1,0:T(8,128)S(1)}, f32[32,2048]{1,0:T(8,128)}, u32[]{:S(2)}) copy-start(f32[32,2048]{1,0:T(8,128)} %get-tuple-element.58.rel_hbm) | copy-start | bytes 786436
  104.0 15.4 %all-to-all-start.6 = ((f32[16,32,256]{2,1,0:T(8,128)}), f32[16,32,256]{2,1,0:T(8,128)S(1)}, u32[]{:S(2)}, u32[]{:S(2)}) async-start(f32[16,32,256]{2,1,0:T(8,128)} %bitcast.2), calls=%async_computation.6 | async-start | bytes 1048576 | tf_op jit(solution)/shard_map/all_to_all | solution.py:506
  107.7 1.0 copy-start.8
  108.7 7.4 %copy-start.5 = (f32[32,2048]{1,0:T(8,128)S(1)}, f32[32,2048]{1,0:T(8,128)}, u32[]{:S(2)}) copy-start(f32[32,2048]{1,0:T(8,128)} %get-tuple-element.62.rel_hbm) | copy-start | bytes 786436
  108.8 10.6 %copy-start.4 = (f32[32,2048]{1,0:T(8,128)S(1)}, f32[32,2048]{1,0:T(8,128)}, u32[]{:S(2)}) copy-start(f32[32,2048]{1,0:T(8,128)} %get-tuple-element.57.rel_hbm) | copy-start | bytes 786436
  108.8 18.3 %copy-start.3 = (f32[32,2048]{1,0:T(8,128)S(1)}, f32[32,2048]{1,0:T(8,128)}, u32[]{:S(2)}) copy-start(f32[32,2048]{1,0:T(8,128)} %get-tuple-element.56.rel_hbm) | copy-start | bytes 786436
  108.8 18.4 %copy-start.2 = (f32[32,2048]{1,0:T(8,128)S(1)}, f32[32,2048]{1,0:T(8,128)}, u32[]{:S(2)}) copy-start(f32[32,2048]{1,0:T(8,128)} %get-tuple-element.63.rel_hbm) | copy-start | bytes 786436
  108.8 7.4 %collective-permute-start.7 = (f32[32,2048]{1,0:T(8,128)S(1)}, f32[32,2048]{1,0:T(8,128)S(1)}, u32[]{:S(2)}, u32[]{:S(2)}) collective-permute-start(f32[32,2048]{1,0:T(8,128)S(1)} %shard_map.76), channel_id=1, source_target_pairs={{0,224},{16,240},{32,0},{48,16},{64,32},{80,48},{96,64},{112,80},{... | collective-permute-start | bytes 786440 | tf_op jit(solution)/shard_map/ppermute | solution.py:361
  110.4 25.9 %copy-start.1 = (f32[32,2048]{1,0:T(8,128)S(1)}, f32[32,2048]{1,0:T(8,128)}, u32[]{:S(2)}) copy-start(f32[32,2048]{1,0:T(8,128)} %get-tuple-element.55.rel_hbm) | copy-start | bytes 786436
  110.4 28.9 %copy-start = (bf16[4,256,256]{2,1,0:T(8,128)(2,1)S(1)}, bf16[4,256,256]{2,1,0:T(8,128)(2,1)}, u32[]{:S(2)}) copy-start(bf16[4,256,256]{2,1,0:T(8,128)(2,1)} %feats_ref.1) | copy-start | bytes 1572868
  110.4 28.9 %copy-start.6 = (s32[4,128]{1,0:T(4,128)S(1)}, s32[4,128]{1,0:T(4,128)}, u32[]{:S(2)}) copy-start(s32[4,128]{1,0:T(4,128)} %mask_ref.1) | copy-start | bytes 6148
  110.4 8.9 %collective-permute-start.4 = (f32[32,2048]{1,0:T(8,128)S(1)}, f32[32,2048]{1,0:T(8,128)S(1)}, u32[]{:S(2)}, u32[]{:S(2)}) collective-permute-start(f32[32,2048]{1,0:T(8,128)S(1)} %shard_map.74), channel_id=1, source_target_pairs={{0,32},{16,48},{32,64},{48,80},{64,96},{80,112},{96,128},{112,144}... | collective-permute-start | bytes 786440 | tf_op jit(solution)/shard_map/ppermute | solution.py:361
  116.2 10.4 %collective-permute-start.8 = (f32[32,2048]{1,0:T(8,128)S(1)}, f32[32,2048]{1,0:T(8,128)S(1)}, u32[]{:S(2)}, u32[]{:S(2)}) collective-permute-start(f32[32,2048]{1,0:T(8,128)S(1)} %shard_map.77), channel_id=1, source_target_pairs={{0,224},{16,240},{32,0},{48,16},{64,32},{80,48},{96,64},{112,80},{... | collective-permute-start | bytes 786440 | tf_op jit(solution)/shard_map/ppermute | solution.py:361
  119.4 7.7 %collective-permute-start.5 = (f32[32,2048]{1,0:T(8,128)S(1)}, f32[32,2048]{1,0:T(8,128)S(1)}, u32[]{:S(2)}, u32[]{:S(2)}) collective-permute-start(f32[32,2048]{1,0:T(8,128)S(1)} %shard_map.75), channel_id=1, source_target_pairs={{0,32},{16,48},{32,64},{48,80},{64,96},{80,112},{96,128},{112,144}... | collective-permute-start | bytes 786440 | tf_op jit(solution)/shard_map/ppermute | solution.py:361
  120.3 16.0 %all-to-all-start.7 = ((f32[16,32,256]{2,1,0:T(8,128)}), f32[16,32,256]{2,1,0:T(8,128)S(1)}, u32[]{:S(2)}, u32[]{:S(2)}) async-start(f32[16,32,256]{2,1,0:T(8,128)} %shard_map.72), calls=%async_computation.7 | async-start | bytes 1048576 | tf_op jit(solution)/shard_map/all_to_all | solution.py:513
  127.1 6.8 %collective-permute-start.9 = (f32[32,2048]{1,0:T(8,128)S(1)}, f32[32,2048]{1,0:T(8,128)S(1)}, u32[]{:S(2)}, u32[]{:S(2)}) collective-permute-start(f32[32,2048]{1,0:T(8,128)S(1)} %shard_map.78), channel_id=1, source_target_pairs={{0,32},{16,48},{32,64},{48,80},{64,96},{80,112},{96,128},{112,144}... | collective-permute-start | bytes 786440 | tf_op jit(solution)/shard_map/ppermute | solution.py:361
  127.3 9.0 %collective-permute-start.10 = (f32[32,2048]{1,0:T(8,128)S(1)}, f32[32,2048]{1,0:T(8,128)S(1)}, u32[]{:S(2)}, u32[]{:S(2)}) collective-permute-start(f32[32,2048]{1,0:T(8,128)S(1)} %shard_map.79), channel_id=1, source_target_pairs={{0,224},{16,240},{32,0},{48,16},{64,32},{80,48},{96,64},{112,80},{... | collective-permute-start | bytes 786440 | tf_op jit(solution)/shard_map/ppermute | solution.py:361
  136.4 5.1 %collective-permute-start.11 = (f32[16,2048]{1,0:T(8,128)S(1)}, f32[16,2048]{1,0:T(8,128)S(1)}, u32[]{:S(2)}, u32[]{:S(2)}) collective-permute-start(f32[16,2048]{1,0:T(8,128)S(1)} %get-tuple-element.69), channel_id=1, source_target_pairs={{0,16},{16,0},{32,48},{48,32},{64,80},{80,64},{96,112},{112,96},{1... | collective-permute-start | bytes 393224 | tf_op jit(solution)/shard_map/ppermute | solution.py:357

commit v8 on v7

--- a/solution.py
+++ b/solution.py
@@ -69,10 +69,17 @@
 
 
 def prep_kernel(
-    teacher_hbm, student_hbm, mask_hbm, zt_ref, zs_ref, teacher_ref, student_ref, mask_ref, sems
+    where_ref, teacher_hbm, student_hbm, mask_hbm, proto_hbm, zt_ref, zs_ref, proto_ref,
+    teacher_ref, student_ref, mask_ref, sems,
 ):
-    mask_copy, teacher_copy, student_copy = fetch(
-        ((mask_hbm, mask_ref), (teacher_hbm, teacher_ref), (student_hbm, student_ref)), sems
+    wide = proto_ref.shape[1]
+    mine = pl.ds(pl.multiple_of(where_ref[0] * wide, wide), wide)
+    mask_copy, teacher_copy, student_copy, proto_copy = fetch(
+        (
+            (mask_hbm, mask_ref), (teacher_hbm, teacher_ref), (student_hbm, student_ref),
+            (proto_hbm.at[:, mine], proto_ref),
+        ),
+        sems,
     )
     mask_copy.wait()
     slots = mask_ref.shape[1]
@@ -83,9 +90,10 @@
         for i in range(feats.shape[0]):
             rows, norm = masked_rows(feats[i], mask_ref[i : i + 1, :])
             out[i * slots : (i + 1) * slots, :] = (rows / norm).astype(BF16).astype(F32)
-
-
-def proto_kernel(where_ref, proto_ref, full_ref, unit_ref, back_ref, scale_ref):
+    proto_copy.wait()
+
+
+def proto_kernel(proto_ref, full_ref, unit_ref, back_ref, scale_ref):
     p = proto_ref[...].astype(F32)
     scale = 1.0 / jnp.sqrt(jnp.sum(p * p, axis=0, keepdims=True) + EPSILON)
     full = p * scale
@@ -170,7 +178,7 @@
     c = 1.0 / jnp.sum(parts_ref[...], axis=0)
     c_ref[...] = c
     tiles = c.shape[0]
-    block = 64
+    block = 128
 
     def body(b, carry):
         rows = pl.ds(pl.multiple_of(b * block, block), block)
@@ -214,7 +222,7 @@
         return tuple(out)
 
     zero = tuple(jnp.zeros((8, LANES), F32) for _ in range(tiles))
-    acc = lax.fori_loop(0, e_ref.shape[0] // block, body, zero)
+    acc = lax.fori_loop(0, e_ref.shape[0] // block, body, zero, unroll=2)
     value = jnp.concatenate([jnp.sum(a, axis=0, keepdims=True) for a in acc], axis=0)
     for m in range(Z):
         out_ref[m] = value
@@ -227,7 +235,7 @@
     spread(r_ref, scale / jnp.sum(parts_ref[...], axis=0))
     spread(m_ref, scale / jnp.sum(mass_ref[:, 8:, :], axis=0))
     tiles = e_ref.shape[1] // LANES
-    block = 16
+    block = 64
 
     def body(b, carry):
         rows = pl.ds(pl.multiple_of(b * block, block), block)
@@ -283,7 +291,18 @@
         out_ref[m] = total
 
 
-def last_kernel(gz_ref, feats_ref, mask_ref, out_ref):
+def last_kernel(
+    where_ref, keep_ref, got_ref, gz_ref, feats_ref, mask_ref, student_hbm, protos_hbm,
+    out_ref, sems, place_sems,
+):
+    core, wide = where_ref[0], keep_ref.shape[1]
+    copies = fetch(
+        [
+            (ref, protos_hbm.at[:, pl.ds(pl.multiple_of(lax.rem(core + side, 2) * wide, wide), wide)])
+            for side, ref in enumerate((keep_ref, got_ref))
+        ],
+        place_sems,
+    )
     slots = mask_ref.shape[1]
     for i in range(out_ref.shape[0]):
         mask = mask_ref[i : i + 1, :]
@@ -298,6 +317,9 @@
         out_ref[i] = jnp.dot(hot, high, preferred_element_type=F32) + jnp.dot(
             hot, low, preferred_element_type=F32
         )
+        copies += fetch(((out_ref.at[i], student_hbm.at[i]),), sems.at[pl.ds(i, 1)])
+    for copy in copies:
+        copy.wait()
 
 
 def sum_kernel(a_ref, b_ref, out_ref):
@@ -328,13 +350,6 @@
     total = rel[...] + (up_ref[...] + down_ref[...])
     keep_ref[...] = total[:near, :]
     give_ref[...] = total[near:, :]
-
-
-def place_kernel(where_ref, keep_ref, got_ref, out_ref):
-    wide = keep_ref.shape[1]
-    for side, ref in enumerate((keep_ref, got_ref)):
-        first = lax.rem(where_ref[0] + side, 2) * wide
-        out_ref[:, pl.ds(pl.multiple_of(first, wide), wide)] = ref[...]
 
 
 def shape(*dims, dtype=F32):
@@ -398,41 +413,27 @@
             cost_estimate=kw.get("cost_estimate"),
         )(where, *args)
 
-    zt, zs = pl.pallas_call(
+    zt, zs, protos = pl.pallas_call(
         prep_kernel,
-        in_specs=[pl.BlockSpec(memory_space=pl.ANY)] * 3,
-        out_specs=[whole()] * 2,
-        out_shape=[shape(own, width), shape(own, width)],
+        in_specs=[scalars] + [pl.BlockSpec(memory_space=pl.ANY)] * 4,
+        out_specs=[whole()] * 3,
+        out_shape=[shape(own, width), shape(own, width), hold(width, wide, dtype=BF16)],
         scratch_shapes=[
             VMEM(teacher_feats.shape, BF16), VMEM(student_feats.shape, BF16),
-            VMEM(mask_index.shape, jnp.int32), pltpu.SemaphoreType.DMA((3,)),
+            VMEM(mask_index.shape, jnp.int32), pltpu.SemaphoreType.DMA((4,)),
         ],
         compiler_params=params(16),
-    )(in_hbm(teacher_feats), in_hbm(student_feats), in_hbm(mask_index))
+    )(where, in_hbm(teacher_feats), in_hbm(student_feats), in_hbm(mask_index), in_hbm(prototypes))
     zt_other = other_core(zt)
     zs_other = other_core(zs)
-    steps = 2
-    column_spec = pl.BlockSpec((width, wide // steps), lambda j, w: (0, j))
-    full, unit, back, p_scale = pl.pallas_call(
+    full, unit, back, p_scale = call(
         proto_kernel,
-        grid_spec=pltpu.PrefetchScalarGridSpec(
-            num_scalar_prefetch=1,
-            grid=(steps,),
-            in_specs=[
-                pl.BlockSpec((width, wide // steps), lambda j, w: (0, w[0] * steps + j))
-            ],
-            out_specs=[
-                column_spec, column_spec,
-                pl.BlockSpec((wide // steps, width), lambda j, w: (j, 0)),
-                pl.BlockSpec((1, wide // steps), lambda j, w: (0, j)),
-            ],
-        ),
-        out_shape=[
-            shape(width, wide), shape(width, wide, dtype=BF16),
-            shape(wide, width, dtype=BF16), shape(1, wide),
+        [
+            hold(width, wide), hold(width, wide, dtype=BF16), hold(wide, width, dtype=BF16),
+            shape(1, wide),
         ],
-        compiler_params=params(16),
-    )(where, in_hbm(prototypes))
+        protos,
+    )
 
     exp_cost = cost(2 * tokens * wide * width, tokens * wide)
     e, col_out = placed(
@@ -471,7 +472,7 @@
         scratch=[VMEM((tokens, LANES), F32), VMEM((tokens, LANES), F32)],
     )
     gz, gz_give = placed(
-        token_kernel, [shape(own, width)] * 2, diff, back,
+        token_kernel, [hold(own, width), shape(own, width)], diff, back,
         cost_estimate=cost(2 * tokens * wide * width),
     )
     gz_got = other_core(gz_give)
@@ -511,9 +512,6 @@
     up = step(step_kernel, rel[2], up)
     down = step(step_kernel, rel[7], down)
     gz = lax.all_to_all(gz_share, "proto", 0, 0).reshape(own, width)
-    (grad_student,) = call(
-        last_kernel, [shape(images, patches, width)], gz, student_feats, mask_index
-    )
     up, down = along_z(up, 1), along_z(down, -1)
     up, down = tie((up, down), gz_share)
     up = step(step_kernel, rel[1], up)
@@ -529,7 +527,17 @@
         compiler_params=params(16),
     )(rel[0], up, down)
     got = other_core(give)
-    (grad_protos,) = placed(place_kernel, [shape(near, 2 * wide)], keep, got)
+    grad_student, grad_protos = pl.pallas_call(
+        last_kernel,
+        in_specs=[scalars] + [whole()] * 5,
+        out_specs=[pl.BlockSpec(memory_space=pl.ANY)] * 2,
+        out_shape=[shape(images, patches, width), shape(near, 2 * wide)],
+        scratch_shapes=[
+            VMEM((images, patches, width), F32), pltpu.SemaphoreType.DMA((images,)),
+            pltpu.SemaphoreType.DMA((2,)),
+        ],
+        compiler_params=params(16),
+    )(where, keep, got, gz, student_feats, mask_index)
     return (grad_student, grad_protos)
 
 

time: 143 us -> 142 us (level)
  Pallas kernels: 27.5 us -> 24.6 us
    pallas_call x9, Pallas kernels: 12.1 us -> 9.78 us  [call(): pl.pallas_call(kernel, out_shape=outs, in_specs=[whole()] * len(args), ou...]
    ppermute x4, waiting for transfers between devices: 0.01 us -> 1.69 us  [other_core(): return lax.ppermute(x, 'batch', [(i, i ^ 1) for i in range(RING)])]
    pallas_call x4 -> x3, Pallas kernels: 6.99 us -> 5.76 us  [placed(): pl.pallas_call(kernel, in_specs=[scalars] + [whole()] * len(args), out_sp...]
  transfers between devices with their start and end apart: 14 -> 14, of which waited for: 4 -> 6; matrix products, arithmetic and copies ran while one was open for 0% -> 0% of each run, Pallas kernels for 9% -> 6%
where the time goes in v8:
time: 142 us; the launch traced here: 141 us
  blocking collectives  74.8 us (53%)
  starting transfers between devices  26.2 us (18%)
  Pallas kernels  24.6 us (17%)
  waiting for transfers between devices  13.8 us (10%)
    all_to_all x3, blocking collectives, all_rows(): lax.all_to_all(x, ('batch', 'proto'), 0, 0, axis_index_groups=ROW_GROUPS)  42.1 us
    all_to_all x3, blocking collectives, all_columns(): return lax.all_to_all(x, 'batch', 0, 0, axis_index_groups=Z_GROUPS)  32.7 us
    ppermute x8, waiting for transfers between devices, along_z(): lax.ppermute(x, 'batch', [(i, (i // 2 + d) % Z * 2 + i % 2) for i in rang...  9.84 us
    pallas_call x9, Pallas kernels, call(): pl.pallas_call(kernel, out_shape=outs, in_specs=[whole()] * len(args), ou...  9.78 us
    ppermute x8, starting transfers between devices, along_z(): lax.ppermute(x, 'batch', [(i, (i // 2 + d) % Z * 2 + i % 2) for i in rang...  8.99 us
    ppermute x4, starting transfers between devices, other_core(): return lax.ppermute(x, 'batch', [(i, i ^ 1) for i in range(RING)])  7.2 us
    all_to_all x1, starting transfers between devices, on_device(): gz = lax.all_to_all(gz_share, 'proto', 0, 0).reshape(own, width)  6.27 us
    pallas_call x3, Pallas kernels, placed(): pl.pallas_call(kernel, in_specs=[scalars] + [whole()] * len(args), out_sp...  5.76 us
  transfers between devices with their start and end apart: 14, of which 6 were waited for; matrix products, arithmetic and copies ran while one was open for 0% of the time, Pallas kernels for 6%

profile of v8, /device:TPU:1, one launch (start us, length us, event | category | flops | bytes accessed | tf_op | source)
XLA Modules:
  0.0 141.5 jit_solution(12757338577036306783)
XLA Ops:
  0.7 2.5 %shard_map.59 = (f32[512,256]{1,0:T(8,128)S(1)}, f32[512,256]{1,0:T(8,128)S(1)}, bf16[256,2048]{1,0:T(8,128)(2,1)S(1)}) custom-call(s32[2]{0:T(128)S(1)} %pad_add_fusion.where_ref, bf16[4,256,256]{2,1,0:T(8,128)(2,1)} %teacher_hbm.1, bf16[4,256,256]{2,1,0:T(8,128)(2,1)} %feats_ref.1, s32[4,128]{1,0:T(4,128)} %mask_ref.1, bf16[256,4096]{1,0:T(8,128)(2,1)} %proto_hbm.1), custom_call_target="tpu_custom_call" | custom-call | tf_op jit(solution)/shard_map/pallas_call | solution.py:416
  3.2 3.3 %collective-permute-start = (f32[512,256]{1,0:T(8,128)S(1)}, f32[512,256]{1,0:T(8,128)S(1)}, u32[]{:S(2)}, u32[]{:S(2)}) collective-permute-start(f32[512,256]{1,0:T(8,128)S(1)} %get-tuple-element.37.own_ref), channel_id=1, source_target_pairs={{0,16},{16,0},{32,48},{48,32},{64,80},{80,64},{96,112},{112,96},{1... | collective-permute-start | bytes 1572872 | tf_op jit(solution)/shard_map/ppermute | solution.py:372
  8.1 1.9 %shard_map.61 = (f32[1024,2048]{1,0:T(8,128)S(1)}, f32[8,16,128]{2,1,0:T(8,128)S(1)}) custom-call(s32[2]{0:T(128)S(1)} %pad_add_fusion.where_ref, f32[512,256]{1,0:T(8,128)S(1)} %get-tuple-element.37.own_ref, f32[512,256]{1,0:T(8,128)S(1)} %collective-permute-done.other_ref, bf16[256,2048]{1,0:T(8,128)(2,1)S(1)} %get-tuple-element.39.unit_ref), custom_call_target="tpu_custom_call" | custom-call | flops 1073741824 | tf_op jit(solution)/shard_map/pallas_call | solution.py:406
  10.0 2.0 %shard_map.62 = (f32[1024,2048]{1,0:T(8,128)S(1)}, f32[1024,128]{1,0:T(8,128)S(1)}, bf16[256,1024]{1,0:T(8,128)(2,1)S(1)}) custom-call(s32[2]{0:T(128)S(1)} %pad_add_fusion.where_ref, f32[512,256]{1,0:T(8,128)S(1)} %get-tuple-element.41.own_ref, f32[512,256]{1,0:T(8,128)S(1)} %collective-permute-done.1.other_ref, ...), custom_call_target="tpu_custom_call" | custom-call | flops 1073741824 | tf_op jit(solution)/shard_map/pallas_call | solution.py:406
  12.1 13.5 %all_to_all.40.parts_ref = f32[8,16,128]{2,1,0:T(8,128)S(1)} all-to-all(f32[8,16,128]{2,1,0:T(8,128)S(1)} %get-tuple-element.45), channel_id=1, replica_groups={{0,32,64,96,128,160,192,224},{16,48,80,112,144,176,208,240},{1,33,65,97..., dimensions={0} | all-to-all | bytes 131072 | tf_op jit(solution)/shard_map/all_to_all | solution.py:382
  25.5 1.5 %shard_map.63 = (f32[32,16,128]{2,1,0:T(8,128)S(1)}, f32[16,128]{1,0:T(8,128)}) custom-call(f32[1024,2048]{1,0:T(8,128)S(1)} %get-tuple-element.40.e_ref, f32[8,16,128]{2,1,0:T(8,128)S(1)} %all_to_all.40.parts_ref, f32[1024,128]{1,0:T(8,128)S(1)} %get-tuple-element.44.mass_ref), custom_call_target="tpu_custom_call" | custom-call | tf_op jit(solution)/shard_map/pallas_call | solution.py:41
  27.0 17.0 %all_to_all.41.parts_ref.mass_ref = f32[32,16,128]{2,1,0:T(8,128)S(1)} all-to-all(f32[32,16,128]{2,1,0:T(8,128)S(1)} %get-tuple-element.46), channel_id=1, replica_groups={{0,1,2,3,4,5,6,7,8,9,10,11,12,13,14,15,16,17,18,19,20,21,22,23,24,25,26..., dimensions={0} | all-to-all | bytes 524288 | tf_op jit(solution)/shard_map/all_to_all | solution.py:386
  44.0 0.9 shard_map.64
  44.9 9.6 %all_to_all.42.parts_ref = f32[8,16,128]{2,1,0:T(8,128)S(1)} all-to-all(f32[8,16,128]{2,1,0:T(8,128)S(1)} %shard_map.64), channel_id=1, replica_groups={{0,32,64,96,128,160,192,224},{16,48,80,112,144,176,208,240},{1,33,65,97..., dimensions={0} | all-to-all | bytes 131072 | tf_op jit(solution)/shard_map/all_to_all | solution.py:382
  54.5 1.2 shard_map.65
  55.7 12.8 %all_to_all.43.parts_ref = f32[32,8,128]{2,1,0:T(8,128)S(1)} all-to-all(f32[32,8,128]{2,1,0:T(8,128)S(1)} %get-tuple-element.47), channel_id=1, replica_groups={{0,1,2,3,4,5,6,7,8,9,10,11,12,13,14,15,16,17,18,19,20,21,22,23,24,25,26..., dimensions={0} | all-to-all | bytes 262144 | tf_op jit(solution)/shard_map/all_to_all | solution.py:386
  68.5 0.9 shard_map.66
  69.4 9.6 %all_to_all.44.parts_ref = f32[8,16,128]{2,1,0:T(8,128)S(1)} all-to-all(f32[8,16,128]{2,1,0:T(8,128)S(1)} %shard_map.66), channel_id=1, replica_groups={{0,32,64,96,128,160,192,224},{16,48,80,112,144,176,208,240},{1,33,65,97..., dimensions={0} | all-to-all | bytes 131072 | tf_op jit(solution)/shard_map/all_to_all | solution.py:382
  79.9 12.4 %all_to_all.45.parts_ref = f32[32,8,128]{2,1,0:T(8,128)S(1)} all-to-all(f32[32,8,128]{2,1,0:T(8,128)S(1)} %get-tuple-element.49), channel_id=1, replica_groups={{0,1,2,3,4,5,6,7,8,9,10,11,12,13,14,15,16,17,18,19,20,21,22,23,24,25,26..., dimensions={0} | all-to-all | bytes 262144 | tf_op jit(solution)/shard_map/all_to_all | solution.py:386
  92.2 2.0 %shard_map.68.diff_ref = bf16[1024,2048]{1,0:T(8,128)(2,1)S(1)} custom-call(f32[1024,2048]{1,0:T(8,128)S(1)} %get-tuple-element.40.e_ref, f32[1024,2048]{1,0:T(8,128)S(1)} %get-tuple-element.42.s_ref, f32[16,128]{1,0:T(8,128)S(1)} %get-tuple-element.48.c_ref, f32[32,8,128]{2,1,0:T(8,128)S(1)} %all_to_all.45.parts_ref, ...), custom_call_target="tpu_custom_call" | custom-call | tf_op jit(solution)/shard_map/pallas_call | solution.py:41
  94.2 1.8 %shard_map.69 = (f32[512,256]{1,0:T(8,128)S(1)}, f32[512,256]{1,0:T(8,128)S(1)}) custom-call(s32[2]{0:T(128)S(1)} %pad_add_fusion.where_ref, bf16[1024,2048]{1,0:T(8,128)(2,1)S(1)} %shard_map.68.diff_ref, bf16[2048,256]{1,0:T(8,128)(2,1)S(1)} %get-tuple-element.50.back_ref), custom_call_target="tpu_custom_call" | custom-call | flops 1073741824 | tf_op jit(solution)/shard_map/pallas_call | solution.py:406
  96.6 3.5 %shard_map.70 = (f32[32,2048]{1,0:T(8,128)}, f32[32,2048]{1,0:T(8,128)}, f32[32,2048]{1,0:T(8,128)}, f32[32,2048]{1,0:T(8,128)}, f32[16,2048]{1,0:T(8,128)}, /*i...) custom-call(s32[2]{0:T(128)S(1)} %pad_add_fusion.where_ref, ...), custom_call_target="tpu_custom_call" | custom-call | flops 1073741824 | tf_op jit(solution)/shard_map/pallas_call | solution.py:482
  100.4 1.5 %collective-permute-start.2 = (f32[16,2048]{1,0:T(8,128)}, f32[16,2048]{1,0:T(8,128)S(1)}, u32[]{:S(2)}, u32[]{:S(2)}) collective-permute-start(f32[16,2048]{1,0:T(8,128)} %get-tuple-element.61), channel_id=1, source_target_pairs={{0,32},{16,48},{32,64},{48,80},{64,96},{80,112},{96,128},{112,144}... | collective-permute-start | bytes 393224 | tf_op jit(solution)/shard_map/ppermute | solution.py:376
  101.8 0.9 shard_map.75
  102.7 3.7 %all-to-all-start.6 = ((f32[16,32,256]{2,1,0:T(8,128)}), f32[16,32,256]{2,1,0:T(8,128)S(1)}, u32[]{:S(2)}, u32[]{:S(2)}) async-start(f32[16,32,256]{2,1,0:T(8,128)} %bitcast.2), calls=%async_computation.6 | async-start | bytes 1048576 | tf_op jit(solution)/shard_map/all_to_all | solution.py:507
  106.5 0.9 copy-done.8
  107.5 1.4 collective-permute-start.6
  109.2 5.6 %collective-permute-done.6.got_ref = f32[32,2048]{1,0:T(8,128)S(1)} collective-permute-done((f32[32,2048]{1,0:T(8,128)S(1)}, f32[32,2048]{1,0:T(8,128)S(1)}, u32[]{:S(2)}, u32[]{:S(2)}) %collective-permute-start.6) | collective-permute-done | bytes 262176 | tf_op jit(solution)/shard_map/ppermute | solution.py:376
  114.9 2.8 %collective-permute-start.7 = (f32[32,2048]{1,0:T(8,128)S(1)}, f32[32,2048]{1,0:T(8,128)S(1)}, u32[]{:S(2)}, u32[]{:S(2)}) collective-permute-start(f32[32,2048]{1,0:T(8,128)S(1)} %shard_map.74), channel_id=1, source_target_pairs={{0,224},{16,240},{32,0},{48,16},{64,32},{80,48},{96,64},{112,80},{... | collective-permute-start | bytes 786440 | tf_op jit(solution)/shard_map/ppermute | solution.py:376
  117.8 0.9 shard_map.76
  118.7 6.3 %all-to-all-start.7 = ((f32[16,32,256]{2,1,0:T(8,128)}), f32[16,32,256]{2,1,0:T(8,128)S(1)}, u32[]{:S(2)}, u32[]{:S(2)}) async-start(f32[16,32,256]{2,1,0:T(8,128)} %shard_map.76), calls=%async_computation.7 | async-start | bytes 1048576 | tf_op jit(solution)/shard_map/all_to_all | solution.py:514
  125.5 2.7 %collective-permute-start.10 = (f32[32,2048]{1,0:T(8,128)S(1)}, f32[32,2048]{1,0:T(8,128)S(1)}, u32[]{:S(2)}, u32[]{:S(2)}) collective-permute-start(f32[32,2048]{1,0:T(8,128)S(1)} %shard_map.78), channel_id=1, source_target_pairs={{0,224},{16,240},{32,0},{48,16},{64,32},{80,48},{96,64},{112,80},{... | collective-permute-start | bytes 786440 | tf_op jit(solution)/shard_map/ppermute | solution.py:376
  128.2 3.9 %collective-permute-done.9.up_ref = f32[32,2048]{1,0:T(8,128)S(1)} collective-permute-done((f32[32,2048]{1,0:T(8,128)S(1)}, f32[32,2048]{1,0:T(8,128)S(1)}, u32[]{:S(2)}, u32[]{:S(2)}) %collective-permute-start.9) | collective-permute-done | bytes 262176 | tf_op jit(solution)/shard_map/ppermute | solution.py:376
  132.2 2.3 %all-to-all-done.7 = f32[16,32,256]{2,1,0:T(8,128)S(1)} async-done(((f32[16,32,256]{2,1,0:T(8,128)}), f32[16,32,256]{2,1,0:T(8,128)S(1)}, u32[]{:S(2)}, u32[]{:S(2)}) %all-to-all-start.7) | async-done | bytes 524320 | tf_op jit(solution)/shard_map/all_to_all | solution.py:514
  134.5 3.2 %collective-permute-start.11 = (f32[16,2048]{1,0:T(8,128)S(1)}, f32[16,2048]{1,0:T(8,128)S(1)}, u32[]{:S(2)}, u32[]{:S(2)}) collective-permute-start(f32[16,2048]{1,0:T(8,128)S(1)} %get-tuple-element.71), channel_id=1, source_target_pairs={{0,16},{16,0},{32,48},{48,32},{64,80},{80,64},{96,112},{112,96},{1... | collective-permute-start | bytes 393224 | tf_op jit(solution)/shard_map/ppermute | solution.py:372
  137.7 1.0 collective-permute-done.11.got_ref
  138.7 2.6 %shard_map.80 = (f32[4,256,256]{2,1,0:T(8,128)}, f32[16,4096]{1,0:T(8,128)}) custom-call(s32[2]{0:T(128)S(1)} %pad_add_fusion.where_ref, f32[16,2048]{1,0:T(8,128)S(1)} %get-tuple-element.70.keep_ref, f32[16,2048]{1,0:T(8,128)S(1)} %collective-permute-done.11.got_ref, f32[512,256]{1,0:T(8,128)S(1)} %bitcast.4, bf16[4,256,256]{2,1,0:T(8,128)(2,1)S(1)} %copy-done, ...), custom_call_target="tpu_custom_call" | custom-call | tf_op jit(solution)/shard_map/pallas_call | solution.py:530
  (43 shorter events, 4.5 us)
Async XLA Ops:
  3.2 4.9 %collective-permute-start = (f32[512,256]{1,0:T(8,128)S(1)}, f32[512,256]{1,0:T(8,128)S(1)}, u32[]{:S(2)}, u32[]{:S(2)}) collective-permute-start(f32[512,256]{1,0:T(8,128)S(1)} %get-tuple-element.37.own_ref), channel_id=1, source_target_pairs={{0,16},{16,0},{32,48},{48,32},{64,80},{80,64},{96,112},{112,96},{1... | collective-permute-start | bytes 1572872 | tf_op jit(solution)/shard_map/ppermute | solution.py:372
  6.5 3.5 %collective-permute-start.1 = (f32[512,256]{1,0:T(8,128)S(1)}, f32[512,256]{1,0:T(8,128)S(1)}, u32[]{:S(2)}, u32[]{:S(2)}) collective-permute-start(f32[512,256]{1,0:T(8,128)S(1)} %get-tuple-element.41.own_ref), channel_id=1, source_target_pairs={{0,16},{16,0},{32,48},{48,32},{64,80},{80,64},{96,112},{112,96},{1... | collective-permute-start | bytes 1572872 | tf_op jit(solution)/shard_map/ppermute | solution.py:372
  96.0 5.9 %collective-permute-start.8 = (f32[512,256]{1,0:T(8,128)S(1)}, f32[512,256]{1,0:T(8,128)S(1)}, u32[]{:S(2)}, u32[]{:S(2)}) collective-permute-start(f32[512,256]{1,0:T(8,128)S(1)} %get-tuple-element.52), channel_id=1, source_target_pairs={{0,16},{16,0},{32,48},{48,32},{64,80},{80,64},{96,112},{112,96},{1... | collective-permute-start | bytes 1572872 | tf_op jit(solution)/shard_map/ppermute | solution.py:372
  100.1 6.3 %collective-permute-start.5 = (f32[16,2048]{1,0:T(8,128)}, f32[16,2048]{1,0:T(8,128)S(1)}, u32[]{:S(2)}, u32[]{:S(2)}) collective-permute-start(f32[16,2048]{1,0:T(8,128)} %get-tuple-element.64), channel_id=1, source_target_pairs={{0,224},{16,240},{32,0},{48,16},{64,32},{80,48},{96,64},{112,80},{... | collective-permute-start | bytes 393224 | tf_op jit(solution)/shard_map/ppermute | solution.py:376
  100.4 8.5 %collective-permute-start.2 = (f32[16,2048]{1,0:T(8,128)}, f32[16,2048]{1,0:T(8,128)S(1)}, u32[]{:S(2)}, u32[]{:S(2)}) collective-permute-start(f32[16,2048]{1,0:T(8,128)} %get-tuple-element.61), channel_id=1, source_target_pairs={{0,32},{16,48},{32,64},{48,80},{64,96},{80,112},{96,128},{112,144}... | collective-permute-start | bytes 393224 | tf_op jit(solution)/shard_map/ppermute | solution.py:376
  102.7 6.2 %copy-start.7 = (f32[32,2048]{1,0:T(8,128)S(1)}, f32[32,2048]{1,0:T(8,128)}, u32[]{:S(2)}) copy-start(f32[32,2048]{1,0:T(8,128)} %get-tuple-element.60.rel_hbm) | copy-start | bytes 786436
  102.7 15.1 %all-to-all-start.6 = ((f32[16,32,256]{2,1,0:T(8,128)}), f32[16,32,256]{2,1,0:T(8,128)S(1)}, u32[]{:S(2)}, u32[]{:S(2)}) async-start(f32[16,32,256]{2,1,0:T(8,128)} %bitcast.2), calls=%async_computation.6 | async-start | bytes 1048576 | tf_op jit(solution)/shard_map/all_to_all | solution.py:507
  106.4 1.0 copy-start.8
  107.4 7.4 %copy-start.5 = (f32[32,2048]{1,0:T(8,128)S(1)}, f32[32,2048]{1,0:T(8,128)}, u32[]{:S(2)}) copy-start(f32[32,2048]{1,0:T(8,128)} %get-tuple-element.62.rel_hbm) | copy-start | bytes 786436
  107.5 10.2 %copy-start.4 = (f32[32,2048]{1,0:T(8,128)S(1)}, f32[32,2048]{1,0:T(8,128)}, u32[]{:S(2)}) copy-start(f32[32,2048]{1,0:T(8,128)} %get-tuple-element.59.rel_hbm) | copy-start | bytes 786436
  107.5 17.8 %copy-start.3 = (f32[32,2048]{1,0:T(8,128)S(1)}, f32[32,2048]{1,0:T(8,128)}, u32[]{:S(2)}) copy-start(f32[32,2048]{1,0:T(8,128)} %get-tuple-element.58.rel_hbm) | copy-start | bytes 786436
  107.5 18.0 %copy-start.2 = (f32[32,2048]{1,0:T(8,128)S(1)}, f32[32,2048]{1,0:T(8,128)}, u32[]{:S(2)}) copy-start(f32[32,2048]{1,0:T(8,128)} %get-tuple-element.65.rel_hbm) | copy-start | bytes 786436
  107.5 7.4 %collective-permute-start.6 = (f32[32,2048]{1,0:T(8,128)S(1)}, f32[32,2048]{1,0:T(8,128)S(1)}, u32[]{:S(2)}, u32[]{:S(2)}) collective-permute-start(f32[32,2048]{1,0:T(8,128)S(1)} %shard_map.73), channel_id=1, source_target_pairs={{0,224},{16,240},{32,0},{48,16},{64,32},{80,48},{96,64},{112,80},{... | collective-permute-start | bytes 786440 | tf_op jit(solution)/shard_map/ppermute | solution.py:376
  108.9 25.5 %copy-start.1 = (f32[32,2048]{1,0:T(8,128)S(1)}, f32[32,2048]{1,0:T(8,128)}, u32[]{:S(2)}) copy-start(f32[32,2048]{1,0:T(8,128)} %get-tuple-element.57.rel_hbm) | copy-start | bytes 786436
  108.9 29.8 %copy-start = (bf16[4,256,256]{2,1,0:T(8,128)(2,1)S(1)}, bf16[4,256,256]{2,1,0:T(8,128)(2,1)}, u32[]{:S(2)}) copy-start(bf16[4,256,256]{2,1,0:T(8,128)(2,1)} %feats_ref.1) | copy-start | bytes 1572868
  108.9 29.7 %copy-start.6 = (s32[4,128]{1,0:T(4,128)S(1)}, s32[4,128]{1,0:T(4,128)}, u32[]{:S(2)}) copy-start(s32[4,128]{1,0:T(4,128)} %mask_ref.1) | copy-start | bytes 6148
  109.0 8.7 %collective-permute-start.3 = (f32[32,2048]{1,0:T(8,128)S(1)}, f32[32,2048]{1,0:T(8,128)S(1)}, u32[]{:S(2)}, u32[]{:S(2)}) collective-permute-start(f32[32,2048]{1,0:T(8,128)S(1)} %shard_map.71), channel_id=1, source_target_pairs={{0,32},{16,48},{32,64},{48,80},{64,96},{80,112},{96,128},{112,144}... | collective-permute-start | bytes 786440 | tf_op jit(solution)/shard_map/ppermute | solution.py:376
  114.9 10.1 %collective-permute-start.7 = (f32[32,2048]{1,0:T(8,128)S(1)}, f32[32,2048]{1,0:T(8,128)S(1)}, u32[]{:S(2)}, u32[]{:S(2)}) collective-permute-start(f32[32,2048]{1,0:T(8,128)S(1)} %shard_map.74), channel_id=1, source_target_pairs={{0,224},{16,240},{32,0},{48,16},{64,32},{80,48},{96,64},{112,80},{... | collective-permute-start | bytes 786440 | tf_op jit(solution)/shard_map/ppermute | solution.py:376
  117.7 7.5 %collective-permute-start.4 = (f32[32,2048]{1,0:T(8,128)S(1)}, f32[32,2048]{1,0:T(8,128)S(1)}, u32[]{:S(2)}, u32[]{:S(2)}) collective-permute-start(f32[32,2048]{1,0:T(8,128)S(1)} %shard_map.72), channel_id=1, source_target_pairs={{0,32},{16,48},{32,64},{48,80},{64,96},{80,112},{96,128},{112,144}... | collective-permute-start | bytes 786440 | tf_op jit(solution)/shard_map/ppermute | solution.py:376
  118.7 15.8 %all-to-all-start.7 = ((f32[16,32,256]{2,1,0:T(8,128)}), f32[16,32,256]{2,1,0:T(8,128)S(1)}, u32[]{:S(2)}, u32[]{:S(2)}) async-start(f32[16,32,256]{2,1,0:T(8,128)} %shard_map.76), calls=%async_computation.7 | async-start | bytes 1048576 | tf_op jit(solution)/shard_map/all_to_all | solution.py:514
  125.3 6.8 %collective-permute-start.9 = (f32[32,2048]{1,0:T(8,128)S(1)}, f32[32,2048]{1,0:T(8,128)S(1)}, u32[]{:S(2)}, u32[]{:S(2)}) collective-permute-start(f32[32,2048]{1,0:T(8,128)S(1)} %shard_map.77), channel_id=1, source_target_pairs={{0,32},{16,48},{32,64},{48,80},{64,96},{80,112},{96,128},{112,144}... | collective-permute-start | bytes 786440 | tf_op jit(solution)/shard_map/ppermute | solution.py:376
  125.5 8.9 %collective-permute-start.10 = (f32[32,2048]{1,0:T(8,128)S(1)}, f32[32,2048]{1,0:T(8,128)S(1)}, u32[]{:S(2)}, u32[]{:S(2)}) collective-permute-start(f32[32,2048]{1,0:T(8,128)S(1)} %shard_map.78), channel_id=1, source_target_pairs={{0,224},{16,240},{32,0},{48,16},{64,32},{80,48},{96,64},{112,80},{... | collective-permute-start | bytes 786440 | tf_op jit(solution)/shard_map/ppermute | solution.py:376
  134.5 4.1 %collective-permute-start.11 = (f32[16,2048]{1,0:T(8,128)S(1)}, f32[16,2048]{1,0:T(8,128)S(1)}, u32[]{:S(2)}, u32[]{:S(2)}) collective-permute-start(f32[16,2048]{1,0:T(8,128)S(1)} %get-tuple-element.71), channel_id=1, source_target_pairs={{0,16},{16,0},{32,48},{48,32},{64,80},{80,64},{96,112},{112,96},{1... | collective-permute-start | bytes 393224 | tf_op jit(solution)/shard_map/ppermute | solution.py:372

commit v9 on v8

--- a/solution.py
+++ b/solution.py
@@ -291,8 +291,19 @@
         out_ref[m] = total
 
 
+def again_kernel(feats_ref, mask_ref, full_ref, norm_ref, hot_ref):
+    slots = mask_ref.shape[1]
+    for i in range(feats_ref.shape[0]):
+        rows = slice(i * slots, (i + 1) * slots)
+        mask = mask_ref[i : i + 1, :]
+        xs, norm = masked_rows(feats_ref[i], mask)
+        full_ref[rows, :] = xs / norm
+        norm_ref[rows, :] = norm
+        hot_ref[i] = one_hot_t(mask, feats_ref.shape[1], BF16)
+
+
 def last_kernel(
-    where_ref, keep_ref, got_ref, gz_ref, feats_ref, mask_ref, student_hbm, protos_hbm,
+    where_ref, keep_ref, got_ref, gz_ref, full_ref, norm_ref, hot_ref, student_hbm, protos_hbm,
     out_ref, sems, place_sems,
 ):
     core, wide = where_ref[0], keep_ref.shape[1]
@@ -303,15 +314,14 @@
         ],
         place_sems,
     )
-    slots = mask_ref.shape[1]
+    slots = hot_ref.shape[2]
     for i in range(out_ref.shape[0]):
-        mask = mask_ref[i : i + 1, :]
-        xs, norm = masked_rows(feats_ref[i], mask)
-        zsf = xs / norm
-        gz = gz_ref[i * slots : (i + 1) * slots, :]
+        rows = slice(i * slots, (i + 1) * slots)
+        zsf = full_ref[rows, :]
+        gz = gz_ref[rows, :]
         proj = jnp.sum(zsf * gz, axis=1, keepdims=True)
-        grad = (gz - zsf * proj) / norm
-        hot = one_hot_t(mask, out_ref.shape[1], BF16)
+        grad = (gz - zsf * proj) / norm_ref[rows, :]
+        hot = hot_ref[i]
         high = grad.astype(BF16)
         low = (grad - high.astype(F32)).astype(BF16)
         out_ref[i] = jnp.dot(hot, high, preferred_element_type=F32) + jnp.dot(
@@ -527,9 +537,14 @@
         compiler_params=params(16),
     )(rel[0], up, down)
     got = other_core(give)
+    again = call(
+        again_kernel,
+        [shape(own, width), shape(own, 1), shape(images, patches, slots, dtype=BF16)],
+        student_feats, tie(mask_index, give),
+    )
     grad_student, grad_protos = pl.pallas_call(
         last_kernel,
-        in_specs=[scalars] + [whole()] * 5,
+        in_specs=[scalars] + [whole()] * 6,
         out_specs=[pl.BlockSpec(memory_space=pl.ANY)] * 2,
         out_shape=[shape(images, patches, width), shape(near, 2 * wide)],
         scratch_shapes=[
@@ -537,7 +552,7 @@
             pltpu.SemaphoreType.DMA((2,)),
         ],
         compiler_params=params(16),
-    )(where, keep, got, gz, student_feats, mask_index)
+    )(where, keep, got, gz, *again)
     return (grad_student, grad_protos)
 
 

time: 142 us -> 142 us (level)
    pallas_call x9 -> x10, Pallas kernels: 9.78 us -> 10.2 us  [call(): pl.pallas_call(kernel, out_shape=outs, in_specs=[whole()] * len(args), ou...]
where the time goes in v9:
time: 142 us; the launch traced here: 141 us
  blocking collectives  74.8 us (53%)
  starting transfers between devices  26.2 us (18%)
  Pallas kernels  24.4 us (17%)
  waiting for transfers between devices  13.4 us (9%)
    all_to_all x3, blocking collectives, all_rows(): lax.all_to_all(x, ('batch', 'proto'), 0, 0, axis_index_groups=ROW_GROUPS)  42.1 us
    all_to_all x3, blocking collectives, all_columns(): return lax.all_to_all(x, 'batch', 0, 0, axis_index_groups=Z_GROUPS)  32.7 us
    pallas_call x10, Pallas kernels, call(): pl.pallas_call(kernel, out_shape=outs, in_specs=[whole()] * len(args), ou...  10.2 us
    ppermute x8, waiting for transfers between devices, along_z(): lax.ppermute(x, 'batch', [(i, (i // 2 + d) % Z * 2 + i % 2) for i in rang...  9.84 us
    ppermute x8, starting transfers between devices, along_z(): lax.ppermute(x, 'batch', [(i, (i // 2 + d) % Z * 2 + i % 2) for i in rang...  8.99 us
    ppermute x4, starting transfers between devices, other_core(): return lax.ppermute(x, 'batch', [(i, i ^ 1) for i in range(RING)])  7.2 us
    all_to_all x1, starting transfers between devices, on_device(): gz = lax.all_to_all(gz_share, 'proto', 0, 0).reshape(own, width)  6.27 us
    pallas_call x3, Pallas kernels, placed(): pl.pallas_call(kernel, in_specs=[scalars] + [whole()] * len(args), out_sp...  5.76 us
  transfers between devices with their start and end apart: 14, of which 6 were waited for; matrix products, arithmetic and copies ran while one was open for 0% of the time, Pallas kernels for 6%

profile of v9, /device:TPU:1, one launch (start us, length us, event | category | flops | bytes accessed | tf_op | source)
XLA Modules:
  0.0 140.9 jit_solution(4895823615857697840)
XLA Ops:
  0.7 2.5 %shard_map.59 = (f32[512,256]{1,0:T(8,128)S(1)}, f32[512,256]{1,0:T(8,128)S(1)}, bf16[256,2048]{1,0:T(8,128)(2,1)S(1)}) custom-call(s32[2]{0:T(128)S(1)} %pad_add_fusion.where_ref, bf16[4,256,256]{2,1,0:T(8,128)(2,1)} %teacher_hbm.1, bf16[4,256,256]{2,1,0:T(8,128)(2,1)} %feats_ref.1, s32[4,128]{1,0:T(4,128)} %mask_ref, bf16[256,4096]{1,0:T(8,128)(2,1)} %proto_hbm.1), custom_call_target="tpu_custom_call" | custom-call | tf_op jit(solution)/shard_map/pallas_call | solution.py:426
  3.2 3.3 %collective-permute-start = (f32[512,256]{1,0:T(8,128)S(1)}, f32[512,256]{1,0:T(8,128)S(1)}, u32[]{:S(2)}, u32[]{:S(2)}) collective-permute-start(f32[512,256]{1,0:T(8,128)S(1)} %get-tuple-element.41.own_ref), channel_id=1, source_target_pairs={{0,16},{16,0},{32,48},{48,32},{64,80},{80,64},{96,112},{112,96},{1... | collective-permute-start | bytes 1572872 | tf_op jit(solution)/shard_map/ppermute | solution.py:382
  8.1 1.9 %shard_map.61 = (f32[1024,2048]{1,0:T(8,128)S(1)}, f32[8,16,128]{2,1,0:T(8,128)S(1)}) custom-call(s32[2]{0:T(128)S(1)} %pad_add_fusion.where_ref, f32[512,256]{1,0:T(8,128)S(1)} %get-tuple-element.41.own_ref, f32[512,256]{1,0:T(8,128)S(1)} %collective-permute-done.other_ref, bf16[256,2048]{1,0:T(8,128)(2,1)S(1)} %get-tuple-element.43.unit_ref), custom_call_target="tpu_custom_call" | custom-call | flops 1073741824 | tf_op jit(solution)/shard_map/pallas_call | solution.py:416
  10.0 2.0 %shard_map.62 = (f32[1024,2048]{1,0:T(8,128)S(1)}, f32[1024,128]{1,0:T(8,128)S(1)}, bf16[256,1024]{1,0:T(8,128)(2,1)S(1)}) custom-call(s32[2]{0:T(128)S(1)} %pad_add_fusion.where_ref, f32[512,256]{1,0:T(8,128)S(1)} %get-tuple-element.45.own_ref, f32[512,256]{1,0:T(8,128)S(1)} %collective-permute-done.1.other_ref, ...), custom_call_target="tpu_custom_call" | custom-call | flops 1073741824 | tf_op jit(solution)/shard_map/pallas_call | solution.py:416
  12.1 13.5 %all_to_all.40.parts_ref = f32[8,16,128]{2,1,0:T(8,128)S(1)} all-to-all(f32[8,16,128]{2,1,0:T(8,128)S(1)} %get-tuple-element.49), channel_id=1, replica_groups={{0,32,64,96,128,160,192,224},{16,48,80,112,144,176,208,240},{1,33,65,97..., dimensions={0} | all-to-all | bytes 131072 | tf_op jit(solution)/shard_map/all_to_all | solution.py:392
  25.5 1.5 %shard_map.63 = (f32[32,16,128]{2,1,0:T(8,128)S(1)}, f32[16,128]{1,0:T(8,128)}) custom-call(f32[1024,2048]{1,0:T(8,128)S(1)} %get-tuple-element.44.e_ref, f32[8,16,128]{2,1,0:T(8,128)S(1)} %all_to_all.40.parts_ref, f32[1024,128]{1,0:T(8,128)S(1)} %get-tuple-element.48.mass_ref), custom_call_target="tpu_custom_call" | custom-call | tf_op jit(solution)/shard_map/pallas_call | solution.py:41
  27.0 17.0 %all_to_all.41.parts_ref.mass_ref = f32[32,16,128]{2,1,0:T(8,128)S(1)} all-to-all(f32[32,16,128]{2,1,0:T(8,128)S(1)} %get-tuple-element.50), channel_id=1, replica_groups={{0,1,2,3,4,5,6,7,8,9,10,11,12,13,14,15,16,17,18,19,20,21,22,23,24,25,26..., dimensions={0} | all-to-all | bytes 524288 | tf_op jit(solution)/shard_map/all_to_all | solution.py:396
  44.0 0.9 shard_map.64
  44.9 9.6 %all_to_all.42.parts_ref = f32[8,16,128]{2,1,0:T(8,128)S(1)} all-to-all(f32[8,16,128]{2,1,0:T(8,128)S(1)} %shard_map.64), channel_id=1, replica_groups={{0,32,64,96,128,160,192,224},{16,48,80,112,144,176,208,240},{1,33,65,97..., dimensions={0} | all-to-all | bytes 131072 | tf_op jit(solution)/shard_map/all_to_all | solution.py:392
  54.5 1.2 shard_map.65
  55.7 12.8 %all_to_all.43.parts_ref = f32[32,8,128]{2,1,0:T(8,128)S(1)} all-to-all(f32[32,8,128]{2,1,0:T(8,128)S(1)} %get-tuple-element.51), channel_id=1, replica_groups={{0,1,2,3,4,5,6,7,8,9,10,11,12,13,14,15,16,17,18,19,20,21,22,23,24,25,26..., dimensions={0} | all-to-all | bytes 262144 | tf_op jit(solution)/shard_map/all_to_all | solution.py:396
  68.5 0.9 shard_map.66
  69.4 9.6 %all_to_all.44.parts_ref = f32[8,16,128]{2,1,0:T(8,128)S(1)} all-to-all(f32[8,16,128]{2,1,0:T(8,128)S(1)} %shard_map.66), channel_id=1, replica_groups={{0,32,64,96,128,160,192,224},{16,48,80,112,144,176,208,240},{1,33,65,97..., dimensions={0} | all-to-all | bytes 131072 | tf_op jit(solution)/shard_map/all_to_all | solution.py:392
  79.0 0.8 shard_map.67
  79.9 12.4 %all_to_all.45.parts_ref = f32[32,8,128]{2,1,0:T(8,128)S(1)} all-to-all(f32[32,8,128]{2,1,0:T(8,128)S(1)} %get-tuple-element.53), channel_id=1, replica_groups={{0,1,2,3,4,5,6,7,8,9,10,11,12,13,14,15,16,17,18,19,20,21,22,23,24,25,26..., dimensions={0} | all-to-all | bytes 262144 | tf_op jit(solution)/shard_map/all_to_all | solution.py:396
  92.2 2.0 %shard_map.68.diff_ref = bf16[1024,2048]{1,0:T(8,128)(2,1)S(1)} custom-call(f32[1024,2048]{1,0:T(8,128)S(1)} %get-tuple-element.44.e_ref, f32[1024,2048]{1,0:T(8,128)S(1)} %get-tuple-element.46.s_ref, f32[16,128]{1,0:T(8,128)S(1)} %get-tuple-element.52.c_ref, f32[32,8,128]{2,1,0:T(8,128)S(1)} %all_to_all.45.parts_ref, ...), custom_call_target="tpu_custom_call" | custom-call | tf_op jit(solution)/shard_map/pallas_call | solution.py:41
  94.2 1.8 %shard_map.69 = (f32[512,256]{1,0:T(8,128)S(1)}, f32[512,256]{1,0:T(8,128)S(1)}) custom-call(s32[2]{0:T(128)S(1)} %pad_add_fusion.where_ref, bf16[1024,2048]{1,0:T(8,128)(2,1)S(1)} %shard_map.68.diff_ref, bf16[2048,256]{1,0:T(8,128)(2,1)S(1)} %get-tuple-element.54.back_ref), custom_call_target="tpu_custom_call" | custom-call | flops 1073741824 | tf_op jit(solution)/shard_map/pallas_call | solution.py:416
  96.6 3.5 %shard_map.70 = (f32[32,2048]{1,0:T(8,128)}, f32[32,2048]{1,0:T(8,128)}, f32[32,2048]{1,0:T(8,128)}, f32[32,2048]{1,0:T(8,128)}, f32[16,2048]{1,0:T(8,128)}, /*i...) custom-call(s32[2]{0:T(128)S(1)} %pad_add_fusion.where_ref, ...), custom_call_target="tpu_custom_call" | custom-call | flops 1073741824 | tf_op jit(solution)/shard_map/pallas_call | solution.py:492
  100.4 1.5 %collective-permute-start.2 = (f32[16,2048]{1,0:T(8,128)}, f32[16,2048]{1,0:T(8,128)S(1)}, u32[]{:S(2)}, u32[]{:S(2)}) collective-permute-start(f32[16,2048]{1,0:T(8,128)} %get-tuple-element.65), channel_id=1, source_target_pairs={{0,32},{16,48},{32,64},{48,80},{64,96},{80,112},{96,128},{112,144}... | collective-permute-start | bytes 393224 | tf_op jit(solution)/shard_map/ppermute | solution.py:386
  101.8 0.9 shard_map.75
  102.7 3.7 %all-to-all-start.6 = ((f32[16,32,256]{2,1,0:T(8,128)}), f32[16,32,256]{2,1,0:T(8,128)S(1)}, u32[]{:S(2)}, u32[]{:S(2)}) async-start(f32[16,32,256]{2,1,0:T(8,128)} %bitcast.2), calls=%async_computation.6 | async-start | bytes 1048576 | tf_op jit(solution)/shard_map/all_to_all | solution.py:517
  106.4 0.9 copy-done.8
  107.5 1.4 collective-permute-start.6
  109.2 5.6 %collective-permute-done.6.got_ref = f32[32,2048]{1,0:T(8,128)S(1)} collective-permute-done((f32[32,2048]{1,0:T(8,128)S(1)}, f32[32,2048]{1,0:T(8,128)S(1)}, u32[]{:S(2)}, u32[]{:S(2)}) %collective-permute-start.6) | collective-permute-done | bytes 262176 | tf_op jit(solution)/shard_map/ppermute | solution.py:386
  114.9 2.8 %collective-permute-start.7 = (f32[32,2048]{1,0:T(8,128)S(1)}, f32[32,2048]{1,0:T(8,128)S(1)}, u32[]{:S(2)}, u32[]{:S(2)}) collective-permute-start(f32[32,2048]{1,0:T(8,128)S(1)} %shard_map.74), channel_id=1, source_target_pairs={{0,224},{16,240},{32,0},{48,16},{64,32},{80,48},{96,64},{112,80},{... | collective-permute-start | bytes 786440 | tf_op jit(solution)/shard_map/ppermute | solution.py:386
  117.8 0.9 shard_map.76
  118.7 6.3 %all-to-all-start.7 = ((f32[16,32,256]{2,1,0:T(8,128)}), f32[16,32,256]{2,1,0:T(8,128)S(1)}, u32[]{:S(2)}, u32[]{:S(2)}) async-start(f32[16,32,256]{2,1,0:T(8,128)} %shard_map.76), calls=%async_computation.7 | async-start | bytes 1048576 | tf_op jit(solution)/shard_map/all_to_all | solution.py:524
  125.5 2.7 %collective-permute-start.10 = (f32[32,2048]{1,0:T(8,128)S(1)}, f32[32,2048]{1,0:T(8,128)S(1)}, u32[]{:S(2)}, u32[]{:S(2)}) collective-permute-start(f32[32,2048]{1,0:T(8,128)S(1)} %shard_map.78), channel_id=1, source_target_pairs={{0,224},{16,240},{32,0},{48,16},{64,32},{80,48},{96,64},{112,80},{... | collective-permute-start | bytes 786440 | tf_op jit(solution)/shard_map/ppermute | solution.py:386
  128.2 3.9 %collective-permute-done.9.up_ref = f32[32,2048]{1,0:T(8,128)S(1)} collective-permute-done((f32[32,2048]{1,0:T(8,128)S(1)}, f32[32,2048]{1,0:T(8,128)S(1)}, u32[]{:S(2)}, u32[]{:S(2)}) %collective-permute-start.9) | collective-permute-done | bytes 262176 | tf_op jit(solution)/shard_map/ppermute | solution.py:386
  132.1 2.3 %all-to-all-done.7 = f32[16,32,256]{2,1,0:T(8,128)S(1)} async-done(((f32[16,32,256]{2,1,0:T(8,128)}), f32[16,32,256]{2,1,0:T(8,128)S(1)}, u32[]{:S(2)}, u32[]{:S(2)}) %all-to-all-start.7) | async-done | bytes 524320 | tf_op jit(solution)/shard_map/all_to_all | solution.py:524
  134.5 3.2 %collective-permute-start.11 = (f32[16,2048]{1,0:T(8,128)S(1)}, f32[16,2048]{1,0:T(8,128)S(1)}, u32[]{:S(2)}, u32[]{:S(2)}) collective-permute-start(f32[16,2048]{1,0:T(8,128)S(1)} %get-tuple-element.75), channel_id=1, source_target_pairs={{0,16},{16,0},{32,48},{48,32},{64,80},{80,64},{96,112},{112,96},{1... | collective-permute-start | bytes 393224 | tf_op jit(solution)/shard_map/ppermute | solution.py:382
  138.7 2.1 %shard_map.81 = (f32[4,256,256]{2,1,0:T(8,128)}, f32[16,4096]{1,0:T(8,128)}) custom-call(s32[2]{0:T(128)S(1)} %pad_add_fusion.where_ref, f32[16,2048]{1,0:T(8,128)S(1)} %get-tuple-element.74.keep_ref, f32[16,2048]{1,0:T(8,128)S(1)} %collective-permute-done.11.got_ref, f32[512,256]{1,0:T(8,128)S(1)} %bitcast.4, f32[512,256]{1,0:T(8,128)S(1)} %get-tuple-element.77.full_ref, ...), custom_call_target="tpu_custom_call" | custom-call | tf_op jit(solution)/shard_map/pallas_call | solution.py:545
  (44 shorter events, 4.6 us)
Async XLA Ops:
  3.2 4.9 %collective-permute-start = (f32[512,256]{1,0:T(8,128)S(1)}, f32[512,256]{1,0:T(8,128)S(1)}, u32[]{:S(2)}, u32[]{:S(2)}) collective-permute-start(f32[512,256]{1,0:T(8,128)S(1)} %get-tuple-element.41.own_ref), channel_id=1, source_target_pairs={{0,16},{16,0},{32,48},{48,32},{64,80},{80,64},{96,112},{112,96},{1... | collective-permute-start | bytes 1572872 | tf_op jit(solution)/shard_map/ppermute | solution.py:382
  6.5 3.5 %collective-permute-start.1 = (f32[512,256]{1,0:T(8,128)S(1)}, f32[512,256]{1,0:T(8,128)S(1)}, u32[]{:S(2)}, u32[]{:S(2)}) collective-permute-start(f32[512,256]{1,0:T(8,128)S(1)} %get-tuple-element.45.own_ref), channel_id=1, source_target_pairs={{0,16},{16,0},{32,48},{48,32},{64,80},{80,64},{96,112},{112,96},{1... | collective-permute-start | bytes 1572872 | tf_op jit(solution)/shard_map/ppermute | solution.py:382
  96.0 5.9 %collective-permute-start.8 = (f32[512,256]{1,0:T(8,128)S(1)}, f32[512,256]{1,0:T(8,128)S(1)}, u32[]{:S(2)}, u32[]{:S(2)}) collective-permute-start(f32[512,256]{1,0:T(8,128)S(1)} %get-tuple-element.56), channel_id=1, source_target_pairs={{0,16},{16,0},{32,48},{48,32},{64,80},{80,64},{96,112},{112,96},{1... | collective-permute-start | bytes 1572872 | tf_op jit(solution)/shard_map/ppermute | solution.py:382
  100.1 6.3 %collective-permute-start.5 = (f32[16,2048]{1,0:T(8,128)}, f32[16,2048]{1,0:T(8,128)S(1)}, u32[]{:S(2)}, u32[]{:S(2)}) collective-permute-start(f32[16,2048]{1,0:T(8,128)} %get-tuple-element.68), channel_id=1, source_target_pairs={{0,224},{16,240},{32,0},{48,16},{64,32},{80,48},{96,64},{112,80},{... | collective-permute-start | bytes 393224 | tf_op jit(solution)/shard_map/ppermute | solution.py:386
  100.4 8.5 %collective-permute-start.2 = (f32[16,2048]{1,0:T(8,128)}, f32[16,2048]{1,0:T(8,128)S(1)}, u32[]{:S(2)}, u32[]{:S(2)}) collective-permute-start(f32[16,2048]{1,0:T(8,128)} %get-tuple-element.65), channel_id=1, source_target_pairs={{0,32},{16,48},{32,64},{48,80},{64,96},{80,112},{96,128},{112,144}... | collective-permute-start | bytes 393224 | tf_op jit(solution)/shard_map/ppermute | solution.py:386
  102.7 6.2 %copy-start.7 = (f32[32,2048]{1,0:T(8,128)S(1)}, f32[32,2048]{1,0:T(8,128)}, u32[]{:S(2)}) copy-start(f32[32,2048]{1,0:T(8,128)} %get-tuple-element.64.rel_hbm) | copy-start | bytes 786436
  102.7 15.1 %all-to-all-start.6 = ((f32[16,32,256]{2,1,0:T(8,128)}), f32[16,32,256]{2,1,0:T(8,128)S(1)}, u32[]{:S(2)}, u32[]{:S(2)}) async-start(f32[16,32,256]{2,1,0:T(8,128)} %bitcast.2), calls=%async_computation.6 | async-start | bytes 1048576 | tf_op jit(solution)/shard_map/all_to_all | solution.py:517
  106.4 1.0 copy-start.8
  107.4 7.4 %copy-start.5 = (f32[32,2048]{1,0:T(8,128)S(1)}, f32[32,2048]{1,0:T(8,128)}, u32[]{:S(2)}) copy-start(f32[32,2048]{1,0:T(8,128)} %get-tuple-element.66.rel_hbm) | copy-start | bytes 786436
  107.5 10.2 %copy-start.4 = (f32[32,2048]{1,0:T(8,128)S(1)}, f32[32,2048]{1,0:T(8,128)}, u32[]{:S(2)}) copy-start(f32[32,2048]{1,0:T(8,128)} %get-tuple-element.63.rel_hbm) | copy-start | bytes 786436
  107.5 17.8 %copy-start.3 = (f32[32,2048]{1,0:T(8,128)S(1)}, f32[32,2048]{1,0:T(8,128)}, u32[]{:S(2)}) copy-start(f32[32,2048]{1,0:T(8,128)} %get-tuple-element.62.rel_hbm) | copy-start | bytes 786436
  107.5 18.0 %copy-start.2 = (f32[32,2048]{1,0:T(8,128)S(1)}, f32[32,2048]{1,0:T(8,128)}, u32[]{:S(2)}) copy-start(f32[32,2048]{1,0:T(8,128)} %get-tuple-element.69.rel_hbm) | copy-start | bytes 786436
  107.5 7.4 %collective-permute-start.6 = (f32[32,2048]{1,0:T(8,128)S(1)}, f32[32,2048]{1,0:T(8,128)S(1)}, u32[]{:S(2)}, u32[]{:S(2)}) collective-permute-start(f32[32,2048]{1,0:T(8,128)S(1)} %shard_map.73), channel_id=1, source_target_pairs={{0,224},{16,240},{32,0},{48,16},{64,32},{80,48},{96,64},{112,80},{... | collective-permute-start | bytes 786440 | tf_op jit(solution)/shard_map/ppermute | solution.py:386
  108.9 25.5 %copy-start.1 = (f32[32,2048]{1,0:T(8,128)S(1)}, f32[32,2048]{1,0:T(8,128)}, u32[]{:S(2)}) copy-start(f32[32,2048]{1,0:T(8,128)} %get-tuple-element.61.rel_hbm) | copy-start | bytes 786436
  108.9 28.8 %copy-start = (bf16[4,256,256]{2,1,0:T(8,128)(2,1)S(1)}, bf16[4,256,256]{2,1,0:T(8,128)(2,1)}, u32[]{:S(2)}) copy-start(bf16[4,256,256]{2,1,0:T(8,128)(2,1)} %feats_ref.1) | copy-start | bytes 1572868
  108.9 28.8 %copy-start.6 = (s32[4,128]{1,0:T(4,128)S(1)}, s32[4,128]{1,0:T(4,128)}, u32[]{:S(2)}) copy-start(s32[4,128]{1,0:T(4,128)} %mask_ref) | copy-start | bytes 6148
  109.0 8.7 %collective-permute-start.3 = (f32[32,2048]{1,0:T(8,128)S(1)}, f32[32,2048]{1,0:T(8,128)S(1)}, u32[]{:S(2)}, u32[]{:S(2)}) collective-permute-start(f32[32,2048]{1,0:T(8,128)S(1)} %shard_map.71), channel_id=1, source_target_pairs={{0,32},{16,48},{32,64},{48,80},{64,96},{80,112},{96,128},{112,144}... | collective-permute-start | bytes 786440 | tf_op jit(solution)/shard_map/ppermute | solution.py:386
  114.9 10.1 %collective-permute-start.7 = (f32[32,2048]{1,0:T(8,128)S(1)}, f32[32,2048]{1,0:T(8,128)S(1)}, u32[]{:S(2)}, u32[]{:S(2)}) collective-permute-start(f32[32,2048]{1,0:T(8,128)S(1)} %shard_map.74), channel_id=1, source_target_pairs={{0,224},{16,240},{32,0},{48,16},{64,32},{80,48},{96,64},{112,80},{... | collective-permute-start | bytes 786440 | tf_op jit(solution)/shard_map/ppermute | solution.py:386
  117.7 7.5 %collective-permute-start.4 = (f32[32,2048]{1,0:T(8,128)S(1)}, f32[32,2048]{1,0:T(8,128)S(1)}, u32[]{:S(2)}, u32[]{:S(2)}) collective-permute-start(f32[32,2048]{1,0:T(8,128)S(1)} %shard_map.72), channel_id=1, source_target_pairs={{0,32},{16,48},{32,64},{48,80},{64,96},{80,112},{96,128},{112,144}... | collective-permute-start | bytes 786440 | tf_op jit(solution)/shard_map/ppermute | solution.py:386
  118.7 15.8 %all-to-all-start.7 = ((f32[16,32,256]{2,1,0:T(8,128)}), f32[16,32,256]{2,1,0:T(8,128)S(1)}, u32[]{:S(2)}, u32[]{:S(2)}) async-start(f32[16,32,256]{2,1,0:T(8,128)} %shard_map.76), calls=%async_computation.7 | async-start | bytes 1048576 | tf_op jit(solution)/shard_map/all_to_all | solution.py:524
  125.3 6.8 %collective-permute-start.9 = (f32[32,2048]{1,0:T(8,128)S(1)}, f32[32,2048]{1,0:T(8,128)S(1)}, u32[]{:S(2)}, u32[]{:S(2)}) collective-permute-start(f32[32,2048]{1,0:T(8,128)S(1)} %shard_map.77), channel_id=1, source_target_pairs={{0,32},{16,48},{32,64},{48,80},{64,96},{80,112},{96,128},{112,144}... | collective-permute-start | bytes 786440 | tf_op jit(solution)/shard_map/ppermute | solution.py:386
  125.5 8.9 %collective-permute-start.10 = (f32[32,2048]{1,0:T(8,128)S(1)}, f32[32,2048]{1,0:T(8,128)S(1)}, u32[]{:S(2)}, u32[]{:S(2)}) collective-permute-start(f32[32,2048]{1,0:T(8,128)S(1)} %shard_map.78), channel_id=1, source_target_pairs={{0,224},{16,240},{32,0},{48,16},{64,32},{80,48},{96,64},{112,80},{... | collective-permute-start | bytes 786440 | tf_op jit(solution)/shard_map/ppermute | solution.py:386
  134.5 4.1 %collective-permute-start.11 = (f32[16,2048]{1,0:T(8,128)S(1)}, f32[16,2048]{1,0:T(8,128)S(1)}, u32[]{:S(2)}, u32[]{:S(2)}) collective-permute-start(f32[16,2048]{1,0:T(8,128)S(1)} %get-tuple-element.75), channel_id=1, source_target_pairs={{0,16},{16,0},{32,48},{48,32},{64,80},{80,64},{96,112},{112,96},{1... | collective-permute-start | bytes 393224 | tf_op jit(solution)/shard_map/ppermute | solution.py:382

commit v10 on v9

--- a/solution.py
+++ b/solution.py
@@ -125,7 +125,7 @@
 def teacher_exp_kernel(where_ref, own_ref, other_ref, unit_ref, e_ref, col_ref):
     half = own_ref.shape[0]
     wide = unit_ref.shape[1]
-    block = 256
+    block = 512
     for w in range(wide // WIDE):
         columns = pl.ds(w * WIDE, WIDE)
         unit = unit_ref[:, columns]
@@ -152,7 +152,7 @@
 ):
     half = own_ref.shape[0]
     wide = unit_ref.shape[1]
-    block = 256
+    block = 512
     for side, ref in enumerate((own_ref, other_ref)):
         turned_ref[:, core_rows(where_ref, side, half)] = ref[...].T.astype(BF16)
     for w in range(wide // WIDE):
@@ -461,15 +461,15 @@
     mass = None
     for sweep in range(ITERS):
         col_parts = all_columns(col_out)
-        extra = [mass_acc] if sweep == 0 else []
+        extra = [mass_acc] if sweep == 1 else []
         row_out, c = call(
-            row_kernel if sweep else row_mass_kernel,
+            row_mass_kernel if extra else row_kernel,
             [shape(ROWS, row_tiles * (1 + len(extra)), LANES), shape(lane_tiles, LANES)],
             e, col_parts, *extra,
             scratch=[VMEM((tokens, LANES), F32)],
         )
         row_parts = all_rows(row_out)
-        if sweep == 0:
+        if extra:
             mass = row_parts
         if sweep < ITERS - 1:
             (col_out,) = call(

time: 142 us -> 141 us (level)
  no operation moved by 1% of the time
where the time goes in v10:
time: 141 us
  blocking collectives  74.8 us (53%)
  starting transfers between devices  26.2 us (19%)
  Pallas kernels  24.4 us (17%)
  waiting for transfers between devices  13.4 us (10%)
    all_to_all x3, blocking collectives, all_rows(): lax.all_to_all(x, ('batch', 'proto'), 0, 0, axis_index_groups=ROW_GROUPS)  42.1 us
    all_to_all x3, blocking collectives, all_columns(): return lax.all_to_all(x, 'batch', 0, 0, axis_index_groups=Z_GROUPS)  32.7 us
    pallas_call x10, Pallas kernels, call(): pl.pallas_call(kernel, out_shape=outs, in_specs=[whole()] * len(args), ou...  10.2 us
    ppermute x8, waiting for transfers between devices, along_z(): lax.ppermute(x, 'batch', [(i, (i // 2 + d) % Z * 2 + i % 2) for i in rang...  9.84 us
    ppermute x8, starting transfers between devices, along_z(): lax.ppermute(x, 'batch', [(i, (i // 2 + d) % Z * 2 + i % 2) for i in rang...  8.99 us
    ppermute x4, starting transfers between devices, other_core(): return lax.ppermute(x, 'batch', [(i, i ^ 1) for i in range(RING)])  7.2 us
    all_to_all x1, starting transfers between devices, on_device(): gz = lax.all_to_all(gz_share, 'proto', 0, 0).reshape(own, width)  6.27 us
    pallas_call x3, Pallas kernels, placed(): pl.pallas_call(kernel, in_specs=[scalars] + [whole()] * len(args), out_sp...  5.73 us
  transfers between devices with their start and end apart: 14, of which 6 were waited for; matrix products, arithmetic and copies ran while one was open for 0% of the time, Pallas kernels for 6%

profile of v10, /device:TPU:1, one launch (start us, length us, event | category | flops | bytes accessed | tf_op | source)
XLA Modules:
  0.0 140.9 jit_solution(8557380892687655569)
XLA Ops:
  0.7 2.5 %shard_map.59 = (f32[512,256]{1,0:T(8,128)S(1)}, f32[512,256]{1,0:T(8,128)S(1)}, bf16[256,2048]{1,0:T(8,128)(2,1)S(1)}) custom-call(s32[2]{0:T(128)S(1)} %pad_add_fusion.where_ref, bf16[4,256,256]{2,1,0:T(8,128)(2,1)} %teacher_hbm.1, bf16[4,256,256]{2,1,0:T(8,128)(2,1)} %feats_ref.1, s32[4,128]{1,0:T(4,128)} %mask_ref, bf16[256,4096]{1,0:T(8,128)(2,1)} %proto_hbm.1), custom_call_target="tpu_custom_call" | custom-call | tf_op jit(solution)/shard_map/pallas_call | solution.py:426
  3.2 3.3 %collective-permute-start = (f32[512,256]{1,0:T(8,128)S(1)}, f32[512,256]{1,0:T(8,128)S(1)}, u32[]{:S(2)}, u32[]{:S(2)}) collective-permute-start(f32[512,256]{1,0:T(8,128)S(1)} %get-tuple-element.41.own_ref), channel_id=1, source_target_pairs={{0,16},{16,0},{32,48},{48,32},{64,80},{80,64},{96,112},{112,96},{1... | collective-permute-start | bytes 1572872 | tf_op jit(solution)/shard_map/ppermute | solution.py:382
  8.1 1.9 %shard_map.61 = (f32[1024,2048]{1,0:T(8,128)S(1)}, f32[8,16,128]{2,1,0:T(8,128)S(1)}) custom-call(s32[2]{0:T(128)S(1)} %pad_add_fusion.where_ref, f32[512,256]{1,0:T(8,128)S(1)} %get-tuple-element.41.own_ref, f32[512,256]{1,0:T(8,128)S(1)} %collective-permute-done.other_ref, bf16[256,2048]{1,0:T(8,128)(2,1)S(1)} %get-tuple-element.43.unit_ref), custom_call_target="tpu_custom_call" | custom-call | flops 1073741824 | tf_op jit(solution)/shard_map/pallas_call | solution.py:416
  10.0 2.0 %shard_map.62 = (f32[1024,2048]{1,0:T(8,128)S(1)}, f32[1024,128]{1,0:T(8,128)S(1)}, bf16[256,1024]{1,0:T(8,128)(2,1)S(1)}) custom-call(s32[2]{0:T(128)S(1)} %pad_add_fusion.where_ref, f32[512,256]{1,0:T(8,128)S(1)} %get-tuple-element.45.own_ref, f32[512,256]{1,0:T(8,128)S(1)} %collective-permute-done.1.other_ref, ...), custom_call_target="tpu_custom_call" | custom-call | flops 1073741824 | tf_op jit(solution)/shard_map/pallas_call | solution.py:416
  12.0 13.5 %all_to_all.40.parts_ref = f32[8,16,128]{2,1,0:T(8,128)S(1)} all-to-all(f32[8,16,128]{2,1,0:T(8,128)S(1)} %get-tuple-element.49), channel_id=1, replica_groups={{0,32,64,96,128,160,192,224},{16,48,80,112,144,176,208,240},{1,33,65,97..., dimensions={0} | all-to-all | bytes 131072 | tf_op jit(solution)/shard_map/all_to_all | solution.py:392
  25.5 1.2 shard_map.63
  26.7 16.2 %all_to_all.41.parts_ref = f32[32,8,128]{2,1,0:T(8,128)S(1)} all-to-all(f32[32,8,128]{2,1,0:T(8,128)S(1)} %get-tuple-element.50), channel_id=1, replica_groups={{0,1,2,3,4,5,6,7,8,9,10,11,12,13,14,15,16,17,18,19,20,21,22,23,24,25,26..., dimensions={0} | all-to-all | bytes 262144 | tf_op jit(solution)/shard_map/all_to_all | solution.py:396
  42.9 0.9 shard_map.64
  43.8 9.6 %all_to_all.42.parts_ref = f32[8,16,128]{2,1,0:T(8,128)S(1)} all-to-all(f32[8,16,128]{2,1,0:T(8,128)S(1)} %shard_map.64), channel_id=1, replica_groups={{0,32,64,96,128,160,192,224},{16,48,80,112,144,176,208,240},{1,33,65,97..., dimensions={0} | all-to-all | bytes 131072 | tf_op jit(solution)/shard_map/all_to_all | solution.py:392
  53.4 1.5 %shard_map.65 = (f32[32,16,128]{2,1,0:T(8,128)S(1)}, f32[16,128]{1,0:T(8,128)}) custom-call(f32[1024,2048]{1,0:T(8,128)S(1)} %get-tuple-element.44.e_ref, f32[8,16,128]{2,1,0:T(8,128)S(1)} %all_to_all.42.parts_ref, f32[1024,128]{1,0:T(8,128)S(1)} %get-tuple-element.48.mass_ref), custom_call_target="tpu_custom_call" | custom-call | tf_op jit(solution)/shard_map/pallas_call | solution.py:41
  54.9 13.1 %all_to_all.43.parts_ref.mass_ref = f32[32,16,128]{2,1,0:T(8,128)S(1)} all-to-all(f32[32,16,128]{2,1,0:T(8,128)S(1)} %get-tuple-element.51), channel_id=1, replica_groups={{0,1,2,3,4,5,6,7,8,9,10,11,12,13,14,15,16,17,18,19,20,21,22,23,24,25,26..., dimensions={0} | all-to-all | bytes 524288 | tf_op jit(solution)/shard_map/all_to_all | solution.py:396
  68.0 0.9 shard_map.66
  68.9 9.6 %all_to_all.44.parts_ref = f32[8,16,128]{2,1,0:T(8,128)S(1)} all-to-all(f32[8,16,128]{2,1,0:T(8,128)S(1)} %shard_map.66), channel_id=1, replica_groups={{0,32,64,96,128,160,192,224},{16,48,80,112,144,176,208,240},{1,33,65,97..., dimensions={0} | all-to-all | bytes 131072 | tf_op jit(solution)/shard_map/all_to_all | solution.py:392
  78.5 0.8 shard_map.67
  79.4 12.8 %all_to_all.45.parts_ref = f32[32,8,128]{2,1,0:T(8,128)S(1)} all-to-all(f32[32,8,128]{2,1,0:T(8,128)S(1)} %get-tuple-element.53), channel_id=1, replica_groups={{0,1,2,3,4,5,6,7,8,9,10,11,12,13,14,15,16,17,18,19,20,21,22,23,24,25,26..., dimensions={0} | all-to-all | bytes 262144 | tf_op jit(solution)/shard_map/all_to_all | solution.py:396
  92.2 2.0 %shard_map.68.diff_ref = bf16[1024,2048]{1,0:T(8,128)(2,1)S(1)} custom-call(f32[1024,2048]{1,0:T(8,128)S(1)} %get-tuple-element.44.e_ref, f32[1024,2048]{1,0:T(8,128)S(1)} %get-tuple-element.46.s_ref, f32[16,128]{1,0:T(8,128)S(1)} %get-tuple-element.52.c_ref, f32[32,8,128]{2,1,0:T(8,128)S(1)} %all_to_all.45.parts_ref, ...), custom_call_target="tpu_custom_call" | custom-call | tf_op jit(solution)/shard_map/pallas_call | solution.py:41
  94.2 1.8 %shard_map.69 = (f32[512,256]{1,0:T(8,128)S(1)}, f32[512,256]{1,0:T(8,128)S(1)}) custom-call(s32[2]{0:T(128)S(1)} %pad_add_fusion.where_ref, bf16[1024,2048]{1,0:T(8,128)(2,1)S(1)} %shard_map.68.diff_ref, bf16[2048,256]{1,0:T(8,128)(2,1)S(1)} %get-tuple-element.54.back_ref), custom_call_target="tpu_custom_call" | custom-call | flops 1073741824 | tf_op jit(solution)/shard_map/pallas_call | solution.py:416
  96.6 3.5 %shard_map.70 = (f32[32,2048]{1,0:T(8,128)}, f32[32,2048]{1,0:T(8,128)}, f32[32,2048]{1,0:T(8,128)}, f32[32,2048]{1,0:T(8,128)}, f32[16,2048]{1,0:T(8,128)}, /*i...) custom-call(s32[2]{0:T(128)S(1)} %pad_add_fusion.where_ref, ...), custom_call_target="tpu_custom_call" | custom-call | flops 1073741824 | tf_op jit(solution)/shard_map/pallas_call | solution.py:492
  100.3 1.5 %collective-permute-start.2 = (f32[16,2048]{1,0:T(8,128)}, f32[16,2048]{1,0:T(8,128)S(1)}, u32[]{:S(2)}, u32[]{:S(2)}) collective-permute-start(f32[16,2048]{1,0:T(8,128)} %get-tuple-element.65), channel_id=1, source_target_pairs={{0,32},{16,48},{32,64},{48,80},{64,96},{80,112},{96,128},{112,144}... | collective-permute-start | bytes 393224 | tf_op jit(solution)/shard_map/ppermute | solution.py:386
  101.8 0.9 shard_map.75
  102.7 3.7 %all-to-all-start.6 = ((f32[16,32,256]{2,1,0:T(8,128)}), f32[16,32,256]{2,1,0:T(8,128)S(1)}, u32[]{:S(2)}, u32[]{:S(2)}) async-start(f32[16,32,256]{2,1,0:T(8,128)} %bitcast.2), calls=%async_computation.6 | async-start | bytes 1048576 | tf_op jit(solution)/shard_map/all_to_all | solution.py:517
  106.4 0.9 copy-done.8
  107.4 1.4 collective-permute-start.6
  109.2 5.6 %collective-permute-done.6.got_ref = f32[32,2048]{1,0:T(8,128)S(1)} collective-permute-done((f32[32,2048]{1,0:T(8,128)S(1)}, f32[32,2048]{1,0:T(8,128)S(1)}, u32[]{:S(2)}, u32[]{:S(2)}) %collective-permute-start.6) | collective-permute-done | bytes 262176 | tf_op jit(solution)/shard_map/ppermute | solution.py:386
  114.9 2.8 %collective-permute-start.7 = (f32[32,2048]{1,0:T(8,128)S(1)}, f32[32,2048]{1,0:T(8,128)S(1)}, u32[]{:S(2)}, u32[]{:S(2)}) collective-permute-start(f32[32,2048]{1,0:T(8,128)S(1)} %shard_map.74), channel_id=1, source_target_pairs={{0,224},{16,240},{32,0},{48,16},{64,32},{80,48},{96,64},{112,80},{... | collective-permute-start | bytes 786440 | tf_op jit(solution)/shard_map/ppermute | solution.py:386
  117.8 0.9 shard_map.76
  118.7 6.3 %all-to-all-start.7 = ((f32[16,32,256]{2,1,0:T(8,128)}), f32[16,32,256]{2,1,0:T(8,128)S(1)}, u32[]{:S(2)}, u32[]{:S(2)}) async-start(f32[16,32,256]{2,1,0:T(8,128)} %shard_map.76), calls=%async_computation.7 | async-start | bytes 1048576 | tf_op jit(solution)/shard_map/all_to_all | solution.py:524
  125.5 2.7 %collective-permute-start.10 = (f32[32,2048]{1,0:T(8,128)S(1)}, f32[32,2048]{1,0:T(8,128)S(1)}, u32[]{:S(2)}, u32[]{:S(2)}) collective-permute-start(f32[32,2048]{1,0:T(8,128)S(1)} %shard_map.78), channel_id=1, source_target_pairs={{0,224},{16,240},{32,0},{48,16},{64,32},{80,48},{96,64},{112,80},{... | collective-permute-start | bytes 786440 | tf_op jit(solution)/shard_map/ppermute | solution.py:386
  128.2 3.9 %collective-permute-done.9.up_ref = f32[32,2048]{1,0:T(8,128)S(1)} collective-permute-done((f32[32,2048]{1,0:T(8,128)S(1)}, f32[32,2048]{1,0:T(8,128)S(1)}, u32[]{:S(2)}, u32[]{:S(2)}) %collective-permute-start.9) | collective-permute-done | bytes 262176 | tf_op jit(solution)/shard_map/ppermute | solution.py:386
  132.1 2.3 %all-to-all-done.7 = f32[16,32,256]{2,1,0:T(8,128)S(1)} async-done(((f32[16,32,256]{2,1,0:T(8,128)}), f32[16,32,256]{2,1,0:T(8,128)S(1)}, u32[]{:S(2)}, u32[]{:S(2)}) %all-to-all-start.7) | async-done | bytes 524320 | tf_op jit(solution)/shard_map/all_to_all | solution.py:524
  134.5 3.2 %collective-permute-start.11 = (f32[16,2048]{1,0:T(8,128)S(1)}, f32[16,2048]{1,0:T(8,128)S(1)}, u32[]{:S(2)}, u32[]{:S(2)}) collective-permute-start(f32[16,2048]{1,0:T(8,128)S(1)} %get-tuple-element.75), channel_id=1, source_target_pairs={{0,16},{16,0},{32,48},{48,32},{64,80},{80,64},{96,112},{112,96},{1... | collective-permute-start | bytes 393224 | tf_op jit(solution)/shard_map/ppermute | solution.py:382
  138.6 2.1 %shard_map.81 = (f32[4,256,256]{2,1,0:T(8,128)}, f32[16,4096]{1,0:T(8,128)}) custom-call(s32[2]{0:T(128)S(1)} %pad_add_fusion.where_ref, f32[16,2048]{1,0:T(8,128)S(1)} %get-tuple-element.74.keep_ref, f32[16,2048]{1,0:T(8,128)S(1)} %collective-permute-done.11.got_ref, f32[512,256]{1,0:T(8,128)S(1)} %bitcast.4, f32[512,256]{1,0:T(8,128)S(1)} %get-tuple-element.77.full_ref, ...), custom_call_target="tpu_custom_call" | custom-call | tf_op jit(solution)/shard_map/pallas_call | solution.py:545
  (44 shorter events, 4.6 us)
Async XLA Ops:
  3.2 4.9 %collective-permute-start = (f32[512,256]{1,0:T(8,128)S(1)}, f32[512,256]{1,0:T(8,128)S(1)}, u32[]{:S(2)}, u32[]{:S(2)}) collective-permute-start(f32[512,256]{1,0:T(8,128)S(1)} %get-tuple-element.41.own_ref), channel_id=1, source_target_pairs={{0,16},{16,0},{32,48},{48,32},{64,80},{80,64},{96,112},{112,96},{1... | collective-permute-start | bytes 1572872 | tf_op jit(solution)/shard_map/ppermute | solution.py:382
  6.5 3.5 %collective-permute-start.1 = (f32[512,256]{1,0:T(8,128)S(1)}, f32[512,256]{1,0:T(8,128)S(1)}, u32[]{:S(2)}, u32[]{:S(2)}) collective-permute-start(f32[512,256]{1,0:T(8,128)S(1)} %get-tuple-element.45.own_ref), channel_id=1, source_target_pairs={{0,16},{16,0},{32,48},{48,32},{64,80},{80,64},{96,112},{112,96},{1... | collective-permute-start | bytes 1572872 | tf_op jit(solution)/shard_map/ppermute | solution.py:382
  95.9 5.9 %collective-permute-start.8 = (f32[512,256]{1,0:T(8,128)S(1)}, f32[512,256]{1,0:T(8,128)S(1)}, u32[]{:S(2)}, u32[]{:S(2)}) collective-permute-start(f32[512,256]{1,0:T(8,128)S(1)} %get-tuple-element.56), channel_id=1, source_target_pairs={{0,16},{16,0},{32,48},{48,32},{64,80},{80,64},{96,112},{112,96},{1... | collective-permute-start | bytes 1572872 | tf_op jit(solution)/shard_map/ppermute | solution.py:382
  100.1 6.3 %collective-permute-start.5 = (f32[16,2048]{1,0:T(8,128)}, f32[16,2048]{1,0:T(8,128)S(1)}, u32[]{:S(2)}, u32[]{:S(2)}) collective-permute-start(f32[16,2048]{1,0:T(8,128)} %get-tuple-element.68), channel_id=1, source_target_pairs={{0,224},{16,240},{32,0},{48,16},{64,32},{80,48},{96,64},{112,80},{... | collective-permute-start | bytes 393224 | tf_op jit(solution)/shard_map/ppermute | solution.py:386
  100.3 8.5 %collective-permute-start.2 = (f32[16,2048]{1,0:T(8,128)}, f32[16,2048]{1,0:T(8,128)S(1)}, u32[]{:S(2)}, u32[]{:S(2)}) collective-permute-start(f32[16,2048]{1,0:T(8,128)} %get-tuple-element.65), channel_id=1, source_target_pairs={{0,32},{16,48},{32,64},{48,80},{64,96},{80,112},{96,128},{112,144}... | collective-permute-start | bytes 393224 | tf_op jit(solution)/shard_map/ppermute | solution.py:386
  102.7 6.2 %copy-start.7 = (f32[32,2048]{1,0:T(8,128)S(1)}, f32[32,2048]{1,0:T(8,128)}, u32[]{:S(2)}) copy-start(f32[32,2048]{1,0:T(8,128)} %get-tuple-element.64.rel_hbm) | copy-start | bytes 786436
  102.7 15.1 %all-to-all-start.6 = ((f32[16,32,256]{2,1,0:T(8,128)}), f32[16,32,256]{2,1,0:T(8,128)S(1)}, u32[]{:S(2)}, u32[]{:S(2)}) async-start(f32[16,32,256]{2,1,0:T(8,128)} %bitcast.2), calls=%async_computation.6 | async-start | bytes 1048576 | tf_op jit(solution)/shard_map/all_to_all | solution.py:517
  106.4 1.0 copy-start.8
  107.4 7.4 %copy-start.5 = (f32[32,2048]{1,0:T(8,128)S(1)}, f32[32,2048]{1,0:T(8,128)}, u32[]{:S(2)}) copy-start(f32[32,2048]{1,0:T(8,128)} %get-tuple-element.66.rel_hbm) | copy-start | bytes 786436
  107.4 10.2 %copy-start.4 = (f32[32,2048]{1,0:T(8,128)S(1)}, f32[32,2048]{1,0:T(8,128)}, u32[]{:S(2)}) copy-start(f32[32,2048]{1,0:T(8,128)} %get-tuple-element.63.rel_hbm) | copy-start | bytes 786436
  107.4 17.8 %copy-start.3 = (f32[32,2048]{1,0:T(8,128)S(1)}, f32[32,2048]{1,0:T(8,128)}, u32[]{:S(2)}) copy-start(f32[32,2048]{1,0:T(8,128)} %get-tuple-element.62.rel_hbm) | copy-start | bytes 786436
  107.4 18.0 %copy-start.2 = (f32[32,2048]{1,0:T(8,128)S(1)}, f32[32,2048]{1,0:T(8,128)}, u32[]{:S(2)}) copy-start(f32[32,2048]{1,0:T(8,128)} %get-tuple-element.69.rel_hbm) | copy-start | bytes 786436
  107.4 7.4 %collective-permute-start.6 = (f32[32,2048]{1,0:T(8,128)S(1)}, f32[32,2048]{1,0:T(8,128)S(1)}, u32[]{:S(2)}, u32[]{:S(2)}) collective-permute-start(f32[32,2048]{1,0:T(8,128)S(1)} %shard_map.73), channel_id=1, source_target_pairs={{0,224},{16,240},{32,0},{48,16},{64,32},{80,48},{96,64},{112,80},{... | collective-permute-start | bytes 786440 | tf_op jit(solution)/shard_map/ppermute | solution.py:386
  108.9 25.5 %copy-start.1 = (f32[32,2048]{1,0:T(8,128)S(1)}, f32[32,2048]{1,0:T(8,128)}, u32[]{:S(2)}) copy-start(f32[32,2048]{1,0:T(8,128)} %get-tuple-element.61.rel_hbm) | copy-start | bytes 786436
  108.9 28.8 %copy-start = (bf16[4,256,256]{2,1,0:T(8,128)(2,1)S(1)}, bf16[4,256,256]{2,1,0:T(8,128)(2,1)}, u32[]{:S(2)}) copy-start(bf16[4,256,256]{2,1,0:T(8,128)(2,1)} %feats_ref.1) | copy-start | bytes 1572868
  108.9 28.8 %copy-start.6 = (s32[4,128]{1,0:T(4,128)S(1)}, s32[4,128]{1,0:T(4,128)}, u32[]{:S(2)}) copy-start(s32[4,128]{1,0:T(4,128)} %mask_ref) | copy-start | bytes 6148
  108.9 8.7 %collective-permute-start.3 = (f32[32,2048]{1,0:T(8,128)S(1)}, f32[32,2048]{1,0:T(8,128)S(1)}, u32[]{:S(2)}, u32[]{:S(2)}) collective-permute-start(f32[32,2048]{1,0:T(8,128)S(1)} %shard_map.71), channel_id=1, source_target_pairs={{0,32},{16,48},{32,64},{48,80},{64,96},{80,112},{96,128},{112,144}... | collective-permute-start | bytes 786440 | tf_op jit(solution)/shard_map/ppermute | solution.py:386
  114.9 10.1 %collective-permute-start.7 = (f32[32,2048]{1,0:T(8,128)S(1)}, f32[32,2048]{1,0:T(8,128)S(1)}, u32[]{:S(2)}, u32[]{:S(2)}) collective-permute-start(f32[32,2048]{1,0:T(8,128)S(1)} %shard_map.74), channel_id=1, source_target_pairs={{0,224},{16,240},{32,0},{48,16},{64,32},{80,48},{96,64},{112,80},{... | collective-permute-start | bytes 786440 | tf_op jit(solution)/shard_map/ppermute | solution.py:386
  117.7 7.5 %collective-permute-start.4 = (f32[32,2048]{1,0:T(8,128)S(1)}, f32[32,2048]{1,0:T(8,128)S(1)}, u32[]{:S(2)}, u32[]{:S(2)}) collective-permute-start(f32[32,2048]{1,0:T(8,128)S(1)} %shard_map.72), channel_id=1, source_target_pairs={{0,32},{16,48},{32,64},{48,80},{64,96},{80,112},{96,128},{112,144}... | collective-permute-start | bytes 786440 | tf_op jit(solution)/shard_map/ppermute | solution.py:386
  118.7 15.8 %all-to-all-start.7 = ((f32[16,32,256]{2,1,0:T(8,128)}), f32[16,32,256]{2,1,0:T(8,128)S(1)}, u32[]{:S(2)}, u32[]{:S(2)}) async-start(f32[16,32,256]{2,1,0:T(8,128)} %shard_map.76), calls=%async_computation.7 | async-start | bytes 1048576 | tf_op jit(solution)/shard_map/all_to_all | solution.py:524
  125.3 6.8 %collective-permute-start.9 = (f32[32,2048]{1,0:T(8,128)S(1)}, f32[32,2048]{1,0:T(8,128)S(1)}, u32[]{:S(2)}, u32[]{:S(2)}) collective-permute-start(f32[32,2048]{1,0:T(8,128)S(1)} %shard_map.77), channel_id=1, source_target_pairs={{0,32},{16,48},{32,64},{48,80},{64,96},{80,112},{96,128},{112,144}... | collective-permute-start | bytes 786440 | tf_op jit(solution)/shard_map/ppermute | solution.py:386
  125.5 8.9 %collective-permute-start.10 = (f32[32,2048]{1,0:T(8,128)S(1)}, f32[32,2048]{1,0:T(8,128)S(1)}, u32[]{:S(2)}, u32[]{:S(2)}) collective-permute-start(f32[32,2048]{1,0:T(8,128)S(1)} %shard_map.78), channel_id=1, source_target_pairs={{0,224},{16,240},{32,0},{48,16},{64,32},{80,48},{96,64},{112,80},{... | collective-permute-start | bytes 786440 | tf_op jit(solution)/shard_map/ppermute | solution.py:386
  134.5 4.1 %collective-permute-start.11 = (f32[16,2048]{1,0:T(8,128)S(1)}, f32[16,2048]{1,0:T(8,128)S(1)}, u32[]{:S(2)}, u32[]{:S(2)}) collective-permute-start(f32[16,2048]{1,0:T(8,128)S(1)} %get-tuple-element.75), channel_id=1, source_target_pairs={{0,16},{16,0},{32,48},{48,32},{64,80},{80,64},{96,112},{112,96},{1... | collective-permute-start | bytes 393224 | tf_op jit(solution)/shard_map/ppermute | solution.py:382
